TPU v7x, 32 devices: a whole 2x2x4 slice. The times are simulated.
32 devices in a mesh: band: 16 (over z, y, core), strip: 2 (over x).
Axes of the slice: x: 2, y: 2, z: 4, core: 2. Of those that a mesh axis runs over, the one named last changes fastest.
Arguments:
- activations: bfloat16 [16, 320, 12, 128], P('band', None, 'strip'), may hold values from -6 to 6
- out_grad: bfloat16 [16, 320, 12, 128], P('band', None, 'strip'), may hold values from -6 to 6
- kernel: bfloat16 [320, 9, 320], P('band', None, 'strip'), may hold values from -0.109375 to 0.109375
Outputs:
- input_grad: bfloat16 [16, 320, 12, 128], P('band', None, 'strip')
- kernel_grad: float32 [320, 9, 320], P('band', None, 'strip')
All inputs are finite; a program needn't handle non-finite values.
Results may differ from a plain program's by a relative error of at most 0.001.
Values may be sent and summed in bfloat16 or wider, within the bound.
No kernel may reach another device: no remote copies, remote signals or barrier semaphores. Data moves between devices by JAX's collectives and lax.ppermute only.
A program may use at most 64 MiB of HBM per device.

v0:
```python
import math

import jax
import jax.numpy as jnp
from jax import lax
from jax.sharding import PartitionSpec as P

OFFSETS = ((-1, -1), (-1, 0), (-1, 1), (0, -1), (0, 0), (0, 1), (1, -1), (1, 0), (1, 1))


def extended(cells, sides, width):
    for axis, dim in sides:
        count = lax.axis_size(axis)
        ends = count - 1
        head = lax.slice_in_dim(cells, 0, width, axis=dim)
        tail = lax.slice_in_dim(cells, cells.shape[dim] - width, cells.shape[dim], axis=dim)
        cells = jnp.concatenate(
            [
                lax.ppermute(tail, axis, [(i, (i + 1) % count) for i in range(ends)]),
                cells,
                lax.ppermute(head, axis, [((i + 1) % count, i) for i in range(ends)]),
            ],
            axis=dim,
        )
    return cells


def tap_slice(field, row_step, col_step):
    row_count = field.shape[2] - 2
    col_count = field.shape[3] - 2
    return field[
        :, :, 1 + row_step : 1 + row_step + row_count, 1 + col_step : 1 + col_step + col_count
    ]


def body(activations, out_grad, kernel):
    images = activations.shape[0]
    row_count = activations.shape[2]
    col_count = activations.shape[3]
    cell_total = images * lax.axis_size("band") * row_count * lax.axis_size("strip") * col_count
    grad_scale = 1.0 / math.sqrt(cell_total)
    grad_padded = extended(out_grad, (("strip", 2),), 1)
    grad_padded = jnp.pad(grad_padded, ((0, 0), (0, 0), (0, 0), (1, 1)))
    kernel_full_cols = lax.all_gather(kernel, "strip", axis=2, tiled=True)
    kernel_whole = lax.all_gather(kernel_full_cols, "band", axis=0, tiled=True)
    summed = jnp.zeros((images, kernel_whole.shape[0], row_count, col_count), jnp.float32)
    for tap_index, (row_step, col_step) in enumerate(OFFSETS):
        shifted = tap_slice(grad_padded, -row_step, -col_step)
        summed = summed + jnp.einsum(
            "io,bohw->bihw",
            kernel_whole[:, tap_index, :],
            shifted,
            preferred_element_type=jnp.float32,
        )
    input_grad = summed.astype(jnp.bfloat16)
    blocks = []
    for tap_index, (row_step, col_step) in enumerate(OFFSETS):
        grad_side = tap_slice(grad_padded, -row_step, -col_step)
        blocks.append(
            jnp.einsum("bihw,bohw->io", activations, grad_side, preferred_element_type=jnp.float32)
        )
    local_terms = jnp.stack(blocks, axis=1)
    partial_value = lax.psum_scatter(local_terms, "strip", scatter_dimension=2, tiled=True)
    kernel_sum = lax.psum_scatter(partial_value, "band", scatter_dimension=0, tiled=True)
    return (input_grad, kernel_sum * grad_scale)


def solution(mesh):
    in_specs = (
        P("band", None, "strip", None),
        P("band", None, "strip", None),
        P("band", None, "strip"),
    )
    out_specs = (P("band", None, "strip", None), P("band", None, "strip"))
    return jax.shard_map(body, mesh=mesh, in_specs=in_specs, out_specs=out_specs, check_vma=False)
```

profile of v0, /device:TPU:0, one launch (start us, length us, event | category | flops | bytes accessed | tf_op | source)
XLA Modules:
  0.0 203.2 jit_solution(4545481308751019310)
XLA Ops:
  8.0 0.0 copy-start
  8.0 0.0 copy-start.1
  8.0 0.0 reduce-scatter.3.cloned.1.call-start
  8.1 1.0 fusion.42
  9.1 4.8 %collective-permute-start = (bf16[1,320,1,128]{3,1,2,0:T(8,128)(2,1)S(1)}, bf16[1,320,1,128]{3,1,2,0:T(8,128)(2,1)S(1)}, u32[]{:S(2)}, u32[]{:S(2)}) collective-permute-start(bf16[1,320,1,128]{3,1,2,0:T(8,128)(2,1)S(1)} %get-tuple-element.15), channel_id=1, source_target_pairs={{0,1},{2,3},{4,5},{6,7},{8,9},{10,11},{12,13},{14,15},{16,17},{18,... | collective-permute-start | bytes 245768 | tf_op jit(solution)/shard_map/ppermute | solution.py:19
  13.9 1.3 collective-permute-start.1
  15.2 0.7 collective-permute-done
  16.0 4.3 %collective-permute-done.1 = bf16[1,320,1,128]{3,1,2,0:T(8,128)(2,1)S(1)} collective-permute-done((bf16[1,320,1,128]{3,1,2,0:T(8,128)(2,1)S(1)}, bf16[1,320,1,128]{3,1,2,0:T(8,128)(2,1)S(1)}, u32[]{:S(2)}, u32[]{:S(2)}) %collective-permute-start.1) | collective-permute-done | bytes 81952 | tf_op jit(solution)/shard_map/ppermute | solution.py:21
  20.3 1.7 fusion.6
  22.0 0.0 copy-done
  22.0 1.3 fusion.17
  23.2 0.0 copy-done.1
  23.3 1.2 fusion.16
  24.5 1.2 fusion.15
  25.7 1.3 fusion.14
  27.0 1.2 fusion.13
  28.2 1.2 fusion.12
  29.4 1.3 fusion.11
  30.7 1.2 fusion.10
  31.9 0.0 copy-start.2
  31.9 1.2 fusion.9
  33.1 0.0 reduce-scatter.3.cloned.1.call-update
  33.2 0.0 all-gather.2.cloned.1.call-start
  33.2 0.0 copy-done.2
  33.2 0.6 copy.7
  33.8 26.3 %all_gather.6 = bf16[20,9,320]{0,1,2:T(8,128)(2,1)} all-gather(bf16[20,9,160]{0,1,2:T(8,128)(2,1)S(1)} %copy.7), channel_id=1, replica_groups=mesh['band'=16,'strip'=2] {'strip'}, dimensions={2}, use_global_device_ids=true | all-gather | bytes 172800 | tf_op jit(solution)/shard_map/all_gather | solution.py:44
  60.1 3.4 %copy.8 = bf16[20,9,320]{2,1,0:T(8,128)(2,1)} copy(bf16[20,9,320]{0,1,2:T(8,128)(2,1)} %all_gather.6) | data formatting | bytes 230400 | tf_op jit(solution)/shard_map/all_gather | solution.py:44
  63.4 0.0 all-gather.2.cloned.1.call-update
  63.5 0.2 reduce-scatter.5.cloned.1.call-start
  63.7 34.7 %reduce-scatter.3.cloned.1.call-done = f32[320,9,160]{0,2,1:T(8,128)} async-done(((f32[320,9,320]{0,2,1:T(8,128)}), f32[320,9,160]{0,2,1:T(8,128)}) %reduce-scatter.3.cloned.1.call-update) | async-done | bytes 1843216 | tf_op jit(solution)/shard_map/reduce_scatter | solution.py:63
  98.4 6.8 %copy.19 = f32[320,9,160]{2,1,0:T(8,128)} copy(f32[320,9,160]{0,2,1:T(8,128)} %reduce-scatter.3.cloned.1.call-done) | data formatting | bytes 3686400 | tf_op jit(solution)/shard_map/reduce_scatter | solution.py:63
  105.2 0.0 reduce-scatter.5.cloned.1.call-update
  105.2 8.2 %all-gather.2.cloned.1.call-done = bf16[320,9,320]{2,1,0:T(8,128)(2,1)} async-done(((bf16[20,9,320]{2,1,0:T(8,128)(2,1)}), bf16[320,9,320]{2,1,0:T(8,128)(2,1)}) %all-gather.2.cloned.1.call-update) | async-done | bytes 1843216 | tf_op jit(solution)/shard_map/all_gather | solution.py:45
  113.4 10.9 %fusion.41 = (bf16[320,1,320]{2,1,0:T(2,128)(2,1)S(1)}, bf16[320,1,320]{2,1,0:T(2,128)(2,1)S(1)}, bf16[320,1,320]{2,1,0:T(2,128)(2,1)S(1)}, bf16[320,1,320]{2,1,...) fusion(bf16[320,9,320]{2,1,0:T(8,128)(2,1)} %all-gather.2.clone, ...), kind=kLoop, calls=%fused_computation.73 | loop fusion | bytes 3686400 | tf_op jit(solution)/shard_map/slice | solution.py:51
  124.3 0.5 fusion.31
  124.8 0.4 fusion.32
  125.3 0.4 convolution_add_fusion.6
  125.7 0.4 convolution_add_fusion.5
  126.1 0.5 convolution_add_fusion.4
  126.6 0.4 convolution_add_fusion.3
  127.0 0.4 convolution_add_fusion.2
  127.5 0.5 convolution_add_fusion.1
  128.0 1.2 fusion.8
  129.2 64.7 %reduce-scatter.5.cloned.1.call-done = f32[20,9,160]{2,1,0:T(8,128)} async-done(((f32[320,9,160]{2,1,0:T(8,128)}), f32[20,9,160]{2,1,0:T(8,128)}) %reduce-scatter.5.cloned.1.call-update) | async-done | bytes 115216 | tf_op jit(solution)/shard_map/reduce_scatter | solution.py:64
  193.9 1.0 broadcast_multiply_fusion
  194.9 0.8 copy.20
Async XLA Ops:
  8.0 14.0 %copy-start = (bf16[1,320,6,128]{3,1,2,0:T(8,128)(2,1)S(1)}, bf16[1,320,6,128]{3,1,2,0:T(8,128)(2,1)}, u32[]{:S(2)}) copy-start(bf16[1,320,6,128]{3,1,2,0:T(8,128)(2,1)} %param.3) | copy-start | bytes 1474564
  8.0 15.2 %copy-start.1 = (bf16[1,320,6,128]{3,1,2,0:T(8,128)(2,1)S(1)}, bf16[1,320,6,128]{3,1,2,0:T(8,128)(2,1)}, u32[]{:S(2)}) copy-start(bf16[1,320,6,128]{3,1,2,0:T(8,128)(2,1)} %param.4) | copy-start | bytes 1474564
  8.0 90.4 %reduce-scatter.3.cloned.1.call-start = ((), (), s32[]{:S(2)}) async-start(), calls=%async_computation.3 | async-start | bytes 6635520 | tf_op jit(solution)/shard_map/reduce_scatter | solution.py:63
  9.1 6.9 %collective-permute-start = (bf16[1,320,1,128]{3,1,2,0:T(8,128)(2,1)S(1)}, bf16[1,320,1,128]{3,1,2,0:T(8,128)(2,1)S(1)}, u32[]{:S(2)}, u32[]{:S(2)}) collective-permute-start(bf16[1,320,1,128]{3,1,2,0:T(8,128)(2,1)S(1)} %get-tuple-element.15), channel_id=1, source_target_pairs={{0,1},{2,3},{4,5},{6,7},{8,9},{10,11},{12,13},{14,15},{16,17},{18,... | collective-permute-start | bytes 245768 | tf_op jit(solution)/shard_map/ppermute | solution.py:19
  13.9 6.3 %collective-permute-start.1 = (bf16[1,320,1,128]{3,1,2,0:T(8,128)(2,1)S(1)}, bf16[1,320,1,128]{3,1,2,0:T(8,128)(2,1)S(1)}, u32[]{:S(2)}, u32[]{:S(2)}) collective-permute-start(bf16[1,320,1,128]{3,1,2,0:T(8,128)(2,1)S(1)} %get-tuple-element.16), channel_id=1, source_target_pairs={{1,0},{3,2},{5,4},{7,6},{9,8},{11,10},{13,12},{15,14},{17,16},{19,... | collective-permute-start | bytes 245768 | tf_op jit(solution)/shard_map/ppermute | solution.py:21
  31.9 1.3 copy-start.2
  33.2 80.2 %all-gather.2.cloned.1.call-start = ((), (), s32[]{:S(2)}) async-start(), calls=%async_computation.2 | async-start | bytes 4177920 | tf_op jit(solution)/shard_map/all_gather | solution.py:45
  63.5 130.5 %reduce-scatter.5.cloned.1.call-start = ((), (), s32[]{:S(2)}) async-start(), calls=%async_computation.4 | async-start | bytes 5570560 | tf_op jit(solution)/shard_map/reduce_scatter | solution.py:64
Sparse Core Ops, SparseCore 0:
  33.3 65.0 reduce-scatter.2
Sparse Core Ops, SparseCore 1:
  63.5 49.8 all-gather.1
  117.1 76.7 reduce-scatter.4
where the time goes:
time: 204 us; the launch traced here: 203 us
  waiting for transfers between devices  113 us (55%)
  blocking collectives  26.3 us (13%)
  local copies, waits for them, and re-layouts  23.4 us (11%)
  matrix products  16 us (8%)
  between operations  15.6 us (8%)
  starting transfers between devices  6.45 us (3%)
  other arithmetic  2.69 us (1%)
    reduce_scatter x1, waiting for transfers between devices, body(): lax.psum_scatter(partial_value, 'band', scatter_dimension=0, tiled=True)  64.7 us
    reduce_scatter x1, waiting for transfers between devices, body(): lax.psum_scatter(local_terms, 'strip', scatter_dimension=2, tiled=True)  34.7 us
    all_gather x1, blocking collectives, body(): kernel_full_cols = lax.all_gather(kernel, 'strip', axis=2, tiled=True)  26.3 us
    dot_general x9, matrix products, body(): jnp.einsum('bihw,bohw->io', activations, grad_side, preferred_element_typ...  11.2 us
    slice x1, local copies, waits for them, and re-layouts, body(): kernel_whole[:, tap_index, :]  10.9 us
    all_gather x1, waiting for transfers between devices, body(): kernel_whole = lax.all_gather(kernel_full_cols, 'band', axis=0, tiled=True)  8.21 us
    reduce_scatter x1, local copies, waits for them, and re-layouts, body(): lax.psum_scatter(local_terms, 'strip', scatter_dimension=2, tiled=True)  6.76 us
    ppermute x1, starting transfers between devices, extended(): lax.ppermute(tail, axis, [(i, (i + 1) % count) for i in range(ends)])  4.85 us
  transfers between devices with their start and end apart: 5, of which 5 were waited for; matrix products, arithmetic and copies ran while one was open for 13% of the time, Pallas kernels for 0%

commit v1 on v0

v1 whole, which is shorter than its diff:
```python
import functools
import math

import jax
import jax.numpy as jnp
from jax import lax
from jax.experimental import pallas as pl
from jax.experimental.pallas import tpu as pltpu
from jax.sharding import PartitionSpec as P

AXES = ("band", "strip")
TAP_STEPS = (-1, 0, 1)
LANES = 128
TOP_POWER = 2.0**15.5
LEAST_PEAK = 1e-30
VMEM_BYTES = 40 * 2**20


def padded_lanes(count):
    return (count // LANES + 1) * LANES


def swap(value, sizes, band_mask, strip_mask, other_masks=None):
    bands, strips = sizes
    pairs = []
    for b in range(bands):
        for s in range(strips):
            masks = (band_mask, strip_mask)
            if other_masks is not None and b % 2:
                masks = other_masks
            pairs.append((b * strips + s, (b ^ masks[0]) * strips + (s ^ masks[1])))
    return lax.ppermute(value, AXES, pairs)


def call(kernel, out_shape, operands, scratch=(), flops=0):
    moved = sum(x.size * x.dtype.itemsize for x in operands)
    return pl.pallas_call(
        kernel,
        out_shape=out_shape,
        in_specs=[pl.BlockSpec(memory_space=pltpu.VMEM)] * len(operands),
        out_specs=jax.tree.map(lambda _: pl.BlockSpec(memory_space=pltpu.VMEM), out_shape),
        scratch_shapes=list(scratch),
        compiler_params=pltpu.CompilerParams(vmem_limit_bytes=VMEM_BYTES),
        cost_estimate=pl.CostEstimate(flops=flops, bytes_accessed=2 * moved, transcendentals=0),
    )(*operands)


def encoded(peak, value, used):
    lane = lax.broadcasted_iota(jnp.int32, value.shape, value.ndim - 1)
    ratio = value * (TOP_POWER / peak)
    square = ratio * ratio
    power = ratio * jnp.abs(ratio) * square * (square * square)
    return jnp.where(lane < used, power, peak).astype(jnp.bfloat16)


def decoded(message):
    power = message.astype(jnp.float32)
    peak = power[0:1, message.shape[1] - 1 : message.shape[1]]
    root = jnp.sqrt(jnp.sqrt(jnp.sqrt(jnp.abs(power))))
    return jnp.where(power < 0, -root, root) * (peak * (1.0 / TOP_POWER))


def peak_of(value, used):
    lane = lax.broadcasted_iota(jnp.int32, value.shape, value.ndim - 1)
    largest = jnp.max(jnp.where(lane < used, jnp.abs(value), 0.0))
    largest = jnp.maximum(largest * (1.0 + 2.0**-6), LEAST_PEAK)
    return jnp.full((1, 1), largest, jnp.float32).astype(jnp.bfloat16).astype(jnp.float32)


class Plan:
    def __init__(self, images, channels, rows, width, bands, strips):
        self.images, self.channels, self.rows, self.width = images, channels, rows, width
        self.bands, self.strips = bands, strips
        self.sizes = (bands, strips)
        self.depth = channels // bands
        self.cols = channels // strips
        self.blocks = bands // 2
        self.half = channels // 2
        self.strip_bits = strips.bit_length() - 1
        self.band_bits = bands.bit_length() - 1
        assert bands == 1 << self.band_bits and strips == 1 << self.strip_bits
        assert self.band_bits >= 2 and self.strip_bits >= 1
        self.top_strip = 1 << (self.strip_bits - 1)
        self.rest_strip = [1 << k for k in reversed(range(self.strip_bits - 1))]
        self.rest_band = [1 << k for k in range(2, self.band_bits)]
        self.inner = self.blocks // 2
        self.half_used = len(TAP_STEPS) * self.half
        self.half_lanes = padded_lanes(self.half_used)
        self.used = len(TAP_STEPS) * self.cols
        self.lanes = padded_lanes(self.used)
        self.block_rows = len(TAP_STEPS) * self.depth

    def block_of(self, slot, low):
        bits = self.band_bits - 2
        turned = sum(((slot >> k) & 1) << (bits - 1 - k) for k in range(bits))
        return turned * 2 + low

    def slot_of(self, difference):
        bits = self.band_bits - 2
        return sum(((difference >> (k + 1)) & 1) << (bits - 1 - k) for k in range(bits))


def place(plan):
    band, strip = lax.axis_index("band"), lax.axis_index("strip")
    core = band % 2
    low = (band // 2) % 2
    high = strip // plan.top_strip
    return band, strip, core, low, high


def grad_row(plan, grad_ref, top_ref, bottom_ref, image, row, start, strip):
    if row < 0:
        piece = top_ref[image, pl.ds(start, plan.half), :]
        return jnp.where(strip > 0, piece, jnp.zeros_like(piece))
    if row >= plan.rows:
        piece = bottom_ref[image, pl.ds(start, plan.half), :]
        return jnp.where(strip < plan.strips - 1, piece, jnp.zeros_like(piece))
    return grad_ref[image, row, pl.ds(start, plan.half), :]


def moved(value, step):
    width = value.shape[-1]
    if step == 0:
        return value
    lane = lax.broadcasted_iota(jnp.int32, value.shape, value.ndim - 1)
    turned = pltpu.roll(value, (-step) % width, value.ndim - 1)
    inside = lane < width - step if step > 0 else lane >= -step
    return jnp.where(inside, turned, 0.0)


def terms_kernel(plan, sends, act0, act1, grad0, grad1, top0, top1, bottom0, bottom1, out, left, right):
    _, strip, core, low, high = place(plan)
    mine = jnp.where(core == 0, high, low)
    first = 1 - mine if sends else mine
    sources = ((act0, grad0, top0, bottom0), (act1, grad1, top1, bottom1))
    chunks = [(d, n, h) for d in range(2) for n in range(plan.images) for h in range(plan.rows)]
    depth, width = plan.depth, plan.width
    for at, (d, n, h) in enumerate(chunks):
        cells = sources[d][0][n, h].astype(jnp.float32)
        blocks = []
        for m in range(plan.blocks):
            begin = 2 * m * depth
            blocks.append(
                jnp.where(
                    core == 0,
                    cells[begin : begin + depth],
                    cells[begin + depth : begin + 2 * depth],
                )
            )
        for y in range(2):
            pieces = []
            for slot in range(plan.inner):
                for step in TAP_STEPS:
                    pieces.append(moved(blocks[plan.block_of(slot, y)], step))
            left[y, :, at * width : (at + 1) * width] = jnp.concatenate(pieces, axis=0).astype(jnp.bfloat16)
    for q in range(2):
        y = jnp.where(core == 0, q, first)
        x = jnp.where(core == 0, first, q)
        start = pl.multiple_of(x * plan.half, 16)
        for at, (d, n, h) in enumerate(chunks):
            _, grad, top, bottom = sources[d]
            for r, row_step in enumerate(TAP_STEPS):
                right[r * plan.half : (r + 1) * plan.half, at * width : (at + 1) * width] = grad_row(
                    plan, grad, top, bottom, n, h - row_step, start, strip
                )
        total = lax.dot_general(
            left[y], right[...], (((1,), (1,)), ((), ())), preferred_element_type=jnp.float32
        )
        spare = plan.half_lanes - plan.half_used
        total = jnp.concatenate([total, jnp.zeros((total.shape[0], spare), jnp.float32)], axis=1)
        if sends:
            out[q] = encoded(peak_of(total, plan.half_used), total, plan.half_used)
        else:
            out[q] = total


def turn_kernel(plan, keep, message, send, kept):
    _, _, core, low, high = place(plan)
    mine = jnp.where(core == 0, low, high)
    total = keep[1 - mine] + decoded(message[1 - mine])
    send[...] = encoded(peak_of(total, plan.half_used), total, plan.half_used)
    kept[...] = keep[mine] + decoded(message[mine])


def halve_kernel(plan, mask, used, keep, message, send, kept):
    band = lax.axis_index("band")
    side = (band // mask) % 2
    total = keep[...] + decoded(message[...])
    rows = total.shape[0] // 2
    lower, upper = total[:rows], total[rows:]
    given = jnp.where(side == 0, upper, lower)
    send[...] = encoded(peak_of(given, used), given, used)
    kept[...] = jnp.where(side == 0, lower, upper)


def last_kernel(plan, scale, keep, message, out):
    total = (keep[...] + decoded(message[...])) * scale
    depth, cols = plan.depth, plan.cols
    for r in range(len(TAP_STEPS)):
        for c in range(len(TAP_STEPS)):
            out[r * len(TAP_STEPS) + c] = total[c * depth : (c + 1) * depth, r * cols : (r + 1) * cols]


def pack_kernel(plan, kernel, out):
    rows = []
    for c in range(len(TAP_STEPS)):
        pieces = [kernel[r * len(TAP_STEPS) + c].astype(jnp.float32) for r in range(len(TAP_STEPS))]
        pieces.append(jnp.zeros((plan.depth, plan.lanes - plan.used), jnp.float32))
        rows.append(jnp.concatenate(pieces, axis=1))
    out[...] = jnp.concatenate(rows, axis=0).astype(jnp.bfloat16)


def cells_kernel(plan, own, other, grad0, grad1, top0, top1, bottom0, bottom1, out0, out1, left, right):
    band, strip, core, low, high = place(plan)
    depth, width, half, lanes = plan.depth, plan.width, plan.half, plan.half_lanes
    steps = len(TAP_STEPS)
    for x in range(2):
        rows = [[] for _ in TAP_STEPS]
        for m in range(plan.blocks):
            difference = m ^ (band // 2)
            by_row, by_col = difference % 2, x ^ high
            one = jnp.where(core == 0, by_row, by_col)
            two = jnp.where(core == 0, by_col, by_row)
            slot = one * plan.inner + plan.slot_of(difference)
            block = jnp.where(two == 0, own[slot], other[slot]).astype(jnp.float32)
            for c in range(steps):
                rows[c].append(block[c * depth : (c + 1) * depth])
        for c in range(steps):
            left[c * half : (c + 1) * half, x * lanes : (x + 1) * lanes] = jnp.concatenate(
                rows[c], axis=0
            ).astype(jnp.bfloat16)
    sources = ((grad0, top0, bottom0), (grad1, top1, bottom1))
    chunks = [(d, n, h) for d in range(2) for n in range(plan.images) for h in range(plan.rows)]
    for at, (d, n, h) in enumerate(chunks):
        grad, top, bottom = sources[d]
        for x in range(2):
            for r, row_step in enumerate(TAP_STEPS):
                begin = x * lanes + r * half
                right[begin : begin + half, at * width : (at + 1) * width] = grad_row(
                    plan, grad, top, bottom, n, h - row_step, x * half, strip
                )
            begin = x * lanes + steps * half
            right[begin : (x + 1) * lanes, at * width : (at + 1) * width] = jnp.zeros(
                (lanes - steps * half, width), jnp.bfloat16
            )
    group = 2
    for begin in range(0, len(chunks), group):
        part = chunks[begin : begin + group]
        product = jnp.dot(
            left[...],
            right[:, begin * width : (begin + len(part)) * width],
            preferred_element_type=jnp.float32,
        )
        for k, (d, n, h) in enumerate(part):
            total = None
            for c, col_step in enumerate(TAP_STEPS):
                term = moved(product[c * half : (c + 1) * half, k * width : (k + 1) * width], -col_step)
                total = term if total is None else total + term
            (out0, out1)[d][n, h] = total.astype(jnp.bfloat16)


def weave_kernel(plan, mine, theirs, out):
    core = lax.axis_index("band") % 2
    depth = plan.depth
    for n in range(plan.images):
        for h in range(plan.rows):
            a, b = mine[n, h].astype(jnp.float32), theirs[n, h].astype(jnp.float32)
            even, odd = jnp.where(core == 0, a, b), jnp.where(core == 0, b, a)
            pieces = []
            for m in range(plan.blocks):
                pieces += [even[m * depth : (m + 1) * depth], odd[m * depth : (m + 1) * depth]]
            out[n, h] = jnp.concatenate(pieces, axis=0).astype(jnp.bfloat16)


def whole_kernel(plan, kernel):
    sizes, f32 = plan.sizes, jnp.float32
    shape = jax.ShapeDtypeStruct((plan.block_rows, plan.lanes), jnp.bfloat16)
    packed = call(functools.partial(pack_kernel, plan), shape, [kernel])[None]
    for mask in reversed(plan.rest_band):
        packed = jnp.concatenate([packed, swap(packed, sizes, mask, 0)], axis=0)
    if plan.rest_strip:
        packed = packed[None]
        for mask in reversed(plan.rest_strip):
            packed = jnp.concatenate([packed, swap(packed, sizes, 0, mask)], axis=0)
        count = packed.shape[0]
        order = jnp.arange(count) ^ (lax.axis_index("strip") % count)
        packed = jnp.take(packed, order, axis=0)[..., : plan.used]
        packed = packed.reshape(count, plan.inner, plan.block_rows, len(TAP_STEPS), plan.cols)
        packed = packed.transpose(1, 2, 3, 0, 4).reshape(plan.inner, plan.block_rows, plan.half_used)
        packed = jnp.pad(packed, ((0, 0), (0, 0), (0, plan.half_lanes - plan.half_used)))
    by_row, by_col = (2, 0), (0, plan.top_strip)
    packed = jnp.concatenate([packed, swap(packed, sizes, *by_row, other_masks=by_col)], axis=0)
    return packed, swap(packed, sizes, *by_col, other_masks=by_row)


def narrowed(plan, total):
    rows = total.shape[0]
    total = total[:, : plan.half_used].reshape(rows, len(TAP_STEPS), plan.half)
    for mask in plan.rest_strip:
        side = (lax.axis_index("strip") // mask) % 2
        parts = total.reshape(rows, len(TAP_STEPS), 2, total.shape[2] // 2)
        kept = jnp.where(side == 0, parts[:, :, 0], parts[:, :, 1])
        given = jnp.where(side == 0, parts[:, :, 1], parts[:, :, 0])
        total = kept + swap(given, plan.sizes, 0, mask)
    total = total.reshape(rows, plan.used)
    return jnp.pad(total, ((0, 0), (0, plan.lanes - plan.used)))


def kernel_terms(plan, cells, scale):
    sizes, f32 = plan.sizes, jnp.float32
    rows, lanes = plan.inner * plan.block_rows, plan.half_lanes
    depth = 2 * plan.images * plan.rows * plan.width
    scratch = [
        pltpu.VMEM((2, rows, depth), jnp.bfloat16),
        pltpu.VMEM((plan.half_used, depth), jnp.bfloat16),
    ]
    flops = 4 * rows * plan.half_used * depth
    send = call(
        functools.partial(terms_kernel, plan, True),
        jax.ShapeDtypeStruct((2, rows, lanes), jnp.bfloat16), cells, scratch, flops,
    )
    keep = call(
        functools.partial(terms_kernel, plan, False),
        jax.ShapeDtypeStruct((2, rows, lanes), f32), cells, scratch, flops,
    )
    by_row, by_col = (2, 0), (0, plan.top_strip)
    come = swap(send, sizes, *by_col, other_masks=by_row)
    send, keep = call(
        functools.partial(turn_kernel, plan),
        (jax.ShapeDtypeStruct((rows, lanes), jnp.bfloat16), jax.ShapeDtypeStruct((rows, lanes), f32)),
        [keep, come],
    )
    come = swap(send, sizes, *by_row, other_masks=by_col)
    if plan.rest_strip:
        total = keep[:, :] + decoded(come)
        keep = narrowed(plan, total)
        come = jnp.zeros(keep.shape, jnp.bfloat16)
    for mask in plan.rest_band:
        rows //= 2
        send, keep = call(
            functools.partial(halve_kernel, plan, mask, plan.used),
            (
                jax.ShapeDtypeStruct((rows, plan.lanes), jnp.bfloat16),
                jax.ShapeDtypeStruct((rows, plan.lanes), f32),
            ),
            [keep, come],
        )
        come = swap(send, sizes, mask, 0)
    return call(
        functools.partial(last_kernel, plan, scale),
        jax.ShapeDtypeStruct((len(TAP_STEPS) ** 2, plan.depth, plan.cols), f32),
        [keep, come],
    )


def borders(plan, grad):
    strip = lax.axis_index("strip")
    first, last = grad[:, 0], grad[:, plan.rows - 1]
    if plan.strips == 2:
        come = swap(jnp.where(strip == 0, last, first), plan.sizes, 0, 1)
        return [come]
    ends = plan.strips - 1
    return [
        lax.ppermute(last, "strip", [(i, i + 1) for i in range(ends)]),
        lax.ppermute(first, "strip", [(i + 1, i) for i in range(ends)]),
    ]


def body(activations, out_grad, kernel):
    images, channels, rows, width = activations.shape
    bands, strips = lax.axis_size("band"), lax.axis_size("strip")
    plan = Plan(images, channels, rows, width, bands, strips)
    scale = 1.0 / math.sqrt(images * bands * rows * strips * width)
    act = activations.transpose(0, 2, 1, 3)
    grad = out_grad.transpose(0, 2, 1, 3)
    edges = borders(plan, grad)
    act1 = swap(act, plan.sizes, 1, 0)
    grad1 = swap(grad, plan.sizes, 1, 0)
    edges1 = [swap(edge, plan.sizes, 1, 0) for edge in edges]
    near = [grad, grad1, edges[0], edges1[0], edges[-1], edges1[-1]]
    kernel_grad = kernel_terms(plan, [act, act1, *near], scale)
    packed = whole_kernel(plan, kernel.transpose(1, 0, 2))
    depth = 2 * images * rows * width
    shape = jax.ShapeDtypeStruct((images, rows, plan.half, width), jnp.bfloat16)
    mine, given = call(
        functools.partial(cells_kernel, plan),
        (shape, shape),
        [*packed, *near],
        [
            pltpu.VMEM((len(TAP_STEPS) * plan.half, 2 * plan.half_lanes), jnp.bfloat16),
            pltpu.VMEM((2 * plan.half_lanes, depth), jnp.bfloat16),
        ],
        2 * len(TAP_STEPS) * plan.half * 2 * plan.half_lanes * depth,
    )
    theirs = swap(given, plan.sizes, 1, 0)
    input_grad = call(
        functools.partial(weave_kernel, plan),
        jax.ShapeDtypeStruct((images, rows, channels, width), jnp.bfloat16),
        [mine, theirs],
    )
    return input_grad.transpose(0, 2, 1, 3), kernel_grad.transpose(1, 0, 2)


def solution(mesh):
    in_specs = (
        P("band", None, "strip", None),
        P("band", None, "strip", None),
        P("band", None, "strip"),
    )
    out_specs = (P("band", None, "strip", None), P("band", None, "strip"))
    return jax.shard_map(body, mesh=mesh, in_specs=in_specs, out_specs=out_specs, check_vma=False)
```

time: 204 us -> 57.5 us (0.28)
  waiting for transfers between devices: 113 us -> 30.8 us
  blocking collectives: 26.3 us -> 0 us
  local copies, waits for them, and re-layouts: 23.4 us -> 0.96 us
  matrix products: 16 us -> 0 us
  between operations: 15.6 us -> 0.75 us
  Pallas kernels: 0 us -> 10.8 us
  starting transfers between devices: 6.45 us -> 14 us
  other arithmetic: 2.69 us -> 0.11 us
    reduce_scatter x2 -> x0, waiting for transfers between devices: 99.5 us -> none  [the longest x1 64.7 us: body(): lax.psum_scatter(partial_value, 'band', scatter_dimension=0, tiled=True)]
    all_gather x1 -> x0, blocking collectives: 26.3 us -> none  [body(): kernel_full_cols = lax.all_gather(kernel, 'strip', axis=2, tiled=True)]
    ppermute x2 -> x13, waiting for transfers between devices: 5.03 us -> 30.8 us  [swap(): return lax.ppermute(value, AXES, pairs)]
    dot_general x18 -> x0, matrix products: 16 us -> none  [the longest x9 11.2 us: body(): jnp.einsum('bihw,bohw->io', activations, grad_side, preferred_element_typ...]
    slice x2 -> x0, local copies, waits for them, and re-layouts: 11.9 us -> none  [the longest x1 10.9 us: body(): kernel_whole[:, tap_index, :]]
    pallas_call x0 -> x9, Pallas kernels: none -> 10.8 us  [call(): pl.pallas_call(kernel, out_shape=out_shape, in_specs=[pl.BlockSpec(memory...]
    all_gather x1 -> x0, waiting for transfers between devices: 8.21 us -> none  [body(): kernel_whole = lax.all_gather(kernel_full_cols, 'band', axis=0, tiled=True)]
    ppermute x2 -> x13, starting transfers between devices: 6.14 us -> 14 us  [swap(): return lax.ppermute(value, AXES, pairs)]
  transfers between devices with their start and end apart: 5 -> 13, of which waited for: 5 -> 8; matrix products, arithmetic and copies ran while one was open for 13% -> 0% of each run, Pallas kernels for 0% -> 17%
where the time goes in v1:
time: 57.5 us; the launch traced here: 57.4 us
  waiting for transfers between devices  30.8 us (54%)
  starting transfers between devices  14 us (24%)
  Pallas kernels  10.8 us (19%)
  local copies, waits for them, and re-layouts  0.96 us (2%)
  between operations  0.75 us (1%)
    ppermute x13, waiting for transfers between devices, swap(): return lax.ppermute(value, AXES, pairs)  30.8 us
    ppermute x13, starting transfers between devices, swap(): return lax.ppermute(value, AXES, pairs)  14 us
    pallas_call x9, Pallas kernels, call(): pl.pallas_call(kernel, out_shape=out_shape, in_specs=[pl.BlockSpec(memory...  10.8 us
  transfers between devices with their start and end apart: 13, of which 8 were waited for; matrix products, arithmetic and copies ran while one was open for 0% of the time, Pallas kernels for 17%

profile of v1, /device:TPU:0, one launch (start us, length us, event | category | flops | bytes accessed | tf_op | source)
XLA Modules:
  0.0 57.4 jit_solution(17721103020862042259)
XLA Ops:
  0.6 0.0 copy-start
  0.6 0.0 copy-start.2
  0.7 0.9 %copy-done.2 = bf16[20,9,160]{2,0,1:T(8,128)(2,1)S(1)} copy-done((bf16[20,9,160]{2,0,1:T(8,128)(2,1)S(1)}, bf16[20,9,160]{2,0,1:T(8,128)(2,1)}, u32[]{:S(2)}) %copy-start.2) | copy-done | bytes 57624
  1.6 0.1 shard_map.50
  1.7 0.0 copy-start.1
  1.7 4.1 %collective-permute-start = (bf16[1,60,512]{2,1,0:T(8,128)(2,1)S(1)}, bf16[1,60,512]{2,1,0:T(8,128)(2,1)S(1)}, u32[]{:S(2)}, u32[]{:S(2)}) collective-permute-start(bf16[1,60,512]{2,1,0:T(8,128)(2,1)S(1)} %bitcast.16), channel_id=1, source_target_pairs={{0,16},{1,17},{2,18},{3,19},{4,20},{5,21},{6,22},{7,23},{8,24},{9,... | collective-permute-start | bytes 184328 | tf_op jit(solution)/shard_map/ppermute | solution.py:32
  5.8 3.6 %collective-permute-done = bf16[1,60,512]{2,1,0:T(8,128)(2,1)S(1)} collective-permute-done((bf16[1,60,512]{2,1,0:T(8,128)(2,1)S(1)}, bf16[1,60,512]{2,1,0:T(8,128)(2,1)S(1)}, u32[]{:S(2)}, u32[]{:S(2)}) %collective-permute-start) | collective-permute-done | bytes 61472 | tf_op jit(solution)/shard_map/ppermute | solution.py:32
  9.5 0.6 %collective-permute-start.1 = (bf16[2,60,512]{2,1,0:T(8,128)(2,1)S(1)}, bf16[2,60,512]{2,1,0:T(8,128)(2,1)S(1)}, u32[]{:S(2)}, u32[]{:S(2)}) collective-permute-start(bf16[2,60,512]{2,1,0:T(8,128)(2,1)S(1)} %pad_maximum_fusion.2), channel_id=1, source_target_pairs={{0,8},{1,9},{2,10},{3,11},{4,12},{5,13},{6,14},{7,15},{8,0},{9,1},... | collective-permute-start | bytes 368648 | tf_op jit(solution)/shard_map/ppermute | solution.py:32
  10.1 0.0 collective-permute-start.4
  10.1 0.5 collective-permute-start.8
  10.6 3.9 %collective-permute-done.1 = bf16[2,60,512]{2,1,0:T(8,128)(2,1)S(1)} collective-permute-done((bf16[2,60,512]{2,1,0:T(8,128)(2,1)S(1)}, bf16[2,60,512]{2,1,0:T(8,128)(2,1)S(1)}, u32[]{:S(2)}, u32[]{:S(2)}) %collective-permute-start.1) | collective-permute-done | bytes 122912 | tf_op jit(solution)/shard_map/ppermute | solution.py:32
  14.5 1.8 %collective-permute-start.2 = (bf16[4,60,512]{2,1,0:T(8,128)(2,1)S(1)}, bf16[4,60,512]{2,1,0:T(8,128)(2,1)S(1)}, u32[]{:S(2)}, u32[]{:S(2)}) collective-permute-start(bf16[4,60,512]{2,1,0:T(8,128)(2,1)S(1)} %pad_maximum_fusion.1), channel_id=1, source_target_pairs={{0,4},{1,5},{2,3},{3,2},{4,0},{5,1},{6,7},{7,6},{8,12},{9,13},{10,... | collective-permute-start | bytes 737288 | tf_op jit(solution)/shard_map/ppermute | solution.py:32
  16.3 0.0 copy-done
  16.4 1.6 %collective-permute-start.5 = (bf16[1,320,128]{2,1,0:T(8,128)(2,1)S(1)}, bf16[1,320,128]{2,1,0:T(8,128)(2,1)S(1)}, u32[]{:S(2)}, u32[]{:S(2)}) collective-permute-start(bf16[1,320,128]{2,1,0:T(8,128)(2,1)S(1)} %fusion), channel_id=1, source_target_pairs={{0,1},{1,0},{2,3},{3,2},{4,5},{5,4},{6,7},{7,6},{8,9},{9,8},{10,11... | collective-permute-start | bytes 245768 | tf_op jit(solution)/shard_map/ppermute | solution.py:32
  17.9 2.9 %collective-permute-done.5.top0.bottom0 = bf16[1,320,128]{2,1,0:T(8,128)(2,1)S(1)} collective-permute-done((bf16[1,320,128]{2,1,0:T(8,128)(2,1)S(1)}, bf16[1,320,128]{2,1,0:T(8,128)(2,1)S(1)}, u32[]{:S(2)}, u32[]{:S(2)}) %collective-permute-start.5) | collective-permute-done | bytes 81952 | tf_op jit(solution)/shard_map/ppermute | solution.py:32
  20.9 0.0 collective-permute-start.6
  20.9 1.3 %collective-permute-done.6.top1.bottom1 = bf16[1,320,128]{2,1,0:T(8,128)(2,1)S(1)} collective-permute-done((bf16[1,320,128]{2,1,0:T(8,128)(2,1)S(1)}, bf16[1,320,128]{2,1,0:T(8,128)(2,1)S(1)}, u32[]{:S(2)}, u32[]{:S(2)}) %collective-permute-start.6) | collective-permute-done | bytes 81952 | tf_op jit(solution)/shard_map/ppermute | solution.py:32
  22.1 0.0 collective-permute-done.4.grad1
  22.1 0.0 collective-permute-done.8.act1
  22.1 0.0 copy-done.1
  22.1 2.3 %shard_map.54 = bf16[2,240,512]{2,1,0:T(8,128)(2,1)S(1)} custom-call(bf16[1,6,320,128]{3,2,1,0:T(8,128)(2,1)S(1)} %bitcast.14, bf16[1,6,320,128]{3,2,1,0:T(8,128)(2,1)S(1)} %collective-permute-done.8.act1, bf16[1,6,320,128]{3,2,1,0:T(8,128)(2,1)S(1)} %bitcast.10, bf16[1,6,320,128]{3,2,1,0:T(8,128)(2,1)S(1)} %collective-permute-done.4.grad1, ...), custom_call_target="tpu_custom_call" | custom-call | flops 707788800 | bytes 4587520 | tf_op jit(solution)/shard_map/pallas_call | solution.py:37
  24.5 1.5 %collective-permute-start.9 = (bf16[2,240,512]{2,1,0:T(8,128)(2,1)S(1)}, bf16[2,240,512]{2,1,0:T(8,128)(2,1)S(1)}, u32[]{:S(2)}, u32[]{:S(2)}) collective-permute-start(bf16[2,240,512]{2,1,0:T(8,128)(2,1)S(1)} %shard_map.54), channel_id=1, source_target_pairs={{0,1},{1,0},{2,6},{3,7},{4,5},{5,4},{6,2},{7,3},{8,9},{9,8},{10,14... | collective-permute-start | bytes 1474568 | tf_op jit(solution)/shard_map/ppermute | solution.py:32
  26.0 0.0 collective-permute-done.2
  26.0 0.1 pad_maximum_fusion.own
  26.1 0.6 %collective-permute-start.3 = (bf16[8,60,512]{2,1,0:T(8,128)(2,1)S(1)}, bf16[8,60,512]{2,1,0:T(8,128)(2,1)S(1)}, u32[]{:S(2)}, u32[]{:S(2)}) collective-permute-start(bf16[8,60,512]{2,1,0:T(8,128)(2,1)S(1)} %pad_maximum_fusion.own), channel_id=1, source_target_pairs={{0,1},{1,0},{2,6},{3,7},{4,5},{5,4},{6,2},{7,3},{8,9},{9,8},{10,14... | collective-permute-start | bytes 1474568 | tf_op jit(solution)/shard_map/ppermute | solution.py:32
  26.7 1.7 %shard_map.53.keep = f32[2,240,512]{2,1,0:T(8,128)S(1)} custom-call(bf16[1,6,320,128]{3,2,1,0:T(8,128)(2,1)S(1)} %bitcast.15, bf16[1,6,320,128]{3,2,1,0:T(8,128)(2,1)S(1)} %collective-permute-done.8.act1, bf16[1,6,320,128]{3,2,1,0:T(8,128)(2,1)S(1)} %bitcast.11, bf16[1,6,320,128]{3,2,1,0:T(8,128)(2,1)S(1)} %collective-permute-done.4.grad1, ...), custom_call_target="tpu_custom_call" | custom-call | flops 707788800 | bytes 4587520 | tf_op jit(solution)/shard_map/pallas_call | solution.py:37
  28.4 4.9 %collective-permute-done.9.message = bf16[2,240,512]{2,1,0:T(8,128)(2,1)S(1)} collective-permute-done((bf16[2,240,512]{2,1,0:T(8,128)(2,1)S(1)}, bf16[2,240,512]{2,1,0:T(8,128)(2,1)S(1)}, u32[]{:S(2)}, u32[]{:S(2)}) %collective-permute-start.9) | collective-permute-done | bytes 491552 | tf_op jit(solution)/shard_map/ppermute | solution.py:32
  33.4 1.4 %shard_map.55 = (bf16[240,512]{1,0:T(8,128)(2,1)S(1)}, f32[240,512]{1,0:T(8,128)S(1)}) custom-call(f32[2,240,512]{2,1,0:T(8,128)S(1)} %shard_map.53.keep, bf16[2,240,512]{2,1,0:T(8,128)(2,1)S(1)} %collective-permute-done.9.message), custom_call_target="tpu_custom_call" | custom-call | bytes 2949120 | tf_op jit(solution)/shard_map/pallas_call | solution.py:37
  34.8 0.4 collective-permute-start.10
  35.2 6.0 %collective-permute-done.3.other = bf16[8,60,512]{2,1,0:T(8,128)(2,1)S(1)} collective-permute-done((bf16[8,60,512]{2,1,0:T(8,128)(2,1)S(1)}, bf16[8,60,512]{2,1,0:T(8,128)(2,1)S(1)}, u32[]{:S(2)}, u32[]{:S(2)}) %collective-permute-start.3) | collective-permute-done | bytes 491552 | tf_op jit(solution)/shard_map/ppermute | solution.py:32
  41.2 2.0 %shard_map.51 = (bf16[1,6,160,128]{3,2,1,0:T(8,128)(2,1)S(1)}, bf16[1,6,160,128]{3,2,1,0:T(8,128)(2,1)S(1)}) custom-call(bf16[8,60,512]{2,1,0:T(8,128)(2,1)S(1)} %pad_maximum_fusion.own, bf16[8,60,512]{2,1,0:T(8,128)(2,1)S(1)} %collective-permute-done.3.other, bf16[1,6,320,128]{3,2,1,0:T(8,128)(2,1)S(1)} %bitcast.12, ...), custom_call_target="tpu_custom_call" | custom-call | flops 1509949440 | bytes 4587520 | tf_op jit(solution)/shard_map/pallas_call | solution.py:37
  43.2 0.1 collective-permute-start.7
  43.3 0.0 collective-permute-done.10.message
  43.3 0.8 %shard_map.56 = (bf16[120,512]{1,0:T(8,128)(2,1)S(1)}, f32[120,512]{1,0:T(8,128)S(1)}) custom-call(f32[240,512]{1,0:T(8,128)S(1)} %get-tuple-element.12.keep, bf16[240,512]{1,0:T(8,128)(2,1)S(1)} %collective-permute-done.10.message), custom_call_target="tpu_custom_call" | custom-call | bytes 1474560 | tf_op jit(solution)/shard_map/pallas_call | solution.py:37
  44.1 0.4 collective-permute-start.11
  44.5 5.4 %collective-permute-done.11.message = bf16[120,512]{1,0:T(8,128)(2,1)S(1)} collective-permute-done((bf16[120,512]{1,0:T(8,128)(2,1)S(1)}, bf16[120,512]{1,0:T(8,128)(2,1)S(1)}, u32[]{:S(2)}, u32[]{:S(2)}) %collective-permute-start.11) | collective-permute-done | bytes 122912 | tf_op jit(solution)/shard_map/ppermute | solution.py:32
  49.9 0.5 shard_map.57
  50.4 2.4 %collective-permute-start.12 = (bf16[60,512]{1,0:T(8,128)(2,1)S(1)}, bf16[60,512]{1,0:T(8,128)(2,1)S(1)}, u32[]{:S(2)}, u32[]{:S(2)}) collective-permute-start(bf16[60,512]{1,0:T(8,128)(2,1)S(1)} %get-tuple-element.17), channel_id=1, source_target_pairs={{0,16},{1,17},{2,18},{3,19},{4,20},{5,21},{6,22},{7,23},{8,24},{9,... | collective-permute-start | bytes 184328 | tf_op jit(solution)/shard_map/ppermute | solution.py:32
  52.7 0.0 collective-permute-done.7.theirs
  52.7 0.9 %shard_map.52 = bf16[1,6,320,128]{3,2,1,0:T(8,128)(2,1)} custom-call(bf16[1,6,160,128]{3,2,1,0:T(8,128)(2,1)S(1)} %get-tuple-element.10.mine, bf16[1,6,160,128]{3,2,1,0:T(8,128)(2,1)S(1)} %collective-permute-done.7.theirs), custom_call_target="tpu_custom_call" | custom-call | bytes 983040 | tf_op jit(solution)/shard_map/pallas_call | solution.py:37
  53.7 2.8 %collective-permute-done.12.message = bf16[60,512]{1,0:T(8,128)(2,1)S(1)} collective-permute-done((bf16[60,512]{1,0:T(8,128)(2,1)S(1)}, bf16[60,512]{1,0:T(8,128)(2,1)S(1)}, u32[]{:S(2)}, u32[]{:S(2)}) %collective-permute-start.12) | collective-permute-done | bytes 61472 | tf_op jit(solution)/shard_map/ppermute | solution.py:32
  56.5 0.9 %shard_map.58 = f32[9,20,160]{2,1,0:T(8,128)} custom-call(f32[60,512]{1,0:T(8,128)S(1)} %get-tuple-element.16.keep, bf16[60,512]{1,0:T(8,128)(2,1)S(1)} %collective-permute-done.12.message), custom_call_target="tpu_custom_call" | custom-call | bytes 368640 | tf_op jit(solution)/shard_map/pallas_call | solution.py:37
  (3 shorter events, 0.1 us)
Async XLA Ops:
  0.6 15.7 %copy-start = (bf16[1,320,6,128]{3,1,2,0:T(8,128)(2,1)S(1)}, bf16[1,320,6,128]{3,1,2,0:T(8,128)(2,1)}, u32[]{:S(2)}) copy-start(bf16[1,320,6,128]{3,1,2,0:T(8,128)(2,1)} %param.4) | copy-start | bytes 1474564
  0.6 1.0 %copy-start.2 = (bf16[20,9,160]{2,0,1:T(8,128)(2,1)S(1)}, bf16[20,9,160]{2,0,1:T(8,128)(2,1)}, u32[]{:S(2)}) copy-start(bf16[20,9,160]{2,0,1:T(8,128)(2,1)} %param.5) | copy-start | bytes 172804
  1.7 20.5 %copy-start.1 = (bf16[1,320,6,128]{3,1,2,0:T(8,128)(2,1)S(1)}, bf16[1,320,6,128]{3,1,2,0:T(8,128)(2,1)}, u32[]{:S(2)}) copy-start(bf16[1,320,6,128]{3,1,2,0:T(8,128)(2,1)} %param.3) | copy-start | bytes 1474564
  1.7 7.8 %collective-permute-start = (bf16[1,60,512]{2,1,0:T(8,128)(2,1)S(1)}, bf16[1,60,512]{2,1,0:T(8,128)(2,1)S(1)}, u32[]{:S(2)}, u32[]{:S(2)}) collective-permute-start(bf16[1,60,512]{2,1,0:T(8,128)(2,1)S(1)} %bitcast.16), channel_id=1, source_target_pairs={{0,16},{1,17},{2,18},{3,19},{4,20},{5,21},{6,22},{7,23},{8,24},{9,... | collective-permute-start | bytes 184328 | tf_op jit(solution)/shard_map/ppermute | solution.py:32
  9.5 5.0 %collective-permute-start.1 = (bf16[2,60,512]{2,1,0:T(8,128)(2,1)S(1)}, bf16[2,60,512]{2,1,0:T(8,128)(2,1)S(1)}, u32[]{:S(2)}, u32[]{:S(2)}) collective-permute-start(bf16[2,60,512]{2,1,0:T(8,128)(2,1)S(1)} %pad_maximum_fusion.2), channel_id=1, source_target_pairs={{0,8},{1,9},{2,10},{3,11},{4,12},{5,13},{6,14},{7,15},{8,0},{9,1},... | collective-permute-start | bytes 368648 | tf_op jit(solution)/shard_map/ppermute | solution.py:32
  10.1 12.0 %collective-permute-start.4 = (bf16[1,6,320,128]{3,2,1,0:T(8,128)(2,1)}, bf16[1,6,320,128]{3,2,1,0:T(8,128)(2,1)S(1)}, u32[]{:S(2)}, u32[]{:S(2)}) collective-permute-start(bf16[1,6,320,128]{3,2,1,0:T(8,128)(2,1)} %bitcast.8), channel_id=1, source_target_pairs={{0,2},{1,3},{2,0},{3,1},{4,6},{5,7},{6,4},{7,5},{8,10},{9,11},{10,... | collective-permute-start | bytes 1474568 | tf_op jit(solution)/shard_map/ppermute | solution.py:32
  10.1 12.0 %collective-permute-start.8 = (bf16[1,6,320,128]{3,2,1,0:T(8,128)(2,1)}, bf16[1,6,320,128]{3,2,1,0:T(8,128)(2,1)S(1)}, u32[]{:S(2)}, u32[]{:S(2)}) collective-permute-start(bf16[1,6,320,128]{3,2,1,0:T(8,128)(2,1)} %bitcast.13), channel_id=1, source_target_pairs={{0,2},{1,3},{2,0},{3,1},{4,6},{5,7},{6,4},{7,5},{8,10},{9,11},{10,... | collective-permute-start | bytes 1474568 | tf_op jit(solution)/shard_map/ppermute | solution.py:32
  14.5 11.5 %collective-permute-start.2 = (bf16[4,60,512]{2,1,0:T(8,128)(2,1)S(1)}, bf16[4,60,512]{2,1,0:T(8,128)(2,1)S(1)}, u32[]{:S(2)}, u32[]{:S(2)}) collective-permute-start(bf16[4,60,512]{2,1,0:T(8,128)(2,1)S(1)} %pad_maximum_fusion.1), channel_id=1, source_target_pairs={{0,4},{1,5},{2,3},{3,2},{4,0},{5,1},{6,7},{7,6},{8,12},{9,13},{10,... | collective-permute-start | bytes 737288 | tf_op jit(solution)/shard_map/ppermute | solution.py:32
  16.4 4.5 %collective-permute-start.5 = (bf16[1,320,128]{2,1,0:T(8,128)(2,1)S(1)}, bf16[1,320,128]{2,1,0:T(8,128)(2,1)S(1)}, u32[]{:S(2)}, u32[]{:S(2)}) collective-permute-start(bf16[1,320,128]{2,1,0:T(8,128)(2,1)S(1)} %fusion), channel_id=1, source_target_pairs={{0,1},{1,0},{2,3},{3,2},{4,5},{5,4},{6,7},{7,6},{8,9},{9,8},{10,11... | collective-permute-start | bytes 245768 | tf_op jit(solution)/shard_map/ppermute | solution.py:32
  20.9 1.3 %collective-permute-start.6 = (bf16[1,320,128]{2,1,0:T(8,128)(2,1)S(1)}, bf16[1,320,128]{2,1,0:T(8,128)(2,1)S(1)}, u32[]{:S(2)}, u32[]{:S(2)}) collective-permute-start(bf16[1,320,128]{2,1,0:T(8,128)(2,1)S(1)} %collective-permute-done.5.top0.bottom0), channel_id=1, source_target_pairs={{0,2},{1,3},{2,0},{3,1},{4,6},{5,7},{6,4},{7,5},{8,10},{9,11},{10,... | collective-permute-start | bytes 245768 | tf_op jit(solution)/shard_map/ppermute | solution.py:32
  24.5 8.9 %collective-permute-start.9 = (bf16[2,240,512]{2,1,0:T(8,128)(2,1)S(1)}, bf16[2,240,512]{2,1,0:T(8,128)(2,1)S(1)}, u32[]{:S(2)}, u32[]{:S(2)}) collective-permute-start(bf16[2,240,512]{2,1,0:T(8,128)(2,1)S(1)} %shard_map.54), channel_id=1, source_target_pairs={{0,1},{1,0},{2,6},{3,7},{4,5},{5,4},{6,2},{7,3},{8,9},{9,8},{10,14... | collective-permute-start | bytes 1474568 | tf_op jit(solution)/shard_map/ppermute | solution.py:32
  26.1 15.1 %collective-permute-start.3 = (bf16[8,60,512]{2,1,0:T(8,128)(2,1)S(1)}, bf16[8,60,512]{2,1,0:T(8,128)(2,1)S(1)}, u32[]{:S(2)}, u32[]{:S(2)}) collective-permute-start(bf16[8,60,512]{2,1,0:T(8,128)(2,1)S(1)} %pad_maximum_fusion.own), channel_id=1, source_target_pairs={{0,1},{1,0},{2,6},{3,7},{4,5},{5,4},{6,2},{7,3},{8,9},{9,8},{10,14... | collective-permute-start | bytes 1474568 | tf_op jit(solution)/shard_map/ppermute | solution.py:32
  34.8 8.4 %collective-permute-start.10 = (bf16[240,512]{1,0:T(8,128)(2,1)S(1)}, bf16[240,512]{1,0:T(8,128)(2,1)S(1)}, u32[]{:S(2)}, u32[]{:S(2)}) collective-permute-start(bf16[240,512]{1,0:T(8,128)(2,1)S(1)} %get-tuple-element.13), channel_id=1, source_target_pairs={{0,4},{1,5},{2,3},{3,2},{4,0},{5,1},{6,7},{7,6},{8,12},{9,13},{10,... | collective-permute-start | bytes 737288 | tf_op jit(solution)/shard_map/ppermute | solution.py:32
  43.2 9.6 %collective-permute-start.7 = (bf16[1,6,160,128]{3,2,1,0:T(8,128)(2,1)S(1)}, bf16[1,6,160,128]{3,2,1,0:T(8,128)(2,1)S(1)}, u32[]{:S(2)}, u32[]{:S(2)}) collective-permute-start(bf16[1,6,160,128]{3,2,1,0:T(8,128)(2,1)S(1)} %get-tuple-element.11), channel_id=1, source_target_pairs={{0,2},{1,3},{2,0},{3,1},{4,6},{5,7},{6,4},{7,5},{8,10},{9,11},{10,... | collective-permute-start | bytes 737288 | tf_op jit(solution)/shard_map/ppermute | solution.py:32
  44.1 5.8 %collective-permute-start.11 = (bf16[120,512]{1,0:T(8,128)(2,1)S(1)}, bf16[120,512]{1,0:T(8,128)(2,1)S(1)}, u32[]{:S(2)}, u32[]{:S(2)}) collective-permute-start(bf16[120,512]{1,0:T(8,128)(2,1)S(1)} %get-tuple-element.15), channel_id=1, source_target_pairs={{0,8},{1,9},{2,10},{3,11},{4,12},{5,13},{6,14},{7,15},{8,0},{9,1},... | collective-permute-start | bytes 368648 | tf_op jit(solution)/shard_map/ppermute | solution.py:32
  50.4 6.1 %collective-permute-start.12 = (bf16[60,512]{1,0:T(8,128)(2,1)S(1)}, bf16[60,512]{1,0:T(8,128)(2,1)S(1)}, u32[]{:S(2)}, u32[]{:S(2)}) collective-permute-start(bf16[60,512]{1,0:T(8,128)(2,1)S(1)} %get-tuple-element.17), channel_id=1, source_target_pairs={{0,16},{1,17},{2,18},{3,19},{4,20},{5,21},{6,22},{7,23},{8,24},{9,... | collective-permute-start | bytes 184328 | tf_op jit(solution)/shard_map/ppermute | solution.py:32

commit v2 on v1

--- a/solution.py
+++ b/solution.py
@@ -14,6 +14,7 @@
 TOP_POWER = 2.0**15.5
 LEAST_PEAK = 1e-30
 VMEM_BYTES = 40 * 2**20
+LAST_FLOPS = 10**10
 
 
 def padded_lanes(count):
@@ -32,12 +33,13 @@
     return lax.ppermute(value, AXES, pairs)
 
 
-def call(kernel, out_shape, operands, scratch=(), flops=0):
+def call(kernel, out_shape, operands, scratch=(), flops=0, far=0):
     moved = sum(x.size * x.dtype.itemsize for x in operands)
+    spaces = [pl.ANY] * far + [pltpu.VMEM] * (len(operands) - far)
     return pl.pallas_call(
         kernel,
         out_shape=out_shape,
-        in_specs=[pl.BlockSpec(memory_space=pltpu.VMEM)] * len(operands),
+        in_specs=[pl.BlockSpec(memory_space=space) for space in spaces],
         out_specs=jax.tree.map(lambda _: pl.BlockSpec(memory_space=pltpu.VMEM), out_shape),
         scratch_shapes=list(scratch),
         compiler_params=pltpu.CompilerParams(vmem_limit_bytes=VMEM_BYTES),
@@ -96,8 +98,7 @@
         return turned * 2 + low
 
     def slot_of(self, difference):
-        bits = self.band_bits - 2
-        return sum(((difference >> (k + 1)) & 1) << (bits - 1 - k) for k in range(bits))
+        return (difference // 2) % self.inner
 
 
 def place(plan):
@@ -128,7 +129,15 @@
     return jnp.where(inside, turned, 0.0)
 
 
-def terms_kernel(plan, sends, act0, act1, grad0, grad1, top0, top1, bottom0, bottom1, out, left, right):
+def near_kernel(far0, far1, near0, near1, sems):
+    copies = [pltpu.make_async_copy(far0, near0, sems.at[0]), pltpu.make_async_copy(far1, near1, sems.at[1])]
+    for copy in copies:
+        copy.start()
+    for copy in copies:
+        copy.wait()
+
+
+def terms_kernel(plan, sends, act0, grad0, act1, grad1, top0, top1, bottom0, bottom1, out, left, right):
     _, strip, core, low, high = place(plan)
     mine = jnp.where(core == 0, high, low)
     first = 1 - mine if sends else mine
@@ -174,23 +183,26 @@
             out[q] = total
 
 
-def turn_kernel(plan, keep, message, send, kept):
+def turn_kernel(plan, sends, keep, message, out):
     _, _, core, low, high = place(plan)
     mine = jnp.where(core == 0, low, high)
-    total = keep[1 - mine] + decoded(message[1 - mine])
-    send[...] = encoded(peak_of(total, plan.half_used), total, plan.half_used)
-    kept[...] = keep[mine] + decoded(message[mine])
-
-
-def halve_kernel(plan, mask, used, keep, message, send, kept):
-    band = lax.axis_index("band")
-    side = (band // mask) % 2
+    if sends:
+        total = keep[1 - mine] + decoded(message[1 - mine])
+        out[...] = encoded(peak_of(total, plan.half_used), total, plan.half_used)
+    else:
+        out[...] = keep[mine] + decoded(message[mine])
+
+
+def halve_kernel(plan, mask, used, sends, keep, message, out):
+    side = (lax.axis_index("band") // mask) % 2
     total = keep[...] + decoded(message[...])
     rows = total.shape[0] // 2
     lower, upper = total[:rows], total[rows:]
-    given = jnp.where(side == 0, upper, lower)
-    send[...] = encoded(peak_of(given, used), given, used)
-    kept[...] = jnp.where(side == 0, lower, upper)
+    if sends:
+        given = jnp.where(side == 0, upper, lower)
+        out[...] = encoded(peak_of(given, used), given, used)
+    else:
+        out[...] = jnp.where(side == 0, lower, upper)
 
 
 def last_kernel(plan, scale, keep, message, out):
@@ -272,12 +284,26 @@
             out[n, h] = jnp.concatenate(pieces, axis=0).astype(jnp.bfloat16)
 
 
-def whole_kernel(plan, kernel):
-    sizes, f32 = plan.sizes, jnp.float32
+def after(value, *others):
+    return lax.optimization_barrier((value, *others))[0]
+
+
+def joined(packed, come, start):
+    return after(jnp.concatenate([packed, after(come, start)], axis=0), start)
+
+
+def first_kernel(plan, kernel):
     shape = jax.ShapeDtypeStruct((plan.block_rows, plan.lanes), jnp.bfloat16)
     packed = call(functools.partial(pack_kernel, plan), shape, [kernel])[None]
-    for mask in reversed(plan.rest_band):
-        packed = jnp.concatenate([packed, swap(packed, sizes, mask, 0)], axis=0)
+    return [packed] + [swap(packed, plan.sizes, mask, 0) for mask in plan.rest_band[:1]]
+
+
+def whole_kernel(plan, packed, starts):
+    sizes = plan.sizes
+    starts = list(starts)
+    packed = joined(*packed, starts.pop(0)) if len(packed) > 1 else packed[0]
+    for mask in plan.rest_band[1:]:
+        packed = joined(packed, swap(packed, sizes, mask, 0), starts.pop(0))
     if plan.rest_strip:
         packed = packed[None]
         for mask in reversed(plan.rest_strip):
@@ -289,7 +315,7 @@
         packed = packed.transpose(1, 2, 3, 0, 4).reshape(plan.inner, plan.block_rows, plan.half_used)
         packed = jnp.pad(packed, ((0, 0), (0, 0), (0, plan.half_lanes - plan.half_used)))
     by_row, by_col = (2, 0), (0, plan.top_strip)
-    packed = jnp.concatenate([packed, swap(packed, sizes, *by_row, other_masks=by_col)], axis=0)
+    packed = joined(packed, swap(packed, sizes, *by_row, other_masks=by_col), starts.pop(0))
     return packed, swap(packed, sizes, *by_col, other_masks=by_row)
 
 
@@ -315,42 +341,45 @@
         pltpu.VMEM((plan.half_used, depth), jnp.bfloat16),
     ]
     flops = 4 * rows * plan.half_used * depth
+    steps = []
+
+    def done(value):
+        steps.append(value)
+        return value
+
+    shape = (2, rows, lanes)
     send = call(
         functools.partial(terms_kernel, plan, True),
-        jax.ShapeDtypeStruct((2, rows, lanes), jnp.bfloat16), cells, scratch, flops,
+        jax.ShapeDtypeStruct(shape, jnp.bfloat16), cells, scratch, flops,
     )
-    keep = call(
+    keep = done(call(
         functools.partial(terms_kernel, plan, False),
-        jax.ShapeDtypeStruct((2, rows, lanes), f32), cells, scratch, flops,
-    )
+        jax.ShapeDtypeStruct(shape, f32), [*cells[:4], after(cells[4], send), *cells[5:]], scratch, flops,
+    ))
     by_row, by_col = (2, 0), (0, plan.top_strip)
     come = swap(send, sizes, *by_col, other_masks=by_row)
-    send, keep = call(
-        functools.partial(turn_kernel, plan),
-        (jax.ShapeDtypeStruct((rows, lanes), jnp.bfloat16), jax.ShapeDtypeStruct((rows, lanes), f32)),
-        [keep, come],
-    )
+    shape = (rows, lanes)
+    turn = functools.partial(turn_kernel, plan)
+    send = call(functools.partial(turn, True), jax.ShapeDtypeStruct(shape, jnp.bfloat16), [keep, come])
+    keep = done(call(functools.partial(turn, False), jax.ShapeDtypeStruct(shape, f32), [after(keep, send), come]))
     come = swap(send, sizes, *by_row, other_masks=by_col)
     if plan.rest_strip:
-        total = keep[:, :] + decoded(come)
-        keep = narrowed(plan, total)
+        keep = narrowed(plan, keep + decoded(come))
         come = jnp.zeros(keep.shape, jnp.bfloat16)
     for mask in plan.rest_band:
         rows //= 2
-        send, keep = call(
-            functools.partial(halve_kernel, plan, mask, plan.used),
-            (
-                jax.ShapeDtypeStruct((rows, plan.lanes), jnp.bfloat16),
-                jax.ShapeDtypeStruct((rows, plan.lanes), f32),
-            ),
-            [keep, come],
-        )
+        shape = (rows, plan.lanes)
+        halve = functools.partial(halve_kernel, plan, mask, plan.used)
+        send = call(functools.partial(halve, True), jax.ShapeDtypeStruct(shape, jnp.bfloat16), [keep, come])
+        keep = done(call(functools.partial(halve, False), jax.ShapeDtypeStruct(shape, f32), [after(keep, send), come]))
         come = swap(send, sizes, mask, 0)
-    return call(
+    total = call(
         functools.partial(last_kernel, plan, scale),
         jax.ShapeDtypeStruct((len(TAP_STEPS) ** 2, plan.depth, plan.cols), f32),
         [keep, come],
+        flops=LAST_FLOPS,
     )
+    return total, steps
 
 
 def borders(plan, grad):
@@ -376,21 +405,26 @@
     edges = borders(plan, grad)
     act1 = swap(act, plan.sizes, 1, 0)
     grad1 = swap(grad, plan.sizes, 1, 0)
+    shape = jax.ShapeDtypeStruct(act.shape, act.dtype)
+    act0, grad0 = call(near_kernel, (shape, shape), [act, grad], [pltpu.SemaphoreType.DMA((2,))], far=2)
+    edges = [after(edge, act0, grad0) for edge in edges]
     edges1 = [swap(edge, plan.sizes, 1, 0) for edge in edges]
-    near = [grad, grad1, edges[0], edges1[0], edges[-1], edges1[-1]]
-    kernel_grad = kernel_terms(plan, [act, act1, *near], scale)
-    packed = whole_kernel(plan, kernel.transpose(1, 0, 2))
+    near = [grad1, edges[0], edges1[0], edges[-1], edges1[-1]]
+    packed = first_kernel(plan, kernel.transpose(1, 0, 2))
+    near[2] = after(near[2], packed[-1])
+    kernel_grad, steps = kernel_terms(plan, [act0, grad0, act1, *near], scale)
+    packed = whole_kernel(plan, packed, steps + [steps[-1]] * plan.band_bits)
+    packed = (after(packed[0], steps[-1]), packed[1])
     depth = 2 * images * rows * width
     shape = jax.ShapeDtypeStruct((images, rows, plan.half, width), jnp.bfloat16)
     mine, given = call(
         functools.partial(cells_kernel, plan),
         (shape, shape),
-        [*packed, *near],
+        [*packed, grad0, *near],
         [
             pltpu.VMEM((len(TAP_STEPS) * plan.half, 2 * plan.half_lanes), jnp.bfloat16),
             pltpu.VMEM((2 * plan.half_lanes, depth), jnp.bfloat16),
         ],
-        2 * len(TAP_STEPS) * plan.half * 2 * plan.half_lanes * depth,
     )
     theirs = swap(given, plan.sizes, 1, 0)
     input_grad = call(

time: 57.5 us -> 49.1 us (0.85)
  waiting for transfers between devices: 30.8 us -> 14.3 us
  starting transfers between devices: 14 us -> 18.2 us
  Pallas kernels: 10.8 us -> 12.3 us
  local copies, waits for them, and re-layouts: 0.96 us -> 2.22 us
  other arithmetic: 0.11 us -> 1.04 us
    ppermute x13, waiting for transfers between devices: 30.8 us -> 14.3 us  [swap(): return lax.ppermute(value, AXES, pairs)]
    ppermute x13, starting transfers between devices: 14 us -> 18.2 us  [swap(): return lax.ppermute(value, AXES, pairs)]
    pallas_call x9 -> x13, Pallas kernels: 10.8 us -> 12.3 us  [call(): pl.pallas_call(kernel, out_shape=out_shape, in_specs=[pl.BlockSpec(memory...]
    unnamed x6, local copies, waits for them, and re-layouts: 0.96 us -> 2.22 us
    select_n x1, other arithmetic: 0.01 us -> 0.94 us  [borders(): come = swap(jnp.where(strip == 0, last, first), plan.sizes, 0, 1)]
  transfers between devices with their start and end apart: 13 -> 13, of which waited for: 8 -> 6; matrix products, arithmetic and copies ran while one was open for 0% -> 2% of each run, Pallas kernels for 17% -> 19%
where the time goes in v2:
time: 49.1 us; the launch traced here: 48.8 us
  starting transfers between devices  18.2 us (37%)
  waiting for transfers between devices  14.3 us (29%)
  Pallas kernels  12.3 us (25%)
  local copies, waits for them, and re-layouts  2.22 us (5%)
  other arithmetic  1.04 us (2%)
  between operations  0.79 us (2%)
    ppermute x13, starting transfers between devices, swap(): return lax.ppermute(value, AXES, pairs)  18.2 us
    ppermute x13, waiting for transfers between devices, swap(): return lax.ppermute(value, AXES, pairs)  14.3 us
    pallas_call x13, Pallas kernels, call(): pl.pallas_call(kernel, out_shape=out_shape, in_specs=[pl.BlockSpec(memory...  12.3 us
    unnamed x6, local copies, waits for them, and re-layouts  2.22 us
  transfers between devices with their start and end apart: 13, of which 6 were waited for; matrix products, arithmetic and copies ran while one was open for 2% of the time, Pallas kernels for 19%

profile of v2, /device:TPU:0, one launch (start us, length us, event | category | flops | bytes accessed | tf_op | source)
XLA Modules:
  0.0 48.8 jit_solution(8126385585232940255)
XLA Ops:
  0.6 0.5 %collective-permute-start.1 = (bf16[1,6,320,128]{3,2,1,0:T(8,128)(2,1)}, bf16[1,6,320,128]{3,2,1,0:T(8,128)(2,1)S(1)}, u32[]{:S(2)}, u32[]{:S(2)}) collective-permute-start(bf16[1,6,320,128]{3,2,1,0:T(8,128)(2,1)} %bitcast.11), channel_id=1, source_target_pairs={{0,2},{1,3},{2,0},{3,1},{4,6},{5,7},{6,4},{7,5},{8,10},{9,11},{10,... | collective-permute-start | bytes 1474568 | tf_op jit(solution)/shard_map/ppermute | solution.py:33
  1.1 0.1 collective-permute-start.2
  1.2 0.9 %fusion = bf16[1,320,128]{2,1,0:T(8,128)(2,1)S(1)} fusion(bf16[1,6,320,128]{3,2,1,0:T(8,128)(2,1)} %bitcast.9, pred[]{:T(512)S(6)} %eq.3), kind=kLoop, calls=%fused_computation.4 | loop fusion | flops 40960 | bytes 245761 | tf_op jit(solution)/shard_map/jit(_where)/select_n | solution.py:389
  2.2 3.0 %collective-permute-start.3 = (bf16[1,320,128]{2,1,0:T(8,128)(2,1)S(1)}, bf16[1,320,128]{2,1,0:T(8,128)(2,1)S(1)}, u32[]{:S(2)}, u32[]{:S(2)}) collective-permute-start(bf16[1,320,128]{2,1,0:T(8,128)(2,1)S(1)} %fusion), channel_id=1, source_target_pairs={{0,1},{1,0},{2,3},{3,2},{4,5},{5,4},{6,7},{7,6},{8,9},{9,8},{10,11... | collective-permute-start | bytes 245768 | tf_op jit(solution)/shard_map/ppermute | solution.py:33
  5.1 0.0 copy-start
  5.2 1.0 %copy-done = bf16[1,320,6,128]{3,1,2,0:T(8,128)(2,1)S(1)} copy-done((bf16[1,320,6,128]{3,1,2,0:T(8,128)(2,1)S(1)}, bf16[1,320,6,128]{3,1,2,0:T(8,128)(2,1)}, u32[]{:S(2)}) %copy-start) | copy-done | bytes 491544
  6.2 0.0 copy-start.1
  6.2 1.0 %copy-done.1 = bf16[1,320,6,128]{3,1,2,0:T(8,128)(2,1)S(1)} copy-done((bf16[1,320,6,128]{3,1,2,0:T(8,128)(2,1)S(1)}, bf16[1,320,6,128]{3,1,2,0:T(8,128)(2,1)}, u32[]{:S(2)}) %copy-start.1) | copy-done | bytes 491544
  7.2 0.0 copy-start.2
  7.2 0.6 %shard_map.51 = (bf16[1,6,320,128]{3,2,1,0:T(8,128)(2,1)S(1)}, bf16[1,6,320,128]{3,2,1,0:T(8,128)(2,1)S(1)}) custom-call(bf16[1,6,320,128]{3,2,1,0:T(8,128)(2,1)S(1)} %bitcast.12, bf16[1,6,320,128]{3,2,1,0:T(8,128)(2,1)S(1)} %bitcast.10), custom_call_target="tpu_custom_call" | custom-call | bytes 1966080 | tf_op jit(solution)/shard_map/pallas_call | solution.py:39
  7.9 0.0 collective-permute-done.3.top0.bottom0
  7.9 0.1 collective-permute-start.4
  8.0 0.2 copy-done.2
  8.1 0.1 shard_map.50
  8.2 1.6 %collective-permute-start = (bf16[1,60,512]{2,1,0:T(8,128)(2,1)S(1)}, bf16[1,60,512]{2,1,0:T(8,128)(2,1)S(1)}, u32[]{:S(2)}, u32[]{:S(2)}) collective-permute-start(bf16[1,60,512]{2,1,0:T(8,128)(2,1)S(1)} %bitcast.13), channel_id=1, source_target_pairs={{0,8},{1,9},{2,10},{3,11},{4,12},{5,13},{6,14},{7,15},{8,0},{9,1},... | collective-permute-start | bytes 184328 | tf_op jit(solution)/shard_map/ppermute | solution.py:33
  9.8 2.8 %collective-permute-done = bf16[1,60,512]{2,1,0:T(8,128)(2,1)S(1)} collective-permute-done((bf16[1,60,512]{2,1,0:T(8,128)(2,1)S(1)}, bf16[1,60,512]{2,1,0:T(8,128)(2,1)S(1)}, u32[]{:S(2)}, u32[]{:S(2)}) %collective-permute-start) | collective-permute-done | bytes 61472 | tf_op jit(solution)/shard_map/ppermute | solution.py:33
  12.6 0.0 collective-permute-done.4.top1.bottom1
  12.6 0.0 collective-permute-done.1.act1
  12.6 0.0 collective-permute-done.2.grad1
  12.6 2.3 %shard_map.52 = bf16[2,240,512]{2,1,0:T(8,128)(2,1)S(1)} custom-call(bf16[1,6,320,128]{3,2,1,0:T(8,128)(2,1)S(1)} %get-tuple-element.19.act0, bf16[1,6,320,128]{3,2,1,0:T(8,128)(2,1)S(1)} %get-tuple-element.20.grad0, bf16[1,6,320,128]{3,2,1,0:T(8,128)(2,1)S(1)} %collective-permute-done.1.act1, bf16[1,6,320,128]{3,2,1,0:T(8,128)(2,1)S(1)} %collective-permute-done.2.grad1, ...), custom_call_target="tpu_custom_call" | custom-call | flops 707788800 | bytes 4587520 | tf_op jit(solution)/shard_map/pallas_call | solution.py:39
  14.9 1.7 %collective-permute-start.6 = (bf16[2,240,512]{2,1,0:T(8,128)(2,1)S(1)}, bf16[2,240,512]{2,1,0:T(8,128)(2,1)S(1)}, u32[]{:S(2)}, u32[]{:S(2)}) collective-permute-start(bf16[2,240,512]{2,1,0:T(8,128)(2,1)S(1)} %shard_map.52), channel_id=1, source_target_pairs={{0,1},{1,0},{2,6},{3,7},{4,5},{5,4},{6,2},{7,3},{8,9},{9,8},{10,14... | collective-permute-start | bytes 1474568 | tf_op jit(solution)/shard_map/ppermute | solution.py:33
  16.6 1.7 %shard_map.53.keep = f32[2,240,512]{2,1,0:T(8,128)S(1)} custom-call(bf16[1,6,320,128]{3,2,1,0:T(8,128)(2,1)S(1)} %get-tuple-element.19.act0, bf16[1,6,320,128]{3,2,1,0:T(8,128)(2,1)S(1)} %get-tuple-element.20.grad0, bf16[1,6,320,128]{3,2,1,0:T(8,128)(2,1)S(1)} %collective-permute-done.1.act1, bf16[1,6,320,128]{3,2,1,0:T(8,128)(2,1)S(1)} %collective-permute-done.2.grad1, ...), custom_call_target="tpu_custom_call" | custom-call | flops 707788800 | bytes 4587520 | tf_op jit(solution)/shard_map/pallas_call | solution.py:39
  18.4 2.7 %collective-permute-start.5 = (bf16[2,60,512]{2,1,0:T(8,128)(2,1)S(1)}, bf16[2,60,512]{2,1,0:T(8,128)(2,1)S(1)}, u32[]{:S(2)}, u32[]{:S(2)}) collective-permute-start(bf16[2,60,512]{2,1,0:T(8,128)(2,1)S(1)} %pad_maximum_fusion.2), channel_id=1, source_target_pairs={{0,16},{1,17},{2,18},{3,19},{4,20},{5,21},{6,22},{7,23},{8,24},{9,... | collective-permute-start | bytes 368648 | tf_op jit(solution)/shard_map/ppermute | solution.py:33
  21.1 2.8 %collective-permute-done.6.message = bf16[2,240,512]{2,1,0:T(8,128)(2,1)S(1)} collective-permute-done((bf16[2,240,512]{2,1,0:T(8,128)(2,1)S(1)}, bf16[2,240,512]{2,1,0:T(8,128)(2,1)S(1)}, u32[]{:S(2)}, u32[]{:S(2)}) %collective-permute-start.6) | collective-permute-done | bytes 491552 | tf_op jit(solution)/shard_map/ppermute | solution.py:33
  23.8 1.0 %shard_map.54 = bf16[240,512]{1,0:T(8,128)(2,1)S(1)} custom-call(f32[2,240,512]{2,1,0:T(8,128)S(1)} %shard_map.53.keep, bf16[2,240,512]{2,1,0:T(8,128)(2,1)S(1)} %collective-permute-done.6.message), custom_call_target="tpu_custom_call" | custom-call | bytes 2949120 | tf_op jit(solution)/shard_map/pallas_call | solution.py:39
  24.8 1.7 %collective-permute-start.8 = (bf16[240,512]{1,0:T(8,128)(2,1)S(1)}, bf16[240,512]{1,0:T(8,128)(2,1)S(1)}, u32[]{:S(2)}, u32[]{:S(2)}) collective-permute-start(bf16[240,512]{1,0:T(8,128)(2,1)S(1)} %shard_map.54), channel_id=1, source_target_pairs={{0,4},{1,5},{2,3},{3,2},{4,0},{5,1},{6,7},{7,6},{8,12},{9,13},{10,... | collective-permute-start | bytes 737288 | tf_op jit(solution)/shard_map/ppermute | solution.py:33
  26.6 0.6 %shard_map.55.keep = f32[240,512]{1,0:T(8,128)S(1)} custom-call(f32[2,240,512]{2,1,0:T(8,128)S(1)} %shard_map.53.keep, bf16[2,240,512]{2,1,0:T(8,128)(2,1)S(1)} %collective-permute-done.6.message), custom_call_target="tpu_custom_call" | custom-call | bytes 2949120 | tf_op jit(solution)/shard_map/pallas_call | solution.py:39
  27.1 0.0 collective-permute-done.5
  27.2 0.5 collective-permute-start.7
  27.6 3.4 %collective-permute-done.8.message = bf16[240,512]{1,0:T(8,128)(2,1)S(1)} collective-permute-done((bf16[240,512]{1,0:T(8,128)(2,1)S(1)}, bf16[240,512]{1,0:T(8,128)(2,1)S(1)}, u32[]{:S(2)}, u32[]{:S(2)}) %collective-permute-start.8) | collective-permute-done | bytes 245792 | tf_op jit(solution)/shard_map/ppermute | solution.py:33
  31.1 0.8 %shard_map.56 = bf16[120,512]{1,0:T(8,128)(2,1)S(1)} custom-call(f32[240,512]{1,0:T(8,128)S(1)} %shard_map.55.keep, bf16[240,512]{1,0:T(8,128)(2,1)S(1)} %collective-permute-done.8.message), custom_call_target="tpu_custom_call" | custom-call | bytes 1474560 | tf_op jit(solution)/shard_map/pallas_call | solution.py:39
  31.9 0.6 %shard_map.57.keep = f32[120,512]{1,0:T(8,128)S(1)} custom-call(f32[240,512]{1,0:T(8,128)S(1)} %shard_map.55.keep, bf16[240,512]{1,0:T(8,128)(2,1)S(1)} %collective-permute-done.8.message), custom_call_target="tpu_custom_call" | custom-call | bytes 1474560 | tf_op jit(solution)/shard_map/pallas_call | solution.py:39
  32.5 1.4 %collective-permute-done.7 = bf16[4,60,512]{2,1,0:T(8,128)(2,1)S(1)} collective-permute-done((bf16[4,60,512]{2,1,0:T(8,128)(2,1)S(1)}, bf16[4,60,512]{2,1,0:T(8,128)(2,1)S(1)}, u32[]{:S(2)}, u32[]{:S(2)}) %collective-permute-start.7) | collective-permute-done | bytes 245792 | tf_op jit(solution)/shard_map/ppermute | solution.py:33
  33.9 0.1 pad_maximum_fusion.own
  33.9 1.7 %collective-permute-start.10 = (bf16[8,60,512]{2,1,0:T(8,128)(2,1)S(1)}, bf16[8,60,512]{2,1,0:T(8,128)(2,1)S(1)}, u32[]{:S(2)}, u32[]{:S(2)}) collective-permute-start(bf16[8,60,512]{2,1,0:T(8,128)(2,1)S(1)} %pad_maximum_fusion.own), channel_id=1, source_target_pairs={{0,1},{1,0},{2,6},{3,7},{4,5},{5,4},{6,2},{7,3},{8,9},{9,8},{10,14... | collective-permute-start | bytes 1474568 | tf_op jit(solution)/shard_map/ppermute | solution.py:33
  35.6 1.6 %collective-permute-start.9 = (bf16[120,512]{1,0:T(8,128)(2,1)S(1)}, bf16[120,512]{1,0:T(8,128)(2,1)S(1)}, u32[]{:S(2)}, u32[]{:S(2)}) collective-permute-start(bf16[120,512]{1,0:T(8,128)(2,1)S(1)} %shard_map.56), channel_id=1, source_target_pairs={{0,8},{1,9},{2,10},{3,11},{4,12},{5,13},{6,14},{7,15},{8,0},{9,1},... | collective-permute-start | bytes 368648 | tf_op jit(solution)/shard_map/ppermute | solution.py:33
  37.2 3.3 %collective-permute-done.9.message = bf16[120,512]{1,0:T(8,128)(2,1)S(1)} collective-permute-done((bf16[120,512]{1,0:T(8,128)(2,1)S(1)}, bf16[120,512]{1,0:T(8,128)(2,1)S(1)}, u32[]{:S(2)}, u32[]{:S(2)}) %collective-permute-start.9) | collective-permute-done | bytes 122912 | tf_op jit(solution)/shard_map/ppermute | solution.py:33
  40.5 0.5 shard_map.58
  41.0 3.0 %collective-permute-start.12 = (bf16[60,512]{1,0:T(8,128)(2,1)S(1)}, bf16[60,512]{1,0:T(8,128)(2,1)S(1)}, u32[]{:S(2)}, u32[]{:S(2)}) collective-permute-start(bf16[60,512]{1,0:T(8,128)(2,1)S(1)} %shard_map.58), channel_id=1, source_target_pairs={{0,16},{1,17},{2,18},{3,19},{4,20},{5,21},{6,22},{7,23},{8,24},{9,... | collective-permute-start | bytes 184328 | tf_op jit(solution)/shard_map/ppermute | solution.py:33
  44.0 0.3 shard_map.59.keep
  44.3 0.0 collective-permute-done.10.other
  44.3 2.0 %shard_map.60 = (bf16[1,6,160,128]{3,2,1,0:T(8,128)(2,1)S(1)}, bf16[1,6,160,128]{3,2,1,0:T(8,128)(2,1)S(1)}) custom-call(bf16[8,60,512]{2,1,0:T(8,128)(2,1)S(1)} %pad_maximum_fusion.own, bf16[8,60,512]{2,1,0:T(8,128)(2,1)S(1)} %collective-permute-done.10.other, bf16[1,6,320,128]{3,2,1,0:T(8,128)(2,1)S(1)} %get-tuple-element.20.grad0, ...), custom_call_target="tpu_custom_call" | custom-call | bytes 4587520 | tf_op jit(solution)/shard_map/pallas_call | solution.py:39
  46.3 0.1 collective-permute-start.11
  46.4 0.0 collective-permute-done.12.message
  46.4 0.9 %shard_map.62 = f32[9,20,160]{2,1,0:T(8,128)} custom-call(f32[60,512]{1,0:T(8,128)S(1)} %shard_map.59.keep, bf16[60,512]{1,0:T(8,128)(2,1)S(1)} %collective-permute-done.12.message), custom_call_target="tpu_custom_call" | custom-call | flops 10000000000 | bytes 368640 | tf_op jit(solution)/shard_map/pallas_call | solution.py:39
  47.3 0.6 %collective-permute-done.11.theirs = bf16[1,6,160,128]{3,2,1,0:T(8,128)(2,1)S(1)} collective-permute-done((bf16[1,6,160,128]{3,2,1,0:T(8,128)(2,1)S(1)}, bf16[1,6,160,128]{3,2,1,0:T(8,128)(2,1)S(1)}, u32[]{:S(2)}, u32[]{:S(2)}) %collective-permute-start.11) | collective-permute-done | bytes 245792 | tf_op jit(solution)/shard_map/ppermute | solution.py:33
  47.9 0.9 %shard_map.61 = bf16[1,6,320,128]{3,2,1,0:T(8,128)(2,1)} custom-call(bf16[1,6,160,128]{3,2,1,0:T(8,128)(2,1)S(1)} %get-tuple-element.34.mine, bf16[1,6,160,128]{3,2,1,0:T(8,128)(2,1)S(1)} %collective-permute-done.11.theirs), custom_call_target="tpu_custom_call" | custom-call | bytes 983040 | tf_op jit(solution)/shard_map/pallas_call | solution.py:39
  (2 shorter events, 0.0 us)
Async XLA Ops:
  0.6 12.0 %collective-permute-start.1 = (bf16[1,6,320,128]{3,2,1,0:T(8,128)(2,1)}, bf16[1,6,320,128]{3,2,1,0:T(8,128)(2,1)S(1)}, u32[]{:S(2)}, u32[]{:S(2)}) collective-permute-start(bf16[1,6,320,128]{3,2,1,0:T(8,128)(2,1)} %bitcast.11), channel_id=1, source_target_pairs={{0,2},{1,3},{2,0},{3,1},{4,6},{5,7},{6,4},{7,5},{8,10},{9,11},{10,... | collective-permute-start | bytes 1474568 | tf_op jit(solution)/shard_map/ppermute | solution.py:33
  1.1 11.5 %collective-permute-start.2 = (bf16[1,6,320,128]{3,2,1,0:T(8,128)(2,1)}, bf16[1,6,320,128]{3,2,1,0:T(8,128)(2,1)S(1)}, u32[]{:S(2)}, u32[]{:S(2)}) collective-permute-start(bf16[1,6,320,128]{3,2,1,0:T(8,128)(2,1)} %bitcast.8), channel_id=1, source_target_pairs={{0,2},{1,3},{2,0},{3,1},{4,6},{5,7},{6,4},{7,5},{8,10},{9,11},{10,... | collective-permute-start | bytes 1474568 | tf_op jit(solution)/shard_map/ppermute | solution.py:33
  2.2 5.7 %collective-permute-start.3 = (bf16[1,320,128]{2,1,0:T(8,128)(2,1)S(1)}, bf16[1,320,128]{2,1,0:T(8,128)(2,1)S(1)}, u32[]{:S(2)}, u32[]{:S(2)}) collective-permute-start(bf16[1,320,128]{2,1,0:T(8,128)(2,1)S(1)} %fusion), channel_id=1, source_target_pairs={{0,1},{1,0},{2,3},{3,2},{4,5},{5,4},{6,7},{7,6},{8,9},{9,8},{10,11... | collective-permute-start | bytes 245768 | tf_op jit(solution)/shard_map/ppermute | solution.py:33
  5.1 1.0 %copy-start = (bf16[1,320,6,128]{3,1,2,0:T(8,128)(2,1)S(1)}, bf16[1,320,6,128]{3,1,2,0:T(8,128)(2,1)}, u32[]{:S(2)}) copy-start(bf16[1,320,6,128]{3,1,2,0:T(8,128)(2,1)} %param.4) | copy-start | bytes 1474564
  6.2 1.0 %copy-start.1 = (bf16[1,320,6,128]{3,1,2,0:T(8,128)(2,1)S(1)}, bf16[1,320,6,128]{3,1,2,0:T(8,128)(2,1)}, u32[]{:S(2)}) copy-start(bf16[1,320,6,128]{3,1,2,0:T(8,128)(2,1)} %param.3) | copy-start | bytes 1474564
  7.2 0.9 %copy-start.2 = (bf16[20,9,160]{2,0,1:T(8,128)(2,1)S(1)}, bf16[20,9,160]{2,0,1:T(8,128)(2,1)}, u32[]{:S(2)}) copy-start(bf16[20,9,160]{2,0,1:T(8,128)(2,1)} %param.5) | copy-start | bytes 172804
  7.9 4.7 %collective-permute-start.4 = (bf16[1,320,128]{2,1,0:T(8,128)(2,1)S(1)}, bf16[1,320,128]{2,1,0:T(8,128)(2,1)S(1)}, u32[]{:S(2)}, u32[]{:S(2)}) collective-permute-start(bf16[1,320,128]{2,1,0:T(8,128)(2,1)S(1)} %collective-permute-done.3.top0.bottom0), channel_id=1, source_target_pairs={{0,2},{1,3},{2,0},{3,1},{4,6},{5,7},{6,4},{7,5},{8,10},{9,11},{10,... | collective-permute-start | bytes 245768 | tf_op jit(solution)/shard_map/ppermute | solution.py:33
  8.2 4.4 %collective-permute-start = (bf16[1,60,512]{2,1,0:T(8,128)(2,1)S(1)}, bf16[1,60,512]{2,1,0:T(8,128)(2,1)S(1)}, u32[]{:S(2)}, u32[]{:S(2)}) collective-permute-start(bf16[1,60,512]{2,1,0:T(8,128)(2,1)S(1)} %bitcast.13), channel_id=1, source_target_pairs={{0,8},{1,9},{2,10},{3,11},{4,12},{5,13},{6,14},{7,15},{8,0},{9,1},... | collective-permute-start | bytes 184328 | tf_op jit(solution)/shard_map/ppermute | solution.py:33
  14.9 8.9 %collective-permute-start.6 = (bf16[2,240,512]{2,1,0:T(8,128)(2,1)S(1)}, bf16[2,240,512]{2,1,0:T(8,128)(2,1)S(1)}, u32[]{:S(2)}, u32[]{:S(2)}) collective-permute-start(bf16[2,240,512]{2,1,0:T(8,128)(2,1)S(1)} %shard_map.52), channel_id=1, source_target_pairs={{0,1},{1,0},{2,6},{3,7},{4,5},{5,4},{6,2},{7,3},{8,9},{9,8},{10,14... | collective-permute-start | bytes 1474568 | tf_op jit(solution)/shard_map/ppermute | solution.py:33
  18.4 8.7 %collective-permute-start.5 = (bf16[2,60,512]{2,1,0:T(8,128)(2,1)S(1)}, bf16[2,60,512]{2,1,0:T(8,128)(2,1)S(1)}, u32[]{:S(2)}, u32[]{:S(2)}) collective-permute-start(bf16[2,60,512]{2,1,0:T(8,128)(2,1)S(1)} %pad_maximum_fusion.2), channel_id=1, source_target_pairs={{0,16},{1,17},{2,18},{3,19},{4,20},{5,21},{6,22},{7,23},{8,24},{9,... | collective-permute-start | bytes 368648 | tf_op jit(solution)/shard_map/ppermute | solution.py:33
  24.8 6.3 %collective-permute-start.8 = (bf16[240,512]{1,0:T(8,128)(2,1)S(1)}, bf16[240,512]{1,0:T(8,128)(2,1)S(1)}, u32[]{:S(2)}, u32[]{:S(2)}) collective-permute-start(bf16[240,512]{1,0:T(8,128)(2,1)S(1)} %shard_map.54), channel_id=1, source_target_pairs={{0,4},{1,5},{2,3},{3,2},{4,0},{5,1},{6,7},{7,6},{8,12},{9,13},{10,... | collective-permute-start | bytes 737288 | tf_op jit(solution)/shard_map/ppermute | solution.py:33
  27.2 6.7 %collective-permute-start.7 = (bf16[4,60,512]{2,1,0:T(8,128)(2,1)S(1)}, bf16[4,60,512]{2,1,0:T(8,128)(2,1)S(1)}, u32[]{:S(2)}, u32[]{:S(2)}) collective-permute-start(bf16[4,60,512]{2,1,0:T(8,128)(2,1)S(1)} %pad_maximum_fusion.1), channel_id=1, source_target_pairs={{0,4},{1,5},{2,3},{3,2},{4,0},{5,1},{6,7},{7,6},{8,12},{9,13},{10,... | collective-permute-start | bytes 737288 | tf_op jit(solution)/shard_map/ppermute | solution.py:33
  33.9 10.3 %collective-permute-start.10 = (bf16[8,60,512]{2,1,0:T(8,128)(2,1)S(1)}, bf16[8,60,512]{2,1,0:T(8,128)(2,1)S(1)}, u32[]{:S(2)}, u32[]{:S(2)}) collective-permute-start(bf16[8,60,512]{2,1,0:T(8,128)(2,1)S(1)} %pad_maximum_fusion.own), channel_id=1, source_target_pairs={{0,1},{1,0},{2,6},{3,7},{4,5},{5,4},{6,2},{7,3},{8,9},{9,8},{10,14... | collective-permute-start | bytes 1474568 | tf_op jit(solution)/shard_map/ppermute | solution.py:33
  35.6 4.9 %collective-permute-start.9 = (bf16[120,512]{1,0:T(8,128)(2,1)S(1)}, bf16[120,512]{1,0:T(8,128)(2,1)S(1)}, u32[]{:S(2)}, u32[]{:S(2)}) collective-permute-start(bf16[120,512]{1,0:T(8,128)(2,1)S(1)} %shard_map.56), channel_id=1, source_target_pairs={{0,8},{1,9},{2,10},{3,11},{4,12},{5,13},{6,14},{7,15},{8,0},{9,1},... | collective-permute-start | bytes 368648 | tf_op jit(solution)/shard_map/ppermute | solution.py:33
  41.0 5.4 %collective-permute-start.12 = (bf16[60,512]{1,0:T(8,128)(2,1)S(1)}, bf16[60,512]{1,0:T(8,128)(2,1)S(1)}, u32[]{:S(2)}, u32[]{:S(2)}) collective-permute-start(bf16[60,512]{1,0:T(8,128)(2,1)S(1)} %shard_map.58), channel_id=1, source_target_pairs={{0,16},{1,17},{2,18},{3,19},{4,20},{5,21},{6,22},{7,23},{8,24},{9,... | collective-permute-start | bytes 184328 | tf_op jit(solution)/shard_map/ppermute | solution.py:33
  46.3 1.6 %collective-permute-start.11 = (bf16[1,6,160,128]{3,2,1,0:T(8,128)(2,1)S(1)}, bf16[1,6,160,128]{3,2,1,0:T(8,128)(2,1)S(1)}, u32[]{:S(2)}, u32[]{:S(2)}) collective-permute-start(bf16[1,6,160,128]{3,2,1,0:T(8,128)(2,1)S(1)} %get-tuple-element.35), channel_id=1, source_target_pairs={{0,2},{1,3},{2,0},{3,1},{4,6},{5,7},{6,4},{7,5},{8,10},{9,11},{10,... | collective-permute-start | bytes 737288 | tf_op jit(solution)/shard_map/ppermute | solution.py:33

commit v3 on v2

v3 whole, which is shorter than its diff:
```python
import functools
import math

import jax
import jax.numpy as jnp
from jax import lax
from jax.experimental import pallas as pl
from jax.experimental.pallas import tpu as pltpu
from jax.sharding import PartitionSpec as P

AXES = ("band", "strip")
TAP_STEPS = (-1, 0, 1)
LANES = 128
TOP_POWER = 2.0**15.5
LEAST_PEAK = 1e-30
VMEM_BYTES = 40 * 2**20
PACK_FLOPS = 10**10
LAST_FLOPS = 10**10


def padded_lanes(count):
    return (count // LANES + 1) * LANES


def swap(value, sizes, *masks):
    bands, strips = sizes
    pairs = []
    for b in range(bands):
        for s in range(strips):
            masks_here = masks[b % len(masks)]
            pairs.append((b * strips + s, (b ^ masks_here[0]) * strips + (s ^ masks_here[1])))
    return lax.ppermute(value, AXES, pairs)


def call(kernel, out_shape, operands, scratch=(), flops=0):
    return pl.pallas_call(
        kernel,
        out_shape=out_shape,
        in_specs=[pl.BlockSpec(memory_space=pltpu.VMEM)] * len(operands),
        out_specs=jax.tree.map(lambda _: pl.BlockSpec(memory_space=pltpu.VMEM), out_shape),
        scratch_shapes=list(scratch),
        compiler_params=pltpu.CompilerParams(vmem_limit_bytes=VMEM_BYTES),
        cost_estimate=pl.CostEstimate(flops=flops, bytes_accessed=0, transcendentals=0),
    )(*operands)


def encoded(peak, value, used):
    lane = lax.broadcasted_iota(jnp.int32, value.shape, value.ndim - 1)
    ratio = value * (TOP_POWER / peak)
    square = ratio * ratio
    power = ratio * jnp.abs(ratio) * square * (square * square)
    return jnp.where(lane < used, power, peak).astype(jnp.bfloat16)


def decoded(message):
    power = message.astype(jnp.float32)
    peak = power[0:1, message.shape[1] - 1 : message.shape[1]]
    root = jnp.sqrt(jnp.sqrt(jnp.sqrt(jnp.abs(power))))
    return jnp.where(power < 0, -root, root) * (peak * (1.0 / TOP_POWER))


def peak_of(value, used):
    lane = lax.broadcasted_iota(jnp.int32, value.shape, value.ndim - 1)
    largest = jnp.max(jnp.where(lane < used, jnp.abs(value), 0.0))
    largest = jnp.maximum(largest * (1.0 + 2.0**-6), LEAST_PEAK)
    return jnp.full((1, 1), largest, jnp.float32).astype(jnp.bfloat16).astype(jnp.float32)


class Plan:
    def __init__(self, images, channels, rows, width, bands, strips):
        self.images, self.channels, self.rows, self.width = images, channels, rows, width
        self.bands, self.strips = bands, strips
        self.sizes = (bands, strips)
        self.depth = channels // bands
        self.cols = channels // strips
        self.blocks = bands // 2
        self.half = channels // 2
        self.strip_bits = strips.bit_length() - 1
        self.band_bits = bands.bit_length() - 1
        assert bands == 1 << self.band_bits and strips == 1 << self.strip_bits
        assert self.band_bits >= 3 and self.strip_bits >= 1
        self.top_strip = 1 << (self.strip_bits - 1)
        self.rest_strip = [1 << k for k in reversed(range(self.strip_bits - 1))]
        self.rest_band = [1 << k for k in range(3, self.band_bits)]
        self.inner = self.blocks // 4
        self.half_used = len(TAP_STEPS) * self.half
        self.half_lanes = padded_lanes(self.half_used)
        self.used = len(TAP_STEPS) * self.cols
        self.lanes = padded_lanes(self.used)
        self.block_rows = len(TAP_STEPS) * self.depth
        self.part_rows = self.inner * self.block_rows
        self.cells = 2 * images * rows * width
        by_row, by_next, by_col = (2, 0), (4, 0), (0, self.top_strip)
        self.term_masks = ((by_col, by_row), (by_row, by_next), (by_next, by_col))
        self.gather_masks = ((by_next, by_col), (by_row, by_next), (by_col, by_row))

    def block_of(self, slot, by_next, by_row):
        bits = self.band_bits - 3
        turned = sum(((slot >> k) & 1) << (bits - 1 - k) for k in range(bits))
        return turned * 4 + by_next * 2 + by_row

    def chunks(self):
        return [(d, n, h) for d in range(2) for n in range(self.images) for h in range(self.rows)]


def place(plan):
    band, strip = lax.axis_index("band"), lax.axis_index("strip")
    return band % 2, (band // 2) % 2, (band // 4) % 2, strip // plan.top_strip


def mine(plan):
    core, by_row, by_next, by_col = place(plan)
    order = ((by_col, by_row, by_next), (by_row, by_next, by_col))
    return [jnp.where(core == 0, a, b) for a, b in zip(*order)]


def part_at(plan, bits):
    core = lax.axis_index("band") % 2
    first, second, third = bits
    order = ((second, third, first), (first, second, third))
    return [jnp.where(core == 0, a, b) for a, b in zip(*order)]


def grad_row(plan, grad_ref, top_ref, bottom_ref, image, row, start, strip):
    if row < 0:
        piece = top_ref[image, pl.ds(start, plan.half), :]
        return jnp.where(strip > 0, piece, jnp.zeros_like(piece))
    if row >= plan.rows:
        piece = bottom_ref[image, pl.ds(start, plan.half), :]
        return jnp.where(strip < plan.strips - 1, piece, jnp.zeros_like(piece))
    return grad_ref[image, row, pl.ds(start, plan.half), :]


def moved(value, step):
    width = value.shape[-1]
    if step == 0:
        return value
    lane = lax.broadcasted_iota(jnp.int32, value.shape, value.ndim - 1)
    turned = pltpu.roll(value, (-step) % width, value.ndim - 1)
    inside = lane < width - step if step > 0 else lane >= -step
    return jnp.where(inside, turned, 0.0)


def acts_kernel(plan, act0, act1, out):
    core = lax.axis_index("band") % 2
    depth, width = plan.depth, plan.width
    for at, (d, n, h) in enumerate(plan.chunks()):
        cells = (act0, act1)[d][n, h].astype(jnp.float32)
        shifted = []
        for m in range(plan.blocks):
            begin = 2 * m * depth
            even, odd = cells[begin : begin + depth], cells[begin + depth : begin + 2 * depth]
            block = jnp.where(core == 0, even, odd)
            shifted.append([moved(block, step) for step in TAP_STEPS])
        for y in range(2):
            for z in range(2):
                pieces = []
                for slot in range(plan.inner):
                    pieces += shifted[plan.block_of(slot, z, y)]
                out[y, z, :, at * width : (at + 1) * width] = jnp.concatenate(pieces, axis=0).astype(jnp.bfloat16)


def grads_kernel(plan, grad0, grad1, top0, top1, bottom0, bottom1, out):
    strip = lax.axis_index("strip")
    half, width = plan.half, plan.width
    sources = ((grad0, top0, bottom0), (grad1, top1, bottom1))
    for at, (d, n, h) in enumerate(plan.chunks()):
        cells = slice(at * width, (at + 1) * width)
        for x in range(2):
            for r, row_step in enumerate(TAP_STEPS):
                out[x, r * half : (r + 1) * half, cells] = grad_row(
                    plan, *sources[d], n, h - row_step, x * half, strip
                )
            out[x, plan.half_used :, cells] = jnp.zeros((plan.half_lanes - plan.half_used, width), jnp.bfloat16)


def part_terms(plan, acts, grads, bits):
    y, z, x = part_at(plan, bits)
    return lax.dot_general(acts[y, z], grads[x], (((1,), (1,)), ((), ())), preferred_element_type=jnp.float32)


def send_kernel(plan, same, acts, grads, out):
    first, second, third = mine(plan)
    for k in range(2):
        total = part_terms(plan, acts, grads, (1 - first, second if same else 1 - second, third if k else 1 - third))
        out[k] = encoded(peak_of(total, plan.half_used), total, plan.half_used)


def keep_kernel(plan, acts, grads, out):
    first, second, third = mine(plan)
    for j in range(2):
        for k in range(2):
            out[j, k] = part_terms(plan, acts, grads, (first, second if j else 1 - second, third if k else 1 - third))


def turn_kernel(plan, same, keep, message, out):
    for k in range(2):
        total = keep[1 if same else 0, k] + decoded(message[k])
        out[k] = total if same else encoded(peak_of(total, plan.half_used), total, plan.half_used)


def part_kernel(plan, same, keep, message, out):
    k = 1 if same else 0
    total = keep[k] + decoded(message[k])
    out[...] = total if same else encoded(peak_of(total, plan.half_used), total, plan.half_used)


def halve_kernel(plan, mask, used, same, keep, message, out):
    side = (lax.axis_index("band") // mask) % 2
    total = keep[...] + decoded(message[...])
    rows = total.shape[0] // 2
    lower, upper = total[:rows], total[rows:]
    if same:
        out[...] = jnp.where(side == 0, lower, upper)
    else:
        given = jnp.where(side == 0, upper, lower)
        out[...] = encoded(peak_of(given, used), given, used)


def last_kernel(plan, scale, keep, message, out):
    total = (keep[...] + decoded(message[...])) * scale
    depth, cols = plan.depth, plan.cols
    for r in range(len(TAP_STEPS)):
        for c in range(len(TAP_STEPS)):
            out[r * len(TAP_STEPS) + c] = total[c * depth : (c + 1) * depth, r * cols : (r + 1) * cols]


def pack_kernel(plan, kernel, out):
    rows = []
    for c in range(len(TAP_STEPS)):
        pieces = [kernel[r * len(TAP_STEPS) + c].astype(jnp.float32) for r in range(len(TAP_STEPS))]
        pieces.append(jnp.zeros((plan.depth, plan.lanes - plan.used), jnp.float32))
        rows.append(jnp.concatenate(pieces, axis=1))
    out[...] = jnp.concatenate(rows, axis=0).astype(jnp.bfloat16)


def cells_kernel(plan, own, other, grads, out0, out1, left):
    core, row_bit, next_bit, col_bit = place(plan)
    rest = lax.axis_index("band") // 8
    depth, width, half, lanes = plan.depth, plan.width, plan.half, plan.half_lanes
    steps = len(TAP_STEPS)
    for x in range(2):
        rows = [[] for _ in TAP_STEPS]
        for m in range(plan.blocks):
            row, behind, col = (m % 2) ^ row_bit, (m // 2 % 2) ^ next_bit, x ^ col_bit
            one = jnp.where(core == 0, behind, col)
            two = jnp.where(core == 0, row, behind)
            three = jnp.where(core == 0, col, row)
            slot = (two * 2 + one) * plan.inner + ((m // 4) ^ rest)
            block = jnp.where(three == 0, own[slot], other[slot]).astype(jnp.float32)
            for c in range(steps):
                rows[c].append(block[c * depth : (c + 1) * depth])
        for c in range(steps):
            left[c * half : (c + 1) * half, x * lanes : (x + 1) * lanes] = jnp.concatenate(
                rows[c], axis=0
            ).astype(jnp.bfloat16)
    group = 2
    chunks = plan.chunks()
    for begin in range(0, len(chunks), group):
        part = chunks[begin : begin + group]
        product = jnp.dot(
            left[...],
            grads[:, begin * width : (begin + len(part)) * width],
            preferred_element_type=jnp.float32,
        )
        for k, (d, n, h) in enumerate(part):
            total = None
            for c, col_step in enumerate(TAP_STEPS):
                term = moved(product[c * half : (c + 1) * half, k * width : (k + 1) * width], -col_step)
                total = term if total is None else total + term
            (out0, out1)[d][n, h] = total.astype(jnp.bfloat16)


def weave_kernel(plan, own, theirs, out):
    core = lax.axis_index("band") % 2
    depth = plan.depth
    for n in range(plan.images):
        for h in range(plan.rows):
            a, b = own[n, h].astype(jnp.float32), theirs[n, h].astype(jnp.float32)
            even, odd = jnp.where(core == 0, a, b), jnp.where(core == 0, b, a)
            pieces = []
            for m in range(plan.blocks):
                pieces += [even[m * depth : (m + 1) * depth], odd[m * depth : (m + 1) * depth]]
            out[n, h] = jnp.concatenate(pieces, axis=0).astype(jnp.bfloat16)


def after(value, *others):
    return lax.optimization_barrier((value, *others))[0]


def joined(packed, come, start):
    return after(jnp.concatenate([packed, after(come, start)], axis=0), start)


def first_kernel(plan, kernel):
    shape = jax.ShapeDtypeStruct((plan.block_rows, plan.lanes), jnp.bfloat16)
    packed = call(functools.partial(pack_kernel, plan), shape, [kernel], flops=PACK_FLOPS)[None]
    return [packed] + [swap(packed, plan.sizes, (mask, 0)) for mask in plan.rest_band[:1]]


def whole_kernel(plan, packed, starts):
    sizes = plan.sizes
    starts = list(starts)
    packed = joined(*packed, starts.pop(0)) if len(packed) > 1 else packed[0]
    for mask in plan.rest_band[1:]:
        packed = jnp.concatenate([packed, swap(packed, sizes, (mask, 0))], axis=0)
    if plan.rest_strip:
        packed = packed[None]
        for mask in reversed(plan.rest_strip):
            packed = jnp.concatenate([packed, swap(packed, sizes, (0, mask))], axis=0)
        count = packed.shape[0]
        order = jnp.arange(count) ^ (lax.axis_index("strip") % count)
        packed = jnp.take(packed, order, axis=0)[..., : plan.used]
        packed = packed.reshape(count, plan.inner, plan.block_rows, len(TAP_STEPS), plan.cols)
        packed = packed.transpose(1, 2, 3, 0, 4).reshape(plan.inner, plan.block_rows, plan.half_used)
        packed = jnp.pad(packed, ((0, 0), (0, 0), (0, plan.half_lanes - plan.half_used)))
    for masks in plan.gather_masks[:-1]:
        packed = joined(packed, swap(packed, sizes, *masks), starts.pop(0))
    return packed, swap(packed, sizes, *plan.gather_masks[-1])


def narrowed(plan, total):
    rows = total.shape[0]
    total = total[:, : plan.half_used].reshape(rows, len(TAP_STEPS), plan.half)
    for mask in plan.rest_strip:
        side = (lax.axis_index("strip") // mask) % 2
        parts = total.reshape(rows, len(TAP_STEPS), 2, total.shape[2] // 2)
        kept = jnp.where(side == 0, parts[:, :, 0], parts[:, :, 1])
        given = jnp.where(side == 0, parts[:, :, 1], parts[:, :, 0])
        total = kept + swap(given, plan.sizes, (0, mask))
    total = total.reshape(rows, plan.used)
    return jnp.pad(total, ((0, 0), (0, plan.lanes - plan.used)))


def kernel_terms(plan, acts, grads, gathered, scale):
    sizes, f32 = plan.sizes, jnp.float32
    rows, lanes = plan.part_rows, plan.half_lanes
    flops = 0

    def run(kernel, shape, kind, operands, flops=0):
        return call(kernel, jax.ShapeDtypeStruct(shape, kind), operands, flops=flops)

    part = functools.partial
    b16 = jnp.bfloat16
    shape = (2, rows, lanes)
    send0 = run(part(send_kernel, plan, False), shape, b16, [acts, grads], flops)
    send1 = run(part(send_kernel, plan, True), shape, b16, [after(acts, send0, gathered), grads], flops)
    keep = run(part(keep_kernel, plan), (2, *shape), f32, [after(acts, send1), grads], 2 * flops)
    steps = [send1, keep]
    come0 = swap(send0, sizes, *plan.term_masks[0])
    come1 = swap(send1, sizes, *plan.term_masks[0])
    send = run(part(turn_kernel, plan, False), shape, b16, [keep, come0])
    come = swap(send, sizes, *plan.term_masks[1])
    keep = run(part(turn_kernel, plan, True), shape, f32, [after(keep, send), come1])
    steps.append(keep)
    shape = shape[1:]
    send = run(part(part_kernel, plan, False), shape, b16, [keep, come])
    keep = run(part(part_kernel, plan, True), shape, f32, [after(keep, send), come])
    steps.append(keep)
    come = swap(send, sizes, *plan.term_masks[2])
    if plan.rest_strip:
        keep = narrowed(plan, keep + decoded(come))
        come = jnp.zeros(keep.shape, b16)
    for mask in plan.rest_band:
        rows //= 2
        shape = (rows, plan.lanes)
        halve = part(halve_kernel, plan, mask, plan.used)
        send = run(part(halve, False), shape, b16, [keep, come])
        keep = run(part(halve, True), shape, f32, [after(keep, send), come])
        steps.append(keep)
        come = swap(send, sizes, (mask, 0))
    total = call(
        part(last_kernel, plan, scale),
        jax.ShapeDtypeStruct((len(TAP_STEPS) ** 2, plan.depth, plan.cols), f32),
        [keep, come],
        flops=LAST_FLOPS,
    )
    return total, steps


def borders(plan, grad):
    strip = lax.axis_index("strip")
    first, last = grad[:, 0], grad[:, plan.rows - 1]
    if plan.strips == 2:
        come = swap(jnp.where(strip == 0, last, first), plan.sizes, (0, 1))
        return [come]
    ends = plan.strips - 1
    return [
        lax.ppermute(last, "strip", [(i, i + 1) for i in range(ends)]),
        lax.ppermute(first, "strip", [(i + 1, i) for i in range(ends)]),
    ]


def body(activations, out_grad, kernel):
    images, channels, rows, width = activations.shape
    bands, strips = lax.axis_size("band"), lax.axis_size("strip")
    plan = Plan(images, channels, rows, width, bands, strips)
    scale = 1.0 / math.sqrt(images * bands * rows * strips * width)
    act = activations.transpose(0, 2, 1, 3)
    grad = out_grad.transpose(0, 2, 1, 3)
    edges = borders(plan, grad)
    act1 = swap(act, plan.sizes, (1, 0))
    grad1 = swap(grad, plan.sizes, (1, 0))
    packed = first_kernel(plan, kernel.transpose(1, 0, 2))
    shape = (2, 2, plan.part_rows, plan.cells)
    acts = call(functools.partial(acts_kernel, plan), jax.ShapeDtypeStruct(shape, act.dtype), [act, act1])
    edges = [after(edge, acts) for edge in edges]
    edges1 = [swap(edge, plan.sizes, (1, 0)) for edge in edges]
    shape = (2, plan.half_lanes, plan.cells)
    grads = call(
        functools.partial(grads_kernel, plan),
        jax.ShapeDtypeStruct(shape, grad.dtype),
        [grad, grad1, edges[0], edges1[0], edges[-1], edges1[-1]],
    )
    kernel_grad, steps = kernel_terms(plan, acts, grads, packed[-1], scale)
    packed = whole_kernel(plan, packed, steps + [steps[-1]] * plan.band_bits)
    shape = jax.ShapeDtypeStruct((images, rows, plan.half, width), jnp.bfloat16)
    own, given = call(
        functools.partial(cells_kernel, plan),
        (shape, shape),
        [after(packed[0], steps[-1]), packed[1], grads.reshape(2 * plan.half_lanes, plan.cells)],
        [pltpu.VMEM((len(TAP_STEPS) * plan.half, 2 * plan.half_lanes), jnp.bfloat16)],
    )
    theirs = swap(given, plan.sizes, (1, 0))
    input_grad = call(
        functools.partial(weave_kernel, plan),
        jax.ShapeDtypeStruct((images, rows, channels, width), jnp.bfloat16),
        [own, theirs],
    )
    return input_grad.transpose(0, 2, 1, 3), kernel_grad.transpose(1, 0, 2)


def solution(mesh):
    in_specs = (
        P("band", None, "strip", None),
        P("band", None, "strip", None),
        P("band", None, "strip"),
    )
    out_specs = (P("band", None, "strip", None), P("band", None, "strip"))
    return jax.shard_map(body, mesh=mesh, in_specs=in_specs, out_specs=out_specs, check_vma=False)
```

time: 49.1 us -> 52.6 us (1.071)
  starting transfers between devices: 18.2 us -> 20.1 us
  waiting for transfers between devices: 14.3 us -> 15.9 us
    ppermute x13 -> x14, starting transfers between devices: 18.2 us -> 20.1 us  [swap(): return lax.ppermute(value, AXES, pairs)]
    ppermute x13 -> x14, waiting for transfers between devices: 14.3 us -> 15.9 us  [swap(): return lax.ppermute(value, AXES, pairs)]
    pallas_call x13 -> x15, Pallas kernels: 12.3 us -> 12.7 us  [call(): pl.pallas_call(kernel, out_shape=out_shape, in_specs=[pl.BlockSpec(memory...]
  transfers between devices with their start and end apart: 13 -> 14, of which waited for: 6 -> 9; matrix products, arithmetic and copies ran while one was open for 2% -> 2% of each run, Pallas kernels for 19% -> 20%
where the time goes in v3:
time: 52.6 us; the launch traced here: 52.4 us
  starting transfers between devices  20.1 us (38%)
  waiting for transfers between devices  15.9 us (30%)
  Pallas kernels  12.7 us (24%)
  local copies, waits for them, and re-layouts  1.93 us (4%)
  other arithmetic  1.04 us (2%)
  between operations  0.78 us (1%)
    ppermute x14, starting transfers between devices, swap(): return lax.ppermute(value, AXES, pairs)  20.1 us
    ppermute x14, waiting for transfers between devices, swap(): return lax.ppermute(value, AXES, pairs)  15.9 us
    pallas_call x15, Pallas kernels, call(): pl.pallas_call(kernel, out_shape=out_shape, in_specs=[pl.BlockSpec(memory...  12.7 us
    unnamed x6, local copies, waits for them, and re-layouts  1.93 us
  transfers between devices with their start and end apart: 14, of which 9 were waited for; matrix products, arithmetic and copies ran while one was open for 2% of the time, Pallas kernels for 20%

profile of v3, /device:TPU:0, one launch (start us, length us, event | category | flops | bytes accessed | tf_op | source)
XLA Modules:
  0.0 52.4 jit_solution(10750759225305920905)
XLA Ops:
  0.6 0.5 collective-permute-start.1
  1.1 0.9 %fusion = bf16[1,320,128]{2,1,0:T(8,128)(2,1)S(1)} fusion(bf16[1,6,320,128]{3,2,1,0:T(8,128)(2,1)} %bitcast.10, pred[]{:T(512)S(6)} %eq.3), kind=kLoop, calls=%fused_computation.4 | loop fusion | flops 40960 | bytes 245761 | tf_op jit(solution)/shard_map/jit(_where)/select_n | solution.py:385
  2.1 2.6 %collective-permute-start.3 = (bf16[1,320,128]{2,1,0:T(8,128)(2,1)S(1)}, bf16[1,320,128]{2,1,0:T(8,128)(2,1)S(1)}, u32[]{:S(2)}, u32[]{:S(2)}) collective-permute-start(bf16[1,320,128]{2,1,0:T(8,128)(2,1)S(1)} %fusion), channel_id=1, source_target_pairs={{0,1},{1,0},{2,3},{3,2},{4,5},{5,4},{6,7},{7,6},{8,9},{9,8},{10,11... | collective-permute-start | bytes 245768 | tf_op jit(solution)/shard_map/ppermute | solution.py:32
  4.7 0.2 collective-permute-start.2
  4.9 0.0 collective-permute-done.1.act1
  4.9 0.0 copy-start.1
  4.9 1.0 %copy-done.1 = bf16[1,320,6,128]{3,1,2,0:T(8,128)(2,1)S(1)} copy-done((bf16[1,320,6,128]{3,1,2,0:T(8,128)(2,1)S(1)}, bf16[1,320,6,128]{3,1,2,0:T(8,128)(2,1)}, u32[]{:S(2)}) %copy-start.1) | copy-done | bytes 491544
  5.9 0.6 %shard_map.51.acts = bf16[2,2,120,1536]{3,2,1,0:T(8,128)(2,1)S(1)} custom-call(bf16[1,6,320,128]{3,2,1,0:T(8,128)(2,1)S(1)} %bitcast.14, bf16[1,6,320,128]{3,2,1,0:T(8,128)(2,1)S(1)} %collective-permute-done.1.act1), custom_call_target="tpu_custom_call" | custom-call | tf_op jit(solution)/shard_map/pallas_call | solution.py:36
  6.5 1.3 %collective-permute-done.3.top0.bottom0 = bf16[1,320,128]{2,1,0:T(8,128)(2,1)S(1)} collective-permute-done((bf16[1,320,128]{2,1,0:T(8,128)(2,1)S(1)}, bf16[1,320,128]{2,1,0:T(8,128)(2,1)S(1)}, u32[]{:S(2)}, u32[]{:S(2)}) %collective-permute-start.3) | collective-permute-done | bytes 81952 | tf_op jit(solution)/shard_map/ppermute | solution.py:32
  7.8 0.0 collective-permute-start.4
  7.8 0.0 copy-start.2
  7.8 0.9 %copy-done.2 = bf16[20,9,160]{2,0,1:T(8,128)(2,1)S(1)} copy-done((bf16[20,9,160]{2,0,1:T(8,128)(2,1)S(1)}, bf16[20,9,160]{2,0,1:T(8,128)(2,1)}, u32[]{:S(2)}) %copy-start.2) | copy-done | bytes 57624
  8.7 0.0 copy-start
  8.7 0.1 shard_map.50
  8.8 2.9 %collective-permute-start = (bf16[1,60,512]{2,1,0:T(8,128)(2,1)S(1)}, bf16[1,60,512]{2,1,0:T(8,128)(2,1)S(1)}, u32[]{:S(2)}, u32[]{:S(2)}) collective-permute-start(bf16[1,60,512]{2,1,0:T(8,128)(2,1)S(1)} %bitcast.15), channel_id=1, source_target_pairs={{0,16},{1,17},{2,18},{3,19},{4,20},{5,21},{6,22},{7,23},{8,24},{9,... | collective-permute-start | bytes 184328 | tf_op jit(solution)/shard_map/ppermute | solution.py:32
  11.7 0.0 collective-permute-done.2.grad1
  11.7 0.0 collective-permute-done.4.top1.bottom1
  11.7 0.0 copy-done
  11.7 0.5 shard_map.52.grads
  12.1 1.4 %shard_map.53 = bf16[2,120,512]{2,1,0:T(8,128)(2,1)S(1)} custom-call(bf16[2,2,120,1536]{3,2,1,0:T(8,128)(2,1)S(1)} %shard_map.51.acts, bf16[2,512,1536]{2,1,0:T(8,128)(2,1)S(1)} %shard_map.52.grads), custom_call_target="tpu_custom_call" | custom-call | tf_op jit(solution)/shard_map/pallas_call | solution.py:36
  13.6 2.3 %collective-permute-done = bf16[1,60,512]{2,1,0:T(8,128)(2,1)S(1)} collective-permute-done((bf16[1,60,512]{2,1,0:T(8,128)(2,1)S(1)}, bf16[1,60,512]{2,1,0:T(8,128)(2,1)S(1)}, u32[]{:S(2)}, u32[]{:S(2)}) %collective-permute-start) | collective-permute-done | bytes 61472 | tf_op jit(solution)/shard_map/ppermute | solution.py:32
  15.8 1.4 %shard_map.54 = bf16[2,120,512]{2,1,0:T(8,128)(2,1)S(1)} custom-call(bf16[2,2,120,1536]{3,2,1,0:T(8,128)(2,1)S(1)} %shard_map.51.acts, bf16[2,512,1536]{2,1,0:T(8,128)(2,1)S(1)} %shard_map.52.grads), custom_call_target="tpu_custom_call" | custom-call | tf_op jit(solution)/shard_map/pallas_call | solution.py:36
  17.2 0.8 %collective-permute-start.5 = (bf16[2,60,512]{2,1,0:T(8,128)(2,1)S(1)}, bf16[2,60,512]{2,1,0:T(8,128)(2,1)S(1)}, u32[]{:S(2)}, u32[]{:S(2)}) collective-permute-start(bf16[2,60,512]{2,1,0:T(8,128)(2,1)S(1)} %pad_maximum_fusion.2), channel_id=1, source_target_pairs={{0,8},{1,9},{2,3},{3,2},{4,12},{5,13},{6,7},{7,6},{8,0},{9,1},{10,... | collective-permute-start | bytes 368648 | tf_op jit(solution)/shard_map/ppermute | solution.py:32
  18.1 1.5 %collective-permute-start.8 = (bf16[2,120,512]{2,1,0:T(8,128)(2,1)S(1)}, bf16[2,120,512]{2,1,0:T(8,128)(2,1)S(1)}, u32[]{:S(2)}, u32[]{:S(2)}) collective-permute-start(bf16[2,120,512]{2,1,0:T(8,128)(2,1)S(1)} %shard_map.54), channel_id=1, source_target_pairs={{0,1},{1,0},{2,6},{3,7},{4,5},{5,4},{6,2},{7,3},{8,9},{9,8},{10,14... | collective-permute-start | bytes 737288 | tf_op jit(solution)/shard_map/ppermute | solution.py:32
  19.5 0.5 %collective-permute-start.7 = (bf16[2,120,512]{2,1,0:T(8,128)(2,1)S(1)}, bf16[2,120,512]{2,1,0:T(8,128)(2,1)S(1)}, u32[]{:S(2)}, u32[]{:S(2)}) collective-permute-start(bf16[2,120,512]{2,1,0:T(8,128)(2,1)S(1)} %shard_map.53), channel_id=1, source_target_pairs={{0,1},{1,0},{2,6},{3,7},{4,5},{5,4},{6,2},{7,3},{8,9},{9,8},{10,14... | collective-permute-start | bytes 737288 | tf_op jit(solution)/shard_map/ppermute | solution.py:32
  20.1 2.1 %shard_map.55.keep = f32[2,2,120,512]{3,2,1,0:T(8,128)S(1)} custom-call(bf16[2,2,120,1536]{3,2,1,0:T(8,128)(2,1)S(1)} %shard_map.51.acts, bf16[2,512,1536]{2,1,0:T(8,128)(2,1)S(1)} %shard_map.52.grads), custom_call_target="tpu_custom_call" | custom-call | tf_op jit(solution)/shard_map/pallas_call | solution.py:36
  22.2 0.1 collective-permute-done.5
  22.3 1.6 %collective-permute-start.6 = (bf16[4,60,512]{2,1,0:T(8,128)(2,1)S(1)}, bf16[4,60,512]{2,1,0:T(8,128)(2,1)S(1)}, u32[]{:S(2)}, u32[]{:S(2)}) collective-permute-start(bf16[4,60,512]{2,1,0:T(8,128)(2,1)S(1)} %pad_maximum_fusion.1), channel_id=1, source_target_pairs={{0,4},{1,5},{2,10},{3,11},{4,0},{5,1},{6,14},{7,15},{8,12},{9,13},... | collective-permute-start | bytes 737288 | tf_op jit(solution)/shard_map/ppermute | solution.py:32
  24.0 2.9 %collective-permute-done.7.message = bf16[2,120,512]{2,1,0:T(8,128)(2,1)S(1)} collective-permute-done((bf16[2,120,512]{2,1,0:T(8,128)(2,1)S(1)}, bf16[2,120,512]{2,1,0:T(8,128)(2,1)S(1)}, u32[]{:S(2)}, u32[]{:S(2)}) %collective-permute-start.7) | collective-permute-done | bytes 245792 | tf_op jit(solution)/shard_map/ppermute | solution.py:32
  26.9 0.9 %shard_map.56 = bf16[2,120,512]{2,1,0:T(8,128)(2,1)S(1)} custom-call(f32[2,2,120,512]{3,2,1,0:T(8,128)S(1)} %shard_map.55.keep, bf16[2,120,512]{2,1,0:T(8,128)(2,1)S(1)} %collective-permute-done.7.message), custom_call_target="tpu_custom_call" | custom-call | tf_op jit(solution)/shard_map/pallas_call | solution.py:36
  27.8 0.0 collective-permute-done.8.message
  27.8 0.6 %shard_map.57.keep = f32[2,120,512]{2,1,0:T(8,128)S(1)} custom-call(f32[2,2,120,512]{3,2,1,0:T(8,128)S(1)} %shard_map.55.keep, bf16[2,120,512]{2,1,0:T(8,128)(2,1)S(1)} %collective-permute-done.8.message), custom_call_target="tpu_custom_call" | custom-call | tf_op jit(solution)/shard_map/pallas_call | solution.py:36
  28.4 0.3 collective-permute-done.6
  28.8 0.1 pad_maximum_fusion.own
  28.8 1.6 %collective-permute-start.11 = (bf16[8,60,512]{2,1,0:T(8,128)(2,1)S(1)}, bf16[8,60,512]{2,1,0:T(8,128)(2,1)S(1)}, u32[]{:S(2)}, u32[]{:S(2)}) collective-permute-start(bf16[8,60,512]{2,1,0:T(8,128)(2,1)S(1)} %pad_maximum_fusion.own), channel_id=1, source_target_pairs={{0,1},{1,0},{2,6},{3,7},{4,5},{5,4},{6,2},{7,3},{8,9},{9,8},{10,14... | collective-permute-start | bytes 1474568 | tf_op jit(solution)/shard_map/ppermute | solution.py:32
  30.4 1.5 %collective-permute-start.9 = (bf16[2,120,512]{2,1,0:T(8,128)(2,1)S(1)}, bf16[2,120,512]{2,1,0:T(8,128)(2,1)S(1)}, u32[]{:S(2)}, u32[]{:S(2)}) collective-permute-start(bf16[2,120,512]{2,1,0:T(8,128)(2,1)S(1)} %shard_map.56), channel_id=1, source_target_pairs={{0,4},{1,5},{2,10},{3,11},{4,0},{5,1},{6,14},{7,15},{8,12},{9,13},... | collective-permute-start | bytes 737288 | tf_op jit(solution)/shard_map/ppermute | solution.py:32
  31.9 5.8 %collective-permute-done.9.message = bf16[2,120,512]{2,1,0:T(8,128)(2,1)S(1)} collective-permute-done((bf16[2,120,512]{2,1,0:T(8,128)(2,1)S(1)}, bf16[2,120,512]{2,1,0:T(8,128)(2,1)S(1)}, u32[]{:S(2)}, u32[]{:S(2)}) %collective-permute-start.9) | collective-permute-done | bytes 245792 | tf_op jit(solution)/shard_map/ppermute | solution.py:32
  37.8 0.5 shard_map.58
  38.3 2.1 %collective-permute-start.10 = (bf16[120,512]{1,0:T(8,128)(2,1)S(1)}, bf16[120,512]{1,0:T(8,128)(2,1)S(1)}, u32[]{:S(2)}, u32[]{:S(2)}) collective-permute-start(bf16[120,512]{1,0:T(8,128)(2,1)S(1)} %shard_map.58), channel_id=1, source_target_pairs={{0,8},{1,9},{2,3},{3,2},{4,12},{5,13},{6,7},{7,6},{8,0},{9,1},{10,... | collective-permute-start | bytes 368648 | tf_op jit(solution)/shard_map/ppermute | solution.py:32
  40.4 0.3 shard_map.59.keep
  40.6 2.6 %collective-permute-done.10.message = bf16[120,512]{1,0:T(8,128)(2,1)S(1)} collective-permute-done((bf16[120,512]{1,0:T(8,128)(2,1)S(1)}, bf16[120,512]{1,0:T(8,128)(2,1)S(1)}, u32[]{:S(2)}, u32[]{:S(2)}) %collective-permute-start.10) | collective-permute-done | bytes 122912 | tf_op jit(solution)/shard_map/ppermute | solution.py:32
  43.2 0.5 shard_map.60
  43.7 4.1 %collective-permute-start.13 = (bf16[60,512]{1,0:T(8,128)(2,1)S(1)}, bf16[60,512]{1,0:T(8,128)(2,1)S(1)}, u32[]{:S(2)}, u32[]{:S(2)}) collective-permute-start(bf16[60,512]{1,0:T(8,128)(2,1)S(1)} %shard_map.60), channel_id=1, source_target_pairs={{0,16},{1,17},{2,18},{3,19},{4,20},{5,21},{6,22},{7,23},{8,24},{9,... | collective-permute-start | bytes 184328 | tf_op jit(solution)/shard_map/ppermute | solution.py:32
  47.8 0.3 shard_map.61.keep
  48.1 0.0 collective-permute-done.11.other
  48.1 1.8 %shard_map.62 = (bf16[1,6,160,128]{3,2,1,0:T(8,128)(2,1)S(1)}, bf16[1,6,160,128]{3,2,1,0:T(8,128)(2,1)S(1)}) custom-call(bf16[8,60,512]{2,1,0:T(8,128)(2,1)S(1)} %pad_maximum_fusion.own, bf16[8,60,512]{2,1,0:T(8,128)(2,1)S(1)} %collective-permute-done.11.other, bf16[1024,1536]{1,0:T(8,128)(2,1)S(1)} %bitcast.9), custom_call_target="tpu_custom_call" | custom-call | tf_op jit(solution)/shard_map/pallas_call | solution.py:36
  49.9 0.1 collective-permute-start.12
  50.0 0.1 collective-permute-done.13.message
  50.0 0.9 %shard_map.64 = f32[9,20,160]{2,1,0:T(8,128)} custom-call(f32[60,512]{1,0:T(8,128)S(1)} %shard_map.61.keep, bf16[60,512]{1,0:T(8,128)(2,1)S(1)} %collective-permute-done.13.message), custom_call_target="tpu_custom_call" | custom-call | flops 10000000000 | tf_op jit(solution)/shard_map/pallas_call | solution.py:36
  50.9 0.5 collective-permute-done.12.theirs
  51.5 0.9 %shard_map.63 = bf16[1,6,320,128]{3,2,1,0:T(8,128)(2,1)} custom-call(bf16[1,6,160,128]{3,2,1,0:T(8,128)(2,1)S(1)} %get-tuple-element.30.own, bf16[1,6,160,128]{3,2,1,0:T(8,128)(2,1)S(1)} %collective-permute-done.12.theirs), custom_call_target="tpu_custom_call" | custom-call | tf_op jit(solution)/shard_map/pallas_call | solution.py:36
  (2 shorter events, 0.0 us)
Async XLA Ops:
  0.6 4.2 %collective-permute-start.1 = (bf16[1,6,320,128]{3,2,1,0:T(8,128)(2,1)}, bf16[1,6,320,128]{3,2,1,0:T(8,128)(2,1)S(1)}, u32[]{:S(2)}, u32[]{:S(2)}) collective-permute-start(bf16[1,6,320,128]{3,2,1,0:T(8,128)(2,1)} %bitcast.13), channel_id=1, source_target_pairs={{0,2},{1,3},{2,0},{3,1},{4,6},{5,7},{6,4},{7,5},{8,10},{9,11},{10,... | collective-permute-start | bytes 1474568 | tf_op jit(solution)/shard_map/ppermute | solution.py:32
  2.1 5.7 %collective-permute-start.3 = (bf16[1,320,128]{2,1,0:T(8,128)(2,1)S(1)}, bf16[1,320,128]{2,1,0:T(8,128)(2,1)S(1)}, u32[]{:S(2)}, u32[]{:S(2)}) collective-permute-start(bf16[1,320,128]{2,1,0:T(8,128)(2,1)S(1)} %fusion), channel_id=1, source_target_pairs={{0,1},{1,0},{2,3},{3,2},{4,5},{5,4},{6,7},{7,6},{8,9},{9,8},{10,11... | collective-permute-start | bytes 245768 | tf_op jit(solution)/shard_map/ppermute | solution.py:32
  4.7 7.0 %collective-permute-start.2 = (bf16[1,6,320,128]{3,2,1,0:T(8,128)(2,1)}, bf16[1,6,320,128]{3,2,1,0:T(8,128)(2,1)S(1)}, u32[]{:S(2)}, u32[]{:S(2)}) collective-permute-start(bf16[1,6,320,128]{3,2,1,0:T(8,128)(2,1)} %bitcast.11), channel_id=1, source_target_pairs={{0,2},{1,3},{2,0},{3,1},{4,6},{5,7},{6,4},{7,5},{8,10},{9,11},{10,... | collective-permute-start | bytes 1474568 | tf_op jit(solution)/shard_map/ppermute | solution.py:32
  4.9 1.0 %copy-start.1 = (bf16[1,320,6,128]{3,1,2,0:T(8,128)(2,1)S(1)}, bf16[1,320,6,128]{3,1,2,0:T(8,128)(2,1)}, u32[]{:S(2)}) copy-start(bf16[1,320,6,128]{3,1,2,0:T(8,128)(2,1)} %param.3) | copy-start | bytes 1474564
  7.8 3.9 %collective-permute-start.4 = (bf16[1,320,128]{2,1,0:T(8,128)(2,1)S(1)}, bf16[1,320,128]{2,1,0:T(8,128)(2,1)S(1)}, u32[]{:S(2)}, u32[]{:S(2)}) collective-permute-start(bf16[1,320,128]{2,1,0:T(8,128)(2,1)S(1)} %collective-permute-done.3.top0.bottom0), channel_id=1, source_target_pairs={{0,2},{1,3},{2,0},{3,1},{4,6},{5,7},{6,4},{7,5},{8,10},{9,11},{10,... | collective-permute-start | bytes 245768 | tf_op jit(solution)/shard_map/ppermute | solution.py:32
  7.8 0.9 %copy-start.2 = (bf16[20,9,160]{2,0,1:T(8,128)(2,1)S(1)}, bf16[20,9,160]{2,0,1:T(8,128)(2,1)}, u32[]{:S(2)}) copy-start(bf16[20,9,160]{2,0,1:T(8,128)(2,1)} %param.5) | copy-start | bytes 172804
  8.7 3.0 %copy-start = (bf16[1,320,6,128]{3,1,2,0:T(8,128)(2,1)S(1)}, bf16[1,320,6,128]{3,1,2,0:T(8,128)(2,1)}, u32[]{:S(2)}) copy-start(bf16[1,320,6,128]{3,1,2,0:T(8,128)(2,1)} %param.4) | copy-start | bytes 1474564
  8.8 7.1 %collective-permute-start = (bf16[1,60,512]{2,1,0:T(8,128)(2,1)S(1)}, bf16[1,60,512]{2,1,0:T(8,128)(2,1)S(1)}, u32[]{:S(2)}, u32[]{:S(2)}) collective-permute-start(bf16[1,60,512]{2,1,0:T(8,128)(2,1)S(1)} %bitcast.15), channel_id=1, source_target_pairs={{0,16},{1,17},{2,18},{3,19},{4,20},{5,21},{6,22},{7,23},{8,24},{9,... | collective-permute-start | bytes 184328 | tf_op jit(solution)/shard_map/ppermute | solution.py:32
  17.2 5.0 %collective-permute-start.5 = (bf16[2,60,512]{2,1,0:T(8,128)(2,1)S(1)}, bf16[2,60,512]{2,1,0:T(8,128)(2,1)S(1)}, u32[]{:S(2)}, u32[]{:S(2)}) collective-permute-start(bf16[2,60,512]{2,1,0:T(8,128)(2,1)S(1)} %pad_maximum_fusion.2), channel_id=1, source_target_pairs={{0,8},{1,9},{2,3},{3,2},{4,12},{5,13},{6,7},{7,6},{8,0},{9,1},{10,... | collective-permute-start | bytes 368648 | tf_op jit(solution)/shard_map/ppermute | solution.py:32
  18.1 9.8 %collective-permute-start.8 = (bf16[2,120,512]{2,1,0:T(8,128)(2,1)S(1)}, bf16[2,120,512]{2,1,0:T(8,128)(2,1)S(1)}, u32[]{:S(2)}, u32[]{:S(2)}) collective-permute-start(bf16[2,120,512]{2,1,0:T(8,128)(2,1)S(1)} %shard_map.54), channel_id=1, source_target_pairs={{0,1},{1,0},{2,6},{3,7},{4,5},{5,4},{6,2},{7,3},{8,9},{9,8},{10,14... | collective-permute-start | bytes 737288 | tf_op jit(solution)/shard_map/ppermute | solution.py:32
  19.5 7.3 %collective-permute-start.7 = (bf16[2,120,512]{2,1,0:T(8,128)(2,1)S(1)}, bf16[2,120,512]{2,1,0:T(8,128)(2,1)S(1)}, u32[]{:S(2)}, u32[]{:S(2)}) collective-permute-start(bf16[2,120,512]{2,1,0:T(8,128)(2,1)S(1)} %shard_map.53), channel_id=1, source_target_pairs={{0,1},{1,0},{2,6},{3,7},{4,5},{5,4},{6,2},{7,3},{8,9},{9,8},{10,14... | collective-permute-start | bytes 737288 | tf_op jit(solution)/shard_map/ppermute | solution.py:32
  22.3 6.4 %collective-permute-start.6 = (bf16[4,60,512]{2,1,0:T(8,128)(2,1)S(1)}, bf16[4,60,512]{2,1,0:T(8,128)(2,1)S(1)}, u32[]{:S(2)}, u32[]{:S(2)}) collective-permute-start(bf16[4,60,512]{2,1,0:T(8,128)(2,1)S(1)} %pad_maximum_fusion.1), channel_id=1, source_target_pairs={{0,4},{1,5},{2,10},{3,11},{4,0},{5,1},{6,14},{7,15},{8,12},{9,13},... | collective-permute-start | bytes 737288 | tf_op jit(solution)/shard_map/ppermute | solution.py:32
  28.8 19.3 %collective-permute-start.11 = (bf16[8,60,512]{2,1,0:T(8,128)(2,1)S(1)}, bf16[8,60,512]{2,1,0:T(8,128)(2,1)S(1)}, u32[]{:S(2)}, u32[]{:S(2)}) collective-permute-start(bf16[8,60,512]{2,1,0:T(8,128)(2,1)S(1)} %pad_maximum_fusion.own), channel_id=1, source_target_pairs={{0,1},{1,0},{2,6},{3,7},{4,5},{5,4},{6,2},{7,3},{8,9},{9,8},{10,14... | collective-permute-start | bytes 1474568 | tf_op jit(solution)/shard_map/ppermute | solution.py:32
  30.4 7.3 %collective-permute-start.9 = (bf16[2,120,512]{2,1,0:T(8,128)(2,1)S(1)}, bf16[2,120,512]{2,1,0:T(8,128)(2,1)S(1)}, u32[]{:S(2)}, u32[]{:S(2)}) collective-permute-start(bf16[2,120,512]{2,1,0:T(8,128)(2,1)S(1)} %shard_map.56), channel_id=1, source_target_pairs={{0,4},{1,5},{2,10},{3,11},{4,0},{5,1},{6,14},{7,15},{8,12},{9,13},... | collective-permute-start | bytes 737288 | tf_op jit(solution)/shard_map/ppermute | solution.py:32
  38.3 5.0 %collective-permute-start.10 = (bf16[120,512]{1,0:T(8,128)(2,1)S(1)}, bf16[120,512]{1,0:T(8,128)(2,1)S(1)}, u32[]{:S(2)}, u32[]{:S(2)}) collective-permute-start(bf16[120,512]{1,0:T(8,128)(2,1)S(1)} %shard_map.58), channel_id=1, source_target_pairs={{0,8},{1,9},{2,3},{3,2},{4,12},{5,13},{6,7},{7,6},{8,0},{9,1},{10,... | collective-permute-start | bytes 368648 | tf_op jit(solution)/shard_map/ppermute | solution.py:32
  43.7 6.3 %collective-permute-start.13 = (bf16[60,512]{1,0:T(8,128)(2,1)S(1)}, bf16[60,512]{1,0:T(8,128)(2,1)S(1)}, u32[]{:S(2)}, u32[]{:S(2)}) collective-permute-start(bf16[60,512]{1,0:T(8,128)(2,1)S(1)} %shard_map.60), channel_id=1, source_target_pairs={{0,16},{1,17},{2,18},{3,19},{4,20},{5,21},{6,22},{7,23},{8,24},{9,... | collective-permute-start | bytes 184328 | tf_op jit(solution)/shard_map/ppermute | solution.py:32
  49.9 1.6 %collective-permute-start.12 = (bf16[1,6,160,128]{3,2,1,0:T(8,128)(2,1)S(1)}, bf16[1,6,160,128]{3,2,1,0:T(8,128)(2,1)S(1)}, u32[]{:S(2)}, u32[]{:S(2)}) collective-permute-start(bf16[1,6,160,128]{3,2,1,0:T(8,128)(2,1)S(1)} %get-tuple-element.31), channel_id=1, source_target_pairs={{0,2},{1,3},{2,0},{3,1},{4,6},{5,7},{6,4},{7,5},{8,10},{9,11},{10,... | collective-permute-start | bytes 737288 | tf_op jit(solution)/shard_map/ppermute | solution.py:32

commit v4 on v3

--- a/solution.py
+++ b/solution.py
@@ -12,10 +12,31 @@
 TAP_STEPS = (-1, 0, 1)
 LANES = 128
 TOP_POWER = 2.0**15.5
+LEAST_POWER = 2.0**-126
 LEAST_PEAK = 1e-30
 VMEM_BYTES = 40 * 2**20
-PACK_FLOPS = 10**10
-LAST_FLOPS = 10**10
+HINTS = {
+    "edge": 8.0,
+    "pack": 8.0,
+    "acts": 0.6,
+    "grads": 0.5,
+    "send0": 1.4,
+    "send1": 1.4,
+    "keep0": 1.0,
+    "keep1": 1.0,
+    "turn0": 0.9,
+    "turn1": 0.6,
+    "part0": 0.5,
+    "part1": 0.3,
+    "halve0": 0.5,
+    "halve1": 3.0,
+    "last": 8.0,
+    "cells": 1.8,
+    "weave": 0.9,
+}
+GATHER_STEPS = ("send1", "turn1", "part1")
+CELLS_STEP = "halve1"
+FLOPS_PER_US = 1.15e9
 
 
 def padded_lanes(count):
@@ -32,7 +53,7 @@
     return lax.ppermute(value, AXES, pairs)
 
 
-def call(kernel, out_shape, operands, scratch=(), flops=0):
+def call(name, kernel, out_shape, operands, scratch=()):
     return pl.pallas_call(
         kernel,
         out_shape=out_shape,
@@ -40,7 +61,10 @@
         out_specs=jax.tree.map(lambda _: pl.BlockSpec(memory_space=pltpu.VMEM), out_shape),
         scratch_shapes=list(scratch),
         compiler_params=pltpu.CompilerParams(vmem_limit_bytes=VMEM_BYTES),
-        cost_estimate=pl.CostEstimate(flops=flops, bytes_accessed=0, transcendentals=0),
+        cost_estimate=pl.CostEstimate(
+            flops=int(HINTS[name] * FLOPS_PER_US), bytes_accessed=0, transcendentals=0
+        ),
+        name=name,
     )(*operands)
 
 
@@ -55,13 +79,14 @@
 def decoded(message):
     power = message.astype(jnp.float32)
     peak = power[0:1, message.shape[1] - 1 : message.shape[1]]
-    root = jnp.sqrt(jnp.sqrt(jnp.sqrt(jnp.abs(power))))
+    size = jnp.maximum(jnp.abs(power), LEAST_POWER)
+    fourth = lax.rsqrt(lax.rsqrt(size))
+    root = fourth * lax.rsqrt(fourth)
     return jnp.where(power < 0, -root, root) * (peak * (1.0 / TOP_POWER))
 
 
-def peak_of(value, used):
-    lane = lax.broadcasted_iota(jnp.int32, value.shape, value.ndim - 1)
-    largest = jnp.max(jnp.where(lane < used, jnp.abs(value), 0.0))
+def peak_of(value):
+    largest = jnp.max(jnp.abs(value))
     largest = jnp.maximum(largest * (1.0 + 2.0**-6), LEAST_PEAK)
     return jnp.full((1, 1), largest, jnp.float32).astype(jnp.bfloat16).astype(jnp.float32)
 
@@ -183,26 +208,25 @@
     first, second, third = mine(plan)
     for k in range(2):
         total = part_terms(plan, acts, grads, (1 - first, second if same else 1 - second, third if k else 1 - third))
-        out[k] = encoded(peak_of(total, plan.half_used), total, plan.half_used)
-
-
-def keep_kernel(plan, acts, grads, out):
+        out[k] = encoded(peak_of(total), total, plan.half_used)
+
+
+def keep_kernel(plan, same, acts, grads, out):
     first, second, third = mine(plan)
-    for j in range(2):
-        for k in range(2):
-            out[j, k] = part_terms(plan, acts, grads, (first, second if j else 1 - second, third if k else 1 - third))
+    for k in range(2):
+        out[k] = part_terms(plan, acts, grads, (first, second if same else 1 - second, third if k else 1 - third))
 
 
 def turn_kernel(plan, same, keep, message, out):
     for k in range(2):
-        total = keep[1 if same else 0, k] + decoded(message[k])
-        out[k] = total if same else encoded(peak_of(total, plan.half_used), total, plan.half_used)
+        total = keep[k] + decoded(message[k])
+        out[k] = total if same else encoded(peak_of(total), total, plan.half_used)
 
 
 def part_kernel(plan, same, keep, message, out):
     k = 1 if same else 0
     total = keep[k] + decoded(message[k])
-    out[...] = total if same else encoded(peak_of(total, plan.half_used), total, plan.half_used)
+    out[...] = total if same else encoded(peak_of(total), total, plan.half_used)
 
 
 def halve_kernel(plan, mask, used, same, keep, message, out):
@@ -214,7 +238,7 @@
         out[...] = jnp.where(side == 0, lower, upper)
     else:
         given = jnp.where(side == 0, upper, lower)
-        out[...] = encoded(peak_of(given, used), given, used)
+        out[...] = encoded(peak_of(given), given, used)
 
 
 def last_kernel(plan, scale, keep, message, out):
@@ -294,7 +318,7 @@
 
 def first_kernel(plan, kernel):
     shape = jax.ShapeDtypeStruct((plan.block_rows, plan.lanes), jnp.bfloat16)
-    packed = call(functools.partial(pack_kernel, plan), shape, [kernel], flops=PACK_FLOPS)[None]
+    packed = call("pack", functools.partial(pack_kernel, plan), shape, [kernel])[None]
     return [packed] + [swap(packed, plan.sizes, (mask, 0)) for mask in plan.rest_band[:1]]
 
 
@@ -332,31 +356,30 @@
     return jnp.pad(total, ((0, 0), (0, plan.lanes - plan.used)))
 
 
-def kernel_terms(plan, acts, grads, gathered, scale):
+def kernel_terms(plan, acts, grads, scale):
     sizes, f32 = plan.sizes, jnp.float32
     rows, lanes = plan.part_rows, plan.half_lanes
-    flops = 0
-
-    def run(kernel, shape, kind, operands, flops=0):
-        return call(kernel, jax.ShapeDtypeStruct(shape, kind), operands, flops=flops)
+
+    def run(name, kernel, shape, kind, operands):
+        return call(name, kernel, jax.ShapeDtypeStruct(shape, kind), operands)
 
     part = functools.partial
     b16 = jnp.bfloat16
     shape = (2, rows, lanes)
-    send0 = run(part(send_kernel, plan, False), shape, b16, [acts, grads], flops)
-    send1 = run(part(send_kernel, plan, True), shape, b16, [after(acts, send0, gathered), grads], flops)
-    keep = run(part(keep_kernel, plan), (2, *shape), f32, [after(acts, send1), grads], 2 * flops)
-    steps = [send1, keep]
+    send0 = run("send0", part(send_kernel, plan, False), shape, b16, [acts, grads])
     come0 = swap(send0, sizes, *plan.term_masks[0])
+    send1 = run("send1", part(send_kernel, plan, True), shape, b16, [after(acts, send0), grads])
     come1 = swap(send1, sizes, *plan.term_masks[0])
-    send = run(part(turn_kernel, plan, False), shape, b16, [keep, come0])
+    keep0 = run("keep0", part(keep_kernel, plan, False), shape, f32, [after(acts, send1), grads])
+    send = run("turn0", part(turn_kernel, plan, False), shape, b16, [keep0, come0])
     come = swap(send, sizes, *plan.term_masks[1])
-    keep = run(part(turn_kernel, plan, True), shape, f32, [after(keep, send), come1])
-    steps.append(keep)
+    keep1 = run("keep1", part(keep_kernel, plan, True), shape, f32, [after(acts, send), grads])
+    keep = run("turn1", part(turn_kernel, plan, True), shape, f32, [keep1, come1])
+    steps = {"send1": send1, "keep0": keep0, "turn0": send, "keep1": keep1, "turn1": keep}
     shape = shape[1:]
-    send = run(part(part_kernel, plan, False), shape, b16, [keep, come])
-    keep = run(part(part_kernel, plan, True), shape, f32, [after(keep, send), come])
-    steps.append(keep)
+    send = run("part0", part(part_kernel, plan, False), shape, b16, [keep, come])
+    keep = run("part1", part(part_kernel, plan, True), shape, f32, [after(keep, send), come])
+    steps.update(part0=send, part1=keep)
     come = swap(send, sizes, *plan.term_masks[2])
     if plan.rest_strip:
         keep = narrowed(plan, keep + decoded(come))
@@ -365,25 +388,31 @@
         rows //= 2
         shape = (rows, plan.lanes)
         halve = part(halve_kernel, plan, mask, plan.used)
-        send = run(part(halve, False), shape, b16, [keep, come])
-        keep = run(part(halve, True), shape, f32, [after(keep, send), come])
-        steps.append(keep)
+        send = run("halve0", part(halve, False), shape, b16, [keep, come])
+        keep = run("halve1", part(halve, True), shape, f32, [after(keep, send), come])
+        steps.update(halve0=send, halve1=keep)
         come = swap(send, sizes, (mask, 0))
     total = call(
+        "last",
         part(last_kernel, plan, scale),
         jax.ShapeDtypeStruct((len(TAP_STEPS) ** 2, plan.depth, plan.cols), f32),
         [keep, come],
-        flops=LAST_FLOPS,
     )
     return total, steps
 
 
+def edge_kernel(plan, grad, out):
+    strip = lax.axis_index("strip")
+    for n in range(plan.images):
+        out[n] = jnp.where(strip == 0, grad[n, plan.rows - 1], grad[n, 0])
+
+
 def borders(plan, grad):
-    strip = lax.axis_index("strip")
+    if plan.strips == 2:
+        shape = jax.ShapeDtypeStruct((plan.images, plan.channels, plan.width), grad.dtype)
+        edge = call("edge", functools.partial(edge_kernel, plan), shape, [grad])
+        return [swap(edge, plan.sizes, (0, 1))]
     first, last = grad[:, 0], grad[:, plan.rows - 1]
-    if plan.strips == 2:
-        come = swap(jnp.where(strip == 0, last, first), plan.sizes, (0, 1))
-        return [come]
     ends = plan.strips - 1
     return [
         lax.ppermute(last, "strip", [(i, i + 1) for i in range(ends)]),
@@ -403,26 +432,29 @@
     grad1 = swap(grad, plan.sizes, (1, 0))
     packed = first_kernel(plan, kernel.transpose(1, 0, 2))
     shape = (2, 2, plan.part_rows, plan.cells)
-    acts = call(functools.partial(acts_kernel, plan), jax.ShapeDtypeStruct(shape, act.dtype), [act, act1])
+    acts = call("acts", functools.partial(acts_kernel, plan), jax.ShapeDtypeStruct(shape, act.dtype), [act, act1])
     edges = [after(edge, acts) for edge in edges]
     edges1 = [swap(edge, plan.sizes, (1, 0)) for edge in edges]
     shape = (2, plan.half_lanes, plan.cells)
     grads = call(
+        "grads",
         functools.partial(grads_kernel, plan),
         jax.ShapeDtypeStruct(shape, grad.dtype),
         [grad, grad1, edges[0], edges1[0], edges[-1], edges1[-1]],
     )
-    kernel_grad, steps = kernel_terms(plan, acts, grads, packed[-1], scale)
-    packed = whole_kernel(plan, packed, steps + [steps[-1]] * plan.band_bits)
+    kernel_grad, steps = kernel_terms(plan, acts, grads, scale)
+    packed = whole_kernel(plan, packed, [steps[name] for name in GATHER_STEPS])
     shape = jax.ShapeDtypeStruct((images, rows, plan.half, width), jnp.bfloat16)
     own, given = call(
+        "cells",
         functools.partial(cells_kernel, plan),
         (shape, shape),
-        [after(packed[0], steps[-1]), packed[1], grads.reshape(2 * plan.half_lanes, plan.cells)],
+        [after(packed[0], steps[CELLS_STEP]), packed[1], grads.reshape(2 * plan.half_lanes, plan.cells)],
         [pltpu.VMEM((len(TAP_STEPS) * plan.half, 2 * plan.half_lanes), jnp.bfloat16)],
     )
     theirs = swap(given, plan.sizes, (1, 0))
     input_grad = call(
+        "weave",
         functools.partial(weave_kernel, plan),
         jax.ShapeDtypeStruct((images, rows, channels, width), jnp.bfloat16),
         [own, theirs],

time: 52.6 us -> 45.1 us (0.86)
  waiting for transfers between devices: 15.9 us -> 12.7 us
  starting transfers between devices: 20.1 us -> 17.3 us
  local copies, waits for them, and re-layouts: 1.93 us -> 0.01 us
  Pallas kernels: 12.7 us -> 14 us
  other arithmetic: 1.04 us -> 0.1 us
    ppermute x14, waiting for transfers between devices: 15.9 us -> 12.7 us  [swap(): return lax.ppermute(value, AXES, pairs)]
    ppermute x14, starting transfers between devices: 20.1 us -> 17.3 us  [swap(): return lax.ppermute(value, AXES, pairs)]
    unnamed x6 -> x4, local copies, waits for them, and re-layouts: 1.93 us -> 0.01 us
    pallas_call x15 -> x17, Pallas kernels: 12.7 us -> 14 us  [call(): pl.pallas_call(kernel, out_shape=out_shape, in_specs=[pl.BlockSpec(memory...]
    select_n x1 -> x0, other arithmetic: 0.94 us -> none  [borders(): come = swap(jnp.where(strip == 0, last, first), plan.sizes, (0, 1))]
  transfers between devices with their start and end apart: 14 -> 14, of which waited for: 9 -> 6; matrix products, arithmetic and copies ran while one was open for 2% -> 0% of each run, Pallas kernels for 20% -> 29%
where the time goes in v4:
time: 45.1 us; the launch traced here: 44.9 us
  starting transfers between devices  17.3 us (38%)
  Pallas kernels  14 us (31%)
  waiting for transfers between devices  12.7 us (28%)
  between operations  0.78 us (2%)
    ppermute x14, starting transfers between devices, swap(): return lax.ppermute(value, AXES, pairs)  17.3 us
    pallas_call x17, Pallas kernels, call(): pl.pallas_call(kernel, out_shape=out_shape, in_specs=[pl.BlockSpec(memory...  14 us
    ppermute x14, waiting for transfers between devices, swap(): return lax.ppermute(value, AXES, pairs)  12.7 us
  transfers between devices with their start and end apart: 14, of which 6 were waited for; matrix products, arithmetic and copies ran while one was open for 0% of the time, Pallas kernels for 29%

profile of v4, /device:TPU:0, one launch (start us, length us, event | category | flops | bytes accessed | tf_op | source)
XLA Modules:
  0.0 44.9 jit_solution(8066312020997157362)
XLA Ops:
  0.6 0.5 %collective-permute-start.1 = (bf16[1,6,320,128]{3,2,1,0:T(8,128)(2,1)}, bf16[1,6,320,128]{3,2,1,0:T(8,128)(2,1)S(1)}, u32[]{:S(2)}, u32[]{:S(2)}) collective-permute-start(bf16[1,6,320,128]{3,2,1,0:T(8,128)(2,1)} %bitcast.10), channel_id=1, source_target_pairs={{0,2},{1,3},{2,0},{3,1},{4,6},{5,7},{6,4},{7,5},{8,10},{9,11},{10,... | collective-permute-start | bytes 1474568 | tf_op jit(solution)/shard_map/ppermute | solution.py:53
  1.1 0.0 copy-start
  1.1 0.0 copy-start.1
  1.2 1.1 %edge.1 = bf16[1,320,128]{2,1,0:T(8,128)(2,1)S(1)} custom-call(bf16[1,6,320,128]{3,2,1,0:T(8,128)(2,1)} %bitcast.3.grad.grad0), custom_call_target="tpu_custom_call" | custom-call | flops 9200000000 | tf_op jit(solution)/shard_map/edge/pallas_call | solution.py:57
  2.3 2.6 %collective-permute-start.3 = (bf16[1,320,128]{2,1,0:T(8,128)(2,1)S(1)}, bf16[1,320,128]{2,1,0:T(8,128)(2,1)S(1)}, u32[]{:S(2)}, u32[]{:S(2)}) collective-permute-start(bf16[1,320,128]{2,1,0:T(8,128)(2,1)S(1)} %edge.1), channel_id=1, source_target_pairs={{0,1},{1,0},{2,3},{3,2},{4,5},{5,4},{6,7},{7,6},{8,9},{9,8},{10,11... | collective-permute-start | bytes 245768 | tf_op jit(solution)/shard_map/ppermute | solution.py:53
  4.9 0.2 collective-permute-start.2
  5.1 0.0 collective-permute-done.1.act1
  5.1 0.0 copy-done
  5.1 0.6 %acts.1 = bf16[2,2,120,1536]{3,2,1,0:T(8,128)(2,1)S(1)} custom-call(bf16[1,6,320,128]{3,2,1,0:T(8,128)(2,1)S(1)} %bitcast.11, bf16[1,6,320,128]{3,2,1,0:T(8,128)(2,1)S(1)} %collective-permute-done.1.act1), custom_call_target="tpu_custom_call" | custom-call | flops 690000000 | tf_op jit(solution)/shard_map/acts/pallas_call | solution.py:57
  5.6 2.3 %collective-permute-done.3.top0.bottom0 = bf16[1,320,128]{2,1,0:T(8,128)(2,1)S(1)} collective-permute-done((bf16[1,320,128]{2,1,0:T(8,128)(2,1)S(1)}, bf16[1,320,128]{2,1,0:T(8,128)(2,1)S(1)}, u32[]{:S(2)}, u32[]{:S(2)}) %collective-permute-start.3) | collective-permute-done | bytes 81952 | tf_op jit(solution)/shard_map/ppermute | solution.py:53
  7.9 0.0 collective-permute-start.4
  7.9 0.0 copy-done.1
  7.9 0.1 pack.1
  8.0 2.9 %collective-permute-start = (bf16[1,60,512]{2,1,0:T(8,128)(2,1)S(1)}, bf16[1,60,512]{2,1,0:T(8,128)(2,1)S(1)}, u32[]{:S(2)}, u32[]{:S(2)}) collective-permute-start(bf16[1,60,512]{2,1,0:T(8,128)(2,1)S(1)} %bitcast.8), channel_id=1, source_target_pairs={{0,16},{1,17},{2,18},{3,19},{4,20},{5,21},{6,22},{7,23},{8,24},{9,... | collective-permute-start | bytes 184328 | tf_op jit(solution)/shard_map/ppermute | solution.py:53
  10.9 0.0 collective-permute-done.2.grad1
  11.0 0.0 collective-permute-done.4.top1.bottom1
  11.0 1.5 %grads.1 = bf16[2,512,1536]{2,1,0:T(8,128)(2,1)S(1)} custom-call(bf16[1,6,320,128]{3,2,1,0:T(8,128)(2,1)} %bitcast.3.grad.grad0, bf16[1,6,320,128]{3,2,1,0:T(8,128)(2,1)S(1)} %collective-permute-done.2.grad1, bf16[1,320,128]{2,1,0:T(8,128)(2,1)S(1)} %collective-permute-done.3.top0.bottom0, bf16[1,320,128]{2,1,0:T(8,128)(2,1)S(1)} %collective-permute-done.4.top1.bottom1, ...), custom_call_target="tpu_custom_call" | custom-call | flops 575000000 | tf_op jit(solution)/shard_map/grads/pallas_call | solution.py:57
  12.4 1.4 %send0.1 = bf16[2,120,512]{2,1,0:T(8,128)(2,1)S(1)} custom-call(bf16[2,2,120,1536]{3,2,1,0:T(8,128)(2,1)S(1)} %acts.1, bf16[2,512,1536]{2,1,0:T(8,128)(2,1)S(1)} %grads.1), custom_call_target="tpu_custom_call" | custom-call | flops 1610000000 | tf_op jit(solution)/shard_map/send0/pallas_call | solution.py:57
  13.9 1.6 %collective-permute-start.6 = (bf16[2,120,512]{2,1,0:T(8,128)(2,1)S(1)}, bf16[2,120,512]{2,1,0:T(8,128)(2,1)S(1)}, u32[]{:S(2)}, u32[]{:S(2)}) collective-permute-start(bf16[2,120,512]{2,1,0:T(8,128)(2,1)S(1)} %send0.1), channel_id=1, source_target_pairs={{0,1},{1,0},{2,6},{3,7},{4,5},{5,4},{6,2},{7,3},{8,9},{9,8},{10,14... | collective-permute-start | bytes 737288 | tf_op jit(solution)/shard_map/ppermute | solution.py:53
  15.4 1.4 %send1.1 = bf16[2,120,512]{2,1,0:T(8,128)(2,1)S(1)} custom-call(bf16[2,2,120,1536]{3,2,1,0:T(8,128)(2,1)S(1)} %acts.1, bf16[2,512,1536]{2,1,0:T(8,128)(2,1)S(1)} %grads.1), custom_call_target="tpu_custom_call" | custom-call | flops 1610000000 | tf_op jit(solution)/shard_map/send1/pallas_call | solution.py:57
  16.8 0.6 %collective-permute-start.7 = (bf16[2,120,512]{2,1,0:T(8,128)(2,1)S(1)}, bf16[2,120,512]{2,1,0:T(8,128)(2,1)S(1)}, u32[]{:S(2)}, u32[]{:S(2)}) collective-permute-start(bf16[2,120,512]{2,1,0:T(8,128)(2,1)S(1)} %send1.1), channel_id=1, source_target_pairs={{0,1},{1,0},{2,6},{3,7},{4,5},{5,4},{6,2},{7,3},{8,9},{9,8},{10,14... | collective-permute-start | bytes 737288 | tf_op jit(solution)/shard_map/ppermute | solution.py:53
  17.4 0.0 collective-permute-done
  17.4 1.1 %keep0.1.keep = f32[2,120,512]{2,1,0:T(8,128)S(1)} custom-call(bf16[2,2,120,1536]{3,2,1,0:T(8,128)(2,1)S(1)} %acts.1, bf16[2,512,1536]{2,1,0:T(8,128)(2,1)S(1)} %grads.1), custom_call_target="tpu_custom_call" | custom-call | flops 1150000000 | tf_op jit(solution)/shard_map/keep0/pallas_call | solution.py:57
  18.6 1.6 %collective-permute-start.5 = (bf16[2,60,512]{2,1,0:T(8,128)(2,1)S(1)}, bf16[2,60,512]{2,1,0:T(8,128)(2,1)S(1)}, u32[]{:S(2)}, u32[]{:S(2)}) collective-permute-start(bf16[2,60,512]{2,1,0:T(8,128)(2,1)S(1)} %pad_maximum_fusion.2), channel_id=1, source_target_pairs={{0,8},{1,9},{2,3},{3,2},{4,12},{5,13},{6,7},{7,6},{8,0},{9,1},{10,... | collective-permute-start | bytes 368648 | tf_op jit(solution)/shard_map/ppermute | solution.py:53
  20.2 0.0 collective-permute-done.6.message
  20.2 0.7 %turn0.1 = bf16[2,120,512]{2,1,0:T(8,128)(2,1)S(1)} custom-call(f32[2,120,512]{2,1,0:T(8,128)S(1)} %keep0.1.keep, bf16[2,120,512]{2,1,0:T(8,128)(2,1)S(1)} %collective-permute-done.6.message), custom_call_target="tpu_custom_call" | custom-call | flops 1035000000 | tf_op jit(solution)/shard_map/turn0/pallas_call | solution.py:57
  20.9 1.6 %collective-permute-start.9 = (bf16[2,120,512]{2,1,0:T(8,128)(2,1)S(1)}, bf16[2,120,512]{2,1,0:T(8,128)(2,1)S(1)}, u32[]{:S(2)}, u32[]{:S(2)}) collective-permute-start(bf16[2,120,512]{2,1,0:T(8,128)(2,1)S(1)} %turn0.1), channel_id=1, source_target_pairs={{0,4},{1,5},{2,10},{3,11},{4,0},{5,1},{6,14},{7,15},{8,12},{9,13},... | collective-permute-start | bytes 737288 | tf_op jit(solution)/shard_map/ppermute | solution.py:53
  22.5 1.1 %keep1.1.keep = f32[2,120,512]{2,1,0:T(8,128)S(1)} custom-call(bf16[2,2,120,1536]{3,2,1,0:T(8,128)(2,1)S(1)} %acts.1, bf16[2,512,1536]{2,1,0:T(8,128)(2,1)S(1)} %grads.1), custom_call_target="tpu_custom_call" | custom-call | flops 1150000000 | tf_op jit(solution)/shard_map/keep1/pallas_call | solution.py:57
  23.6 0.8 %collective-permute-done.7.message = bf16[2,120,512]{2,1,0:T(8,128)(2,1)S(1)} collective-permute-done((bf16[2,120,512]{2,1,0:T(8,128)(2,1)S(1)}, bf16[2,120,512]{2,1,0:T(8,128)(2,1)S(1)}, u32[]{:S(2)}, u32[]{:S(2)}) %collective-permute-start.7) | collective-permute-done | bytes 245792 | tf_op jit(solution)/shard_map/ppermute | solution.py:53
  24.5 0.3 turn1.1.keep
  24.8 0.0 collective-permute-done.5
  24.8 1.6 %collective-permute-start.8 = (bf16[4,60,512]{2,1,0:T(8,128)(2,1)S(1)}, bf16[4,60,512]{2,1,0:T(8,128)(2,1)S(1)}, u32[]{:S(2)}, u32[]{:S(2)}) collective-permute-start(bf16[4,60,512]{2,1,0:T(8,128)(2,1)S(1)} %pad_maximum_fusion.1), channel_id=1, source_target_pairs={{0,4},{1,5},{2,10},{3,11},{4,0},{5,1},{6,14},{7,15},{8,12},{9,13},... | collective-permute-start | bytes 737288 | tf_op jit(solution)/shard_map/ppermute | solution.py:53
  26.4 0.8 %collective-permute-done.9.message = bf16[2,120,512]{2,1,0:T(8,128)(2,1)S(1)} collective-permute-done((bf16[2,120,512]{2,1,0:T(8,128)(2,1)S(1)}, bf16[2,120,512]{2,1,0:T(8,128)(2,1)S(1)}, u32[]{:S(2)}, u32[]{:S(2)}) %collective-permute-start.9) | collective-permute-done | bytes 245792 | tf_op jit(solution)/shard_map/ppermute | solution.py:53
  27.2 0.4 part0.1
  27.6 1.5 %collective-permute-start.10 = (bf16[120,512]{1,0:T(8,128)(2,1)S(1)}, bf16[120,512]{1,0:T(8,128)(2,1)S(1)}, u32[]{:S(2)}, u32[]{:S(2)}) collective-permute-start(bf16[120,512]{1,0:T(8,128)(2,1)S(1)} %part0.1), channel_id=1, source_target_pairs={{0,8},{1,9},{2,3},{3,2},{4,12},{5,13},{6,7},{7,6},{8,0},{9,1},{10,... | collective-permute-start | bytes 368648 | tf_op jit(solution)/shard_map/ppermute | solution.py:53
  29.1 0.2 part1.1.keep
  29.3 2.0 %collective-permute-done.8 = bf16[4,60,512]{2,1,0:T(8,128)(2,1)S(1)} collective-permute-done((bf16[4,60,512]{2,1,0:T(8,128)(2,1)S(1)}, bf16[4,60,512]{2,1,0:T(8,128)(2,1)S(1)}, u32[]{:S(2)}, u32[]{:S(2)}) %collective-permute-start.8) | collective-permute-done | bytes 245792 | tf_op jit(solution)/shard_map/ppermute | solution.py:53
  31.3 0.1 pad_maximum_fusion.own
  31.3 1.2 %collective-permute-start.11 = (bf16[8,60,512]{2,1,0:T(8,128)(2,1)S(1)}, bf16[8,60,512]{2,1,0:T(8,128)(2,1)S(1)}, u32[]{:S(2)}, u32[]{:S(2)}) collective-permute-start(bf16[8,60,512]{2,1,0:T(8,128)(2,1)S(1)} %pad_maximum_fusion.own), channel_id=1, source_target_pairs={{0,1},{1,0},{2,6},{3,7},{4,5},{5,4},{6,2},{7,3},{8,9},{9,8},{10,14... | collective-permute-start | bytes 1474568 | tf_op jit(solution)/shard_map/ppermute | solution.py:53
  32.6 0.0 collective-permute-done.10.message
  32.6 0.4 halve0.1
  32.9 1.2 %collective-permute-start.13 = (bf16[60,512]{1,0:T(8,128)(2,1)S(1)}, bf16[60,512]{1,0:T(8,128)(2,1)S(1)}, u32[]{:S(2)}, u32[]{:S(2)}) collective-permute-start(bf16[60,512]{1,0:T(8,128)(2,1)S(1)} %halve0.1), channel_id=1, source_target_pairs={{0,16},{1,17},{2,18},{3,19},{4,20},{5,21},{6,22},{7,23},{8,24},{9,... | collective-permute-start | bytes 184328 | tf_op jit(solution)/shard_map/ppermute | solution.py:53
  34.2 0.2 halve1.1.keep
  34.3 6.2 %collective-permute-done.11.other = bf16[8,60,512]{2,1,0:T(8,128)(2,1)S(1)} collective-permute-done((bf16[8,60,512]{2,1,0:T(8,128)(2,1)S(1)}, bf16[8,60,512]{2,1,0:T(8,128)(2,1)S(1)}, u32[]{:S(2)}, u32[]{:S(2)}) %collective-permute-start.11) | collective-permute-done | bytes 491552 | tf_op jit(solution)/shard_map/ppermute | solution.py:53
  40.6 1.8 %cells.1 = (bf16[1,6,160,128]{3,2,1,0:T(8,128)(2,1)S(1)}, bf16[1,6,160,128]{3,2,1,0:T(8,128)(2,1)S(1)}) custom-call(bf16[8,60,512]{2,1,0:T(8,128)(2,1)S(1)} %pad_maximum_fusion.own, bf16[8,60,512]{2,1,0:T(8,128)(2,1)S(1)} %collective-permute-done.11.other, bf16[1024,1536]{1,0:T(8,128)(2,1)S(1)} %bitcast.7), custom_call_target="tpu_custom_call" | custom-call | flops 2070000000 | tf_op jit(solution)/shard_map/cells/pallas_call | solution.py:57
  42.4 0.1 collective-permute-start.12
  42.4 0.0 collective-permute-done.13.message
  42.5 0.9 %last.1 = f32[9,20,160]{2,1,0:T(8,128)} custom-call(f32[60,512]{1,0:T(8,128)S(1)} %halve1.1.keep, bf16[60,512]{1,0:T(8,128)(2,1)S(1)} %collective-permute-done.13.message), custom_call_target="tpu_custom_call" | custom-call | flops 9200000000 | tf_op jit(solution)/shard_map/last/pallas_call | solution.py:57
  43.4 0.6 %collective-permute-done.12.theirs = bf16[1,6,160,128]{3,2,1,0:T(8,128)(2,1)S(1)} collective-permute-done((bf16[1,6,160,128]{3,2,1,0:T(8,128)(2,1)S(1)}, bf16[1,6,160,128]{3,2,1,0:T(8,128)(2,1)S(1)}, u32[]{:S(2)}, u32[]{:S(2)}) %collective-permute-start.12) | collective-permute-done | bytes 245792 | tf_op jit(solution)/shard_map/ppermute | solution.py:53
  43.9 0.9 %weave.1 = bf16[1,6,320,128]{3,2,1,0:T(8,128)(2,1)} custom-call(bf16[1,6,160,128]{3,2,1,0:T(8,128)(2,1)S(1)} %get-tuple-element.30.own, bf16[1,6,160,128]{3,2,1,0:T(8,128)(2,1)S(1)} %collective-permute-done.12.theirs), custom_call_target="tpu_custom_call" | custom-call | flops 1035000000 | tf_op jit(solution)/shard_map/weave/pallas_call | solution.py:57
  (2 shorter events, 0.0 us)
Async XLA Ops:
  0.6 4.4 %collective-permute-start.1 = (bf16[1,6,320,128]{3,2,1,0:T(8,128)(2,1)}, bf16[1,6,320,128]{3,2,1,0:T(8,128)(2,1)S(1)}, u32[]{:S(2)}, u32[]{:S(2)}) collective-permute-start(bf16[1,6,320,128]{3,2,1,0:T(8,128)(2,1)} %bitcast.10), channel_id=1, source_target_pairs={{0,2},{1,3},{2,0},{3,1},{4,6},{5,7},{6,4},{7,5},{8,10},{9,11},{10,... | collective-permute-start | bytes 1474568 | tf_op jit(solution)/shard_map/ppermute | solution.py:53
  1.1 3.9 %copy-start = (bf16[1,320,6,128]{3,1,2,0:T(8,128)(2,1)S(1)}, bf16[1,320,6,128]{3,1,2,0:T(8,128)(2,1)}, u32[]{:S(2)}) copy-start(bf16[1,320,6,128]{3,1,2,0:T(8,128)(2,1)} %param.3) | copy-start | bytes 1474564
  1.1 6.8 %copy-start.1 = (bf16[20,9,160]{2,0,1:T(8,128)(2,1)S(1)}, bf16[20,9,160]{2,0,1:T(8,128)(2,1)}, u32[]{:S(2)}) copy-start(bf16[20,9,160]{2,0,1:T(8,128)(2,1)} %param.5) | copy-start | bytes 172804
  2.3 5.7 %collective-permute-start.3 = (bf16[1,320,128]{2,1,0:T(8,128)(2,1)S(1)}, bf16[1,320,128]{2,1,0:T(8,128)(2,1)S(1)}, u32[]{:S(2)}, u32[]{:S(2)}) collective-permute-start(bf16[1,320,128]{2,1,0:T(8,128)(2,1)S(1)} %edge.1), channel_id=1, source_target_pairs={{0,1},{1,0},{2,3},{3,2},{4,5},{5,4},{6,7},{7,6},{8,9},{9,8},{10,11... | collective-permute-start | bytes 245768 | tf_op jit(solution)/shard_map/ppermute | solution.py:53
  4.9 6.1 %collective-permute-start.2 = (bf16[1,6,320,128]{3,2,1,0:T(8,128)(2,1)}, bf16[1,6,320,128]{3,2,1,0:T(8,128)(2,1)S(1)}, u32[]{:S(2)}, u32[]{:S(2)}) collective-permute-start(bf16[1,6,320,128]{3,2,1,0:T(8,128)(2,1)} %bitcast.3.grad.grad0), channel_id=1, source_target_pairs={{0,2},{1,3},{2,0},{3,1},{4,6},{5,7},{6,4},{7,5},{8,10},{9,11},{10,... | collective-permute-start | bytes 1474568 | tf_op jit(solution)/shard_map/ppermute | solution.py:53
  7.9 3.0 %collective-permute-start.4 = (bf16[1,320,128]{2,1,0:T(8,128)(2,1)S(1)}, bf16[1,320,128]{2,1,0:T(8,128)(2,1)S(1)}, u32[]{:S(2)}, u32[]{:S(2)}) collective-permute-start(bf16[1,320,128]{2,1,0:T(8,128)(2,1)S(1)} %collective-permute-done.3.top0.bottom0), channel_id=1, source_target_pairs={{0,2},{1,3},{2,0},{3,1},{4,6},{5,7},{6,4},{7,5},{8,10},{9,11},{10,... | collective-permute-start | bytes 245768 | tf_op jit(solution)/shard_map/ppermute | solution.py:53
  8.0 9.4 %collective-permute-start = (bf16[1,60,512]{2,1,0:T(8,128)(2,1)S(1)}, bf16[1,60,512]{2,1,0:T(8,128)(2,1)S(1)}, u32[]{:S(2)}, u32[]{:S(2)}) collective-permute-start(bf16[1,60,512]{2,1,0:T(8,128)(2,1)S(1)} %bitcast.8), channel_id=1, source_target_pairs={{0,16},{1,17},{2,18},{3,19},{4,20},{5,21},{6,22},{7,23},{8,24},{9,... | collective-permute-start | bytes 184328 | tf_op jit(solution)/shard_map/ppermute | solution.py:53
  13.9 6.4 %collective-permute-start.6 = (bf16[2,120,512]{2,1,0:T(8,128)(2,1)S(1)}, bf16[2,120,512]{2,1,0:T(8,128)(2,1)S(1)}, u32[]{:S(2)}, u32[]{:S(2)}) collective-permute-start(bf16[2,120,512]{2,1,0:T(8,128)(2,1)S(1)} %send0.1), channel_id=1, source_target_pairs={{0,1},{1,0},{2,6},{3,7},{4,5},{5,4},{6,2},{7,3},{8,9},{9,8},{10,14... | collective-permute-start | bytes 737288 | tf_op jit(solution)/shard_map/ppermute | solution.py:53
  16.8 7.7 %collective-permute-start.7 = (bf16[2,120,512]{2,1,0:T(8,128)(2,1)S(1)}, bf16[2,120,512]{2,1,0:T(8,128)(2,1)S(1)}, u32[]{:S(2)}, u32[]{:S(2)}) collective-permute-start(bf16[2,120,512]{2,1,0:T(8,128)(2,1)S(1)} %send1.1), channel_id=1, source_target_pairs={{0,1},{1,0},{2,6},{3,7},{4,5},{5,4},{6,2},{7,3},{8,9},{9,8},{10,14... | collective-permute-start | bytes 737288 | tf_op jit(solution)/shard_map/ppermute | solution.py:53
  18.6 6.2 %collective-permute-start.5 = (bf16[2,60,512]{2,1,0:T(8,128)(2,1)S(1)}, bf16[2,60,512]{2,1,0:T(8,128)(2,1)S(1)}, u32[]{:S(2)}, u32[]{:S(2)}) collective-permute-start(bf16[2,60,512]{2,1,0:T(8,128)(2,1)S(1)} %pad_maximum_fusion.2), channel_id=1, source_target_pairs={{0,8},{1,9},{2,3},{3,2},{4,12},{5,13},{6,7},{7,6},{8,0},{9,1},{10,... | collective-permute-start | bytes 368648 | tf_op jit(solution)/shard_map/ppermute | solution.py:53
  20.9 6.3 %collective-permute-start.9 = (bf16[2,120,512]{2,1,0:T(8,128)(2,1)S(1)}, bf16[2,120,512]{2,1,0:T(8,128)(2,1)S(1)}, u32[]{:S(2)}, u32[]{:S(2)}) collective-permute-start(bf16[2,120,512]{2,1,0:T(8,128)(2,1)S(1)} %turn0.1), channel_id=1, source_target_pairs={{0,4},{1,5},{2,10},{3,11},{4,0},{5,1},{6,14},{7,15},{8,12},{9,13},... | collective-permute-start | bytes 737288 | tf_op jit(solution)/shard_map/ppermute | solution.py:53
  24.8 6.4 %collective-permute-start.8 = (bf16[4,60,512]{2,1,0:T(8,128)(2,1)S(1)}, bf16[4,60,512]{2,1,0:T(8,128)(2,1)S(1)}, u32[]{:S(2)}, u32[]{:S(2)}) collective-permute-start(bf16[4,60,512]{2,1,0:T(8,128)(2,1)S(1)} %pad_maximum_fusion.1), channel_id=1, source_target_pairs={{0,4},{1,5},{2,10},{3,11},{4,0},{5,1},{6,14},{7,15},{8,12},{9,13},... | collective-permute-start | bytes 737288 | tf_op jit(solution)/shard_map/ppermute | solution.py:53
  27.6 5.0 %collective-permute-start.10 = (bf16[120,512]{1,0:T(8,128)(2,1)S(1)}, bf16[120,512]{1,0:T(8,128)(2,1)S(1)}, u32[]{:S(2)}, u32[]{:S(2)}) collective-permute-start(bf16[120,512]{1,0:T(8,128)(2,1)S(1)} %part0.1), channel_id=1, source_target_pairs={{0,8},{1,9},{2,3},{3,2},{4,12},{5,13},{6,7},{7,6},{8,0},{9,1},{10,... | collective-permute-start | bytes 368648 | tf_op jit(solution)/shard_map/ppermute | solution.py:53
  31.3 9.2 %collective-permute-start.11 = (bf16[8,60,512]{2,1,0:T(8,128)(2,1)S(1)}, bf16[8,60,512]{2,1,0:T(8,128)(2,1)S(1)}, u32[]{:S(2)}, u32[]{:S(2)}) collective-permute-start(bf16[8,60,512]{2,1,0:T(8,128)(2,1)S(1)} %pad_maximum_fusion.own), channel_id=1, source_target_pairs={{0,1},{1,0},{2,6},{3,7},{4,5},{5,4},{6,2},{7,3},{8,9},{9,8},{10,14... | collective-permute-start | bytes 1474568 | tf_op jit(solution)/shard_map/ppermute | solution.py:53
  32.9 9.5 %collective-permute-start.13 = (bf16[60,512]{1,0:T(8,128)(2,1)S(1)}, bf16[60,512]{1,0:T(8,128)(2,1)S(1)}, u32[]{:S(2)}, u32[]{:S(2)}) collective-permute-start(bf16[60,512]{1,0:T(8,128)(2,1)S(1)} %halve0.1), channel_id=1, source_target_pairs={{0,16},{1,17},{2,18},{3,19},{4,20},{5,21},{6,22},{7,23},{8,24},{9,... | collective-permute-start | bytes 184328 | tf_op jit(solution)/shard_map/ppermute | solution.py:53
  42.4 1.6 %collective-permute-start.12 = (bf16[1,6,160,128]{3,2,1,0:T(8,128)(2,1)S(1)}, bf16[1,6,160,128]{3,2,1,0:T(8,128)(2,1)S(1)}, u32[]{:S(2)}, u32[]{:S(2)}) collective-permute-start(bf16[1,6,160,128]{3,2,1,0:T(8,128)(2,1)S(1)} %get-tuple-element.31), channel_id=1, source_target_pairs={{0,2},{1,3},{2,0},{3,1},{4,6},{5,7},{6,4},{7,5},{8,10},{9,11},{10,... | collective-permute-start | bytes 737288 | tf_op jit(solution)/shard_map/ppermute | solution.py:53

commit v5 on v4

--- a/solution.py
+++ b/solution.py
@@ -31,10 +31,11 @@
     "halve0": 0.5,
     "halve1": 3.0,
     "last": 8.0,
-    "cells": 1.8,
+    "given": 1.2,
+    "own": 0.7,
     "weave": 0.9,
 }
-GATHER_STEPS = ("send1", "turn1", "part1")
+GATHER_STEPS = ("send0", "turn0", "part0")
 CELLS_STEP = "halve1"
 FLOPS_PER_US = 1.15e9
 
@@ -116,7 +117,7 @@
         self.part_rows = self.inner * self.block_rows
         self.cells = 2 * images * rows * width
         by_row, by_next, by_col = (2, 0), (4, 0), (0, self.top_strip)
-        self.term_masks = ((by_col, by_row), (by_row, by_next), (by_next, by_col))
+        self.term_masks = ((by_col, by_next), (by_row, by_col), (by_next, by_row))
         self.gather_masks = ((by_next, by_col), (by_row, by_next), (by_col, by_row))
 
     def block_of(self, slot, by_next, by_row):
@@ -135,14 +136,7 @@
 
 def mine(plan):
     core, by_row, by_next, by_col = place(plan)
-    order = ((by_col, by_row, by_next), (by_row, by_next, by_col))
-    return [jnp.where(core == 0, a, b) for a, b in zip(*order)]
-
-
-def part_at(plan, bits):
-    core = lax.axis_index("band") % 2
-    first, second, third = bits
-    order = ((second, third, first), (first, second, third))
+    order = ((by_col, by_row, by_next), (by_next, by_col, by_row))
     return [jnp.where(core == 0, a, b) for a, b in zip(*order)]
 
 
@@ -177,12 +171,13 @@
             even, odd = cells[begin : begin + depth], cells[begin + depth : begin + 2 * depth]
             block = jnp.where(core == 0, even, odd)
             shifted.append([moved(block, step) for step in TAP_STEPS])
-        for y in range(2):
-            for z in range(2):
-                pieces = []
+        for i in range(2):
+            pieces = []
+            for j in range(2):
                 for slot in range(plan.inner):
-                    pieces += shifted[plan.block_of(slot, z, y)]
-                out[y, z, :, at * width : (at + 1) * width] = jnp.concatenate(pieces, axis=0).astype(jnp.bfloat16)
+                    here, there = shifted[plan.block_of(slot, j, i)], shifted[plan.block_of(slot, i, j)]
+                    pieces += here if i == j else [jnp.where(core == 0, a, b) for a, b in zip(here, there)]
+            out[i, :, at * width : (at + 1) * width] = jnp.concatenate(pieces, axis=0).astype(jnp.bfloat16)
 
 
 def grads_kernel(plan, grad0, grad1, top0, top1, bottom0, bottom1, out):
@@ -199,22 +194,25 @@
             out[x, plan.half_used :, cells] = jnp.zeros((plan.half_lanes - plan.half_used, width), jnp.bfloat16)
 
 
-def part_terms(plan, acts, grads, bits):
-    y, z, x = part_at(plan, bits)
-    return lax.dot_general(acts[y, z], grads[x], (((1,), (1,)), ((), ())), preferred_element_type=jnp.float32)
+def pair_terms(plan, acts, grads, first, second):
+    core = lax.axis_index("band") % 2
+    i, x = jnp.where(core == 0, second, first), jnp.where(core == 0, first, second)
+    return lax.dot_general(acts[i], grads[x], (((1,), (1,)), ((), ())), preferred_element_type=jnp.float32)
 
 
 def send_kernel(plan, same, acts, grads, out):
-    first, second, third = mine(plan)
+    first, second, _ = mine(plan)
+    total = pair_terms(plan, acts, grads, 1 - first, second if same else 1 - second)
     for k in range(2):
-        total = part_terms(plan, acts, grads, (1 - first, second if same else 1 - second, third if k else 1 - third))
-        out[k] = encoded(peak_of(total), total, plan.half_used)
+        half = total[k * plan.part_rows : (k + 1) * plan.part_rows]
+        out[k] = encoded(peak_of(half), half, plan.half_used)
 
 
 def keep_kernel(plan, same, acts, grads, out):
-    first, second, third = mine(plan)
+    first, second, _ = mine(plan)
+    total = pair_terms(plan, acts, grads, first, second if same else 1 - second)
     for k in range(2):
-        out[k] = part_terms(plan, acts, grads, (first, second if same else 1 - second, third if k else 1 - third))
+        out[k] = total[k * plan.part_rows : (k + 1) * plan.part_rows]
 
 
 def turn_kernel(plan, same, keep, message, out):
@@ -224,7 +222,8 @@
 
 
 def part_kernel(plan, same, keep, message, out):
-    k = 1 if same else 0
+    third = mine(plan)[2]
+    k = third if same else 1 - third
     total = keep[k] + decoded(message[k])
     out[...] = total if same else encoded(peak_of(total), total, plan.half_used)
 
@@ -258,11 +257,27 @@
     out[...] = jnp.concatenate(rows, axis=0).astype(jnp.bfloat16)
 
 
-def cells_kernel(plan, own, other, grads, out0, out1, left):
+def cells_of(plan, d, left, grads, out):
+    width, half = plan.width, plan.half
+    rows = [(n, h) for n in range(plan.images) for h in range(plan.rows)]
+    for begin in range(0, len(rows), 2):
+        part = rows[begin : begin + 2]
+        at = (d * len(rows) + begin) * width
+        product = jnp.dot(
+            left[...], grads[:, at : at + len(part) * width], preferred_element_type=jnp.float32
+        )
+        for k, (n, h) in enumerate(part):
+            total = None
+            for c, col_step in enumerate(TAP_STEPS):
+                term = moved(product[c * half : (c + 1) * half, k * width : (k + 1) * width], -col_step)
+                total = term if total is None else total + term
+            out[n, h] = total.astype(jnp.bfloat16)
+
+
+def given_kernel(plan, own, other, grads, out, left):
     core, row_bit, next_bit, col_bit = place(plan)
     rest = lax.axis_index("band") // 8
-    depth, width, half, lanes = plan.depth, plan.width, plan.half, plan.half_lanes
-    steps = len(TAP_STEPS)
+    depth, half, lanes = plan.depth, plan.half, plan.half_lanes
     for x in range(2):
         rows = [[] for _ in TAP_STEPS]
         for m in range(plan.blocks):
@@ -272,27 +287,17 @@
             three = jnp.where(core == 0, col, row)
             slot = (two * 2 + one) * plan.inner + ((m // 4) ^ rest)
             block = jnp.where(three == 0, own[slot], other[slot]).astype(jnp.float32)
-            for c in range(steps):
+            for c in range(len(TAP_STEPS)):
                 rows[c].append(block[c * depth : (c + 1) * depth])
-        for c in range(steps):
+        for c in range(len(TAP_STEPS)):
             left[c * half : (c + 1) * half, x * lanes : (x + 1) * lanes] = jnp.concatenate(
                 rows[c], axis=0
             ).astype(jnp.bfloat16)
-    group = 2
-    chunks = plan.chunks()
-    for begin in range(0, len(chunks), group):
-        part = chunks[begin : begin + group]
-        product = jnp.dot(
-            left[...],
-            grads[:, begin * width : (begin + len(part)) * width],
-            preferred_element_type=jnp.float32,
-        )
-        for k, (d, n, h) in enumerate(part):
-            total = None
-            for c, col_step in enumerate(TAP_STEPS):
-                term = moved(product[c * half : (c + 1) * half, k * width : (k + 1) * width], -col_step)
-                total = term if total is None else total + term
-            (out0, out1)[d][n, h] = total.astype(jnp.bfloat16)
+    cells_of(plan, 1, left, grads, out)
+
+
+def own_kernel(plan, left, grads, out):
+    cells_of(plan, 0, left, grads, out)
 
 
 def weave_kernel(plan, own, theirs, out):
@@ -375,7 +380,7 @@
     come = swap(send, sizes, *plan.term_masks[1])
     keep1 = run("keep1", part(keep_kernel, plan, True), shape, f32, [after(acts, send), grads])
     keep = run("turn1", part(turn_kernel, plan, True), shape, f32, [keep1, come1])
-    steps = {"send1": send1, "keep0": keep0, "turn0": send, "keep1": keep1, "turn1": keep}
+    steps = {"send0": send0, "send1": send1, "keep0": keep0, "turn0": send, "keep1": keep1, "turn1": keep}
     shape = shape[1:]
     send = run("part0", part(part_kernel, plan, False), shape, b16, [keep, come])
     keep = run("part1", part(part_kernel, plan, True), shape, f32, [after(keep, send), come])
@@ -401,23 +406,29 @@
     return total, steps
 
 
-def edge_kernel(plan, grad, out):
+def edge_kernel(plan, grad, out, copy):
     strip = lax.axis_index("strip")
     for n in range(plan.images):
         out[n] = jnp.where(strip == 0, grad[n, plan.rows - 1], grad[n, 0])
+    copy[...] = grad[...]
 
 
 def borders(plan, grad):
     if plan.strips == 2:
         shape = jax.ShapeDtypeStruct((plan.images, plan.channels, plan.width), grad.dtype)
-        edge = call("edge", functools.partial(edge_kernel, plan), shape, [grad])
-        return [swap(edge, plan.sizes, (0, 1))]
+        copy = jax.ShapeDtypeStruct(grad.shape, grad.dtype)
+        edge, grad = call("edge", functools.partial(edge_kernel, plan), (shape, copy), [grad])
+        come = [swap(edge, plan.sizes, (core, 1)) for core in range(2)]
+        return grad, come, come
     first, last = grad[:, 0], grad[:, plan.rows - 1]
-    ends = plan.strips - 1
-    return [
-        lax.ppermute(last, "strip", [(i, i + 1) for i in range(ends)]),
-        lax.ppermute(first, "strip", [(i + 1, i) for i in range(ends)]),
-    ]
+    tops, bottoms = [], []
+    for core in range(2):
+        down = []
+        for b in range(plan.bands):
+            down += [(b * plan.strips + s, (b ^ core) * plan.strips + s + 1) for s in range(plan.strips - 1)]
+        tops.append(lax.ppermute(last, AXES, down))
+        bottoms.append(lax.ppermute(first, AXES, [(b, a) for a, b in down]))
+    return grad, tops, bottoms
 
 
 def body(activations, out_grad, kernel):
@@ -427,31 +438,31 @@
     scale = 1.0 / math.sqrt(images * bands * rows * strips * width)
     act = activations.transpose(0, 2, 1, 3)
     grad = out_grad.transpose(0, 2, 1, 3)
-    edges = borders(plan, grad)
+    grad0, tops, bottoms = borders(plan, grad)
     act1 = swap(act, plan.sizes, (1, 0))
     grad1 = swap(grad, plan.sizes, (1, 0))
     packed = first_kernel(plan, kernel.transpose(1, 0, 2))
-    shape = (2, 2, plan.part_rows, plan.cells)
+    shape = (2, 2 * plan.part_rows, plan.cells)
     acts = call("acts", functools.partial(acts_kernel, plan), jax.ShapeDtypeStruct(shape, act.dtype), [act, act1])
-    edges = [after(edge, acts) for edge in edges]
-    edges1 = [swap(edge, plan.sizes, (1, 0)) for edge in edges]
     shape = (2, plan.half_lanes, plan.cells)
     grads = call(
         "grads",
         functools.partial(grads_kernel, plan),
         jax.ShapeDtypeStruct(shape, grad.dtype),
-        [grad, grad1, edges[0], edges1[0], edges[-1], edges1[-1]],
+        [grad0, grad1, *tops, *bottoms],
     )
     kernel_grad, steps = kernel_terms(plan, acts, grads, scale)
     packed = whole_kernel(plan, packed, [steps[name] for name in GATHER_STEPS])
     shape = jax.ShapeDtypeStruct((images, rows, plan.half, width), jnp.bfloat16)
-    own, given = call(
-        "cells",
-        functools.partial(cells_kernel, plan),
-        (shape, shape),
-        [after(packed[0], steps[CELLS_STEP]), packed[1], grads.reshape(2 * plan.half_lanes, plan.cells)],
-        [pltpu.VMEM((len(TAP_STEPS) * plan.half, 2 * plan.half_lanes), jnp.bfloat16)],
+    left = jax.ShapeDtypeStruct((len(TAP_STEPS) * plan.half, 2 * plan.half_lanes), jnp.bfloat16)
+    grads = grads.reshape(2 * plan.half_lanes, plan.cells)
+    given, left = call(
+        "given",
+        functools.partial(given_kernel, plan),
+        (shape, left),
+        [after(packed[0], steps[CELLS_STEP]), packed[1], grads],
     )
+    own = call("own", functools.partial(own_kernel, plan), shape, [after(left, given), grads])
     theirs = swap(given, plan.sizes, (1, 0))
     input_grad = call(
         "weave",

time: 45.1 us -> 41.7 us (0.925)
  waiting for transfers between devices: 12.7 us -> 9.63 us
  Pallas kernels: 14 us -> 11.3 us
  starting transfers between devices: 17.3 us -> 19.7 us
    ppermute x14, waiting for transfers between devices: 12.7 us -> 9.63 us  [swap(): return lax.ppermute(value, AXES, pairs)]
    pallas_call x17 -> x18, Pallas kernels: 14 us -> 11.3 us  [call(): pl.pallas_call(kernel, out_shape=out_shape, in_specs=[pl.BlockSpec(memory...]
    ppermute x14, starting transfers between devices: 17.3 us -> 19.7 us  [swap(): return lax.ppermute(value, AXES, pairs)]
  transfers between devices with their start and end apart: 14 -> 14, of which waited for: 6 -> 6; matrix products, arithmetic and copies ran while one was open for 0% -> 0% of each run, Pallas kernels for 29% -> 22%
where the time goes in v5:
time: 41.7 us; the launch traced here: 41.6 us
  starting transfers between devices  19.7 us (47%)
  Pallas kernels  11.3 us (27%)
  waiting for transfers between devices  9.63 us (23%)
  between operations  0.81 us (2%)
    ppermute x14, starting transfers between devices, swap(): return lax.ppermute(value, AXES, pairs)  19.7 us
    pallas_call x18, Pallas kernels, call(): pl.pallas_call(kernel, out_shape=out_shape, in_specs=[pl.BlockSpec(memory...  11.3 us
    ppermute x14, waiting for transfers between devices, swap(): return lax.ppermute(value, AXES, pairs)  9.63 us
  transfers between devices with their start and end apart: 14, of which 6 were waited for; matrix products, arithmetic and copies ran while one was open for 0% of the time, Pallas kernels for 22%

profile of v5, /device:TPU:0, one launch (start us, length us, event | category | flops | bytes accessed | tf_op | source)
XLA Modules:
  0.0 41.6 jit_solution(16848267500338705329)
XLA Ops:
  0.6 0.0 copy-start
  0.6 0.0 copy-start.1
  0.6 1.1 %edge.1 = (bf16[1,320,128]{2,1,0:T(8,128)(2,1)S(1)}, bf16[1,6,320,128]{3,2,1,0:T(8,128)(2,1)S(1)}) custom-call(bf16[1,6,320,128]{3,2,1,0:T(8,128)(2,1)} %bitcast.3.grad), custom_call_target="tpu_custom_call" | custom-call | flops 9200000000 | tf_op jit(solution)/shard_map/edge/pallas_call | solution.py:58
  1.8 3.0 %collective-permute-start.3 = (bf16[1,320,128]{2,1,0:T(8,128)(2,1)S(1)}, bf16[1,320,128]{2,1,0:T(8,128)(2,1)S(1)}, u32[]{:S(2)}, u32[]{:S(2)}) collective-permute-start(bf16[1,320,128]{2,1,0:T(8,128)(2,1)S(1)} %get-tuple-element.20), channel_id=1, source_target_pairs={{0,1},{1,0},{2,3},{3,2},{4,5},{5,4},{6,7},{7,6},{8,9},{9,8},{10,11... | collective-permute-start | bytes 245768 | tf_op jit(solution)/shard_map/ppermute | solution.py:54
  4.8 0.0 collective-permute-start.4
  4.8 0.2 collective-permute-start.2
  5.0 0.0 copy-done
  5.0 0.3 collective-permute-start.1
  5.3 0.0 copy-done.1
  5.3 0.1 pack.1
  5.4 2.8 %collective-permute-start = (bf16[1,60,512]{2,1,0:T(8,128)(2,1)S(1)}, bf16[1,60,512]{2,1,0:T(8,128)(2,1)S(1)}, u32[]{:S(2)}, u32[]{:S(2)}) collective-permute-start(bf16[1,60,512]{2,1,0:T(8,128)(2,1)S(1)} %bitcast.9), channel_id=1, source_target_pairs={{0,16},{1,17},{2,18},{3,19},{4,20},{5,21},{6,22},{7,23},{8,24},{9,... | collective-permute-start | bytes 184328 | tf_op jit(solution)/shard_map/ppermute | solution.py:54
  8.2 0.0 collective-permute-done.1.act1
  8.2 0.6 %acts.1 = bf16[2,240,1536]{2,1,0:T(8,128)(2,1)S(1)} custom-call(bf16[1,6,320,128]{3,2,1,0:T(8,128)(2,1)S(1)} %bitcast.12, bf16[1,6,320,128]{3,2,1,0:T(8,128)(2,1)S(1)} %collective-permute-done.1.act1), custom_call_target="tpu_custom_call" | custom-call | flops 690000000 | tf_op jit(solution)/shard_map/acts/pallas_call | solution.py:58
  8.8 0.0 collective-permute-done.3.top0.bottom0
  8.9 0.4 %collective-permute-done.4.top1.bottom1 = bf16[1,320,128]{2,1,0:T(8,128)(2,1)S(1)} collective-permute-done((bf16[1,320,128]{2,1,0:T(8,128)(2,1)S(1)}, bf16[1,320,128]{2,1,0:T(8,128)(2,1)S(1)}, u32[]{:S(2)}, u32[]{:S(2)}) %collective-permute-start.4) | collective-permute-done | bytes 81952 | tf_op jit(solution)/shard_map/ppermute | solution.py:54
  9.3 0.0 collective-permute-done.2.grad1
  9.3 0.5 %grads.1 = bf16[2,512,1536]{2,1,0:T(8,128)(2,1)S(1)} custom-call(bf16[1,6,320,128]{3,2,1,0:T(8,128)(2,1)S(1)} %get-tuple-element.19.grad0, bf16[1,6,320,128]{3,2,1,0:T(8,128)(2,1)S(1)} %collective-permute-done.2.grad1, bf16[1,320,128]{2,1,0:T(8,128)(2,1)S(1)} %collective-permute-done.3.top0.bottom0, ...), custom_call_target="tpu_custom_call" | custom-call | flops 575000000 | tf_op jit(solution)/shard_map/grads/pallas_call | solution.py:58
  9.7 0.9 %send0.1 = bf16[2,120,512]{2,1,0:T(8,128)(2,1)S(1)} custom-call(bf16[2,240,1536]{2,1,0:T(8,128)(2,1)S(1)} %acts.1, bf16[2,512,1536]{2,1,0:T(8,128)(2,1)S(1)} %grads.1), custom_call_target="tpu_custom_call" | custom-call | flops 1610000000 | tf_op jit(solution)/shard_map/send0/pallas_call | solution.py:58
  10.7 1.1 %collective-permute-start.6 = (bf16[2,120,512]{2,1,0:T(8,128)(2,1)S(1)}, bf16[2,120,512]{2,1,0:T(8,128)(2,1)S(1)}, u32[]{:S(2)}, u32[]{:S(2)}) collective-permute-start(bf16[2,120,512]{2,1,0:T(8,128)(2,1)S(1)} %send0.1), channel_id=1, source_target_pairs={{0,1},{1,0},{2,10},{3,11},{4,5},{5,4},{6,14},{7,15},{8,9},{9,8},{1... | collective-permute-start | bytes 737288 | tf_op jit(solution)/shard_map/ppermute | solution.py:54
  11.8 0.9 %send1.1 = bf16[2,120,512]{2,1,0:T(8,128)(2,1)S(1)} custom-call(bf16[2,240,1536]{2,1,0:T(8,128)(2,1)S(1)} %acts.1, bf16[2,512,1536]{2,1,0:T(8,128)(2,1)S(1)} %grads.1), custom_call_target="tpu_custom_call" | custom-call | flops 1610000000 | tf_op jit(solution)/shard_map/send1/pallas_call | solution.py:58
  12.7 1.0 %collective-permute-start.8 = (bf16[2,120,512]{2,1,0:T(8,128)(2,1)S(1)}, bf16[2,120,512]{2,1,0:T(8,128)(2,1)S(1)}, u32[]{:S(2)}, u32[]{:S(2)}) collective-permute-start(bf16[2,120,512]{2,1,0:T(8,128)(2,1)S(1)} %send1.1), channel_id=1, source_target_pairs={{0,1},{1,0},{2,10},{3,11},{4,5},{5,4},{6,14},{7,15},{8,9},{9,8},{1... | collective-permute-start | bytes 737288 | tf_op jit(solution)/shard_map/ppermute | solution.py:54
  13.7 0.0 collective-permute-done
  13.8 1.9 %collective-permute-start.5 = (bf16[2,60,512]{2,1,0:T(8,128)(2,1)S(1)}, bf16[2,60,512]{2,1,0:T(8,128)(2,1)S(1)}, u32[]{:S(2)}, u32[]{:S(2)}) collective-permute-start(bf16[2,60,512]{2,1,0:T(8,128)(2,1)S(1)} %pad_maximum_fusion.2), channel_id=1, source_target_pairs={{0,8},{1,9},{2,3},{3,2},{4,12},{5,13},{6,7},{7,6},{8,0},{9,1},{10,... | collective-permute-start | bytes 368648 | tf_op jit(solution)/shard_map/ppermute | solution.py:54
  15.6 0.6 %keep0.1.keep = f32[2,120,512]{2,1,0:T(8,128)S(1)} custom-call(bf16[2,240,1536]{2,1,0:T(8,128)(2,1)S(1)} %acts.1, bf16[2,512,1536]{2,1,0:T(8,128)(2,1)S(1)} %grads.1), custom_call_target="tpu_custom_call" | custom-call | flops 1150000000 | tf_op jit(solution)/shard_map/keep0/pallas_call | solution.py:58
  16.2 1.5 %collective-permute-done.6.message = bf16[2,120,512]{2,1,0:T(8,128)(2,1)S(1)} collective-permute-done((bf16[2,120,512]{2,1,0:T(8,128)(2,1)S(1)}, bf16[2,120,512]{2,1,0:T(8,128)(2,1)S(1)}, u32[]{:S(2)}, u32[]{:S(2)}) %collective-permute-start.6) | collective-permute-done | bytes 245792 | tf_op jit(solution)/shard_map/ppermute | solution.py:54
  17.8 0.7 %turn0.1 = bf16[2,120,512]{2,1,0:T(8,128)(2,1)S(1)} custom-call(f32[2,120,512]{2,1,0:T(8,128)S(1)} %keep0.1.keep, bf16[2,120,512]{2,1,0:T(8,128)(2,1)S(1)} %collective-permute-done.6.message), custom_call_target="tpu_custom_call" | custom-call | flops 1035000000 | tf_op jit(solution)/shard_map/turn0/pallas_call | solution.py:58
  18.5 1.9 %collective-permute-start.9 = (bf16[2,120,512]{2,1,0:T(8,128)(2,1)S(1)}, bf16[2,120,512]{2,1,0:T(8,128)(2,1)S(1)}, u32[]{:S(2)}, u32[]{:S(2)}) collective-permute-start(bf16[2,120,512]{2,1,0:T(8,128)(2,1)S(1)} %turn0.1), channel_id=1, source_target_pairs={{0,4},{1,5},{2,3},{3,2},{4,0},{5,1},{6,7},{7,6},{8,12},{9,13},{10,... | collective-permute-start | bytes 737288 | tf_op jit(solution)/shard_map/ppermute | solution.py:54
  20.4 0.0 collective-permute-done.5
  20.4 1.5 %collective-permute-start.7 = (bf16[4,60,512]{2,1,0:T(8,128)(2,1)S(1)}, bf16[4,60,512]{2,1,0:T(8,128)(2,1)S(1)}, u32[]{:S(2)}, u32[]{:S(2)}) collective-permute-start(bf16[4,60,512]{2,1,0:T(8,128)(2,1)S(1)} %pad_maximum_fusion.1), channel_id=1, source_target_pairs={{0,4},{1,5},{2,10},{3,11},{4,0},{5,1},{6,14},{7,15},{8,12},{9,13},... | collective-permute-start | bytes 737288 | tf_op jit(solution)/shard_map/ppermute | solution.py:54
  21.9 0.6 %keep1.1.keep = f32[2,120,512]{2,1,0:T(8,128)S(1)} custom-call(bf16[2,240,1536]{2,1,0:T(8,128)(2,1)S(1)} %acts.1, bf16[2,512,1536]{2,1,0:T(8,128)(2,1)S(1)} %grads.1), custom_call_target="tpu_custom_call" | custom-call | flops 1150000000 | tf_op jit(solution)/shard_map/keep1/pallas_call | solution.py:58
  22.5 0.0 collective-permute-done.8.message
  22.6 0.3 turn1.1.keep
  22.9 1.9 %collective-permute-done.9.message = bf16[2,120,512]{2,1,0:T(8,128)(2,1)S(1)} collective-permute-done((bf16[2,120,512]{2,1,0:T(8,128)(2,1)S(1)}, bf16[2,120,512]{2,1,0:T(8,128)(2,1)S(1)}, u32[]{:S(2)}, u32[]{:S(2)}) %collective-permute-start.9) | collective-permute-done | bytes 245792 | tf_op jit(solution)/shard_map/ppermute | solution.py:54
  24.7 0.4 part0.1
  25.1 2.0 %collective-permute-start.10 = (bf16[120,512]{1,0:T(8,128)(2,1)S(1)}, bf16[120,512]{1,0:T(8,128)(2,1)S(1)}, u32[]{:S(2)}, u32[]{:S(2)}) collective-permute-start(bf16[120,512]{1,0:T(8,128)(2,1)S(1)} %part0.1), channel_id=1, source_target_pairs={{0,8},{1,9},{2,6},{3,7},{4,12},{5,13},{6,2},{7,3},{8,0},{9,1},{10,... | collective-permute-start | bytes 368648 | tf_op jit(solution)/shard_map/ppermute | solution.py:54
  27.1 1.1 %collective-permute-done.7 = bf16[4,60,512]{2,1,0:T(8,128)(2,1)S(1)} collective-permute-done((bf16[4,60,512]{2,1,0:T(8,128)(2,1)S(1)}, bf16[4,60,512]{2,1,0:T(8,128)(2,1)S(1)}, u32[]{:S(2)}, u32[]{:S(2)}) %collective-permute-start.7) | collective-permute-done | bytes 245792 | tf_op jit(solution)/shard_map/ppermute | solution.py:54
  28.2 0.1 pad_maximum_fusion.own
  28.3 0.9 %collective-permute-start.11 = (bf16[8,60,512]{2,1,0:T(8,128)(2,1)S(1)}, bf16[8,60,512]{2,1,0:T(8,128)(2,1)S(1)}, u32[]{:S(2)}, u32[]{:S(2)}) collective-permute-start(bf16[8,60,512]{2,1,0:T(8,128)(2,1)S(1)} %pad_maximum_fusion.own), channel_id=1, source_target_pairs={{0,1},{1,0},{2,6},{3,7},{4,5},{5,4},{6,2},{7,3},{8,9},{9,8},{10,14... | collective-permute-start | bytes 1474568 | tf_op jit(solution)/shard_map/ppermute | solution.py:54
  29.2 0.2 part1.1.keep
  29.4 0.7 %collective-permute-done.10.message = bf16[120,512]{1,0:T(8,128)(2,1)S(1)} collective-permute-done((bf16[120,512]{1,0:T(8,128)(2,1)S(1)}, bf16[120,512]{1,0:T(8,128)(2,1)S(1)}, u32[]{:S(2)}, u32[]{:S(2)}) %collective-permute-start.10) | collective-permute-done | bytes 122912 | tf_op jit(solution)/shard_map/ppermute | solution.py:54
  30.0 0.4 halve0.1
  30.4 3.0 %collective-permute-start.13 = (bf16[60,512]{1,0:T(8,128)(2,1)S(1)}, bf16[60,512]{1,0:T(8,128)(2,1)S(1)}, u32[]{:S(2)}, u32[]{:S(2)}) collective-permute-start(bf16[60,512]{1,0:T(8,128)(2,1)S(1)} %halve0.1), channel_id=1, source_target_pairs={{0,16},{1,17},{2,18},{3,19},{4,20},{5,21},{6,22},{7,23},{8,24},{9,... | collective-permute-start | bytes 184328 | tf_op jit(solution)/shard_map/ppermute | solution.py:54
  33.4 0.2 halve1.1.keep
  33.6 4.0 %collective-permute-done.11.other = bf16[8,60,512]{2,1,0:T(8,128)(2,1)S(1)} collective-permute-done((bf16[8,60,512]{2,1,0:T(8,128)(2,1)S(1)}, bf16[8,60,512]{2,1,0:T(8,128)(2,1)S(1)}, u32[]{:S(2)}, u32[]{:S(2)}) %collective-permute-start.11) | collective-permute-done | bytes 491552 | tf_op jit(solution)/shard_map/ppermute | solution.py:54
  37.5 1.1 %given.1 = (bf16[1,6,160,128]{3,2,1,0:T(8,128)(2,1)S(1)}, bf16[480,1024]{1,0:T(8,128)(2,1)S(1)}) custom-call(bf16[8,60,512]{2,1,0:T(8,128)(2,1)S(1)} %pad_maximum_fusion.own, bf16[8,60,512]{2,1,0:T(8,128)(2,1)S(1)} %collective-permute-done.11.other, bf16[1024,1536]{1,0:T(8,128)(2,1)S(1)} %bitcast.7), custom_call_target="tpu_custom_call" | custom-call | flops 1380000000 | tf_op jit(solution)/shard_map/given/pallas_call | solution.py:58
  38.6 0.1 collective-permute-start.12
  38.7 0.0 collective-permute-done.13.message
  38.7 0.9 %last.1 = f32[9,20,160]{2,1,0:T(8,128)} custom-call(f32[60,512]{1,0:T(8,128)S(1)} %halve1.1.keep, bf16[60,512]{1,0:T(8,128)(2,1)S(1)} %collective-permute-done.13.message), custom_call_target="tpu_custom_call" | custom-call | flops 9200000000 | tf_op jit(solution)/shard_map/last/pallas_call | solution.py:58
  39.6 1.0 %own.1 = bf16[1,6,160,128]{3,2,1,0:T(8,128)(2,1)S(1)} custom-call(bf16[480,1024]{1,0:T(8,128)(2,1)S(1)} %get-tuple-element.35.left, bf16[1024,1536]{1,0:T(8,128)(2,1)S(1)} %bitcast.8), custom_call_target="tpu_custom_call" | custom-call | flops 805000000 | tf_op jit(solution)/shard_map/own/pallas_call | solution.py:58
  40.6 0.0 collective-permute-done.12.theirs
  40.6 0.9 %weave.1 = bf16[1,6,320,128]{3,2,1,0:T(8,128)(2,1)} custom-call(bf16[1,6,160,128]{3,2,1,0:T(8,128)(2,1)S(1)} %own.1, bf16[1,6,160,128]{3,2,1,0:T(8,128)(2,1)S(1)} %collective-permute-done.12.theirs), custom_call_target="tpu_custom_call" | custom-call | flops 1035000000 | tf_op jit(solution)/shard_map/weave/pallas_call | solution.py:58
  (2 shorter events, 0.0 us)
Async XLA Ops:
  0.6 4.4 %copy-start = (bf16[1,320,6,128]{3,1,2,0:T(8,128)(2,1)S(1)}, bf16[1,320,6,128]{3,1,2,0:T(8,128)(2,1)}, u32[]{:S(2)}) copy-start(bf16[1,320,6,128]{3,1,2,0:T(8,128)(2,1)} %param.3) | copy-start | bytes 1474564
  0.6 4.7 %copy-start.1 = (bf16[20,9,160]{2,0,1:T(8,128)(2,1)S(1)}, bf16[20,9,160]{2,0,1:T(8,128)(2,1)}, u32[]{:S(2)}) copy-start(bf16[20,9,160]{2,0,1:T(8,128)(2,1)} %param.5) | copy-start | bytes 172804
  1.8 7.0 %collective-permute-start.3 = (bf16[1,320,128]{2,1,0:T(8,128)(2,1)S(1)}, bf16[1,320,128]{2,1,0:T(8,128)(2,1)S(1)}, u32[]{:S(2)}, u32[]{:S(2)}) collective-permute-start(bf16[1,320,128]{2,1,0:T(8,128)(2,1)S(1)} %get-tuple-element.20), channel_id=1, source_target_pairs={{0,1},{1,0},{2,3},{3,2},{4,5},{5,4},{6,7},{7,6},{8,9},{9,8},{10,11... | collective-permute-start | bytes 245768 | tf_op jit(solution)/shard_map/ppermute | solution.py:54
  4.8 4.5 %collective-permute-start.4 = (bf16[1,320,128]{2,1,0:T(8,128)(2,1)S(1)}, bf16[1,320,128]{2,1,0:T(8,128)(2,1)S(1)}, u32[]{:S(2)}, u32[]{:S(2)}) collective-permute-start(bf16[1,320,128]{2,1,0:T(8,128)(2,1)S(1)} %get-tuple-element.20), channel_id=1, source_target_pairs={{0,3},{1,2},{2,1},{3,0},{4,7},{5,6},{6,5},{7,4},{8,11},{9,10},{10,... | collective-permute-start | bytes 245768 | tf_op jit(solution)/shard_map/ppermute | solution.py:54
  4.8 4.5 %collective-permute-start.2 = (bf16[1,6,320,128]{3,2,1,0:T(8,128)(2,1)}, bf16[1,6,320,128]{3,2,1,0:T(8,128)(2,1)S(1)}, u32[]{:S(2)}, u32[]{:S(2)}) collective-permute-start(bf16[1,6,320,128]{3,2,1,0:T(8,128)(2,1)} %bitcast.3.grad), channel_id=1, source_target_pairs={{0,2},{1,3},{2,0},{3,1},{4,6},{5,7},{6,4},{7,5},{8,10},{9,11},{10,... | collective-permute-start | bytes 1474568 | tf_op jit(solution)/shard_map/ppermute | solution.py:54
  5.0 3.2 %collective-permute-start.1 = (bf16[1,6,320,128]{3,2,1,0:T(8,128)(2,1)S(1)}, bf16[1,6,320,128]{3,2,1,0:T(8,128)(2,1)S(1)}, u32[]{:S(2)}, u32[]{:S(2)}) collective-permute-start(bf16[1,6,320,128]{3,2,1,0:T(8,128)(2,1)S(1)} %bitcast.11), channel_id=1, source_target_pairs={{0,2},{1,3},{2,0},{3,1},{4,6},{5,7},{6,4},{7,5},{8,10},{9,11},{10,... | collective-permute-start | bytes 1474568 | tf_op jit(solution)/shard_map/ppermute | solution.py:54
  5.4 8.3 %collective-permute-start = (bf16[1,60,512]{2,1,0:T(8,128)(2,1)S(1)}, bf16[1,60,512]{2,1,0:T(8,128)(2,1)S(1)}, u32[]{:S(2)}, u32[]{:S(2)}) collective-permute-start(bf16[1,60,512]{2,1,0:T(8,128)(2,1)S(1)} %bitcast.9), channel_id=1, source_target_pairs={{0,16},{1,17},{2,18},{3,19},{4,20},{5,21},{6,22},{7,23},{8,24},{9,... | collective-permute-start | bytes 184328 | tf_op jit(solution)/shard_map/ppermute | solution.py:54
  10.7 7.1 %collective-permute-start.6 = (bf16[2,120,512]{2,1,0:T(8,128)(2,1)S(1)}, bf16[2,120,512]{2,1,0:T(8,128)(2,1)S(1)}, u32[]{:S(2)}, u32[]{:S(2)}) collective-permute-start(bf16[2,120,512]{2,1,0:T(8,128)(2,1)S(1)} %send0.1), channel_id=1, source_target_pairs={{0,1},{1,0},{2,10},{3,11},{4,5},{5,4},{6,14},{7,15},{8,9},{9,8},{1... | collective-permute-start | bytes 737288 | tf_op jit(solution)/shard_map/ppermute | solution.py:54
  12.7 9.8 %collective-permute-start.8 = (bf16[2,120,512]{2,1,0:T(8,128)(2,1)S(1)}, bf16[2,120,512]{2,1,0:T(8,128)(2,1)S(1)}, u32[]{:S(2)}, u32[]{:S(2)}) collective-permute-start(bf16[2,120,512]{2,1,0:T(8,128)(2,1)S(1)} %send1.1), channel_id=1, source_target_pairs={{0,1},{1,0},{2,10},{3,11},{4,5},{5,4},{6,14},{7,15},{8,9},{9,8},{1... | collective-permute-start | bytes 737288 | tf_op jit(solution)/shard_map/ppermute | solution.py:54
  13.8 6.6 %collective-permute-start.5 = (bf16[2,60,512]{2,1,0:T(8,128)(2,1)S(1)}, bf16[2,60,512]{2,1,0:T(8,128)(2,1)S(1)}, u32[]{:S(2)}, u32[]{:S(2)}) collective-permute-start(bf16[2,60,512]{2,1,0:T(8,128)(2,1)S(1)} %pad_maximum_fusion.2), channel_id=1, source_target_pairs={{0,8},{1,9},{2,3},{3,2},{4,12},{5,13},{6,7},{7,6},{8,0},{9,1},{10,... | collective-permute-start | bytes 368648 | tf_op jit(solution)/shard_map/ppermute | solution.py:54
  18.5 6.3 %collective-permute-start.9 = (bf16[2,120,512]{2,1,0:T(8,128)(2,1)S(1)}, bf16[2,120,512]{2,1,0:T(8,128)(2,1)S(1)}, u32[]{:S(2)}, u32[]{:S(2)}) collective-permute-start(bf16[2,120,512]{2,1,0:T(8,128)(2,1)S(1)} %turn0.1), channel_id=1, source_target_pairs={{0,4},{1,5},{2,3},{3,2},{4,0},{5,1},{6,7},{7,6},{8,12},{9,13},{10,... | collective-permute-start | bytes 737288 | tf_op jit(solution)/shard_map/ppermute | solution.py:54
  20.4 7.8 %collective-permute-start.7 = (bf16[4,60,512]{2,1,0:T(8,128)(2,1)S(1)}, bf16[4,60,512]{2,1,0:T(8,128)(2,1)S(1)}, u32[]{:S(2)}, u32[]{:S(2)}) collective-permute-start(bf16[4,60,512]{2,1,0:T(8,128)(2,1)S(1)} %pad_maximum_fusion.1), channel_id=1, source_target_pairs={{0,4},{1,5},{2,10},{3,11},{4,0},{5,1},{6,14},{7,15},{8,12},{9,13},... | collective-permute-start | bytes 737288 | tf_op jit(solution)/shard_map/ppermute | solution.py:54
  25.1 4.9 %collective-permute-start.10 = (bf16[120,512]{1,0:T(8,128)(2,1)S(1)}, bf16[120,512]{1,0:T(8,128)(2,1)S(1)}, u32[]{:S(2)}, u32[]{:S(2)}) collective-permute-start(bf16[120,512]{1,0:T(8,128)(2,1)S(1)} %part0.1), channel_id=1, source_target_pairs={{0,8},{1,9},{2,6},{3,7},{4,12},{5,13},{6,2},{7,3},{8,0},{9,1},{10,... | collective-permute-start | bytes 368648 | tf_op jit(solution)/shard_map/ppermute | solution.py:54
  28.3 9.2 %collective-permute-start.11 = (bf16[8,60,512]{2,1,0:T(8,128)(2,1)S(1)}, bf16[8,60,512]{2,1,0:T(8,128)(2,1)S(1)}, u32[]{:S(2)}, u32[]{:S(2)}) collective-permute-start(bf16[8,60,512]{2,1,0:T(8,128)(2,1)S(1)} %pad_maximum_fusion.own), channel_id=1, source_target_pairs={{0,1},{1,0},{2,6},{3,7},{4,5},{5,4},{6,2},{7,3},{8,9},{9,8},{10,14... | collective-permute-start | bytes 1474568 | tf_op jit(solution)/shard_map/ppermute | solution.py:54
  30.4 8.3 %collective-permute-start.13 = (bf16[60,512]{1,0:T(8,128)(2,1)S(1)}, bf16[60,512]{1,0:T(8,128)(2,1)S(1)}, u32[]{:S(2)}, u32[]{:S(2)}) collective-permute-start(bf16[60,512]{1,0:T(8,128)(2,1)S(1)} %halve0.1), channel_id=1, source_target_pairs={{0,16},{1,17},{2,18},{3,19},{4,20},{5,21},{6,22},{7,23},{8,24},{9,... | collective-permute-start | bytes 184328 | tf_op jit(solution)/shard_map/ppermute | solution.py:54
  38.6 2.0 %collective-permute-start.12 = (bf16[1,6,160,128]{3,2,1,0:T(8,128)(2,1)S(1)}, bf16[1,6,160,128]{3,2,1,0:T(8,128)(2,1)S(1)}, u32[]{:S(2)}, u32[]{:S(2)}) collective-permute-start(bf16[1,6,160,128]{3,2,1,0:T(8,128)(2,1)S(1)} %get-tuple-element.34), channel_id=1, source_target_pairs={{0,2},{1,3},{2,0},{3,1},{4,6},{5,7},{6,4},{7,5},{8,10},{9,11},{10,... | collective-permute-start | bytes 737288 | tf_op jit(solution)/shard_map/ppermute | solution.py:54

commit v6 on v5

--- a/solution.py
+++ b/solution.py
@@ -35,7 +35,7 @@
     "own": 0.7,
     "weave": 0.9,
 }
-GATHER_STEPS = ("send0", "turn0", "part0")
+GATHER_STEP = "part0"
 CELLS_STEP = "halve1"
 FLOPS_PER_US = 1.15e9
 
@@ -117,8 +117,8 @@
         self.part_rows = self.inner * self.block_rows
         self.cells = 2 * images * rows * width
         by_row, by_next, by_col = (2, 0), (4, 0), (0, self.top_strip)
-        self.term_masks = ((by_col, by_next), (by_row, by_col), (by_next, by_row))
-        self.gather_masks = ((by_next, by_col), (by_row, by_next), (by_col, by_row))
+        self.term_masks = ((by_col, by_row), (by_next, by_col), (by_row, by_next))
+        self.gather_masks = ((by_col, by_row), (by_row, by_next), (by_next, by_col))
 
     def block_of(self, slot, by_next, by_row):
         bits = self.band_bits - 3
@@ -136,7 +136,7 @@
 
 def mine(plan):
     core, by_row, by_next, by_col = place(plan)
-    order = ((by_col, by_row, by_next), (by_next, by_col, by_row))
+    order = ((by_col, by_next, by_row), (by_row, by_col, by_next))
     return [jnp.where(core == 0, a, b) for a, b in zip(*order)]
 
 
@@ -175,7 +175,7 @@
             pieces = []
             for j in range(2):
                 for slot in range(plan.inner):
-                    here, there = shifted[plan.block_of(slot, j, i)], shifted[plan.block_of(slot, i, j)]
+                    here, there = shifted[plan.block_of(slot, i, j)], shifted[plan.block_of(slot, j, i)]
                     pieces += here if i == j else [jnp.where(core == 0, a, b) for a, b in zip(here, there)]
             out[i, :, at * width : (at + 1) * width] = jnp.concatenate(pieces, axis=0).astype(jnp.bfloat16)
 
@@ -200,12 +200,17 @@
     return lax.dot_general(acts[i], grads[x], (((1,), (1,)), ((), ())), preferred_element_type=jnp.float32)
 
 
-def send_kernel(plan, same, acts, grads, out):
+def send_kernel(plan, same, acts, grads, *rest):
+    packed, out = rest if same else (None, rest[0])
     first, second, _ = mine(plan)
+    rows = plan.part_rows
     total = pair_terms(plan, acts, grads, 1 - first, second if same else 1 - second)
     for k in range(2):
-        half = total[k * plan.part_rows : (k + 1) * plan.part_rows]
-        out[k] = encoded(peak_of(half), half, plan.half_used)
+        half = total[k * rows : (k + 1) * rows]
+        out[k * rows : (k + 1) * rows] = encoded(peak_of(half), half, plan.half_used)
+    if same:
+        blocks = [packed[k].astype(jnp.float32) for k in range(plan.inner)]
+        out[2 * rows :] = jnp.concatenate(blocks, axis=0).astype(jnp.bfloat16)
 
 
 def keep_kernel(plan, same, acts, grads, out):
@@ -215,10 +220,15 @@
         out[k] = total[k * plan.part_rows : (k + 1) * plan.part_rows]
 
 
-def turn_kernel(plan, same, keep, message, out):
+def turn_kernel(plan, same, keep, message, *rest):
+    rows = plan.part_rows
     for k in range(2):
-        total = keep[k] + decoded(message[k])
-        out[k] = total if same else encoded(peak_of(total), total, plan.half_used)
+        total = keep[k] + decoded(message[k * rows : (k + 1) * rows])
+        rest[1 if same else 0][k] = total if same else encoded(peak_of(total), total, plan.half_used)
+    if same:
+        sent, _, gathered = rest
+        gathered[0] = sent[2 * rows :]
+        gathered[1] = message[2 * rows :]
 
 
 def part_kernel(plan, same, keep, message, out):
@@ -282,11 +292,15 @@
         rows = [[] for _ in TAP_STEPS]
         for m in range(plan.blocks):
             row, behind, col = (m % 2) ^ row_bit, (m // 2 % 2) ^ next_bit, x ^ col_bit
-            one = jnp.where(core == 0, behind, col)
+            one = jnp.where(core == 0, col, row)
             two = jnp.where(core == 0, row, behind)
-            three = jnp.where(core == 0, col, row)
-            slot = (two * 2 + one) * plan.inner + ((m // 4) ^ rest)
-            block = jnp.where(three == 0, own[slot], other[slot]).astype(jnp.float32)
+            three = jnp.where(core == 0, behind, col)
+            slot = two * 2 + one
+            pair = jnp.where(three == 0, own[slot], other[slot]).astype(jnp.float32)
+            block = pair[: plan.block_rows]
+            for k in range(1, plan.inner):
+                at = pair[k * plan.block_rows : (k + 1) * plan.block_rows]
+                block = jnp.where(((m // 4) ^ rest) == k, at, block)
             for c in range(len(TAP_STEPS)):
                 rows[c].append(block[c * depth : (c + 1) * depth])
         for c in range(len(TAP_STEPS)):
@@ -317,22 +331,12 @@
     return lax.optimization_barrier((value, *others))[0]
 
 
-def joined(packed, come, start):
-    return after(jnp.concatenate([packed, after(come, start)], axis=0), start)
-
-
-def first_kernel(plan, kernel):
+def first_kernel(plan, kernel, step):
+    sizes = plan.sizes
     shape = jax.ShapeDtypeStruct((plan.block_rows, plan.lanes), jnp.bfloat16)
     packed = call("pack", functools.partial(pack_kernel, plan), shape, [kernel])[None]
-    return [packed] + [swap(packed, plan.sizes, (mask, 0)) for mask in plan.rest_band[:1]]
-
-
-def whole_kernel(plan, packed, starts):
-    sizes = plan.sizes
-    starts = list(starts)
-    packed = joined(*packed, starts.pop(0)) if len(packed) > 1 else packed[0]
-    for mask in plan.rest_band[1:]:
-        packed = jnp.concatenate([packed, swap(packed, sizes, (mask, 0))], axis=0)
+    for mask in reversed(plan.rest_band):
+        packed = jnp.concatenate([packed, after(swap(packed, sizes, (mask, 0)), step)], axis=0)
     if plan.rest_strip:
         packed = packed[None]
         for mask in reversed(plan.rest_strip):
@@ -343,9 +347,13 @@
         packed = packed.reshape(count, plan.inner, plan.block_rows, len(TAP_STEPS), plan.cols)
         packed = packed.transpose(1, 2, 3, 0, 4).reshape(plan.inner, plan.block_rows, plan.half_used)
         packed = jnp.pad(packed, ((0, 0), (0, 0), (0, plan.half_lanes - plan.half_used)))
-    for masks in plan.gather_masks[:-1]:
-        packed = joined(packed, swap(packed, sizes, *masks), starts.pop(0))
-    return packed, swap(packed, sizes, *plan.gather_masks[-1])
+    return packed
+
+
+def whole_kernel(plan, packed, step):
+    packed = jnp.concatenate([packed, swap(packed, plan.sizes, *plan.gather_masks[1])], axis=0)
+    packed = after(packed, step)
+    return packed, swap(packed, plan.sizes, *plan.gather_masks[2])
 
 
 def narrowed(plan, total):
@@ -361,7 +369,7 @@
     return jnp.pad(total, ((0, 0), (0, plan.lanes - plan.used)))
 
 
-def kernel_terms(plan, acts, grads, scale):
+def kernel_terms(plan, acts, grads, kernel, scale):
     sizes, f32 = plan.sizes, jnp.float32
     rows, lanes = plan.part_rows, plan.half_lanes
 
@@ -371,15 +379,17 @@
     part = functools.partial
     b16 = jnp.bfloat16
     shape = (2, rows, lanes)
-    send0 = run("send0", part(send_kernel, plan, False), shape, b16, [acts, grads])
+    send0 = run("send0", part(send_kernel, plan, False), (2 * rows, lanes), b16, [acts, grads])
     come0 = swap(send0, sizes, *plan.term_masks[0])
-    send1 = run("send1", part(send_kernel, plan, True), shape, b16, [after(acts, send0), grads])
+    keep0 = run("keep0", part(keep_kernel, plan, False), shape, f32, [after(acts, send0), grads])
+    packed = first_kernel(plan, kernel, keep0)
+    send1 = run("send1", part(send_kernel, plan, True), (3 * rows, lanes), b16, [after(acts, keep0), grads, packed])
     come1 = swap(send1, sizes, *plan.term_masks[0])
-    keep0 = run("keep0", part(keep_kernel, plan, False), shape, f32, [after(acts, send1), grads])
     send = run("turn0", part(turn_kernel, plan, False), shape, b16, [keep0, come0])
     come = swap(send, sizes, *plan.term_masks[1])
     keep1 = run("keep1", part(keep_kernel, plan, True), shape, f32, [after(acts, send), grads])
-    keep = run("turn1", part(turn_kernel, plan, True), shape, f32, [keep1, come1])
+    shapes = (jax.ShapeDtypeStruct(shape, f32), jax.ShapeDtypeStruct(shape, b16))
+    keep, packed = call("turn1", part(turn_kernel, plan, True), shapes, [keep1, come1, send1])
     steps = {"send0": send0, "send1": send1, "keep0": keep0, "turn0": send, "keep1": keep1, "turn1": keep}
     shape = shape[1:]
     send = run("part0", part(part_kernel, plan, False), shape, b16, [keep, come])
@@ -403,7 +413,7 @@
         jax.ShapeDtypeStruct((len(TAP_STEPS) ** 2, plan.depth, plan.cols), f32),
         [keep, come],
     )
-    return total, steps
+    return total, packed, steps
 
 
 def edge_kernel(plan, grad, out, copy):
@@ -441,7 +451,6 @@
     grad0, tops, bottoms = borders(plan, grad)
     act1 = swap(act, plan.sizes, (1, 0))
     grad1 = swap(grad, plan.sizes, (1, 0))
-    packed = first_kernel(plan, kernel.transpose(1, 0, 2))
     shape = (2, 2 * plan.part_rows, plan.cells)
     acts = call("acts", functools.partial(acts_kernel, plan), jax.ShapeDtypeStruct(shape, act.dtype), [act, act1])
     shape = (2, plan.half_lanes, plan.cells)
@@ -451,8 +460,8 @@
         jax.ShapeDtypeStruct(shape, grad.dtype),
         [grad0, grad1, *tops, *bottoms],
     )
-    kernel_grad, steps = kernel_terms(plan, acts, grads, scale)
-    packed = whole_kernel(plan, packed, [steps[name] for name in GATHER_STEPS])
+    kernel_grad, packed, steps = kernel_terms(plan, acts, grads, kernel.transpose(1, 0, 2), scale)
+    packed = whole_kernel(plan, packed, steps[GATHER_STEP])
     shape = jax.ShapeDtypeStruct((images, rows, plan.half, width), jnp.bfloat16)
     left = jax.ShapeDtypeStruct((len(TAP_STEPS) * plan.half, 2 * plan.half_lanes), jnp.bfloat16)
     grads = grads.reshape(2 * plan.half_lanes, plan.cells)

time: 41.7 us -> 45.1 us (1.082)
  waiting for transfers between devices: 9.63 us -> 15.6 us
  starting transfers between devices: 19.7 us -> 17.1 us
  local copies, waits for them, and re-layouts: 0.01 us -> 1.04 us
  Pallas kernels: 11.3 us -> 10.4 us
    ppermute x14 -> x13, waiting for transfers between devices: 9.63 us -> 15.6 us  [swap(): return lax.ppermute(value, AXES, pairs)]
    ppermute x14 -> x13, starting transfers between devices: 19.7 us -> 17.1 us  [swap(): return lax.ppermute(value, AXES, pairs)]
    unnamed x4 -> x6, local copies, waits for them, and re-layouts: 0.01 us -> 1.04 us
    pallas_call x18, Pallas kernels: 11.3 us -> 10.4 us  [call(): pl.pallas_call(kernel, out_shape=out_shape, in_specs=[pl.BlockSpec(memory...]
  transfers between devices with their start and end apart: 14 -> 13, of which waited for: 6 -> 5; matrix products, arithmetic and copies ran while one was open for 0% -> 0% of each run, Pallas kernels for 22% -> 21%
where the time goes in v6:
time: 45.1 us; the launch traced here: 45 us
  starting transfers between devices  17.1 us (38%)
  waiting for transfers between devices  15.6 us (35%)
  Pallas kernels  10.4 us (23%)
  local copies, waits for them, and re-layouts  1.04 us (2%)
  between operations  0.81 us (2%)
    ppermute x13, starting transfers between devices, swap(): return lax.ppermute(value, AXES, pairs)  17.1 us
    ppermute x13, waiting for transfers between devices, swap(): return lax.ppermute(value, AXES, pairs)  15.6 us
    pallas_call x18, Pallas kernels, call(): pl.pallas_call(kernel, out_shape=out_shape, in_specs=[pl.BlockSpec(memory...  10.4 us
    unnamed x6, local copies, waits for them, and re-layouts  1.04 us
  transfers between devices with their start and end apart: 13, of which 5 were waited for; matrix products, arithmetic and copies ran while one was open for 0% of the time, Pallas kernels for 21%

profile of v6, /device:TPU:0, one launch (start us, length us, event | category | flops | bytes accessed | tf_op | source)
XLA Modules:
  0.0 45.0 jit_solution(17131270104099712372)
XLA Ops:
  0.6 0.0 copy-start
  0.6 0.5 %collective-permute-start.1 = (bf16[1,6,320,128]{3,2,1,0:T(8,128)(2,1)}, bf16[1,6,320,128]{3,2,1,0:T(8,128)(2,1)S(1)}, u32[]{:S(2)}, u32[]{:S(2)}) collective-permute-start(bf16[1,6,320,128]{3,2,1,0:T(8,128)(2,1)} %bitcast.13), channel_id=1, source_target_pairs={{0,2},{1,3},{2,0},{3,1},{4,6},{5,7},{6,4},{7,5},{8,10},{9,11},{10,... | collective-permute-start | bytes 1474568 | tf_op jit(solution)/shard_map/ppermute | solution.py:54
  1.2 0.0 copy-start.1
  1.2 1.0 %copy-done.1 = bf16[1,320,6,128]{3,1,2,0:T(8,128)(2,1)S(1)} copy-done((bf16[1,320,6,128]{3,1,2,0:T(8,128)(2,1)S(1)}, bf16[1,320,6,128]{3,1,2,0:T(8,128)(2,1)}, u32[]{:S(2)}) %copy-start.1) | copy-done | bytes 491544
  2.2 0.0 copy-start.2
  2.2 0.1 edge.1
  2.3 2.7 %collective-permute-start.3 = (bf16[1,320,128]{2,1,0:T(8,128)(2,1)S(1)}, bf16[1,320,128]{2,1,0:T(8,128)(2,1)S(1)}, u32[]{:S(2)}, u32[]{:S(2)}) collective-permute-start(bf16[1,320,128]{2,1,0:T(8,128)(2,1)S(1)} %get-tuple-element.18), channel_id=1, source_target_pairs={{0,3},{1,2},{2,1},{3,0},{4,7},{5,6},{6,5},{7,4},{8,11},{9,10},{10,... | collective-permute-start | bytes 245768 | tf_op jit(solution)/shard_map/ppermute | solution.py:54
  4.9 0.0 collective-permute-start.2
  5.0 0.0 copy-done
  5.0 0.2 collective-permute-start
  5.1 0.0 copy-done.2
  5.1 0.1 pack.1
  5.2 3.0 %collective-permute-start.5 = (bf16[1,60,512]{2,1,0:T(8,128)(2,1)S(1)}, bf16[1,60,512]{2,1,0:T(8,128)(2,1)S(1)}, u32[]{:S(2)}, u32[]{:S(2)}) collective-permute-start(bf16[1,60,512]{2,1,0:T(8,128)(2,1)S(1)} %bitcast.9), channel_id=1, source_target_pairs={{0,16},{1,17},{2,18},{3,19},{4,20},{5,21},{6,22},{7,23},{8,24},{9,... | collective-permute-start | bytes 184328 | tf_op jit(solution)/shard_map/ppermute | solution.py:54
  8.2 0.0 collective-permute-done.act1
  8.2 0.6 %acts.1 = bf16[2,240,1536]{2,1,0:T(8,128)(2,1)S(1)} custom-call(bf16[1,6,320,128]{3,2,1,0:T(8,128)(2,1)S(1)} %bitcast.12, bf16[1,6,320,128]{3,2,1,0:T(8,128)(2,1)S(1)} %collective-permute-done.act1), custom_call_target="tpu_custom_call" | custom-call | flops 690000000 | tf_op jit(solution)/shard_map/acts/pallas_call | solution.py:58
  8.8 0.0 collective-permute-done.3.top1.bottom1
  8.8 0.8 %collective-permute-done.2.top0.bottom0 = bf16[1,320,128]{2,1,0:T(8,128)(2,1)S(1)} collective-permute-done((bf16[1,320,128]{2,1,0:T(8,128)(2,1)S(1)}, bf16[1,320,128]{2,1,0:T(8,128)(2,1)S(1)}, u32[]{:S(2)}, u32[]{:S(2)}) %collective-permute-start.2) | collective-permute-done | bytes 81952 | tf_op jit(solution)/shard_map/ppermute | solution.py:54
  9.7 0.0 collective-permute-done.1.grad1
  9.7 0.5 %grads.1 = bf16[2,512,1536]{2,1,0:T(8,128)(2,1)S(1)} custom-call(bf16[1,6,320,128]{3,2,1,0:T(8,128)(2,1)S(1)} %get-tuple-element.17.grad0, bf16[1,6,320,128]{3,2,1,0:T(8,128)(2,1)S(1)} %collective-permute-done.1.grad1, bf16[1,320,128]{2,1,0:T(8,128)(2,1)S(1)} %collective-permute-done.2.top0.bottom0, ...), custom_call_target="tpu_custom_call" | custom-call | flops 575000000 | tf_op jit(solution)/shard_map/grads/pallas_call | solution.py:58
  10.1 0.9 %send0.1 = bf16[240,512]{1,0:T(8,128)(2,1)S(1)} custom-call(bf16[2,240,1536]{2,1,0:T(8,128)(2,1)S(1)} %acts.1, bf16[2,512,1536]{2,1,0:T(8,128)(2,1)S(1)} %grads.1), custom_call_target="tpu_custom_call" | custom-call | flops 1610000000 | tf_op jit(solution)/shard_map/send0/pallas_call | solution.py:58
  11.1 1.7 %collective-permute-start.4 = (bf16[240,512]{1,0:T(8,128)(2,1)S(1)}, bf16[240,512]{1,0:T(8,128)(2,1)S(1)}, u32[]{:S(2)}, u32[]{:S(2)}) collective-permute-start(bf16[240,512]{1,0:T(8,128)(2,1)S(1)} %send0.1), channel_id=1, source_target_pairs={{0,1},{1,0},{2,6},{3,7},{4,5},{5,4},{6,2},{7,3},{8,9},{9,8},{10,14... | collective-permute-start | bytes 737288 | tf_op jit(solution)/shard_map/ppermute | solution.py:54
  12.8 0.6 %keep0.1.keep = f32[2,120,512]{2,1,0:T(8,128)S(1)} custom-call(bf16[2,240,1536]{2,1,0:T(8,128)(2,1)S(1)} %acts.1, bf16[2,512,1536]{2,1,0:T(8,128)(2,1)S(1)} %grads.1), custom_call_target="tpu_custom_call" | custom-call | flops 1150000000 | tf_op jit(solution)/shard_map/keep0/pallas_call | solution.py:58
  13.4 0.0 collective-permute-done.5
  13.5 0.9 %send1.1.rest_0_ = bf16[360,512]{1,0:T(8,128)(2,1)S(1)} custom-call(bf16[2,240,1536]{2,1,0:T(8,128)(2,1)S(1)} %acts.1, bf16[2,512,1536]{2,1,0:T(8,128)(2,1)S(1)} %grads.1, bf16[2,60,512]{2,1,0:T(8,128)(2,1)S(1)} %pad_maximum_fusion.1.rest_0_), custom_call_target="tpu_custom_call" | custom-call | flops 1610000000 | tf_op jit(solution)/shard_map/send1/pallas_call | solution.py:58
  14.4 0.6 %collective-permute-start.6 = (bf16[360,512]{1,0:T(8,128)(2,1)S(1)}, bf16[360,512]{1,0:T(8,128)(2,1)S(1)}, u32[]{:S(2)}, u32[]{:S(2)}) collective-permute-start(bf16[360,512]{1,0:T(8,128)(2,1)S(1)} %send1.1.rest_0_), channel_id=1, source_target_pairs={{0,1},{1,0},{2,6},{3,7},{4,5},{5,4},{6,2},{7,3},{8,9},{9,8},{10,14... | collective-permute-start | bytes 1105928 | tf_op jit(solution)/shard_map/ppermute | solution.py:54
  14.9 2.4 %collective-permute-done.4.message = bf16[240,512]{1,0:T(8,128)(2,1)S(1)} collective-permute-done((bf16[240,512]{1,0:T(8,128)(2,1)S(1)}, bf16[240,512]{1,0:T(8,128)(2,1)S(1)}, u32[]{:S(2)}, u32[]{:S(2)}) %collective-permute-start.4) | collective-permute-done | bytes 245792 | tf_op jit(solution)/shard_map/ppermute | solution.py:54
  17.3 0.7 %turn0.1 = bf16[2,120,512]{2,1,0:T(8,128)(2,1)S(1)} custom-call(f32[2,120,512]{2,1,0:T(8,128)S(1)} %keep0.1.keep, bf16[240,512]{1,0:T(8,128)(2,1)S(1)} %collective-permute-done.4.message), custom_call_target="tpu_custom_call" | custom-call | flops 1035000000 | tf_op jit(solution)/shard_map/turn0/pallas_call | solution.py:58
  18.0 1.8 %collective-permute-start.8 = (bf16[2,120,512]{2,1,0:T(8,128)(2,1)S(1)}, bf16[2,120,512]{2,1,0:T(8,128)(2,1)S(1)}, u32[]{:S(2)}, u32[]{:S(2)}) collective-permute-start(bf16[2,120,512]{2,1,0:T(8,128)(2,1)S(1)} %turn0.1), channel_id=1, source_target_pairs={{0,8},{1,9},{2,3},{3,2},{4,12},{5,13},{6,7},{7,6},{8,0},{9,1},{10,... | collective-permute-start | bytes 737288 | tf_op jit(solution)/shard_map/ppermute | solution.py:54
  19.9 0.6 %keep1.1.keep = f32[2,120,512]{2,1,0:T(8,128)S(1)} custom-call(bf16[2,240,1536]{2,1,0:T(8,128)(2,1)S(1)} %acts.1, bf16[2,512,1536]{2,1,0:T(8,128)(2,1)S(1)} %grads.1), custom_call_target="tpu_custom_call" | custom-call | flops 1150000000 | tf_op jit(solution)/shard_map/keep1/pallas_call | solution.py:58
  20.5 4.1 %collective-permute-done.6.message = bf16[360,512]{1,0:T(8,128)(2,1)S(1)} collective-permute-done((bf16[360,512]{1,0:T(8,128)(2,1)S(1)}, bf16[360,512]{1,0:T(8,128)(2,1)S(1)}, u32[]{:S(2)}, u32[]{:S(2)}) %collective-permute-start.6) | collective-permute-done | bytes 368672 | tf_op jit(solution)/shard_map/ppermute | solution.py:54
  24.5 0.3 turn1.1
  24.9 1.3 %collective-permute-start.7 = (bf16[2,120,512]{2,1,0:T(8,128)(2,1)S(1)}, bf16[2,120,512]{2,1,0:T(8,128)(2,1)S(1)}, u32[]{:S(2)}, u32[]{:S(2)}) collective-permute-start(bf16[2,120,512]{2,1,0:T(8,128)(2,1)S(1)} %get-tuple-element.23), channel_id=1, source_target_pairs={{0,4},{1,5},{2,10},{3,11},{4,0},{5,1},{6,14},{7,15},{8,12},{9,13},... | collective-permute-start | bytes 737288 | tf_op jit(solution)/shard_map/ppermute | solution.py:54
  26.2 0.0 collective-permute-done.8.message
  26.2 0.4 part0.1
  26.6 1.1 %collective-permute-start.9 = (bf16[120,512]{1,0:T(8,128)(2,1)S(1)}, bf16[120,512]{1,0:T(8,128)(2,1)S(1)}, u32[]{:S(2)}, u32[]{:S(2)}) collective-permute-start(bf16[120,512]{1,0:T(8,128)(2,1)S(1)} %part0.1), channel_id=1, source_target_pairs={{0,4},{1,5},{2,10},{3,11},{4,0},{5,1},{6,14},{7,15},{8,12},{9,13},... | collective-permute-start | bytes 368648 | tf_op jit(solution)/shard_map/ppermute | solution.py:54
  27.7 3.4 %collective-permute-done.7 = bf16[2,120,512]{2,1,0:T(8,128)(2,1)S(1)} collective-permute-done((bf16[2,120,512]{2,1,0:T(8,128)(2,1)S(1)}, bf16[2,120,512]{2,1,0:T(8,128)(2,1)S(1)}, u32[]{:S(2)}, u32[]{:S(2)}) %collective-permute-start.7) | collective-permute-done | bytes 245792 | tf_op jit(solution)/shard_map/ppermute | solution.py:54
  31.2 1.4 %collective-permute-start.10 = (bf16[4,120,512]{2,1,0:T(8,128)(2,1)S(1)}, bf16[4,120,512]{2,1,0:T(8,128)(2,1)S(1)}, u32[]{:S(2)}, u32[]{:S(2)}) collective-permute-start(bf16[4,120,512]{2,1,0:T(8,128)(2,1)S(1)} %pad_maximum_fusion.own), channel_id=1, source_target_pairs={{0,8},{1,9},{2,3},{3,2},{4,12},{5,13},{6,7},{7,6},{8,0},{9,1},{10,... | collective-permute-start | bytes 1474568 | tf_op jit(solution)/shard_map/ppermute | solution.py:54
  32.6 0.2 part1.1.keep
  32.7 0.0 collective-permute-done.9.message
  32.7 0.4 halve0.1
  33.1 2.7 %collective-permute-start.12 = (bf16[60,512]{1,0:T(8,128)(2,1)S(1)}, bf16[60,512]{1,0:T(8,128)(2,1)S(1)}, u32[]{:S(2)}, u32[]{:S(2)}) collective-permute-start(bf16[60,512]{1,0:T(8,128)(2,1)S(1)} %halve0.1), channel_id=1, source_target_pairs={{0,16},{1,17},{2,18},{3,19},{4,20},{5,21},{6,22},{7,23},{8,24},{9,... | collective-permute-start | bytes 184328 | tf_op jit(solution)/shard_map/ppermute | solution.py:54
  35.8 0.2 halve1.1.keep
  35.9 4.8 %collective-permute-done.10.other = bf16[4,120,512]{2,1,0:T(8,128)(2,1)S(1)} collective-permute-done((bf16[4,120,512]{2,1,0:T(8,128)(2,1)S(1)}, bf16[4,120,512]{2,1,0:T(8,128)(2,1)S(1)}, u32[]{:S(2)}, u32[]{:S(2)}) %collective-permute-start.10) | collective-permute-done | bytes 491552 | tf_op jit(solution)/shard_map/ppermute | solution.py:54
  40.8 1.2 %given.1 = (bf16[1,6,160,128]{3,2,1,0:T(8,128)(2,1)S(1)}, bf16[480,1024]{1,0:T(8,128)(2,1)S(1)}) custom-call(bf16[4,120,512]{2,1,0:T(8,128)(2,1)S(1)} %pad_maximum_fusion.own, bf16[4,120,512]{2,1,0:T(8,128)(2,1)S(1)} %collective-permute-done.10.other, bf16[1024,1536]{1,0:T(8,128)(2,1)S(1)} %bitcast.7), custom_call_target="tpu_custom_call" | custom-call | flops 1380000000 | tf_op jit(solution)/shard_map/given/pallas_call | solution.py:58
  42.0 0.1 collective-permute-start.11
  42.1 0.0 collective-permute-done.12.message
  42.1 0.9 %last.1 = f32[9,20,160]{2,1,0:T(8,128)} custom-call(f32[60,512]{1,0:T(8,128)S(1)} %halve1.1.keep, bf16[60,512]{1,0:T(8,128)(2,1)S(1)} %collective-permute-done.12.message), custom_call_target="tpu_custom_call" | custom-call | flops 9200000000 | tf_op jit(solution)/shard_map/last/pallas_call | solution.py:58
  43.0 1.0 %own.1 = bf16[1,6,160,128]{3,2,1,0:T(8,128)(2,1)S(1)} custom-call(bf16[480,1024]{1,0:T(8,128)(2,1)S(1)} %get-tuple-element.31.left, bf16[1024,1536]{1,0:T(8,128)(2,1)S(1)} %bitcast.8), custom_call_target="tpu_custom_call" | custom-call | flops 805000000 | tf_op jit(solution)/shard_map/own/pallas_call | solution.py:58
  44.0 0.0 collective-permute-done.11.theirs
  44.0 0.9 %weave.1 = bf16[1,6,320,128]{3,2,1,0:T(8,128)(2,1)} custom-call(bf16[1,6,160,128]{3,2,1,0:T(8,128)(2,1)S(1)} %own.1, bf16[1,6,160,128]{3,2,1,0:T(8,128)(2,1)S(1)} %collective-permute-done.11.theirs), custom_call_target="tpu_custom_call" | custom-call | flops 1035000000 | tf_op jit(solution)/shard_map/weave/pallas_call | solution.py:58
  (2 shorter events, 0.1 us)
Async XLA Ops:
  0.6 4.3 %copy-start = (bf16[1,320,6,128]{3,1,2,0:T(8,128)(2,1)S(1)}, bf16[1,320,6,128]{3,1,2,0:T(8,128)(2,1)}, u32[]{:S(2)}) copy-start(bf16[1,320,6,128]{3,1,2,0:T(8,128)(2,1)} %param.3) | copy-start | bytes 1474564
  0.6 9.0 %collective-permute-start.1 = (bf16[1,6,320,128]{3,2,1,0:T(8,128)(2,1)}, bf16[1,6,320,128]{3,2,1,0:T(8,128)(2,1)S(1)}, u32[]{:S(2)}, u32[]{:S(2)}) collective-permute-start(bf16[1,6,320,128]{3,2,1,0:T(8,128)(2,1)} %bitcast.13), channel_id=1, source_target_pairs={{0,2},{1,3},{2,0},{3,1},{4,6},{5,7},{6,4},{7,5},{8,10},{9,11},{10,... | collective-permute-start | bytes 1474568 | tf_op jit(solution)/shard_map/ppermute | solution.py:54
  1.2 1.0 %copy-start.1 = (bf16[1,320,6,128]{3,1,2,0:T(8,128)(2,1)S(1)}, bf16[1,320,6,128]{3,1,2,0:T(8,128)(2,1)}, u32[]{:S(2)}) copy-start(bf16[1,320,6,128]{3,1,2,0:T(8,128)(2,1)} %param.4) | copy-start | bytes 1474564
  2.2 2.9 %copy-start.2 = (bf16[20,9,160]{2,0,1:T(8,128)(2,1)S(1)}, bf16[20,9,160]{2,0,1:T(8,128)(2,1)}, u32[]{:S(2)}) copy-start(bf16[20,9,160]{2,0,1:T(8,128)(2,1)} %param.5) | copy-start | bytes 172804
  2.3 6.6 %collective-permute-start.3 = (bf16[1,320,128]{2,1,0:T(8,128)(2,1)S(1)}, bf16[1,320,128]{2,1,0:T(8,128)(2,1)S(1)}, u32[]{:S(2)}, u32[]{:S(2)}) collective-permute-start(bf16[1,320,128]{2,1,0:T(8,128)(2,1)S(1)} %get-tuple-element.18), channel_id=1, source_target_pairs={{0,3},{1,2},{2,1},{3,0},{4,7},{5,6},{6,5},{7,4},{8,11},{9,10},{10,... | collective-permute-start | bytes 245768 | tf_op jit(solution)/shard_map/ppermute | solution.py:54
  4.9 4.8 %collective-permute-start.2 = (bf16[1,320,128]{2,1,0:T(8,128)(2,1)S(1)}, bf16[1,320,128]{2,1,0:T(8,128)(2,1)S(1)}, u32[]{:S(2)}, u32[]{:S(2)}) collective-permute-start(bf16[1,320,128]{2,1,0:T(8,128)(2,1)S(1)} %get-tuple-element.18), channel_id=1, source_target_pairs={{0,1},{1,0},{2,3},{3,2},{4,5},{5,4},{6,7},{7,6},{8,9},{9,8},{10,11... | collective-permute-start | bytes 245768 | tf_op jit(solution)/shard_map/ppermute | solution.py:54
  5.0 3.3 %collective-permute-start = (bf16[1,6,320,128]{3,2,1,0:T(8,128)(2,1)S(1)}, bf16[1,6,320,128]{3,2,1,0:T(8,128)(2,1)S(1)}, u32[]{:S(2)}, u32[]{:S(2)}) collective-permute-start(bf16[1,6,320,128]{3,2,1,0:T(8,128)(2,1)S(1)} %bitcast.11), channel_id=1, source_target_pairs={{0,2},{1,3},{2,0},{3,1},{4,6},{5,7},{6,4},{7,5},{8,10},{9,11},{10,... | collective-permute-start | bytes 1474568 | tf_op jit(solution)/shard_map/ppermute | solution.py:54
  5.2 8.2 %collective-permute-start.5 = (bf16[1,60,512]{2,1,0:T(8,128)(2,1)S(1)}, bf16[1,60,512]{2,1,0:T(8,128)(2,1)S(1)}, u32[]{:S(2)}, u32[]{:S(2)}) collective-permute-start(bf16[1,60,512]{2,1,0:T(8,128)(2,1)S(1)} %bitcast.9), channel_id=1, source_target_pairs={{0,16},{1,17},{2,18},{3,19},{4,20},{5,21},{6,22},{7,23},{8,24},{9,... | collective-permute-start | bytes 184328 | tf_op jit(solution)/shard_map/ppermute | solution.py:54
  11.1 6.3 %collective-permute-start.4 = (bf16[240,512]{1,0:T(8,128)(2,1)S(1)}, bf16[240,512]{1,0:T(8,128)(2,1)S(1)}, u32[]{:S(2)}, u32[]{:S(2)}) collective-permute-start(bf16[240,512]{1,0:T(8,128)(2,1)S(1)} %send0.1), channel_id=1, source_target_pairs={{0,1},{1,0},{2,6},{3,7},{4,5},{5,4},{6,2},{7,3},{8,9},{9,8},{10,14... | collective-permute-start | bytes 737288 | tf_op jit(solution)/shard_map/ppermute | solution.py:54
  14.4 10.1 %collective-permute-start.6 = (bf16[360,512]{1,0:T(8,128)(2,1)S(1)}, bf16[360,512]{1,0:T(8,128)(2,1)S(1)}, u32[]{:S(2)}, u32[]{:S(2)}) collective-permute-start(bf16[360,512]{1,0:T(8,128)(2,1)S(1)} %send1.1.rest_0_), channel_id=1, source_target_pairs={{0,1},{1,0},{2,6},{3,7},{4,5},{5,4},{6,2},{7,3},{8,9},{9,8},{10,14... | collective-permute-start | bytes 1105928 | tf_op jit(solution)/shard_map/ppermute | solution.py:54
  18.0 8.2 %collective-permute-start.8 = (bf16[2,120,512]{2,1,0:T(8,128)(2,1)S(1)}, bf16[2,120,512]{2,1,0:T(8,128)(2,1)S(1)}, u32[]{:S(2)}, u32[]{:S(2)}) collective-permute-start(bf16[2,120,512]{2,1,0:T(8,128)(2,1)S(1)} %turn0.1), channel_id=1, source_target_pairs={{0,8},{1,9},{2,3},{3,2},{4,12},{5,13},{6,7},{7,6},{8,0},{9,1},{10,... | collective-permute-start | bytes 737288 | tf_op jit(solution)/shard_map/ppermute | solution.py:54
  24.9 6.3 %collective-permute-start.7 = (bf16[2,120,512]{2,1,0:T(8,128)(2,1)S(1)}, bf16[2,120,512]{2,1,0:T(8,128)(2,1)S(1)}, u32[]{:S(2)}, u32[]{:S(2)}) collective-permute-start(bf16[2,120,512]{2,1,0:T(8,128)(2,1)S(1)} %get-tuple-element.23), channel_id=1, source_target_pairs={{0,4},{1,5},{2,10},{3,11},{4,0},{5,1},{6,14},{7,15},{8,12},{9,13},... | collective-permute-start | bytes 737288 | tf_op jit(solution)/shard_map/ppermute | solution.py:54
  26.6 6.1 %collective-permute-start.9 = (bf16[120,512]{1,0:T(8,128)(2,1)S(1)}, bf16[120,512]{1,0:T(8,128)(2,1)S(1)}, u32[]{:S(2)}, u32[]{:S(2)}) collective-permute-start(bf16[120,512]{1,0:T(8,128)(2,1)S(1)} %part0.1), channel_id=1, source_target_pairs={{0,4},{1,5},{2,10},{3,11},{4,0},{5,1},{6,14},{7,15},{8,12},{9,13},... | collective-permute-start | bytes 368648 | tf_op jit(solution)/shard_map/ppermute | solution.py:54
  31.2 9.6 %collective-permute-start.10 = (bf16[4,120,512]{2,1,0:T(8,128)(2,1)S(1)}, bf16[4,120,512]{2,1,0:T(8,128)(2,1)S(1)}, u32[]{:S(2)}, u32[]{:S(2)}) collective-permute-start(bf16[4,120,512]{2,1,0:T(8,128)(2,1)S(1)} %pad_maximum_fusion.own), channel_id=1, source_target_pairs={{0,8},{1,9},{2,3},{3,2},{4,12},{5,13},{6,7},{7,6},{8,0},{9,1},{10,... | collective-permute-start | bytes 1474568 | tf_op jit(solution)/shard_map/ppermute | solution.py:54
  33.1 8.9 %collective-permute-start.12 = (bf16[60,512]{1,0:T(8,128)(2,1)S(1)}, bf16[60,512]{1,0:T(8,128)(2,1)S(1)}, u32[]{:S(2)}, u32[]{:S(2)}) collective-permute-start(bf16[60,512]{1,0:T(8,128)(2,1)S(1)} %halve0.1), channel_id=1, source_target_pairs={{0,16},{1,17},{2,18},{3,19},{4,20},{5,21},{6,22},{7,23},{8,24},{9,... | collective-permute-start | bytes 184328 | tf_op jit(solution)/shard_map/ppermute | solution.py:54
  42.0 2.0 %collective-permute-start.11 = (bf16[1,6,160,128]{3,2,1,0:T(8,128)(2,1)S(1)}, bf16[1,6,160,128]{3,2,1,0:T(8,128)(2,1)S(1)}, u32[]{:S(2)}, u32[]{:S(2)}) collective-permute-start(bf16[1,6,160,128]{3,2,1,0:T(8,128)(2,1)S(1)} %get-tuple-element.30), channel_id=1, source_target_pairs={{0,2},{1,3},{2,0},{3,1},{4,6},{5,7},{6,4},{7,5},{8,10},{9,11},{10,... | collective-permute-start | bytes 737288 | tf_op jit(solution)/shard_map/ppermute | solution.py:54

commit v7 on v5

--- a/solution.py
+++ b/solution.py
@@ -17,6 +17,7 @@
 VMEM_BYTES = 40 * 2**20
 HINTS = {
     "edge": 8.0,
+    "pair": 0.2,
     "pack": 8.0,
     "acts": 0.6,
     "grads": 0.5,
@@ -35,7 +36,7 @@
     "own": 0.7,
     "weave": 0.9,
 }
-GATHER_STEPS = ("send0", "turn0", "part0")
+GATHER_STEPS = ("keep0", "turn0", "part0")
 CELLS_STEP = "halve1"
 FLOPS_PER_US = 1.15e9
 
@@ -118,7 +119,7 @@
         self.cells = 2 * images * rows * width
         by_row, by_next, by_col = (2, 0), (4, 0), (0, self.top_strip)
         self.term_masks = ((by_col, by_next), (by_row, by_col), (by_next, by_row))
-        self.gather_masks = ((by_next, by_col), (by_row, by_next), (by_col, by_row))
+        self.gather_masks = ((by_row, by_col), (by_next, by_next), (by_col, by_row))
 
     def block_of(self, slot, by_next, by_row):
         bits = self.band_bits - 3
@@ -282,11 +283,14 @@
         rows = [[] for _ in TAP_STEPS]
         for m in range(plan.blocks):
             row, behind, col = (m % 2) ^ row_bit, (m // 2 % 2) ^ next_bit, x ^ col_bit
-            one = jnp.where(core == 0, behind, col)
-            two = jnp.where(core == 0, row, behind)
+            one = jnp.where(core == 0, row, col)
             three = jnp.where(core == 0, col, row)
-            slot = (two * 2 + one) * plan.inner + ((m // 4) ^ rest)
-            block = jnp.where(three == 0, own[slot], other[slot]).astype(jnp.float32)
+            slot = behind * 2 + one
+            pair = jnp.where(three == 0, own[slot], other[slot]).astype(jnp.float32)
+            block = pair[: plan.block_rows]
+            for k in range(1, plan.inner):
+                at = pair[k * plan.block_rows : (k + 1) * plan.block_rows]
+                block = jnp.where(((m // 4) ^ rest) == k, at, block)
             for c in range(len(TAP_STEPS)):
                 rows[c].append(block[c * depth : (c + 1) * depth])
         for c in range(len(TAP_STEPS)):
@@ -317,24 +321,25 @@
     return lax.optimization_barrier((value, *others))[0]
 
 
-def joined(packed, come, start):
-    return after(jnp.concatenate([packed, after(come, start)], axis=0), start)
+def pair_kernel(plan, *refs):
+    blocks = [ref[k].astype(jnp.float32) for ref in refs[:-1] for k in range(ref.shape[0])]
+    refs[-1][0] = jnp.concatenate(blocks, axis=0).astype(jnp.bfloat16)
 
 
 def first_kernel(plan, kernel):
     shape = jax.ShapeDtypeStruct((plan.block_rows, plan.lanes), jnp.bfloat16)
     packed = call("pack", functools.partial(pack_kernel, plan), shape, [kernel])[None]
+    for mask in plan.rest_band[:0:-1]:
+        packed = jnp.concatenate([packed, swap(packed, plan.sizes, (mask, 0))], axis=0)
     return [packed] + [swap(packed, plan.sizes, (mask, 0)) for mask in plan.rest_band[:1]]
 
 
 def whole_kernel(plan, packed, starts):
     sizes = plan.sizes
     starts = list(starts)
-    packed = joined(*packed, starts.pop(0)) if len(packed) > 1 else packed[0]
-    for mask in plan.rest_band[1:]:
-        packed = jnp.concatenate([packed, swap(packed, sizes, (mask, 0))], axis=0)
+    packed = [*packed[:-1], after(packed[-1], starts[0])]
     if plan.rest_strip:
-        packed = packed[None]
+        packed = jnp.concatenate(packed, axis=0)[None]
         for mask in reversed(plan.rest_strip):
             packed = jnp.concatenate([packed, swap(packed, sizes, (0, mask))], axis=0)
         count = packed.shape[0]
@@ -342,9 +347,13 @@
         packed = jnp.take(packed, order, axis=0)[..., : plan.used]
         packed = packed.reshape(count, plan.inner, plan.block_rows, len(TAP_STEPS), plan.cols)
         packed = packed.transpose(1, 2, 3, 0, 4).reshape(plan.inner, plan.block_rows, plan.half_used)
-        packed = jnp.pad(packed, ((0, 0), (0, 0), (0, plan.half_lanes - plan.half_used)))
+        packed = [jnp.pad(packed, ((0, 0), (0, 0), (0, plan.half_lanes - plan.half_used)))]
+    shape = jax.ShapeDtypeStruct((1, plan.part_rows, plan.half_lanes), jnp.bfloat16)
+    packed = call("pair", functools.partial(pair_kernel, plan), shape, packed)
+    packed = after(packed, starts.pop(0))
     for masks in plan.gather_masks[:-1]:
-        packed = joined(packed, swap(packed, sizes, *masks), starts.pop(0))
+        come = after(swap(packed, sizes, *masks), starts[0])
+        packed = after(jnp.concatenate([packed, come], axis=0), starts.pop(0))
     return packed, swap(packed, sizes, *plan.gather_masks[-1])
 
 
@@ -373,9 +382,9 @@
     shape = (2, rows, lanes)
     send0 = run("send0", part(send_kernel, plan, False), shape, b16, [acts, grads])
     come0 = swap(send0, sizes, *plan.term_masks[0])
-    send1 = run("send1", part(send_kernel, plan, True), shape, b16, [after(acts, send0), grads])
+    keep0 = run("keep0", part(keep_kernel, plan, False), shape, f32, [after(acts, send0), grads])
+    send1 = run("send1", part(send_kernel, plan, True), shape, b16, [after(acts, keep0), grads])
     come1 = swap(send1, sizes, *plan.term_masks[0])
-    keep0 = run("keep0", part(keep_kernel, plan, False), shape, f32, [after(acts, send1), grads])
     send = run("turn0", part(turn_kernel, plan, False), shape, b16, [keep0, come0])
     come = swap(send, sizes, *plan.term_masks[1])
     keep1 = run("keep1", part(keep_kernel, plan, True), shape, f32, [after(acts, send), grads])

time: 41.7 us -> 40.7 us (0.976)
  local copies, waits for them, and re-layouts: 0.01 us -> 1.04 us
  Pallas kernels: 11.3 us -> 10.3 us
  starting transfers between devices: 19.7 us -> 18.9 us
    unnamed x4 -> x6, local copies, waits for them, and re-layouts: 0.01 us -> 1.04 us
    pallas_call x18 -> x19, Pallas kernels: 11.3 us -> 10.3 us  [call(): pl.pallas_call(kernel, out_shape=out_shape, in_specs=[pl.BlockSpec(memory...]
    ppermute x14, starting transfers between devices: 19.7 us -> 18.9 us  [swap(): return lax.ppermute(value, AXES, pairs)]
  transfers between devices with their start and end apart: 14 -> 14, of which waited for: 6 -> 7; matrix products, arithmetic and copies ran while one was open for 0% -> 0% of each run, Pallas kernels for 22% -> 23%
where the time goes in v7:
time: 40.7 us; the launch traced here: 40.5 us
  starting transfers between devices  18.9 us (46%)
  Pallas kernels  10.3 us (25%)
  waiting for transfers between devices  9.38 us (23%)
  local copies, waits for them, and re-layouts  1.04 us (3%)
  between operations  0.81 us (2%)
    ppermute x14, starting transfers between devices, swap(): return lax.ppermute(value, AXES, pairs)  18.9 us
    pallas_call x19, Pallas kernels, call(): pl.pallas_call(kernel, out_shape=out_shape, in_specs=[pl.BlockSpec(memory...  10.3 us
    ppermute x14, waiting for transfers between devices, swap(): return lax.ppermute(value, AXES, pairs)  9.38 us
    unnamed x6, local copies, waits for them, and re-layouts  1.04 us
  transfers between devices with their start and end apart: 14, of which 7 were waited for; matrix products, arithmetic and copies ran while one was open for 0% of the time, Pallas kernels for 23%

profile of v7, /device:TPU:0, one launch (start us, length us, event | category | flops | bytes accessed | tf_op | source)
XLA Modules:
  0.0 40.5 jit_solution(12643268992703642659)
XLA Ops:
  0.6 0.0 copy-start
  0.6 0.5 %collective-permute-start.2 = (bf16[1,6,320,128]{3,2,1,0:T(8,128)(2,1)}, bf16[1,6,320,128]{3,2,1,0:T(8,128)(2,1)S(1)}, u32[]{:S(2)}, u32[]{:S(2)}) collective-permute-start(bf16[1,6,320,128]{3,2,1,0:T(8,128)(2,1)} %bitcast.11), channel_id=1, source_target_pairs={{0,2},{1,3},{2,0},{3,1},{4,6},{5,7},{6,4},{7,5},{8,10},{9,11},{10,... | collective-permute-start | bytes 1474568 | tf_op jit(solution)/shard_map/ppermute | solution.py:55
  1.2 0.0 copy-start.1
  1.2 1.0 %copy-done.1 = bf16[1,320,6,128]{3,1,2,0:T(8,128)(2,1)S(1)} copy-done((bf16[1,320,6,128]{3,1,2,0:T(8,128)(2,1)S(1)}, bf16[1,320,6,128]{3,1,2,0:T(8,128)(2,1)}, u32[]{:S(2)}) %copy-start.1) | copy-done | bytes 491544
  2.2 0.0 copy-start.2
  2.2 0.1 edge.1
  2.3 2.7 %collective-permute-start.4 = (bf16[1,320,128]{2,1,0:T(8,128)(2,1)S(1)}, bf16[1,320,128]{2,1,0:T(8,128)(2,1)S(1)}, u32[]{:S(2)}, u32[]{:S(2)}) collective-permute-start(bf16[1,320,128]{2,1,0:T(8,128)(2,1)S(1)} %get-tuple-element.20), channel_id=1, source_target_pairs={{0,3},{1,2},{2,1},{3,0},{4,7},{5,6},{6,5},{7,4},{8,11},{9,10},{10,... | collective-permute-start | bytes 245768 | tf_op jit(solution)/shard_map/ppermute | solution.py:55
  4.9 0.0 collective-permute-start.3
  5.0 0.0 copy-done
  5.0 0.2 collective-permute-start.1
  5.1 0.0 copy-done.2
  5.1 0.1 pack.1
  5.2 3.0 %collective-permute-start = (bf16[1,60,512]{2,1,0:T(8,128)(2,1)S(1)}, bf16[1,60,512]{2,1,0:T(8,128)(2,1)S(1)}, u32[]{:S(2)}, u32[]{:S(2)}) collective-permute-start(bf16[1,60,512]{2,1,0:T(8,128)(2,1)S(1)} %bitcast.14), channel_id=1, source_target_pairs={{0,16},{1,17},{2,18},{3,19},{4,20},{5,21},{6,22},{7,23},{8,24},{9,... | collective-permute-start | bytes 184328 | tf_op jit(solution)/shard_map/ppermute | solution.py:55
  8.2 0.0 collective-permute-done.1.act1
  8.2 0.6 %acts.1 = bf16[2,240,1536]{2,1,0:T(8,128)(2,1)S(1)} custom-call(bf16[1,6,320,128]{3,2,1,0:T(8,128)(2,1)S(1)} %bitcast.10, bf16[1,6,320,128]{3,2,1,0:T(8,128)(2,1)S(1)} %collective-permute-done.1.act1), custom_call_target="tpu_custom_call" | custom-call | flops 690000000 | tf_op jit(solution)/shard_map/acts/pallas_call | solution.py:59
  8.8 0.0 collective-permute-done.4.top1.bottom1
  8.8 0.8 %collective-permute-done.3.top0.bottom0 = bf16[1,320,128]{2,1,0:T(8,128)(2,1)S(1)} collective-permute-done((bf16[1,320,128]{2,1,0:T(8,128)(2,1)S(1)}, bf16[1,320,128]{2,1,0:T(8,128)(2,1)S(1)}, u32[]{:S(2)}, u32[]{:S(2)}) %collective-permute-start.3) | collective-permute-done | bytes 81952 | tf_op jit(solution)/shard_map/ppermute | solution.py:55
  9.7 0.0 collective-permute-done.2.grad1
  9.7 0.5 %grads.1 = bf16[2,512,1536]{2,1,0:T(8,128)(2,1)S(1)} custom-call(bf16[1,6,320,128]{3,2,1,0:T(8,128)(2,1)S(1)} %get-tuple-element.19.grad0, bf16[1,6,320,128]{3,2,1,0:T(8,128)(2,1)S(1)} %collective-permute-done.2.grad1, bf16[1,320,128]{2,1,0:T(8,128)(2,1)S(1)} %collective-permute-done.3.top0.bottom0, ...), custom_call_target="tpu_custom_call" | custom-call | flops 575000000 | tf_op jit(solution)/shard_map/grads/pallas_call | solution.py:59
  10.1 0.9 %send0.1 = bf16[2,120,512]{2,1,0:T(8,128)(2,1)S(1)} custom-call(bf16[2,240,1536]{2,1,0:T(8,128)(2,1)S(1)} %acts.1, bf16[2,512,1536]{2,1,0:T(8,128)(2,1)S(1)} %grads.1), custom_call_target="tpu_custom_call" | custom-call | flops 1610000000 | tf_op jit(solution)/shard_map/send0/pallas_call | solution.py:59
  11.1 1.7 %collective-permute-start.6 = (bf16[2,120,512]{2,1,0:T(8,128)(2,1)S(1)}, bf16[2,120,512]{2,1,0:T(8,128)(2,1)S(1)}, u32[]{:S(2)}, u32[]{:S(2)}) collective-permute-start(bf16[2,120,512]{2,1,0:T(8,128)(2,1)S(1)} %send0.1), channel_id=1, source_target_pairs={{0,1},{1,0},{2,10},{3,11},{4,5},{5,4},{6,14},{7,15},{8,9},{9,8},{1... | collective-permute-start | bytes 737288 | tf_op jit(solution)/shard_map/ppermute | solution.py:55
  12.8 0.6 %keep0.1.keep = f32[2,120,512]{2,1,0:T(8,128)S(1)} custom-call(bf16[2,240,1536]{2,1,0:T(8,128)(2,1)S(1)} %acts.1, bf16[2,512,1536]{2,1,0:T(8,128)(2,1)S(1)} %grads.1), custom_call_target="tpu_custom_call" | custom-call | flops 1150000000 | tf_op jit(solution)/shard_map/keep0/pallas_call | solution.py:59
  13.4 0.0 collective-permute-done.refs_1_
  13.5 1.6 %collective-permute-start.5 = (bf16[1,120,512]{2,1,0:T(8,128)(2,1)S(1)}, bf16[1,120,512]{2,1,0:T(8,128)(2,1)S(1)}, u32[]{:S(2)}, u32[]{:S(2)}) collective-permute-start(bf16[1,120,512]{2,1,0:T(8,128)(2,1)S(1)} %pair.1), channel_id=1, source_target_pairs={{0,4},{1,5},{2,3},{3,2},{4,0},{5,1},{6,7},{7,6},{8,12},{9,13},{10,... | collective-permute-start | bytes 368648 | tf_op jit(solution)/shard_map/ppermute | solution.py:55
  15.0 0.9 %send1.1 = bf16[2,120,512]{2,1,0:T(8,128)(2,1)S(1)} custom-call(bf16[2,240,1536]{2,1,0:T(8,128)(2,1)S(1)} %acts.1, bf16[2,512,1536]{2,1,0:T(8,128)(2,1)S(1)} %grads.1), custom_call_target="tpu_custom_call" | custom-call | flops 1610000000 | tf_op jit(solution)/shard_map/send1/pallas_call | solution.py:59
  15.9 0.6 %collective-permute-start.8 = (bf16[2,120,512]{2,1,0:T(8,128)(2,1)S(1)}, bf16[2,120,512]{2,1,0:T(8,128)(2,1)S(1)}, u32[]{:S(2)}, u32[]{:S(2)}) collective-permute-start(bf16[2,120,512]{2,1,0:T(8,128)(2,1)S(1)} %send1.1), channel_id=1, source_target_pairs={{0,1},{1,0},{2,10},{3,11},{4,5},{5,4},{6,14},{7,15},{8,9},{9,8},{1... | collective-permute-start | bytes 737288 | tf_op jit(solution)/shard_map/ppermute | solution.py:55
  16.6 2.1 %collective-permute-done.6.message = bf16[2,120,512]{2,1,0:T(8,128)(2,1)S(1)} collective-permute-done((bf16[2,120,512]{2,1,0:T(8,128)(2,1)S(1)}, bf16[2,120,512]{2,1,0:T(8,128)(2,1)S(1)}, u32[]{:S(2)}, u32[]{:S(2)}) %collective-permute-start.6) | collective-permute-done | bytes 245792 | tf_op jit(solution)/shard_map/ppermute | solution.py:55
  18.7 0.7 %turn0.1 = bf16[2,120,512]{2,1,0:T(8,128)(2,1)S(1)} custom-call(f32[2,120,512]{2,1,0:T(8,128)S(1)} %keep0.1.keep, bf16[2,120,512]{2,1,0:T(8,128)(2,1)S(1)} %collective-permute-done.6.message), custom_call_target="tpu_custom_call" | custom-call | flops 1035000000 | tf_op jit(solution)/shard_map/turn0/pallas_call | solution.py:59
  19.3 1.8 %collective-permute-start.9 = (bf16[2,120,512]{2,1,0:T(8,128)(2,1)S(1)}, bf16[2,120,512]{2,1,0:T(8,128)(2,1)S(1)}, u32[]{:S(2)}, u32[]{:S(2)}) collective-permute-start(bf16[2,120,512]{2,1,0:T(8,128)(2,1)S(1)} %turn0.1), channel_id=1, source_target_pairs={{0,4},{1,5},{2,3},{3,2},{4,0},{5,1},{6,7},{7,6},{8,12},{9,13},{10,... | collective-permute-start | bytes 737288 | tf_op jit(solution)/shard_map/ppermute | solution.py:55
  21.1 0.0 collective-permute-done.5
  21.1 1.1 %collective-permute-start.7 = (bf16[2,120,512]{2,1,0:T(8,128)(2,1)S(1)}, bf16[2,120,512]{2,1,0:T(8,128)(2,1)S(1)}, u32[]{:S(2)}, u32[]{:S(2)}) collective-permute-start(bf16[2,120,512]{2,1,0:T(8,128)(2,1)S(1)} %pad_maximum_fusion.1), channel_id=1, source_target_pairs={{0,8},{1,9},{2,10},{3,11},{4,12},{5,13},{6,14},{7,15},{8,0},{9,1},... | collective-permute-start | bytes 737288 | tf_op jit(solution)/shard_map/ppermute | solution.py:55
  22.3 0.6 %keep1.1.keep = f32[2,120,512]{2,1,0:T(8,128)S(1)} custom-call(bf16[2,240,1536]{2,1,0:T(8,128)(2,1)S(1)} %acts.1, bf16[2,512,1536]{2,1,0:T(8,128)(2,1)S(1)} %grads.1), custom_call_target="tpu_custom_call" | custom-call | flops 1150000000 | tf_op jit(solution)/shard_map/keep1/pallas_call | solution.py:59
  22.9 1.8 %collective-permute-done.8.message = bf16[2,120,512]{2,1,0:T(8,128)(2,1)S(1)} collective-permute-done((bf16[2,120,512]{2,1,0:T(8,128)(2,1)S(1)}, bf16[2,120,512]{2,1,0:T(8,128)(2,1)S(1)}, u32[]{:S(2)}, u32[]{:S(2)}) %collective-permute-start.8) | collective-permute-done | bytes 245792 | tf_op jit(solution)/shard_map/ppermute | solution.py:55
  24.7 0.3 turn1.1.keep
  25.0 0.6 %collective-permute-done.9.message = bf16[2,120,512]{2,1,0:T(8,128)(2,1)S(1)} collective-permute-done((bf16[2,120,512]{2,1,0:T(8,128)(2,1)S(1)}, bf16[2,120,512]{2,1,0:T(8,128)(2,1)S(1)}, u32[]{:S(2)}, u32[]{:S(2)}) %collective-permute-start.9) | collective-permute-done | bytes 245792 | tf_op jit(solution)/shard_map/ppermute | solution.py:55
  25.6 0.4 part0.1
  26.0 1.2 %collective-permute-start.10 = (bf16[120,512]{1,0:T(8,128)(2,1)S(1)}, bf16[120,512]{1,0:T(8,128)(2,1)S(1)}, u32[]{:S(2)}, u32[]{:S(2)}) collective-permute-start(bf16[120,512]{1,0:T(8,128)(2,1)S(1)} %part0.1), channel_id=1, source_target_pairs={{0,8},{1,9},{2,6},{3,7},{4,12},{5,13},{6,2},{7,3},{8,0},{9,1},{10,... | collective-permute-start | bytes 368648 | tf_op jit(solution)/shard_map/ppermute | solution.py:55
  27.2 0.2 collective-permute-done.7
  27.5 1.6 %collective-permute-start.11 = (bf16[4,120,512]{2,1,0:T(8,128)(2,1)S(1)}, bf16[4,120,512]{2,1,0:T(8,128)(2,1)S(1)}, u32[]{:S(2)}, u32[]{:S(2)}) collective-permute-start(bf16[4,120,512]{2,1,0:T(8,128)(2,1)S(1)} %pad_maximum_fusion.own), channel_id=1, source_target_pairs={{0,1},{1,0},{2,6},{3,7},{4,5},{5,4},{6,2},{7,3},{8,9},{9,8},{10,14... | collective-permute-start | bytes 1474568 | tf_op jit(solution)/shard_map/ppermute | solution.py:55
  29.0 0.2 part1.1.keep
  29.2 1.8 %collective-permute-done.10.message = bf16[120,512]{1,0:T(8,128)(2,1)S(1)} collective-permute-done((bf16[120,512]{1,0:T(8,128)(2,1)S(1)}, bf16[120,512]{1,0:T(8,128)(2,1)S(1)}, u32[]{:S(2)}, u32[]{:S(2)}) %collective-permute-start.10) | collective-permute-done | bytes 122912 | tf_op jit(solution)/shard_map/ppermute | solution.py:55
  30.9 0.4 halve0.1
  31.3 2.8 %collective-permute-start.13 = (bf16[60,512]{1,0:T(8,128)(2,1)S(1)}, bf16[60,512]{1,0:T(8,128)(2,1)S(1)}, u32[]{:S(2)}, u32[]{:S(2)}) collective-permute-start(bf16[60,512]{1,0:T(8,128)(2,1)S(1)} %halve0.1), channel_id=1, source_target_pairs={{0,16},{1,17},{2,18},{3,19},{4,20},{5,21},{6,22},{7,23},{8,24},{9,... | collective-permute-start | bytes 184328 | tf_op jit(solution)/shard_map/ppermute | solution.py:55
  34.1 0.2 halve1.1.keep
  34.3 2.0 %collective-permute-done.11.other = bf16[4,120,512]{2,1,0:T(8,128)(2,1)S(1)} collective-permute-done((bf16[4,120,512]{2,1,0:T(8,128)(2,1)S(1)}, bf16[4,120,512]{2,1,0:T(8,128)(2,1)S(1)}, u32[]{:S(2)}, u32[]{:S(2)}) %collective-permute-start.11) | collective-permute-done | bytes 491552 | tf_op jit(solution)/shard_map/ppermute | solution.py:55
  36.4 1.2 %given.1 = (bf16[1,6,160,128]{3,2,1,0:T(8,128)(2,1)S(1)}, bf16[480,1024]{1,0:T(8,128)(2,1)S(1)}) custom-call(bf16[4,120,512]{2,1,0:T(8,128)(2,1)S(1)} %pad_maximum_fusion.own, bf16[4,120,512]{2,1,0:T(8,128)(2,1)S(1)} %collective-permute-done.11.other, bf16[1024,1536]{1,0:T(8,128)(2,1)S(1)} %bitcast.7), custom_call_target="tpu_custom_call" | custom-call | flops 1380000000 | tf_op jit(solution)/shard_map/given/pallas_call | solution.py:59
  37.6 0.1 collective-permute-start.12
  37.6 0.0 collective-permute-done.13.message
  37.7 0.9 %last.1 = f32[9,20,160]{2,1,0:T(8,128)} custom-call(f32[60,512]{1,0:T(8,128)S(1)} %halve1.1.keep, bf16[60,512]{1,0:T(8,128)(2,1)S(1)} %collective-permute-done.13.message), custom_call_target="tpu_custom_call" | custom-call | flops 9200000000 | tf_op jit(solution)/shard_map/last/pallas_call | solution.py:59
  38.5 1.0 %own.1 = bf16[1,6,160,128]{3,2,1,0:T(8,128)(2,1)S(1)} custom-call(bf16[480,1024]{1,0:T(8,128)(2,1)S(1)} %get-tuple-element.35.left, bf16[1024,1536]{1,0:T(8,128)(2,1)S(1)} %bitcast.8), custom_call_target="tpu_custom_call" | custom-call | flops 805000000 | tf_op jit(solution)/shard_map/own/pallas_call | solution.py:59
  39.6 0.0 collective-permute-done.12.theirs
  39.6 0.9 %weave.1 = bf16[1,6,320,128]{3,2,1,0:T(8,128)(2,1)} custom-call(bf16[1,6,160,128]{3,2,1,0:T(8,128)(2,1)S(1)} %own.1, bf16[1,6,160,128]{3,2,1,0:T(8,128)(2,1)S(1)} %collective-permute-done.12.theirs), custom_call_target="tpu_custom_call" | custom-call | flops 1035000000 | tf_op jit(solution)/shard_map/weave/pallas_call | solution.py:59
  (3 shorter events, 0.1 us)
Async XLA Ops:
  0.6 4.3 %copy-start = (bf16[1,320,6,128]{3,1,2,0:T(8,128)(2,1)S(1)}, bf16[1,320,6,128]{3,1,2,0:T(8,128)(2,1)}, u32[]{:S(2)}) copy-start(bf16[1,320,6,128]{3,1,2,0:T(8,128)(2,1)} %param.3) | copy-start | bytes 1474564
  0.6 9.0 %collective-permute-start.2 = (bf16[1,6,320,128]{3,2,1,0:T(8,128)(2,1)}, bf16[1,6,320,128]{3,2,1,0:T(8,128)(2,1)S(1)}, u32[]{:S(2)}, u32[]{:S(2)}) collective-permute-start(bf16[1,6,320,128]{3,2,1,0:T(8,128)(2,1)} %bitcast.11), channel_id=1, source_target_pairs={{0,2},{1,3},{2,0},{3,1},{4,6},{5,7},{6,4},{7,5},{8,10},{9,11},{10,... | collective-permute-start | bytes 1474568 | tf_op jit(solution)/shard_map/ppermute | solution.py:55
  1.2 1.0 %copy-start.1 = (bf16[1,320,6,128]{3,1,2,0:T(8,128)(2,1)S(1)}, bf16[1,320,6,128]{3,1,2,0:T(8,128)(2,1)}, u32[]{:S(2)}) copy-start(bf16[1,320,6,128]{3,1,2,0:T(8,128)(2,1)} %param.4) | copy-start | bytes 1474564
  2.2 2.9 %copy-start.2 = (bf16[20,9,160]{2,0,1:T(8,128)(2,1)S(1)}, bf16[20,9,160]{2,0,1:T(8,128)(2,1)}, u32[]{:S(2)}) copy-start(bf16[20,9,160]{2,0,1:T(8,128)(2,1)} %param.5) | copy-start | bytes 172804
  2.3 6.6 %collective-permute-start.4 = (bf16[1,320,128]{2,1,0:T(8,128)(2,1)S(1)}, bf16[1,320,128]{2,1,0:T(8,128)(2,1)S(1)}, u32[]{:S(2)}, u32[]{:S(2)}) collective-permute-start(bf16[1,320,128]{2,1,0:T(8,128)(2,1)S(1)} %get-tuple-element.20), channel_id=1, source_target_pairs={{0,3},{1,2},{2,1},{3,0},{4,7},{5,6},{6,5},{7,4},{8,11},{9,10},{10,... | collective-permute-start | bytes 245768 | tf_op jit(solution)/shard_map/ppermute | solution.py:55
  4.9 4.8 %collective-permute-start.3 = (bf16[1,320,128]{2,1,0:T(8,128)(2,1)S(1)}, bf16[1,320,128]{2,1,0:T(8,128)(2,1)S(1)}, u32[]{:S(2)}, u32[]{:S(2)}) collective-permute-start(bf16[1,320,128]{2,1,0:T(8,128)(2,1)S(1)} %get-tuple-element.20), channel_id=1, source_target_pairs={{0,1},{1,0},{2,3},{3,2},{4,5},{5,4},{6,7},{7,6},{8,9},{9,8},{10,11... | collective-permute-start | bytes 245768 | tf_op jit(solution)/shard_map/ppermute | solution.py:55
  5.0 3.3 %collective-permute-start.1 = (bf16[1,6,320,128]{3,2,1,0:T(8,128)(2,1)S(1)}, bf16[1,6,320,128]{3,2,1,0:T(8,128)(2,1)S(1)}, u32[]{:S(2)}, u32[]{:S(2)}) collective-permute-start(bf16[1,6,320,128]{3,2,1,0:T(8,128)(2,1)S(1)} %bitcast.9), channel_id=1, source_target_pairs={{0,2},{1,3},{2,0},{3,1},{4,6},{5,7},{6,4},{7,5},{8,10},{9,11},{10,... | collective-permute-start | bytes 1474568 | tf_op jit(solution)/shard_map/ppermute | solution.py:55
  5.2 8.2 %collective-permute-start = (bf16[1,60,512]{2,1,0:T(8,128)(2,1)S(1)}, bf16[1,60,512]{2,1,0:T(8,128)(2,1)S(1)}, u32[]{:S(2)}, u32[]{:S(2)}) collective-permute-start(bf16[1,60,512]{2,1,0:T(8,128)(2,1)S(1)} %bitcast.14), channel_id=1, source_target_pairs={{0,16},{1,17},{2,18},{3,19},{4,20},{5,21},{6,22},{7,23},{8,24},{9,... | collective-permute-start | bytes 184328 | tf_op jit(solution)/shard_map/ppermute | solution.py:55
  11.1 7.6 %collective-permute-start.6 = (bf16[2,120,512]{2,1,0:T(8,128)(2,1)S(1)}, bf16[2,120,512]{2,1,0:T(8,128)(2,1)S(1)}, u32[]{:S(2)}, u32[]{:S(2)}) collective-permute-start(bf16[2,120,512]{2,1,0:T(8,128)(2,1)S(1)} %send0.1), channel_id=1, source_target_pairs={{0,1},{1,0},{2,10},{3,11},{4,5},{5,4},{6,14},{7,15},{8,9},{9,8},{1... | collective-permute-start | bytes 737288 | tf_op jit(solution)/shard_map/ppermute | solution.py:55
  13.5 7.6 %collective-permute-start.5 = (bf16[1,120,512]{2,1,0:T(8,128)(2,1)S(1)}, bf16[1,120,512]{2,1,0:T(8,128)(2,1)S(1)}, u32[]{:S(2)}, u32[]{:S(2)}) collective-permute-start(bf16[1,120,512]{2,1,0:T(8,128)(2,1)S(1)} %pair.1), channel_id=1, source_target_pairs={{0,4},{1,5},{2,3},{3,2},{4,0},{5,1},{6,7},{7,6},{8,12},{9,13},{10,... | collective-permute-start | bytes 368648 | tf_op jit(solution)/shard_map/ppermute | solution.py:55
  15.9 8.7 %collective-permute-start.8 = (bf16[2,120,512]{2,1,0:T(8,128)(2,1)S(1)}, bf16[2,120,512]{2,1,0:T(8,128)(2,1)S(1)}, u32[]{:S(2)}, u32[]{:S(2)}) collective-permute-start(bf16[2,120,512]{2,1,0:T(8,128)(2,1)S(1)} %send1.1), channel_id=1, source_target_pairs={{0,1},{1,0},{2,10},{3,11},{4,5},{5,4},{6,14},{7,15},{8,9},{9,8},{1... | collective-permute-start | bytes 737288 | tf_op jit(solution)/shard_map/ppermute | solution.py:55
  19.3 6.3 %collective-permute-start.9 = (bf16[2,120,512]{2,1,0:T(8,128)(2,1)S(1)}, bf16[2,120,512]{2,1,0:T(8,128)(2,1)S(1)}, u32[]{:S(2)}, u32[]{:S(2)}) collective-permute-start(bf16[2,120,512]{2,1,0:T(8,128)(2,1)S(1)} %turn0.1), channel_id=1, source_target_pairs={{0,4},{1,5},{2,3},{3,2},{4,0},{5,1},{6,7},{7,6},{8,12},{9,13},{10,... | collective-permute-start | bytes 737288 | tf_op jit(solution)/shard_map/ppermute | solution.py:55
  21.1 6.3 %collective-permute-start.7 = (bf16[2,120,512]{2,1,0:T(8,128)(2,1)S(1)}, bf16[2,120,512]{2,1,0:T(8,128)(2,1)S(1)}, u32[]{:S(2)}, u32[]{:S(2)}) collective-permute-start(bf16[2,120,512]{2,1,0:T(8,128)(2,1)S(1)} %pad_maximum_fusion.1), channel_id=1, source_target_pairs={{0,8},{1,9},{2,10},{3,11},{4,12},{5,13},{6,14},{7,15},{8,0},{9,1},... | collective-permute-start | bytes 737288 | tf_op jit(solution)/shard_map/ppermute | solution.py:55
  26.0 4.9 %collective-permute-start.10 = (bf16[120,512]{1,0:T(8,128)(2,1)S(1)}, bf16[120,512]{1,0:T(8,128)(2,1)S(1)}, u32[]{:S(2)}, u32[]{:S(2)}) collective-permute-start(bf16[120,512]{1,0:T(8,128)(2,1)S(1)} %part0.1), channel_id=1, source_target_pairs={{0,8},{1,9},{2,6},{3,7},{4,12},{5,13},{6,2},{7,3},{8,0},{9,1},{10,... | collective-permute-start | bytes 368648 | tf_op jit(solution)/shard_map/ppermute | solution.py:55
  27.5 8.9 %collective-permute-start.11 = (bf16[4,120,512]{2,1,0:T(8,128)(2,1)S(1)}, bf16[4,120,512]{2,1,0:T(8,128)(2,1)S(1)}, u32[]{:S(2)}, u32[]{:S(2)}) collective-permute-start(bf16[4,120,512]{2,1,0:T(8,128)(2,1)S(1)} %pad_maximum_fusion.own), channel_id=1, source_target_pairs={{0,1},{1,0},{2,6},{3,7},{4,5},{5,4},{6,2},{7,3},{8,9},{9,8},{10,14... | collective-permute-start | bytes 1474568 | tf_op jit(solution)/shard_map/ppermute | solution.py:55
  31.3 6.4 %collective-permute-start.13 = (bf16[60,512]{1,0:T(8,128)(2,1)S(1)}, bf16[60,512]{1,0:T(8,128)(2,1)S(1)}, u32[]{:S(2)}, u32[]{:S(2)}) collective-permute-start(bf16[60,512]{1,0:T(8,128)(2,1)S(1)} %halve0.1), channel_id=1, source_target_pairs={{0,16},{1,17},{2,18},{3,19},{4,20},{5,21},{6,22},{7,23},{8,24},{9,... | collective-permute-start | bytes 184328 | tf_op jit(solution)/shard_map/ppermute | solution.py:55
  37.6 2.0 %collective-permute-start.12 = (bf16[1,6,160,128]{3,2,1,0:T(8,128)(2,1)S(1)}, bf16[1,6,160,128]{3,2,1,0:T(8,128)(2,1)S(1)}, u32[]{:S(2)}, u32[]{:S(2)}) collective-permute-start(bf16[1,6,160,128]{3,2,1,0:T(8,128)(2,1)S(1)} %get-tuple-element.34), channel_id=1, source_target_pairs={{0,2},{1,3},{2,0},{3,1},{4,6},{5,7},{6,4},{7,5},{8,10},{9,11},{10,... | collective-permute-start | bytes 737288 | tf_op jit(solution)/shard_map/ppermute | solution.py:55

commit v8 on v7

--- a/solution.py
+++ b/solution.py
@@ -119,7 +119,7 @@
         self.cells = 2 * images * rows * width
         by_row, by_next, by_col = (2, 0), (4, 0), (0, self.top_strip)
         self.term_masks = ((by_col, by_next), (by_row, by_col), (by_next, by_row))
-        self.gather_masks = ((by_row, by_col), (by_next, by_next), (by_col, by_row))
+        self.gather_masks = ((by_row, by_row), (by_col, by_next), (by_next, by_col))
 
     def block_of(self, slot, by_next, by_row):
         bits = self.band_bits - 3
@@ -283,9 +283,9 @@
         rows = [[] for _ in TAP_STEPS]
         for m in range(plan.blocks):
             row, behind, col = (m % 2) ^ row_bit, (m // 2 % 2) ^ next_bit, x ^ col_bit
-            one = jnp.where(core == 0, row, col)
-            three = jnp.where(core == 0, col, row)
-            slot = behind * 2 + one
+            two = jnp.where(core == 0, col, behind)
+            three = jnp.where(core == 0, behind, col)
+            slot = two * 2 + row
             pair = jnp.where(three == 0, own[slot], other[slot]).astype(jnp.float32)
             block = pair[: plan.block_rows]
             for k in range(1, plan.inner):

time: 40.7 us -> 42 us (1.032)
  starting transfers between devices: 18.9 us -> 20.1 us
    ppermute x14, starting transfers between devices: 18.9 us -> 20.1 us  [swap(): return lax.ppermute(value, AXES, pairs)]
  transfers between devices with their start and end apart: 14 -> 14, of which waited for: 7 -> 6; matrix products, arithmetic and copies ran while one was open for 0% -> 0% of each run, Pallas kernels for 23% -> 23%
where the time goes in v8:
time: 42 us; the launch traced here: 41.9 us
  starting transfers between devices  20.1 us (48%)
  Pallas kernels  10.4 us (25%)
  waiting for transfers between devices  9.43 us (22%)
  local copies, waits for them, and re-layouts  1.04 us (2%)
  between operations  0.82 us (2%)
    ppermute x14, starting transfers between devices, swap(): return lax.ppermute(value, AXES, pairs)  20.1 us
    pallas_call x19, Pallas kernels, call(): pl.pallas_call(kernel, out_shape=out_shape, in_specs=[pl.BlockSpec(memory...  10.4 us
    ppermute x14, waiting for transfers between devices, swap(): return lax.ppermute(value, AXES, pairs)  9.43 us
    unnamed x6, local copies, waits for them, and re-layouts  1.04 us
  transfers between devices with their start and end apart: 14, of which 6 were waited for; matrix products, arithmetic and copies ran while one was open for 0% of the time, Pallas kernels for 23%

profile of v8, /device:TPU:0, one launch (start us, length us, event | category | flops | bytes accessed | tf_op | source)
XLA Modules:
  0.0 41.9 jit_solution(7484686468559751157)
XLA Ops:
  0.6 0.0 copy-start
  0.6 0.5 %collective-permute-start.2 = (bf16[1,6,320,128]{3,2,1,0:T(8,128)(2,1)}, bf16[1,6,320,128]{3,2,1,0:T(8,128)(2,1)S(1)}, u32[]{:S(2)}, u32[]{:S(2)}) collective-permute-start(bf16[1,6,320,128]{3,2,1,0:T(8,128)(2,1)} %bitcast.11), channel_id=1, source_target_pairs={{0,2},{1,3},{2,0},{3,1},{4,6},{5,7},{6,4},{7,5},{8,10},{9,11},{10,... | collective-permute-start | bytes 1474568 | tf_op jit(solution)/shard_map/ppermute | solution.py:55
  1.2 0.0 copy-start.1
  1.2 1.0 %copy-done.1 = bf16[1,320,6,128]{3,1,2,0:T(8,128)(2,1)S(1)} copy-done((bf16[1,320,6,128]{3,1,2,0:T(8,128)(2,1)S(1)}, bf16[1,320,6,128]{3,1,2,0:T(8,128)(2,1)}, u32[]{:S(2)}) %copy-start.1) | copy-done | bytes 491544
  2.2 0.0 copy-start.2
  2.2 0.1 edge.1
  2.3 2.7 %collective-permute-start.4 = (bf16[1,320,128]{2,1,0:T(8,128)(2,1)S(1)}, bf16[1,320,128]{2,1,0:T(8,128)(2,1)S(1)}, u32[]{:S(2)}, u32[]{:S(2)}) collective-permute-start(bf16[1,320,128]{2,1,0:T(8,128)(2,1)S(1)} %get-tuple-element.20), channel_id=1, source_target_pairs={{0,3},{1,2},{2,1},{3,0},{4,7},{5,6},{6,5},{7,4},{8,11},{9,10},{10,... | collective-permute-start | bytes 245768 | tf_op jit(solution)/shard_map/ppermute | solution.py:55
  4.9 0.0 collective-permute-start.3
  5.0 0.0 copy-done
  5.0 0.2 collective-permute-start.1
  5.1 0.0 copy-done.2
  5.1 0.1 pack.1
  5.2 3.0 %collective-permute-start = (bf16[1,60,512]{2,1,0:T(8,128)(2,1)S(1)}, bf16[1,60,512]{2,1,0:T(8,128)(2,1)S(1)}, u32[]{:S(2)}, u32[]{:S(2)}) collective-permute-start(bf16[1,60,512]{2,1,0:T(8,128)(2,1)S(1)} %bitcast.14), channel_id=1, source_target_pairs={{0,16},{1,17},{2,18},{3,19},{4,20},{5,21},{6,22},{7,23},{8,24},{9,... | collective-permute-start | bytes 184328 | tf_op jit(solution)/shard_map/ppermute | solution.py:55
  8.2 0.0 collective-permute-done.1.act1
  8.2 0.6 %acts.1 = bf16[2,240,1536]{2,1,0:T(8,128)(2,1)S(1)} custom-call(bf16[1,6,320,128]{3,2,1,0:T(8,128)(2,1)S(1)} %bitcast.10, bf16[1,6,320,128]{3,2,1,0:T(8,128)(2,1)S(1)} %collective-permute-done.1.act1), custom_call_target="tpu_custom_call" | custom-call | flops 690000000 | tf_op jit(solution)/shard_map/acts/pallas_call | solution.py:59
  8.8 0.0 collective-permute-done.4.top1.bottom1
  8.8 0.8 %collective-permute-done.3.top0.bottom0 = bf16[1,320,128]{2,1,0:T(8,128)(2,1)S(1)} collective-permute-done((bf16[1,320,128]{2,1,0:T(8,128)(2,1)S(1)}, bf16[1,320,128]{2,1,0:T(8,128)(2,1)S(1)}, u32[]{:S(2)}, u32[]{:S(2)}) %collective-permute-start.3) | collective-permute-done | bytes 81952 | tf_op jit(solution)/shard_map/ppermute | solution.py:55
  9.7 0.0 collective-permute-done.2.grad1
  9.7 0.5 %grads.1 = bf16[2,512,1536]{2,1,0:T(8,128)(2,1)S(1)} custom-call(bf16[1,6,320,128]{3,2,1,0:T(8,128)(2,1)S(1)} %get-tuple-element.19.grad0, bf16[1,6,320,128]{3,2,1,0:T(8,128)(2,1)S(1)} %collective-permute-done.2.grad1, bf16[1,320,128]{2,1,0:T(8,128)(2,1)S(1)} %collective-permute-done.3.top0.bottom0, ...), custom_call_target="tpu_custom_call" | custom-call | flops 575000000 | tf_op jit(solution)/shard_map/grads/pallas_call | solution.py:59
  10.1 0.9 %send0.1 = bf16[2,120,512]{2,1,0:T(8,128)(2,1)S(1)} custom-call(bf16[2,240,1536]{2,1,0:T(8,128)(2,1)S(1)} %acts.1, bf16[2,512,1536]{2,1,0:T(8,128)(2,1)S(1)} %grads.1), custom_call_target="tpu_custom_call" | custom-call | flops 1610000000 | tf_op jit(solution)/shard_map/send0/pallas_call | solution.py:59
  11.1 1.7 %collective-permute-start.6 = (bf16[2,120,512]{2,1,0:T(8,128)(2,1)S(1)}, bf16[2,120,512]{2,1,0:T(8,128)(2,1)S(1)}, u32[]{:S(2)}, u32[]{:S(2)}) collective-permute-start(bf16[2,120,512]{2,1,0:T(8,128)(2,1)S(1)} %send0.1), channel_id=1, source_target_pairs={{0,1},{1,0},{2,10},{3,11},{4,5},{5,4},{6,14},{7,15},{8,9},{9,8},{1... | collective-permute-start | bytes 737288 | tf_op jit(solution)/shard_map/ppermute | solution.py:55
  12.8 0.6 %keep0.1.keep = f32[2,120,512]{2,1,0:T(8,128)S(1)} custom-call(bf16[2,240,1536]{2,1,0:T(8,128)(2,1)S(1)} %acts.1, bf16[2,512,1536]{2,1,0:T(8,128)(2,1)S(1)} %grads.1), custom_call_target="tpu_custom_call" | custom-call | flops 1150000000 | tf_op jit(solution)/shard_map/keep0/pallas_call | solution.py:59
  13.4 0.0 collective-permute-done.refs_1_
  13.5 1.6 %collective-permute-start.5 = (bf16[1,120,512]{2,1,0:T(8,128)(2,1)S(1)}, bf16[1,120,512]{2,1,0:T(8,128)(2,1)S(1)}, u32[]{:S(2)}, u32[]{:S(2)}) collective-permute-start(bf16[1,120,512]{2,1,0:T(8,128)(2,1)S(1)} %pair.1), channel_id=1, source_target_pairs={{0,4},{1,5},{2,6},{3,7},{4,0},{5,1},{6,2},{7,3},{8,12},{9,13},{10,... | collective-permute-start | bytes 368648 | tf_op jit(solution)/shard_map/ppermute | solution.py:55
  15.0 0.9 %send1.1 = bf16[2,120,512]{2,1,0:T(8,128)(2,1)S(1)} custom-call(bf16[2,240,1536]{2,1,0:T(8,128)(2,1)S(1)} %acts.1, bf16[2,512,1536]{2,1,0:T(8,128)(2,1)S(1)} %grads.1), custom_call_target="tpu_custom_call" | custom-call | flops 1610000000 | tf_op jit(solution)/shard_map/send1/pallas_call | solution.py:59
  15.9 0.6 %collective-permute-start.8 = (bf16[2,120,512]{2,1,0:T(8,128)(2,1)S(1)}, bf16[2,120,512]{2,1,0:T(8,128)(2,1)S(1)}, u32[]{:S(2)}, u32[]{:S(2)}) collective-permute-start(bf16[2,120,512]{2,1,0:T(8,128)(2,1)S(1)} %send1.1), channel_id=1, source_target_pairs={{0,1},{1,0},{2,10},{3,11},{4,5},{5,4},{6,14},{7,15},{8,9},{9,8},{1... | collective-permute-start | bytes 737288 | tf_op jit(solution)/shard_map/ppermute | solution.py:55
  16.6 0.8 %collective-permute-done.6.message = bf16[2,120,512]{2,1,0:T(8,128)(2,1)S(1)} collective-permute-done((bf16[2,120,512]{2,1,0:T(8,128)(2,1)S(1)}, bf16[2,120,512]{2,1,0:T(8,128)(2,1)S(1)}, u32[]{:S(2)}, u32[]{:S(2)}) %collective-permute-start.6) | collective-permute-done | bytes 245792 | tf_op jit(solution)/shard_map/ppermute | solution.py:55
  17.3 0.7 %turn0.1 = bf16[2,120,512]{2,1,0:T(8,128)(2,1)S(1)} custom-call(f32[2,120,512]{2,1,0:T(8,128)S(1)} %keep0.1.keep, bf16[2,120,512]{2,1,0:T(8,128)(2,1)S(1)} %collective-permute-done.6.message), custom_call_target="tpu_custom_call" | custom-call | flops 1035000000 | tf_op jit(solution)/shard_map/turn0/pallas_call | solution.py:59
  18.0 1.8 %collective-permute-start.9 = (bf16[2,120,512]{2,1,0:T(8,128)(2,1)S(1)}, bf16[2,120,512]{2,1,0:T(8,128)(2,1)S(1)}, u32[]{:S(2)}, u32[]{:S(2)}) collective-permute-start(bf16[2,120,512]{2,1,0:T(8,128)(2,1)S(1)} %turn0.1), channel_id=1, source_target_pairs={{0,4},{1,5},{2,3},{3,2},{4,0},{5,1},{6,7},{7,6},{8,12},{9,13},{10,... | collective-permute-start | bytes 737288 | tf_op jit(solution)/shard_map/ppermute | solution.py:55
  19.8 0.0 collective-permute-done.5
  19.8 1.6 %collective-permute-start.7 = (bf16[2,120,512]{2,1,0:T(8,128)(2,1)S(1)}, bf16[2,120,512]{2,1,0:T(8,128)(2,1)S(1)}, u32[]{:S(2)}, u32[]{:S(2)}) collective-permute-start(bf16[2,120,512]{2,1,0:T(8,128)(2,1)S(1)} %pad_maximum_fusion.1), channel_id=1, source_target_pairs={{0,1},{1,0},{2,10},{3,11},{4,5},{5,4},{6,14},{7,15},{8,9},{9,8},{1... | collective-permute-start | bytes 737288 | tf_op jit(solution)/shard_map/ppermute | solution.py:55
  21.4 0.6 %keep1.1.keep = f32[2,120,512]{2,1,0:T(8,128)S(1)} custom-call(bf16[2,240,1536]{2,1,0:T(8,128)(2,1)S(1)} %acts.1, bf16[2,512,1536]{2,1,0:T(8,128)(2,1)S(1)} %grads.1), custom_call_target="tpu_custom_call" | custom-call | flops 1150000000 | tf_op jit(solution)/shard_map/keep1/pallas_call | solution.py:59
  22.0 2.7 %collective-permute-done.8.message = bf16[2,120,512]{2,1,0:T(8,128)(2,1)S(1)} collective-permute-done((bf16[2,120,512]{2,1,0:T(8,128)(2,1)S(1)}, bf16[2,120,512]{2,1,0:T(8,128)(2,1)S(1)}, u32[]{:S(2)}, u32[]{:S(2)}) %collective-permute-start.8) | collective-permute-done | bytes 245792 | tf_op jit(solution)/shard_map/ppermute | solution.py:55
  24.7 0.3 turn1.1.keep
  25.0 0.0 collective-permute-done.9.message
  25.0 0.4 part0.1
  25.4 1.8 %collective-permute-start.10 = (bf16[120,512]{1,0:T(8,128)(2,1)S(1)}, bf16[120,512]{1,0:T(8,128)(2,1)S(1)}, u32[]{:S(2)}, u32[]{:S(2)}) collective-permute-start(bf16[120,512]{1,0:T(8,128)(2,1)S(1)} %part0.1), channel_id=1, source_target_pairs={{0,8},{1,9},{2,6},{3,7},{4,12},{5,13},{6,2},{7,3},{8,0},{9,1},{10,... | collective-permute-start | bytes 368648 | tf_op jit(solution)/shard_map/ppermute | solution.py:55
  27.2 0.1 collective-permute-done.7
  27.4 1.8 %collective-permute-start.11 = (bf16[4,120,512]{2,1,0:T(8,128)(2,1)S(1)}, bf16[4,120,512]{2,1,0:T(8,128)(2,1)S(1)}, u32[]{:S(2)}, u32[]{:S(2)}) collective-permute-start(bf16[4,120,512]{2,1,0:T(8,128)(2,1)S(1)} %pad_maximum_fusion.own), channel_id=1, source_target_pairs={{0,8},{1,9},{2,3},{3,2},{4,12},{5,13},{6,7},{7,6},{8,0},{9,1},{10,... | collective-permute-start | bytes 1474568 | tf_op jit(solution)/shard_map/ppermute | solution.py:55
  29.2 0.2 part1.1.keep
  29.3 1.0 %collective-permute-done.10.message = bf16[120,512]{1,0:T(8,128)(2,1)S(1)} collective-permute-done((bf16[120,512]{1,0:T(8,128)(2,1)S(1)}, bf16[120,512]{1,0:T(8,128)(2,1)S(1)}, u32[]{:S(2)}, u32[]{:S(2)}) %collective-permute-start.10) | collective-permute-done | bytes 122912 | tf_op jit(solution)/shard_map/ppermute | solution.py:55
  30.3 0.4 halve0.1
  30.7 2.8 %collective-permute-start.13 = (bf16[60,512]{1,0:T(8,128)(2,1)S(1)}, bf16[60,512]{1,0:T(8,128)(2,1)S(1)}, u32[]{:S(2)}, u32[]{:S(2)}) collective-permute-start(bf16[60,512]{1,0:T(8,128)(2,1)S(1)} %halve0.1), channel_id=1, source_target_pairs={{0,16},{1,17},{2,18},{3,19},{4,20},{5,21},{6,22},{7,23},{8,24},{9,... | collective-permute-start | bytes 184328 | tf_op jit(solution)/shard_map/ppermute | solution.py:55
  33.5 0.2 halve1.1.keep
  33.7 4.0 %collective-permute-done.11.other = bf16[4,120,512]{2,1,0:T(8,128)(2,1)S(1)} collective-permute-done((bf16[4,120,512]{2,1,0:T(8,128)(2,1)S(1)}, bf16[4,120,512]{2,1,0:T(8,128)(2,1)S(1)}, u32[]{:S(2)}, u32[]{:S(2)}) %collective-permute-start.11) | collective-permute-done | bytes 491552 | tf_op jit(solution)/shard_map/ppermute | solution.py:55
  37.7 1.2 %given.1 = (bf16[1,6,160,128]{3,2,1,0:T(8,128)(2,1)S(1)}, bf16[480,1024]{1,0:T(8,128)(2,1)S(1)}) custom-call(bf16[4,120,512]{2,1,0:T(8,128)(2,1)S(1)} %pad_maximum_fusion.own, bf16[4,120,512]{2,1,0:T(8,128)(2,1)S(1)} %collective-permute-done.11.other, bf16[1024,1536]{1,0:T(8,128)(2,1)S(1)} %bitcast.7), custom_call_target="tpu_custom_call" | custom-call | flops 1380000000 | tf_op jit(solution)/shard_map/given/pallas_call | solution.py:59
  38.9 0.1 collective-permute-start.12
  39.0 0.0 collective-permute-done.13.message
  39.0 0.9 %last.1 = f32[9,20,160]{2,1,0:T(8,128)} custom-call(f32[60,512]{1,0:T(8,128)S(1)} %halve1.1.keep, bf16[60,512]{1,0:T(8,128)(2,1)S(1)} %collective-permute-done.13.message), custom_call_target="tpu_custom_call" | custom-call | flops 9200000000 | tf_op jit(solution)/shard_map/last/pallas_call | solution.py:59
  39.9 1.0 %own.1 = bf16[1,6,160,128]{3,2,1,0:T(8,128)(2,1)S(1)} custom-call(bf16[480,1024]{1,0:T(8,128)(2,1)S(1)} %get-tuple-element.35.left, bf16[1024,1536]{1,0:T(8,128)(2,1)S(1)} %bitcast.8), custom_call_target="tpu_custom_call" | custom-call | flops 805000000 | tf_op jit(solution)/shard_map/own/pallas_call | solution.py:59
  40.9 0.0 collective-permute-done.12.theirs
  40.9 0.9 %weave.1 = bf16[1,6,320,128]{3,2,1,0:T(8,128)(2,1)} custom-call(bf16[1,6,160,128]{3,2,1,0:T(8,128)(2,1)S(1)} %own.1, bf16[1,6,160,128]{3,2,1,0:T(8,128)(2,1)S(1)} %collective-permute-done.12.theirs), custom_call_target="tpu_custom_call" | custom-call | flops 1035000000 | tf_op jit(solution)/shard_map/weave/pallas_call | solution.py:59
  (3 shorter events, 0.1 us)
Async XLA Ops:
  0.6 4.3 %copy-start = (bf16[1,320,6,128]{3,1,2,0:T(8,128)(2,1)S(1)}, bf16[1,320,6,128]{3,1,2,0:T(8,128)(2,1)}, u32[]{:S(2)}) copy-start(bf16[1,320,6,128]{3,1,2,0:T(8,128)(2,1)} %param.3) | copy-start | bytes 1474564
  0.6 9.0 %collective-permute-start.2 = (bf16[1,6,320,128]{3,2,1,0:T(8,128)(2,1)}, bf16[1,6,320,128]{3,2,1,0:T(8,128)(2,1)S(1)}, u32[]{:S(2)}, u32[]{:S(2)}) collective-permute-start(bf16[1,6,320,128]{3,2,1,0:T(8,128)(2,1)} %bitcast.11), channel_id=1, source_target_pairs={{0,2},{1,3},{2,0},{3,1},{4,6},{5,7},{6,4},{7,5},{8,10},{9,11},{10,... | collective-permute-start | bytes 1474568 | tf_op jit(solution)/shard_map/ppermute | solution.py:55
  1.2 1.0 %copy-start.1 = (bf16[1,320,6,128]{3,1,2,0:T(8,128)(2,1)S(1)}, bf16[1,320,6,128]{3,1,2,0:T(8,128)(2,1)}, u32[]{:S(2)}) copy-start(bf16[1,320,6,128]{3,1,2,0:T(8,128)(2,1)} %param.4) | copy-start | bytes 1474564
  2.2 2.9 %copy-start.2 = (bf16[20,9,160]{2,0,1:T(8,128)(2,1)S(1)}, bf16[20,9,160]{2,0,1:T(8,128)(2,1)}, u32[]{:S(2)}) copy-start(bf16[20,9,160]{2,0,1:T(8,128)(2,1)} %param.5) | copy-start | bytes 172804
  2.3 6.6 %collective-permute-start.4 = (bf16[1,320,128]{2,1,0:T(8,128)(2,1)S(1)}, bf16[1,320,128]{2,1,0:T(8,128)(2,1)S(1)}, u32[]{:S(2)}, u32[]{:S(2)}) collective-permute-start(bf16[1,320,128]{2,1,0:T(8,128)(2,1)S(1)} %get-tuple-element.20), channel_id=1, source_target_pairs={{0,3},{1,2},{2,1},{3,0},{4,7},{5,6},{6,5},{7,4},{8,11},{9,10},{10,... | collective-permute-start | bytes 245768 | tf_op jit(solution)/shard_map/ppermute | solution.py:55
  4.9 4.8 %collective-permute-start.3 = (bf16[1,320,128]{2,1,0:T(8,128)(2,1)S(1)}, bf16[1,320,128]{2,1,0:T(8,128)(2,1)S(1)}, u32[]{:S(2)}, u32[]{:S(2)}) collective-permute-start(bf16[1,320,128]{2,1,0:T(8,128)(2,1)S(1)} %get-tuple-element.20), channel_id=1, source_target_pairs={{0,1},{1,0},{2,3},{3,2},{4,5},{5,4},{6,7},{7,6},{8,9},{9,8},{10,11... | collective-permute-start | bytes 245768 | tf_op jit(solution)/shard_map/ppermute | solution.py:55
  5.0 3.3 %collective-permute-start.1 = (bf16[1,6,320,128]{3,2,1,0:T(8,128)(2,1)S(1)}, bf16[1,6,320,128]{3,2,1,0:T(8,128)(2,1)S(1)}, u32[]{:S(2)}, u32[]{:S(2)}) collective-permute-start(bf16[1,6,320,128]{3,2,1,0:T(8,128)(2,1)S(1)} %bitcast.9), channel_id=1, source_target_pairs={{0,2},{1,3},{2,0},{3,1},{4,6},{5,7},{6,4},{7,5},{8,10},{9,11},{10,... | collective-permute-start | bytes 1474568 | tf_op jit(solution)/shard_map/ppermute | solution.py:55
  5.2 8.2 %collective-permute-start = (bf16[1,60,512]{2,1,0:T(8,128)(2,1)S(1)}, bf16[1,60,512]{2,1,0:T(8,128)(2,1)S(1)}, u32[]{:S(2)}, u32[]{:S(2)}) collective-permute-start(bf16[1,60,512]{2,1,0:T(8,128)(2,1)S(1)} %bitcast.14), channel_id=1, source_target_pairs={{0,16},{1,17},{2,18},{3,19},{4,20},{5,21},{6,22},{7,23},{8,24},{9,... | collective-permute-start | bytes 184328 | tf_op jit(solution)/shard_map/ppermute | solution.py:55
  11.1 6.3 %collective-permute-start.6 = (bf16[2,120,512]{2,1,0:T(8,128)(2,1)S(1)}, bf16[2,120,512]{2,1,0:T(8,128)(2,1)S(1)}, u32[]{:S(2)}, u32[]{:S(2)}) collective-permute-start(bf16[2,120,512]{2,1,0:T(8,128)(2,1)S(1)} %send0.1), channel_id=1, source_target_pairs={{0,1},{1,0},{2,10},{3,11},{4,5},{5,4},{6,14},{7,15},{8,9},{9,8},{1... | collective-permute-start | bytes 737288 | tf_op jit(solution)/shard_map/ppermute | solution.py:55
  13.5 6.3 %collective-permute-start.5 = (bf16[1,120,512]{2,1,0:T(8,128)(2,1)S(1)}, bf16[1,120,512]{2,1,0:T(8,128)(2,1)S(1)}, u32[]{:S(2)}, u32[]{:S(2)}) collective-permute-start(bf16[1,120,512]{2,1,0:T(8,128)(2,1)S(1)} %pair.1), channel_id=1, source_target_pairs={{0,4},{1,5},{2,6},{3,7},{4,0},{5,1},{6,2},{7,3},{8,12},{9,13},{10,... | collective-permute-start | bytes 368648 | tf_op jit(solution)/shard_map/ppermute | solution.py:55
  15.9 8.7 %collective-permute-start.8 = (bf16[2,120,512]{2,1,0:T(8,128)(2,1)S(1)}, bf16[2,120,512]{2,1,0:T(8,128)(2,1)S(1)}, u32[]{:S(2)}, u32[]{:S(2)}) collective-permute-start(bf16[2,120,512]{2,1,0:T(8,128)(2,1)S(1)} %send1.1), channel_id=1, source_target_pairs={{0,1},{1,0},{2,10},{3,11},{4,5},{5,4},{6,14},{7,15},{8,9},{9,8},{1... | collective-permute-start | bytes 737288 | tf_op jit(solution)/shard_map/ppermute | solution.py:55
  18.0 7.0 %collective-permute-start.9 = (bf16[2,120,512]{2,1,0:T(8,128)(2,1)S(1)}, bf16[2,120,512]{2,1,0:T(8,128)(2,1)S(1)}, u32[]{:S(2)}, u32[]{:S(2)}) collective-permute-start(bf16[2,120,512]{2,1,0:T(8,128)(2,1)S(1)} %turn0.1), channel_id=1, source_target_pairs={{0,4},{1,5},{2,3},{3,2},{4,0},{5,1},{6,7},{7,6},{8,12},{9,13},{10,... | collective-permute-start | bytes 737288 | tf_op jit(solution)/shard_map/ppermute | solution.py:55
  19.8 7.5 %collective-permute-start.7 = (bf16[2,120,512]{2,1,0:T(8,128)(2,1)S(1)}, bf16[2,120,512]{2,1,0:T(8,128)(2,1)S(1)}, u32[]{:S(2)}, u32[]{:S(2)}) collective-permute-start(bf16[2,120,512]{2,1,0:T(8,128)(2,1)S(1)} %pad_maximum_fusion.1), channel_id=1, source_target_pairs={{0,1},{1,0},{2,10},{3,11},{4,5},{5,4},{6,14},{7,15},{8,9},{9,8},{1... | collective-permute-start | bytes 737288 | tf_op jit(solution)/shard_map/ppermute | solution.py:55
  25.4 4.9 %collective-permute-start.10 = (bf16[120,512]{1,0:T(8,128)(2,1)S(1)}, bf16[120,512]{1,0:T(8,128)(2,1)S(1)}, u32[]{:S(2)}, u32[]{:S(2)}) collective-permute-start(bf16[120,512]{1,0:T(8,128)(2,1)S(1)} %part0.1), channel_id=1, source_target_pairs={{0,8},{1,9},{2,6},{3,7},{4,12},{5,13},{6,2},{7,3},{8,0},{9,1},{10,... | collective-permute-start | bytes 368648 | tf_op jit(solution)/shard_map/ppermute | solution.py:55
  27.4 10.3 %collective-permute-start.11 = (bf16[4,120,512]{2,1,0:T(8,128)(2,1)S(1)}, bf16[4,120,512]{2,1,0:T(8,128)(2,1)S(1)}, u32[]{:S(2)}, u32[]{:S(2)}) collective-permute-start(bf16[4,120,512]{2,1,0:T(8,128)(2,1)S(1)} %pad_maximum_fusion.own), channel_id=1, source_target_pairs={{0,8},{1,9},{2,3},{3,2},{4,12},{5,13},{6,7},{7,6},{8,0},{9,1},{10,... | collective-permute-start | bytes 1474568 | tf_op jit(solution)/shard_map/ppermute | solution.py:55
  30.7 8.2 %collective-permute-start.13 = (bf16[60,512]{1,0:T(8,128)(2,1)S(1)}, bf16[60,512]{1,0:T(8,128)(2,1)S(1)}, u32[]{:S(2)}, u32[]{:S(2)}) collective-permute-start(bf16[60,512]{1,0:T(8,128)(2,1)S(1)} %halve0.1), channel_id=1, source_target_pairs={{0,16},{1,17},{2,18},{3,19},{4,20},{5,21},{6,22},{7,23},{8,24},{9,... | collective-permute-start | bytes 184328 | tf_op jit(solution)/shard_map/ppermute | solution.py:55
  38.9 2.0 %collective-permute-start.12 = (bf16[1,6,160,128]{3,2,1,0:T(8,128)(2,1)S(1)}, bf16[1,6,160,128]{3,2,1,0:T(8,128)(2,1)S(1)}, u32[]{:S(2)}, u32[]{:S(2)}) collective-permute-start(bf16[1,6,160,128]{3,2,1,0:T(8,128)(2,1)S(1)} %get-tuple-element.34), channel_id=1, source_target_pairs={{0,2},{1,3},{2,0},{3,1},{4,6},{5,7},{6,4},{7,5},{8,10},{9,11},{10,... | collective-permute-start | bytes 737288 | tf_op jit(solution)/shard_map/ppermute | solution.py:55

commit v9 on v7

--- a/solution.py
+++ b/solution.py
@@ -119,7 +119,7 @@
         self.cells = 2 * images * rows * width
         by_row, by_next, by_col = (2, 0), (4, 0), (0, self.top_strip)
         self.term_masks = ((by_col, by_next), (by_row, by_col), (by_next, by_row))
-        self.gather_masks = ((by_row, by_col), (by_next, by_next), (by_col, by_row))
+        self.gather_masks = ((by_row, by_next), (by_next, by_col), (by_col, by_row))
 
     def block_of(self, slot, by_next, by_row):
         bits = self.band_bits - 3
@@ -283,9 +283,10 @@
         rows = [[] for _ in TAP_STEPS]
         for m in range(plan.blocks):
             row, behind, col = (m % 2) ^ row_bit, (m // 2 % 2) ^ next_bit, x ^ col_bit
-            one = jnp.where(core == 0, row, col)
+            one = jnp.where(core == 0, row, behind)
+            two = jnp.where(core == 0, behind, col)
             three = jnp.where(core == 0, col, row)
-            slot = behind * 2 + one
+            slot = two * 2 + one
             pair = jnp.where(three == 0, own[slot], other[slot]).astype(jnp.float32)
             block = pair[: plan.block_rows]
             for k in range(1, plan.inner):
@@ -382,9 +383,9 @@
     shape = (2, rows, lanes)
     send0 = run("send0", part(send_kernel, plan, False), shape, b16, [acts, grads])
     come0 = swap(send0, sizes, *plan.term_masks[0])
-    keep0 = run("keep0", part(keep_kernel, plan, False), shape, f32, [after(acts, send0), grads])
-    send1 = run("send1", part(send_kernel, plan, True), shape, b16, [after(acts, keep0), grads])
+    send1 = run("send1", part(send_kernel, plan, True), shape, b16, [after(acts, send0), grads])
     come1 = swap(send1, sizes, *plan.term_masks[0])
+    keep0 = run("keep0", part(keep_kernel, plan, False), shape, f32, [after(acts, send1), grads])
     send = run("turn0", part(turn_kernel, plan, False), shape, b16, [keep0, come0])
     come = swap(send, sizes, *plan.term_masks[1])
     keep1 = run("keep1", part(keep_kernel, plan, True), shape, f32, [after(acts, send), grads])

time: 40.7 us -> 39.5 us (0.971)
  waiting for transfers between devices: 9.38 us -> 7.51 us
  Pallas kernels: 10.3 us -> 11.5 us
  local copies, waits for them, and re-layouts: 1.04 us -> 0.01 us
  starting transfers between devices: 18.9 us -> 19.4 us
    ppermute x14, waiting for transfers between devices: 9.38 us -> 7.51 us  [swap(): return lax.ppermute(value, AXES, pairs)]
    pallas_call x19, Pallas kernels: 10.3 us -> 11.5 us  [call(): pl.pallas_call(kernel, out_shape=out_shape, in_specs=[pl.BlockSpec(memory...]
    unnamed x6 -> x4, local copies, waits for them, and re-layouts: 1.04 us -> 0.01 us
    ppermute x14, starting transfers between devices: 18.9 us -> 19.4 us  [swap(): return lax.ppermute(value, AXES, pairs)]
  transfers between devices with their start and end apart: 14 -> 14, of which waited for: 7 -> 6; matrix products, arithmetic and copies ran while one was open for 0% -> 0% of each run, Pallas kernels for 23% -> 24%
where the time goes in v9:
time: 39.5 us; the launch traced here: 39.3 us
  starting transfers between devices  19.4 us (49%)
  Pallas kernels  11.5 us (29%)
  waiting for transfers between devices  7.51 us (19%)
  between operations  0.82 us (2%)
    ppermute x14, starting transfers between devices, swap(): return lax.ppermute(value, AXES, pairs)  19.4 us
    pallas_call x19, Pallas kernels, call(): pl.pallas_call(kernel, out_shape=out_shape, in_specs=[pl.BlockSpec(memory...  11.5 us
    ppermute x14, waiting for transfers between devices, swap(): return lax.ppermute(value, AXES, pairs)  7.51 us
  transfers between devices with their start and end apart: 14, of which 6 were waited for; matrix products, arithmetic and copies ran while one was open for 0% of the time, Pallas kernels for 24%

profile of v9, /device:TPU:0, one launch (start us, length us, event | category | flops | bytes accessed | tf_op | source)
XLA Modules:
  0.0 39.3 jit_solution(12158083586246425273)
XLA Ops:
  0.6 0.0 copy-start
  0.6 0.0 copy-start.1
  0.6 1.1 %edge.1 = (bf16[1,320,128]{2,1,0:T(8,128)(2,1)S(1)}, bf16[1,6,320,128]{3,2,1,0:T(8,128)(2,1)S(1)}) custom-call(bf16[1,6,320,128]{3,2,1,0:T(8,128)(2,1)} %bitcast.3.grad), custom_call_target="tpu_custom_call" | custom-call | flops 9200000000 | tf_op jit(solution)/shard_map/edge/pallas_call | solution.py:59
  1.8 3.0 %collective-permute-start.3 = (bf16[1,320,128]{2,1,0:T(8,128)(2,1)S(1)}, bf16[1,320,128]{2,1,0:T(8,128)(2,1)S(1)}, u32[]{:S(2)}, u32[]{:S(2)}) collective-permute-start(bf16[1,320,128]{2,1,0:T(8,128)(2,1)S(1)} %get-tuple-element.20), channel_id=1, source_target_pairs={{0,1},{1,0},{2,3},{3,2},{4,5},{5,4},{6,7},{7,6},{8,9},{9,8},{10,11... | collective-permute-start | bytes 245768 | tf_op jit(solution)/shard_map/ppermute | solution.py:55
  4.8 0.0 collective-permute-start.4
  4.8 0.2 collective-permute-start.2
  5.0 0.0 copy-done
  5.0 0.3 collective-permute-start.1
  5.3 0.0 copy-done.1
  5.3 0.1 pack.1
  5.4 2.8 %collective-permute-start = (bf16[1,60,512]{2,1,0:T(8,128)(2,1)S(1)}, bf16[1,60,512]{2,1,0:T(8,128)(2,1)S(1)}, u32[]{:S(2)}, u32[]{:S(2)}) collective-permute-start(bf16[1,60,512]{2,1,0:T(8,128)(2,1)S(1)} %bitcast.12), channel_id=1, source_target_pairs={{0,16},{1,17},{2,18},{3,19},{4,20},{5,21},{6,22},{7,23},{8,24},{9,... | collective-permute-start | bytes 184328 | tf_op jit(solution)/shard_map/ppermute | solution.py:55
  8.2 0.0 collective-permute-done.1.act1
  8.2 0.6 %acts.1 = bf16[2,240,1536]{2,1,0:T(8,128)(2,1)S(1)} custom-call(bf16[1,6,320,128]{3,2,1,0:T(8,128)(2,1)S(1)} %bitcast.10, bf16[1,6,320,128]{3,2,1,0:T(8,128)(2,1)S(1)} %collective-permute-done.1.act1), custom_call_target="tpu_custom_call" | custom-call | flops 690000000 | tf_op jit(solution)/shard_map/acts/pallas_call | solution.py:59
  8.8 0.0 collective-permute-done.3.top0.bottom0
  8.9 0.4 %collective-permute-done.4.top1.bottom1 = bf16[1,320,128]{2,1,0:T(8,128)(2,1)S(1)} collective-permute-done((bf16[1,320,128]{2,1,0:T(8,128)(2,1)S(1)}, bf16[1,320,128]{2,1,0:T(8,128)(2,1)S(1)}, u32[]{:S(2)}, u32[]{:S(2)}) %collective-permute-start.4) | collective-permute-done | bytes 81952 | tf_op jit(solution)/shard_map/ppermute | solution.py:55
  9.3 0.0 collective-permute-done.2.grad1
  9.3 0.5 %grads.1 = bf16[2,512,1536]{2,1,0:T(8,128)(2,1)S(1)} custom-call(bf16[1,6,320,128]{3,2,1,0:T(8,128)(2,1)S(1)} %get-tuple-element.19.grad0, bf16[1,6,320,128]{3,2,1,0:T(8,128)(2,1)S(1)} %collective-permute-done.2.grad1, bf16[1,320,128]{2,1,0:T(8,128)(2,1)S(1)} %collective-permute-done.3.top0.bottom0, ...), custom_call_target="tpu_custom_call" | custom-call | flops 575000000 | tf_op jit(solution)/shard_map/grads/pallas_call | solution.py:59
  9.7 0.9 %send0.1 = bf16[2,120,512]{2,1,0:T(8,128)(2,1)S(1)} custom-call(bf16[2,240,1536]{2,1,0:T(8,128)(2,1)S(1)} %acts.1, bf16[2,512,1536]{2,1,0:T(8,128)(2,1)S(1)} %grads.1), custom_call_target="tpu_custom_call" | custom-call | flops 1610000000 | tf_op jit(solution)/shard_map/send0/pallas_call | solution.py:59
  10.7 1.1 %collective-permute-start.6 = (bf16[2,120,512]{2,1,0:T(8,128)(2,1)S(1)}, bf16[2,120,512]{2,1,0:T(8,128)(2,1)S(1)}, u32[]{:S(2)}, u32[]{:S(2)}) collective-permute-start(bf16[2,120,512]{2,1,0:T(8,128)(2,1)S(1)} %send0.1), channel_id=1, source_target_pairs={{0,1},{1,0},{2,10},{3,11},{4,5},{5,4},{6,14},{7,15},{8,9},{9,8},{1... | collective-permute-start | bytes 737288 | tf_op jit(solution)/shard_map/ppermute | solution.py:55
  11.8 0.9 %send1.1 = bf16[2,120,512]{2,1,0:T(8,128)(2,1)S(1)} custom-call(bf16[2,240,1536]{2,1,0:T(8,128)(2,1)S(1)} %acts.1, bf16[2,512,1536]{2,1,0:T(8,128)(2,1)S(1)} %grads.1), custom_call_target="tpu_custom_call" | custom-call | flops 1610000000 | tf_op jit(solution)/shard_map/send1/pallas_call | solution.py:59
  12.7 0.6 %keep0.1.keep = f32[2,120,512]{2,1,0:T(8,128)S(1)} custom-call(bf16[2,240,1536]{2,1,0:T(8,128)(2,1)S(1)} %acts.1, bf16[2,512,1536]{2,1,0:T(8,128)(2,1)S(1)} %grads.1), custom_call_target="tpu_custom_call" | custom-call | flops 1150000000 | tf_op jit(solution)/shard_map/keep0/pallas_call | solution.py:59
  13.4 0.0 collective-permute-done.refs_1_
  13.4 1.6 %collective-permute-start.5 = (bf16[1,120,512]{2,1,0:T(8,128)(2,1)S(1)}, bf16[1,120,512]{2,1,0:T(8,128)(2,1)S(1)}, u32[]{:S(2)}, u32[]{:S(2)}) collective-permute-start(bf16[1,120,512]{2,1,0:T(8,128)(2,1)S(1)} %pair.1), channel_id=1, source_target_pairs={{0,4},{1,5},{2,10},{3,11},{4,0},{5,1},{6,14},{7,15},{8,12},{9,13},... | collective-permute-start | bytes 368648 | tf_op jit(solution)/shard_map/ppermute | solution.py:55
  15.0 1.2 %collective-permute-start.8 = (bf16[2,120,512]{2,1,0:T(8,128)(2,1)S(1)}, bf16[2,120,512]{2,1,0:T(8,128)(2,1)S(1)}, u32[]{:S(2)}, u32[]{:S(2)}) collective-permute-start(bf16[2,120,512]{2,1,0:T(8,128)(2,1)S(1)} %send1.1), channel_id=1, source_target_pairs={{0,1},{1,0},{2,10},{3,11},{4,5},{5,4},{6,14},{7,15},{8,9},{9,8},{1... | collective-permute-start | bytes 737288 | tf_op jit(solution)/shard_map/ppermute | solution.py:55
  16.2 0.8 %collective-permute-done.6.message = bf16[2,120,512]{2,1,0:T(8,128)(2,1)S(1)} collective-permute-done((bf16[2,120,512]{2,1,0:T(8,128)(2,1)S(1)}, bf16[2,120,512]{2,1,0:T(8,128)(2,1)S(1)}, u32[]{:S(2)}, u32[]{:S(2)}) %collective-permute-start.6) | collective-permute-done | bytes 245792 | tf_op jit(solution)/shard_map/ppermute | solution.py:55
  16.9 0.7 %turn0.1 = bf16[2,120,512]{2,1,0:T(8,128)(2,1)S(1)} custom-call(f32[2,120,512]{2,1,0:T(8,128)S(1)} %keep0.1.keep, bf16[2,120,512]{2,1,0:T(8,128)(2,1)S(1)} %collective-permute-done.6.message), custom_call_target="tpu_custom_call" | custom-call | flops 1035000000 | tf_op jit(solution)/shard_map/turn0/pallas_call | solution.py:59
  17.6 1.8 %collective-permute-start.9 = (bf16[2,120,512]{2,1,0:T(8,128)(2,1)S(1)}, bf16[2,120,512]{2,1,0:T(8,128)(2,1)S(1)}, u32[]{:S(2)}, u32[]{:S(2)}) collective-permute-start(bf16[2,120,512]{2,1,0:T(8,128)(2,1)S(1)} %turn0.1), channel_id=1, source_target_pairs={{0,4},{1,5},{2,3},{3,2},{4,0},{5,1},{6,7},{7,6},{8,12},{9,13},{10,... | collective-permute-start | bytes 737288 | tf_op jit(solution)/shard_map/ppermute | solution.py:55
  19.4 0.0 collective-permute-done.5
  19.5 1.6 %collective-permute-start.7 = (bf16[2,120,512]{2,1,0:T(8,128)(2,1)S(1)}, bf16[2,120,512]{2,1,0:T(8,128)(2,1)S(1)}, u32[]{:S(2)}, u32[]{:S(2)}) collective-permute-start(bf16[2,120,512]{2,1,0:T(8,128)(2,1)S(1)} %pad_maximum_fusion.1), channel_id=1, source_target_pairs={{0,8},{1,9},{2,3},{3,2},{4,12},{5,13},{6,7},{7,6},{8,0},{9,1},{10,... | collective-permute-start | bytes 737288 | tf_op jit(solution)/shard_map/ppermute | solution.py:55
  21.1 0.6 %keep1.1.keep = f32[2,120,512]{2,1,0:T(8,128)S(1)} custom-call(bf16[2,240,1536]{2,1,0:T(8,128)(2,1)S(1)} %acts.1, bf16[2,512,1536]{2,1,0:T(8,128)(2,1)S(1)} %grads.1), custom_call_target="tpu_custom_call" | custom-call | flops 1150000000 | tf_op jit(solution)/shard_map/keep1/pallas_call | solution.py:59
  21.7 1.1 %collective-permute-done.8.message = bf16[2,120,512]{2,1,0:T(8,128)(2,1)S(1)} collective-permute-done((bf16[2,120,512]{2,1,0:T(8,128)(2,1)S(1)}, bf16[2,120,512]{2,1,0:T(8,128)(2,1)S(1)}, u32[]{:S(2)}, u32[]{:S(2)}) %collective-permute-start.8) | collective-permute-done | bytes 245792 | tf_op jit(solution)/shard_map/ppermute | solution.py:55
  22.8 0.3 turn1.1.keep
  23.1 0.8 %collective-permute-done.9.message = bf16[2,120,512]{2,1,0:T(8,128)(2,1)S(1)} collective-permute-done((bf16[2,120,512]{2,1,0:T(8,128)(2,1)S(1)}, bf16[2,120,512]{2,1,0:T(8,128)(2,1)S(1)}, u32[]{:S(2)}, u32[]{:S(2)}) %collective-permute-start.9) | collective-permute-done | bytes 245792 | tf_op jit(solution)/shard_map/ppermute | solution.py:55
  23.9 0.4 part0.1
  24.3 1.9 %collective-permute-start.10 = (bf16[120,512]{1,0:T(8,128)(2,1)S(1)}, bf16[120,512]{1,0:T(8,128)(2,1)S(1)}, u32[]{:S(2)}, u32[]{:S(2)}) collective-permute-start(bf16[120,512]{1,0:T(8,128)(2,1)S(1)} %part0.1), channel_id=1, source_target_pairs={{0,8},{1,9},{2,6},{3,7},{4,12},{5,13},{6,2},{7,3},{8,0},{9,1},{10,... | collective-permute-start | bytes 368648 | tf_op jit(solution)/shard_map/ppermute | solution.py:55
  26.1 0.0 collective-permute-done.7
  26.2 0.9 %collective-permute-start.11 = (bf16[4,120,512]{2,1,0:T(8,128)(2,1)S(1)}, bf16[4,120,512]{2,1,0:T(8,128)(2,1)S(1)}, u32[]{:S(2)}, u32[]{:S(2)}) collective-permute-start(bf16[4,120,512]{2,1,0:T(8,128)(2,1)S(1)} %pad_maximum_fusion.own), channel_id=1, source_target_pairs={{0,1},{1,0},{2,6},{3,7},{4,5},{5,4},{6,2},{7,3},{8,9},{9,8},{10,14... | collective-permute-start | bytes 1474568 | tf_op jit(solution)/shard_map/ppermute | solution.py:55
  27.1 0.2 part1.1.keep
  27.3 1.9 %collective-permute-done.10.message = bf16[120,512]{1,0:T(8,128)(2,1)S(1)} collective-permute-done((bf16[120,512]{1,0:T(8,128)(2,1)S(1)}, bf16[120,512]{1,0:T(8,128)(2,1)S(1)}, u32[]{:S(2)}, u32[]{:S(2)}) %collective-permute-start.10) | collective-permute-done | bytes 122912 | tf_op jit(solution)/shard_map/ppermute | solution.py:55
  29.2 0.4 halve0.1
  29.6 2.9 %collective-permute-start.13 = (bf16[60,512]{1,0:T(8,128)(2,1)S(1)}, bf16[60,512]{1,0:T(8,128)(2,1)S(1)}, u32[]{:S(2)}, u32[]{:S(2)}) collective-permute-start(bf16[60,512]{1,0:T(8,128)(2,1)S(1)} %halve0.1), channel_id=1, source_target_pairs={{0,16},{1,17},{2,18},{3,19},{4,20},{5,21},{6,22},{7,23},{8,24},{9,... | collective-permute-start | bytes 184328 | tf_op jit(solution)/shard_map/ppermute | solution.py:55
  32.5 0.2 halve1.1.keep
  32.6 2.4 %collective-permute-done.11.other = bf16[4,120,512]{2,1,0:T(8,128)(2,1)S(1)} collective-permute-done((bf16[4,120,512]{2,1,0:T(8,128)(2,1)S(1)}, bf16[4,120,512]{2,1,0:T(8,128)(2,1)S(1)}, u32[]{:S(2)}, u32[]{:S(2)}) %collective-permute-start.11) | collective-permute-done | bytes 491552 | tf_op jit(solution)/shard_map/ppermute | solution.py:55
  35.1 1.2 %given.1 = (bf16[1,6,160,128]{3,2,1,0:T(8,128)(2,1)S(1)}, bf16[480,1024]{1,0:T(8,128)(2,1)S(1)}) custom-call(bf16[4,120,512]{2,1,0:T(8,128)(2,1)S(1)} %pad_maximum_fusion.own, bf16[4,120,512]{2,1,0:T(8,128)(2,1)S(1)} %collective-permute-done.11.other, bf16[1024,1536]{1,0:T(8,128)(2,1)S(1)} %bitcast.7), custom_call_target="tpu_custom_call" | custom-call | flops 1380000000 | tf_op jit(solution)/shard_map/given/pallas_call | solution.py:59
  36.3 0.1 collective-permute-start.12
  36.4 0.0 collective-permute-done.13.message
  36.4 0.9 %last.1 = f32[9,20,160]{2,1,0:T(8,128)} custom-call(f32[60,512]{1,0:T(8,128)S(1)} %halve1.1.keep, bf16[60,512]{1,0:T(8,128)(2,1)S(1)} %collective-permute-done.13.message), custom_call_target="tpu_custom_call" | custom-call | flops 9200000000 | tf_op jit(solution)/shard_map/last/pallas_call | solution.py:59
  37.3 1.0 %own.1 = bf16[1,6,160,128]{3,2,1,0:T(8,128)(2,1)S(1)} custom-call(bf16[480,1024]{1,0:T(8,128)(2,1)S(1)} %get-tuple-element.35.left, bf16[1024,1536]{1,0:T(8,128)(2,1)S(1)} %bitcast.8), custom_call_target="tpu_custom_call" | custom-call | flops 805000000 | tf_op jit(solution)/shard_map/own/pallas_call | solution.py:59
  38.3 0.0 collective-permute-done.12.theirs
  38.3 0.9 %weave.1 = bf16[1,6,320,128]{3,2,1,0:T(8,128)(2,1)} custom-call(bf16[1,6,160,128]{3,2,1,0:T(8,128)(2,1)S(1)} %own.1, bf16[1,6,160,128]{3,2,1,0:T(8,128)(2,1)S(1)} %collective-permute-done.12.theirs), custom_call_target="tpu_custom_call" | custom-call | flops 1035000000 | tf_op jit(solution)/shard_map/weave/pallas_call | solution.py:59
  (3 shorter events, 0.1 us)
Async XLA Ops:
  0.6 4.4 %copy-start = (bf16[1,320,6,128]{3,1,2,0:T(8,128)(2,1)S(1)}, bf16[1,320,6,128]{3,1,2,0:T(8,128)(2,1)}, u32[]{:S(2)}) copy-start(bf16[1,320,6,128]{3,1,2,0:T(8,128)(2,1)} %param.3) | copy-start | bytes 1474564
  0.6 4.7 %copy-start.1 = (bf16[20,9,160]{2,0,1:T(8,128)(2,1)S(1)}, bf16[20,9,160]{2,0,1:T(8,128)(2,1)}, u32[]{:S(2)}) copy-start(bf16[20,9,160]{2,0,1:T(8,128)(2,1)} %param.5) | copy-start | bytes 172804
  1.8 7.0 %collective-permute-start.3 = (bf16[1,320,128]{2,1,0:T(8,128)(2,1)S(1)}, bf16[1,320,128]{2,1,0:T(8,128)(2,1)S(1)}, u32[]{:S(2)}, u32[]{:S(2)}) collective-permute-start(bf16[1,320,128]{2,1,0:T(8,128)(2,1)S(1)} %get-tuple-element.20), channel_id=1, source_target_pairs={{0,1},{1,0},{2,3},{3,2},{4,5},{5,4},{6,7},{7,6},{8,9},{9,8},{10,11... | collective-permute-start | bytes 245768 | tf_op jit(solution)/shard_map/ppermute | solution.py:55
  4.8 4.5 %collective-permute-start.4 = (bf16[1,320,128]{2,1,0:T(8,128)(2,1)S(1)}, bf16[1,320,128]{2,1,0:T(8,128)(2,1)S(1)}, u32[]{:S(2)}, u32[]{:S(2)}) collective-permute-start(bf16[1,320,128]{2,1,0:T(8,128)(2,1)S(1)} %get-tuple-element.20), channel_id=1, source_target_pairs={{0,3},{1,2},{2,1},{3,0},{4,7},{5,6},{6,5},{7,4},{8,11},{9,10},{10,... | collective-permute-start | bytes 245768 | tf_op jit(solution)/shard_map/ppermute | solution.py:55
  4.8 4.5 %collective-permute-start.2 = (bf16[1,6,320,128]{3,2,1,0:T(8,128)(2,1)}, bf16[1,6,320,128]{3,2,1,0:T(8,128)(2,1)S(1)}, u32[]{:S(2)}, u32[]{:S(2)}) collective-permute-start(bf16[1,6,320,128]{3,2,1,0:T(8,128)(2,1)} %bitcast.3.grad), channel_id=1, source_target_pairs={{0,2},{1,3},{2,0},{3,1},{4,6},{5,7},{6,4},{7,5},{8,10},{9,11},{10,... | collective-permute-start | bytes 1474568 | tf_op jit(solution)/shard_map/ppermute | solution.py:55
  5.0 3.2 %collective-permute-start.1 = (bf16[1,6,320,128]{3,2,1,0:T(8,128)(2,1)S(1)}, bf16[1,6,320,128]{3,2,1,0:T(8,128)(2,1)S(1)}, u32[]{:S(2)}, u32[]{:S(2)}) collective-permute-start(bf16[1,6,320,128]{3,2,1,0:T(8,128)(2,1)S(1)} %bitcast.9), channel_id=1, source_target_pairs={{0,2},{1,3},{2,0},{3,1},{4,6},{5,7},{6,4},{7,5},{8,10},{9,11},{10,... | collective-permute-start | bytes 1474568 | tf_op jit(solution)/shard_map/ppermute | solution.py:55
  5.4 7.9 %collective-permute-start = (bf16[1,60,512]{2,1,0:T(8,128)(2,1)S(1)}, bf16[1,60,512]{2,1,0:T(8,128)(2,1)S(1)}, u32[]{:S(2)}, u32[]{:S(2)}) collective-permute-start(bf16[1,60,512]{2,1,0:T(8,128)(2,1)S(1)} %bitcast.12), channel_id=1, source_target_pairs={{0,16},{1,17},{2,18},{3,19},{4,20},{5,21},{6,22},{7,23},{8,24},{9,... | collective-permute-start | bytes 184328 | tf_op jit(solution)/shard_map/ppermute | solution.py:55
  10.7 6.3 %collective-permute-start.6 = (bf16[2,120,512]{2,1,0:T(8,128)(2,1)S(1)}, bf16[2,120,512]{2,1,0:T(8,128)(2,1)S(1)}, u32[]{:S(2)}, u32[]{:S(2)}) collective-permute-start(bf16[2,120,512]{2,1,0:T(8,128)(2,1)S(1)} %send0.1), channel_id=1, source_target_pairs={{0,1},{1,0},{2,10},{3,11},{4,5},{5,4},{6,14},{7,15},{8,9},{9,8},{1... | collective-permute-start | bytes 737288 | tf_op jit(solution)/shard_map/ppermute | solution.py:55
  13.4 6.0 %collective-permute-start.5 = (bf16[1,120,512]{2,1,0:T(8,128)(2,1)S(1)}, bf16[1,120,512]{2,1,0:T(8,128)(2,1)S(1)}, u32[]{:S(2)}, u32[]{:S(2)}) collective-permute-start(bf16[1,120,512]{2,1,0:T(8,128)(2,1)S(1)} %pair.1), channel_id=1, source_target_pairs={{0,4},{1,5},{2,10},{3,11},{4,0},{5,1},{6,14},{7,15},{8,12},{9,13},... | collective-permute-start | bytes 368648 | tf_op jit(solution)/shard_map/ppermute | solution.py:55
  15.0 7.8 %collective-permute-start.8 = (bf16[2,120,512]{2,1,0:T(8,128)(2,1)S(1)}, bf16[2,120,512]{2,1,0:T(8,128)(2,1)S(1)}, u32[]{:S(2)}, u32[]{:S(2)}) collective-permute-start(bf16[2,120,512]{2,1,0:T(8,128)(2,1)S(1)} %send1.1), channel_id=1, source_target_pairs={{0,1},{1,0},{2,10},{3,11},{4,5},{5,4},{6,14},{7,15},{8,9},{9,8},{1... | collective-permute-start | bytes 737288 | tf_op jit(solution)/shard_map/ppermute | solution.py:55
  17.6 6.3 %collective-permute-start.9 = (bf16[2,120,512]{2,1,0:T(8,128)(2,1)S(1)}, bf16[2,120,512]{2,1,0:T(8,128)(2,1)S(1)}, u32[]{:S(2)}, u32[]{:S(2)}) collective-permute-start(bf16[2,120,512]{2,1,0:T(8,128)(2,1)S(1)} %turn0.1), channel_id=1, source_target_pairs={{0,4},{1,5},{2,3},{3,2},{4,0},{5,1},{6,7},{7,6},{8,12},{9,13},{10,... | collective-permute-start | bytes 737288 | tf_op jit(solution)/shard_map/ppermute | solution.py:55
  19.5 6.7 %collective-permute-start.7 = (bf16[2,120,512]{2,1,0:T(8,128)(2,1)S(1)}, bf16[2,120,512]{2,1,0:T(8,128)(2,1)S(1)}, u32[]{:S(2)}, u32[]{:S(2)}) collective-permute-start(bf16[2,120,512]{2,1,0:T(8,128)(2,1)S(1)} %pad_maximum_fusion.1), channel_id=1, source_target_pairs={{0,8},{1,9},{2,3},{3,2},{4,12},{5,13},{6,7},{7,6},{8,0},{9,1},{10,... | collective-permute-start | bytes 737288 | tf_op jit(solution)/shard_map/ppermute | solution.py:55
  24.3 4.9 %collective-permute-start.10 = (bf16[120,512]{1,0:T(8,128)(2,1)S(1)}, bf16[120,512]{1,0:T(8,128)(2,1)S(1)}, u32[]{:S(2)}, u32[]{:S(2)}) collective-permute-start(bf16[120,512]{1,0:T(8,128)(2,1)S(1)} %part0.1), channel_id=1, source_target_pairs={{0,8},{1,9},{2,6},{3,7},{4,12},{5,13},{6,2},{7,3},{8,0},{9,1},{10,... | collective-permute-start | bytes 368648 | tf_op jit(solution)/shard_map/ppermute | solution.py:55
  26.2 8.9 %collective-permute-start.11 = (bf16[4,120,512]{2,1,0:T(8,128)(2,1)S(1)}, bf16[4,120,512]{2,1,0:T(8,128)(2,1)S(1)}, u32[]{:S(2)}, u32[]{:S(2)}) collective-permute-start(bf16[4,120,512]{2,1,0:T(8,128)(2,1)S(1)} %pad_maximum_fusion.own), channel_id=1, source_target_pairs={{0,1},{1,0},{2,6},{3,7},{4,5},{5,4},{6,2},{7,3},{8,9},{9,8},{10,14... | collective-permute-start | bytes 1474568 | tf_op jit(solution)/shard_map/ppermute | solution.py:55
  29.6 6.8 %collective-permute-start.13 = (bf16[60,512]{1,0:T(8,128)(2,1)S(1)}, bf16[60,512]{1,0:T(8,128)(2,1)S(1)}, u32[]{:S(2)}, u32[]{:S(2)}) collective-permute-start(bf16[60,512]{1,0:T(8,128)(2,1)S(1)} %halve0.1), channel_id=1, source_target_pairs={{0,16},{1,17},{2,18},{3,19},{4,20},{5,21},{6,22},{7,23},{8,24},{9,... | collective-permute-start | bytes 184328 | tf_op jit(solution)/shard_map/ppermute | solution.py:55
  36.3 2.0 %collective-permute-start.12 = (bf16[1,6,160,128]{3,2,1,0:T(8,128)(2,1)S(1)}, bf16[1,6,160,128]{3,2,1,0:T(8,128)(2,1)S(1)}, u32[]{:S(2)}, u32[]{:S(2)}) collective-permute-start(bf16[1,6,160,128]{3,2,1,0:T(8,128)(2,1)S(1)} %get-tuple-element.34), channel_id=1, source_target_pairs={{0,2},{1,3},{2,0},{3,1},{4,6},{5,7},{6,4},{7,5},{8,10},{9,11},{10,... | collective-permute-start | bytes 737288 | tf_op jit(solution)/shard_map/ppermute | solution.py:55

commit v10 on v9

--- a/solution.py
+++ b/solution.py
@@ -31,9 +31,8 @@
     "part1": 0.3,
     "halve0": 0.5,
     "halve1": 3.0,
-    "last": 8.0,
     "given": 1.2,
-    "own": 0.7,
+    "own": 8.0,
     "weave": 0.9,
 }
 GATHER_STEPS = ("keep0", "turn0", "part0")
@@ -55,12 +54,15 @@
     return lax.ppermute(value, AXES, pairs)
 
 
-def call(name, kernel, out_shape, operands, scratch=()):
+def call(name, kernel, out_shape, operands, scratch=(), far=0):
+    outs = jax.tree.map(lambda _: pl.BlockSpec(memory_space=pltpu.VMEM), out_shape)
+    if far:
+        outs = outs[:-far] + (pl.BlockSpec(memory_space=pl.ANY),) * far
     return pl.pallas_call(
         kernel,
         out_shape=out_shape,
         in_specs=[pl.BlockSpec(memory_space=pltpu.VMEM)] * len(operands),
-        out_specs=jax.tree.map(lambda _: pl.BlockSpec(memory_space=pltpu.VMEM), out_shape),
+        out_specs=outs,
         scratch_shapes=list(scratch),
         compiler_params=pltpu.CompilerParams(vmem_limit_bytes=VMEM_BYTES),
         cost_estimate=pl.CostEstimate(
@@ -84,13 +86,25 @@
     size = jnp.maximum(jnp.abs(power), LEAST_POWER)
     fourth = lax.rsqrt(lax.rsqrt(size))
     root = fourth * lax.rsqrt(fourth)
-    return jnp.where(power < 0, -root, root) * (peak * (1.0 / TOP_POWER))
-
-
-def peak_of(value):
-    largest = jnp.max(jnp.abs(value))
-    largest = jnp.maximum(largest * (1.0 + 2.0**-6), LEAST_PEAK)
-    return jnp.full((1, 1), largest, jnp.float32).astype(jnp.bfloat16).astype(jnp.float32)
+    return jnp.where(power < 0, -root, root) * (peak * (1.0 / TOP_POWER)), peak
+
+
+def rounded_up(peak):
+    return jnp.maximum(peak * (1.0 + 2.0**-6), LEAST_PEAK).astype(jnp.bfloat16).astype(jnp.float32)
+
+
+def largest(value):
+    return jnp.full((1, 1), jnp.max(jnp.abs(value)), jnp.float32)
+
+
+def noted(peak, value, used):
+    lane = lax.broadcasted_iota(jnp.int32, value.shape, value.ndim - 1)
+    return jnp.where(lane < used, value, peak)
+
+
+def added(keep, message):
+    value, peak = decoded(message)
+    return keep + value, peak + keep[0:1, keep.shape[1] - 1 : keep.shape[1]]
 
 
 class Plan:
@@ -206,47 +220,39 @@
     total = pair_terms(plan, acts, grads, 1 - first, second if same else 1 - second)
     for k in range(2):
         half = total[k * plan.part_rows : (k + 1) * plan.part_rows]
-        out[k] = encoded(peak_of(half), half, plan.half_used)
+        out[k] = encoded(rounded_up(largest(half)), half, plan.half_used)
 
 
 def keep_kernel(plan, same, acts, grads, out):
     first, second, _ = mine(plan)
     total = pair_terms(plan, acts, grads, first, second if same else 1 - second)
     for k in range(2):
-        out[k] = total[k * plan.part_rows : (k + 1) * plan.part_rows]
+        half = total[k * plan.part_rows : (k + 1) * plan.part_rows]
+        out[k] = noted(largest(half), half, plan.half_used)
 
 
 def turn_kernel(plan, same, keep, message, out):
     for k in range(2):
-        total = keep[k] + decoded(message[k])
-        out[k] = total if same else encoded(peak_of(total), total, plan.half_used)
+        total, peak = added(keep[k], message[k])
+        out[k] = noted(peak, total, plan.half_used) if same else encoded(rounded_up(peak), total, plan.half_used)
 
 
 def part_kernel(plan, same, keep, message, out):
     third = mine(plan)[2]
     k = third if same else 1 - third
-    total = keep[k] + decoded(message[k])
-    out[...] = total if same else encoded(peak_of(total), total, plan.half_used)
+    total, peak = added(keep[k], message[k])
+    out[...] = noted(peak, total, plan.half_used) if same else encoded(rounded_up(peak), total, plan.half_used)
 
 
 def halve_kernel(plan, mask, used, same, keep, message, out):
     side = (lax.axis_index("band") // mask) % 2
-    total = keep[...] + decoded(message[...])
+    total, peak = added(keep[...], message[...])
     rows = total.shape[0] // 2
     lower, upper = total[:rows], total[rows:]
     if same:
-        out[...] = jnp.where(side == 0, lower, upper)
+        out[...] = noted(peak, jnp.where(side == 0, lower, upper), used)
     else:
-        given = jnp.where(side == 0, upper, lower)
-        out[...] = encoded(peak_of(given), given, used)
-
-
-def last_kernel(plan, scale, keep, message, out):
-    total = (keep[...] + decoded(message[...])) * scale
-    depth, cols = plan.depth, plan.cols
-    for r in range(len(TAP_STEPS)):
-        for c in range(len(TAP_STEPS)):
-            out[r * len(TAP_STEPS) + c] = total[c * depth : (c + 1) * depth, r * cols : (r + 1) * cols]
+        out[...] = encoded(rounded_up(peak), jnp.where(side == 0, upper, lower), used)
 
 
 def pack_kernel(plan, kernel, out):
@@ -301,13 +307,22 @@
     cells_of(plan, 1, left, grads, out)
 
 
-def own_kernel(plan, left, grads, out):
+def own_kernel(plan, scale, left, grads, keep, message, out, far, terms, sem):
+    total = added(keep[...], message[...])[0] * scale
+    depth, cols = plan.depth, plan.cols
+    for r in range(len(TAP_STEPS)):
+        for c in range(len(TAP_STEPS)):
+            terms[r * len(TAP_STEPS) + c] = total[c * depth : (c + 1) * depth, r * cols : (r + 1) * cols]
+    copy = pltpu.make_async_copy(terms, far, sem)
+    copy.start()
     cells_of(plan, 0, left, grads, out)
-
-
-def weave_kernel(plan, own, theirs, out):
+    copy.wait()
+
+
+def weave_kernel(plan, own, theirs, far, out, sems):
     core = lax.axis_index("band") % 2
     depth = plan.depth
+    copies = []
     for n in range(plan.images):
         for h in range(plan.rows):
             a, b = own[n, h].astype(jnp.float32), theirs[n, h].astype(jnp.float32)
@@ -316,6 +331,10 @@
             for m in range(plan.blocks):
                 pieces += [even[m * depth : (m + 1) * depth], odd[m * depth : (m + 1) * depth]]
             out[n, h] = jnp.concatenate(pieces, axis=0).astype(jnp.bfloat16)
+            copies.append(pltpu.make_async_copy(out.at[n, h], far.at[n, h], sems.at[n, h]))
+            copies[-1].start()
+    for copy in copies:
+        copy.wait()
 
 
 def after(value, *others):
@@ -368,10 +387,10 @@
         given = jnp.where(side == 0, parts[:, :, 1], parts[:, :, 0])
         total = kept + swap(given, plan.sizes, (0, mask))
     total = total.reshape(rows, plan.used)
-    return jnp.pad(total, ((0, 0), (0, plan.lanes - plan.used)))
-
-
-def kernel_terms(plan, acts, grads, scale):
+    return noted(largest(total), jnp.pad(total, ((0, 0), (0, plan.lanes - plan.used))), plan.used)
+
+
+def kernel_terms(plan, acts, grads):
     sizes, f32 = plan.sizes, jnp.float32
     rows, lanes = plan.part_rows, plan.half_lanes
 
@@ -397,7 +416,7 @@
     steps.update(part0=send, part1=keep)
     come = swap(send, sizes, *plan.term_masks[2])
     if plan.rest_strip:
-        keep = narrowed(plan, keep + decoded(come))
+        keep = narrowed(plan, added(keep, come)[0])
         come = jnp.zeros(keep.shape, b16)
     for mask in plan.rest_band:
         rows //= 2
@@ -407,13 +426,7 @@
         keep = run("halve1", part(halve, True), shape, f32, [after(keep, send), come])
         steps.update(halve0=send, halve1=keep)
         come = swap(send, sizes, (mask, 0))
-    total = call(
-        "last",
-        part(last_kernel, plan, scale),
-        jax.ShapeDtypeStruct((len(TAP_STEPS) ** 2, plan.depth, plan.cols), f32),
-        [keep, come],
-    )
-    return total, steps
+    return keep, come, steps
 
 
 def edge_kernel(plan, grad, out, copy):
@@ -461,7 +474,7 @@
         jax.ShapeDtypeStruct(shape, grad.dtype),
         [grad0, grad1, *tops, *bottoms],
     )
-    kernel_grad, steps = kernel_terms(plan, acts, grads, scale)
+    keep, come, steps = kernel_terms(plan, acts, grads)
     packed = whole_kernel(plan, packed, [steps[name] for name in GATHER_STEPS])
     shape = jax.ShapeDtypeStruct((images, rows, plan.half, width), jnp.bfloat16)
     left = jax.ShapeDtypeStruct((len(TAP_STEPS) * plan.half, 2 * plan.half_lanes), jnp.bfloat16)
@@ -472,14 +485,25 @@
         (shape, left),
         [after(packed[0], steps[CELLS_STEP]), packed[1], grads],
     )
-    own = call("own", functools.partial(own_kernel, plan), shape, [after(left, given), grads])
+    terms = (len(TAP_STEPS) ** 2, plan.depth, plan.cols)
+    own, kernel_grad = call(
+        "own",
+        functools.partial(own_kernel, plan, scale),
+        (shape, jax.ShapeDtypeStruct(terms, jnp.float32)),
+        [after(left, given), grads, keep, come],
+        [pltpu.VMEM(terms, jnp.float32), pltpu.SemaphoreType.DMA(())],
+        far=1,
+    )
     theirs = swap(given, plan.sizes, (1, 0))
+    shape = (images, rows, channels, width)
     input_grad = call(
         "weave",
         functools.partial(weave_kernel, plan),
-        jax.ShapeDtypeStruct((images, rows, channels, width), jnp.bfloat16),
+        (jax.ShapeDtypeStruct(shape, jnp.bfloat16),),
         [own, theirs],
-    )
+        [pltpu.VMEM(shape, jnp.bfloat16), pltpu.SemaphoreType.DMA((images, rows))],
+        far=1,
+    )[0]
     return input_grad.transpose(0, 2, 1, 3), kernel_grad.transpose(1, 0, 2)
 
 

time: 39.5 us -> 38.6 us (0.977)
  Pallas kernels: 11.5 us -> 10.4 us
    pallas_call x19 -> x18, Pallas kernels: 11.5 us -> 10.4 us  [call(): pl.pallas_call(kernel, out_shape=out_shape, in_specs=[pl.BlockSpec(memory...]
  transfers between devices with their start and end apart: 14 -> 14, of which waited for: 6 -> 7; matrix products, arithmetic and copies ran while one was open for 0% -> 0% of each run, Pallas kernels for 24% -> 22%
where the time goes in v10:
time: 38.6 us; the launch traced here: 38.4 us
  starting transfers between devices  19.4 us (50%)
  Pallas kernels  10.4 us (27%)
  waiting for transfers between devices  7.73 us (20%)
  between operations  0.81 us (2%)
    ppermute x14, starting transfers between devices, swap(): return lax.ppermute(value, AXES, pairs)  19.4 us
    pallas_call x18, Pallas kernels, call(): pl.pallas_call(kernel, out_shape=out_shape, in_specs=[pl.BlockSpec(memory...  10.4 us
    ppermute x14, waiting for transfers between devices, swap(): return lax.ppermute(value, AXES, pairs)  7.73 us
  transfers between devices with their start and end apart: 14, of which 7 were waited for; matrix products, arithmetic and copies ran while one was open for 0% of the time, Pallas kernels for 22%

profile of v10, /device:TPU:0, one launch (start us, length us, event | category | flops | bytes accessed | tf_op | source)
XLA Modules:
  0.0 38.4 jit_solution(6347368706371373391)
XLA Ops:
  0.6 0.0 copy-start
  0.6 0.0 copy-start.1
  0.6 1.1 %edge.1 = (bf16[1,320,128]{2,1,0:T(8,128)(2,1)S(1)}, bf16[1,6,320,128]{3,2,1,0:T(8,128)(2,1)S(1)}) custom-call(bf16[1,6,320,128]{3,2,1,0:T(8,128)(2,1)} %bitcast.3.grad), custom_call_target="tpu_custom_call" | custom-call | flops 9200000000 | tf_op jit(solution)/shard_map/edge/pallas_call | solution.py:61
  1.8 3.0 %collective-permute-start.3 = (bf16[1,320,128]{2,1,0:T(8,128)(2,1)S(1)}, bf16[1,320,128]{2,1,0:T(8,128)(2,1)S(1)}, u32[]{:S(2)}, u32[]{:S(2)}) collective-permute-start(bf16[1,320,128]{2,1,0:T(8,128)(2,1)S(1)} %get-tuple-element.22), channel_id=1, source_target_pairs={{0,1},{1,0},{2,3},{3,2},{4,5},{5,4},{6,7},{7,6},{8,9},{9,8},{10,11... | collective-permute-start | bytes 245768 | tf_op jit(solution)/shard_map/ppermute | solution.py:54
  4.8 0.0 collective-permute-start.4
  4.8 0.2 collective-permute-start.2
  5.0 0.0 copy-done
  5.0 0.3 collective-permute-start.1
  5.3 0.0 copy-done.1
  5.3 0.1 pack.1
  5.4 2.8 %collective-permute-start = (bf16[1,60,512]{2,1,0:T(8,128)(2,1)S(1)}, bf16[1,60,512]{2,1,0:T(8,128)(2,1)S(1)}, u32[]{:S(2)}, u32[]{:S(2)}) collective-permute-start(bf16[1,60,512]{2,1,0:T(8,128)(2,1)S(1)} %bitcast.12), channel_id=1, source_target_pairs={{0,16},{1,17},{2,18},{3,19},{4,20},{5,21},{6,22},{7,23},{8,24},{9,... | collective-permute-start | bytes 184328 | tf_op jit(solution)/shard_map/ppermute | solution.py:54
  8.2 0.0 collective-permute-done.1.act1
  8.2 0.6 %acts.1 = bf16[2,240,1536]{2,1,0:T(8,128)(2,1)S(1)} custom-call(bf16[1,6,320,128]{3,2,1,0:T(8,128)(2,1)S(1)} %bitcast.10, bf16[1,6,320,128]{3,2,1,0:T(8,128)(2,1)S(1)} %collective-permute-done.1.act1), custom_call_target="tpu_custom_call" | custom-call | flops 690000000 | tf_op jit(solution)/shard_map/acts/pallas_call | solution.py:61
  8.8 0.0 collective-permute-done.3.top0.bottom0
  8.9 0.4 %collective-permute-done.4.top1.bottom1 = bf16[1,320,128]{2,1,0:T(8,128)(2,1)S(1)} collective-permute-done((bf16[1,320,128]{2,1,0:T(8,128)(2,1)S(1)}, bf16[1,320,128]{2,1,0:T(8,128)(2,1)S(1)}, u32[]{:S(2)}, u32[]{:S(2)}) %collective-permute-start.4) | collective-permute-done | bytes 81952 | tf_op jit(solution)/shard_map/ppermute | solution.py:54
  9.3 0.0 collective-permute-done.2.grad1
  9.3 0.5 %grads.1 = bf16[2,512,1536]{2,1,0:T(8,128)(2,1)S(1)} custom-call(bf16[1,6,320,128]{3,2,1,0:T(8,128)(2,1)S(1)} %get-tuple-element.21.grad0, bf16[1,6,320,128]{3,2,1,0:T(8,128)(2,1)S(1)} %collective-permute-done.2.grad1, bf16[1,320,128]{2,1,0:T(8,128)(2,1)S(1)} %collective-permute-done.3.top0.bottom0, ...), custom_call_target="tpu_custom_call" | custom-call | flops 575000000 | tf_op jit(solution)/shard_map/grads/pallas_call | solution.py:61
  9.7 0.9 %send0.1 = bf16[2,120,512]{2,1,0:T(8,128)(2,1)S(1)} custom-call(bf16[2,240,1536]{2,1,0:T(8,128)(2,1)S(1)} %acts.1, bf16[2,512,1536]{2,1,0:T(8,128)(2,1)S(1)} %grads.1), custom_call_target="tpu_custom_call" | custom-call | flops 1610000000 | tf_op jit(solution)/shard_map/send0/pallas_call | solution.py:61
  10.7 1.1 %collective-permute-start.6 = (bf16[2,120,512]{2,1,0:T(8,128)(2,1)S(1)}, bf16[2,120,512]{2,1,0:T(8,128)(2,1)S(1)}, u32[]{:S(2)}, u32[]{:S(2)}) collective-permute-start(bf16[2,120,512]{2,1,0:T(8,128)(2,1)S(1)} %send0.1), channel_id=1, source_target_pairs={{0,1},{1,0},{2,10},{3,11},{4,5},{5,4},{6,14},{7,15},{8,9},{9,8},{1... | collective-permute-start | bytes 737288 | tf_op jit(solution)/shard_map/ppermute | solution.py:54
  11.8 0.9 %send1.1 = bf16[2,120,512]{2,1,0:T(8,128)(2,1)S(1)} custom-call(bf16[2,240,1536]{2,1,0:T(8,128)(2,1)S(1)} %acts.1, bf16[2,512,1536]{2,1,0:T(8,128)(2,1)S(1)} %grads.1), custom_call_target="tpu_custom_call" | custom-call | flops 1610000000 | tf_op jit(solution)/shard_map/send1/pallas_call | solution.py:61
  12.7 0.8 %keep0.1.keep = f32[2,120,512]{2,1,0:T(8,128)S(1)} custom-call(bf16[2,240,1536]{2,1,0:T(8,128)(2,1)S(1)} %acts.1, bf16[2,512,1536]{2,1,0:T(8,128)(2,1)S(1)} %grads.1), custom_call_target="tpu_custom_call" | custom-call | flops 1150000000 | tf_op jit(solution)/shard_map/keep0/pallas_call | solution.py:61
  13.5 0.0 collective-permute-done.refs_1_
  13.5 1.6 %collective-permute-start.5 = (bf16[1,120,512]{2,1,0:T(8,128)(2,1)S(1)}, bf16[1,120,512]{2,1,0:T(8,128)(2,1)S(1)}, u32[]{:S(2)}, u32[]{:S(2)}) collective-permute-start(bf16[1,120,512]{2,1,0:T(8,128)(2,1)S(1)} %pair.1), channel_id=1, source_target_pairs={{0,4},{1,5},{2,10},{3,11},{4,0},{5,1},{6,14},{7,15},{8,12},{9,13},... | collective-permute-start | bytes 368648 | tf_op jit(solution)/shard_map/ppermute | solution.py:54
  15.1 1.2 %collective-permute-start.8 = (bf16[2,120,512]{2,1,0:T(8,128)(2,1)S(1)}, bf16[2,120,512]{2,1,0:T(8,128)(2,1)S(1)}, u32[]{:S(2)}, u32[]{:S(2)}) collective-permute-start(bf16[2,120,512]{2,1,0:T(8,128)(2,1)S(1)} %send1.1), channel_id=1, source_target_pairs={{0,1},{1,0},{2,10},{3,11},{4,5},{5,4},{6,14},{7,15},{8,9},{9,8},{1... | collective-permute-start | bytes 737288 | tf_op jit(solution)/shard_map/ppermute | solution.py:54
  16.3 0.7 %collective-permute-done.6.message = bf16[2,120,512]{2,1,0:T(8,128)(2,1)S(1)} collective-permute-done((bf16[2,120,512]{2,1,0:T(8,128)(2,1)S(1)}, bf16[2,120,512]{2,1,0:T(8,128)(2,1)S(1)}, u32[]{:S(2)}, u32[]{:S(2)}) %collective-permute-start.6) | collective-permute-done | bytes 245792 | tf_op jit(solution)/shard_map/ppermute | solution.py:54
  16.9 0.5 %turn0.1 = bf16[2,120,512]{2,1,0:T(8,128)(2,1)S(1)} custom-call(f32[2,120,512]{2,1,0:T(8,128)S(1)} %keep0.1.keep, bf16[2,120,512]{2,1,0:T(8,128)(2,1)S(1)} %collective-permute-done.6.message), custom_call_target="tpu_custom_call" | custom-call | flops 1035000000 | tf_op jit(solution)/shard_map/turn0/pallas_call | solution.py:61
  17.4 1.8 %collective-permute-start.9 = (bf16[2,120,512]{2,1,0:T(8,128)(2,1)S(1)}, bf16[2,120,512]{2,1,0:T(8,128)(2,1)S(1)}, u32[]{:S(2)}, u32[]{:S(2)}) collective-permute-start(bf16[2,120,512]{2,1,0:T(8,128)(2,1)S(1)} %turn0.1), channel_id=1, source_target_pairs={{0,4},{1,5},{2,3},{3,2},{4,0},{5,1},{6,7},{7,6},{8,12},{9,13},{10,... | collective-permute-start | bytes 737288 | tf_op jit(solution)/shard_map/ppermute | solution.py:54
  19.2 0.0 collective-permute-done.5
  19.3 1.6 %collective-permute-start.7 = (bf16[2,120,512]{2,1,0:T(8,128)(2,1)S(1)}, bf16[2,120,512]{2,1,0:T(8,128)(2,1)S(1)}, u32[]{:S(2)}, u32[]{:S(2)}) collective-permute-start(bf16[2,120,512]{2,1,0:T(8,128)(2,1)S(1)} %pad_maximum_fusion.1), channel_id=1, source_target_pairs={{0,8},{1,9},{2,3},{3,2},{4,12},{5,13},{6,7},{7,6},{8,0},{9,1},{10,... | collective-permute-start | bytes 737288 | tf_op jit(solution)/shard_map/ppermute | solution.py:54
  20.9 0.7 %keep1.1.keep = f32[2,120,512]{2,1,0:T(8,128)S(1)} custom-call(bf16[2,240,1536]{2,1,0:T(8,128)(2,1)S(1)} %acts.1, bf16[2,512,1536]{2,1,0:T(8,128)(2,1)S(1)} %grads.1), custom_call_target="tpu_custom_call" | custom-call | flops 1150000000 | tf_op jit(solution)/shard_map/keep1/pallas_call | solution.py:61
  21.7 1.6 %collective-permute-done.8.message = bf16[2,120,512]{2,1,0:T(8,128)(2,1)S(1)} collective-permute-done((bf16[2,120,512]{2,1,0:T(8,128)(2,1)S(1)}, bf16[2,120,512]{2,1,0:T(8,128)(2,1)S(1)}, u32[]{:S(2)}, u32[]{:S(2)}) %collective-permute-start.8) | collective-permute-done | bytes 245792 | tf_op jit(solution)/shard_map/ppermute | solution.py:54
  23.3 0.3 turn1.1.keep
  23.6 0.1 collective-permute-done.9.message
  23.7 0.3 part0.1
  24.0 1.9 %collective-permute-start.10 = (bf16[120,512]{1,0:T(8,128)(2,1)S(1)}, bf16[120,512]{1,0:T(8,128)(2,1)S(1)}, u32[]{:S(2)}, u32[]{:S(2)}) collective-permute-start(bf16[120,512]{1,0:T(8,128)(2,1)S(1)} %part0.1), channel_id=1, source_target_pairs={{0,8},{1,9},{2,6},{3,7},{4,12},{5,13},{6,2},{7,3},{8,0},{9,1},{10,... | collective-permute-start | bytes 368648 | tf_op jit(solution)/shard_map/ppermute | solution.py:54
  25.8 0.0 collective-permute-done.7
  25.9 0.9 %collective-permute-start.11 = (bf16[4,120,512]{2,1,0:T(8,128)(2,1)S(1)}, bf16[4,120,512]{2,1,0:T(8,128)(2,1)S(1)}, u32[]{:S(2)}, u32[]{:S(2)}) collective-permute-start(bf16[4,120,512]{2,1,0:T(8,128)(2,1)S(1)} %pad_maximum_fusion.own), channel_id=1, source_target_pairs={{0,1},{1,0},{2,6},{3,7},{4,5},{5,4},{6,2},{7,3},{8,9},{9,8},{10,14... | collective-permute-start | bytes 1474568 | tf_op jit(solution)/shard_map/ppermute | solution.py:54
  26.8 0.2 part1.1.keep
  27.0 1.9 %collective-permute-done.10.message = bf16[120,512]{1,0:T(8,128)(2,1)S(1)} collective-permute-done((bf16[120,512]{1,0:T(8,128)(2,1)S(1)}, bf16[120,512]{1,0:T(8,128)(2,1)S(1)}, u32[]{:S(2)}, u32[]{:S(2)}) %collective-permute-start.10) | collective-permute-done | bytes 122912 | tf_op jit(solution)/shard_map/ppermute | solution.py:54
  28.9 0.2 halve0.1
  29.1 2.9 %collective-permute-start.12 = (bf16[60,512]{1,0:T(8,128)(2,1)S(1)}, bf16[60,512]{1,0:T(8,128)(2,1)S(1)}, u32[]{:S(2)}, u32[]{:S(2)}) collective-permute-start(bf16[60,512]{1,0:T(8,128)(2,1)S(1)} %halve0.1), channel_id=1, source_target_pairs={{0,16},{1,17},{2,18},{3,19},{4,20},{5,21},{6,22},{7,23},{8,24},{9,... | collective-permute-start | bytes 184328 | tf_op jit(solution)/shard_map/ppermute | solution.py:54
  32.0 0.2 halve1.1.keep
  32.2 2.6 %collective-permute-done.11.other = bf16[4,120,512]{2,1,0:T(8,128)(2,1)S(1)} collective-permute-done((bf16[4,120,512]{2,1,0:T(8,128)(2,1)S(1)}, bf16[4,120,512]{2,1,0:T(8,128)(2,1)S(1)}, u32[]{:S(2)}, u32[]{:S(2)}) %collective-permute-start.11) | collective-permute-done | bytes 491552 | tf_op jit(solution)/shard_map/ppermute | solution.py:54
  34.8 1.2 %given.1 = (bf16[1,6,160,128]{3,2,1,0:T(8,128)(2,1)S(1)}, bf16[480,1024]{1,0:T(8,128)(2,1)S(1)}) custom-call(bf16[4,120,512]{2,1,0:T(8,128)(2,1)S(1)} %pad_maximum_fusion.own, bf16[4,120,512]{2,1,0:T(8,128)(2,1)S(1)} %collective-permute-done.11.other, bf16[1024,1536]{1,0:T(8,128)(2,1)S(1)} %bitcast.7), custom_call_target="tpu_custom_call" | custom-call | flops 1380000000 | tf_op jit(solution)/shard_map/given/pallas_call | solution.py:61
  36.0 0.1 collective-permute-start.13
  36.1 0.0 collective-permute-done.12.message
  36.1 1.1 %own.1 = (bf16[1,6,160,128]{3,2,1,0:T(8,128)(2,1)S(1)}, f32[9,20,160]{2,1,0:T(8,128)}) custom-call(bf16[480,1024]{1,0:T(8,128)(2,1)S(1)} %get-tuple-element.37.left, bf16[1024,1536]{1,0:T(8,128)(2,1)S(1)} %bitcast.8, f32[60,512]{1,0:T(8,128)S(1)} %halve1.1.keep, bf16[60,512]{1,0:T(8,128)(2,1)S(1)} %collective-permute-done.12.message), custom_call_target="tpu_custom_call" | custom-call | flops 9200000000 | tf_op jit(solution)/shard_map/own/pallas_call | solution.py:61
  37.2 0.4 %collective-permute-done.13.theirs = bf16[1,6,160,128]{3,2,1,0:T(8,128)(2,1)S(1)} collective-permute-done((bf16[1,6,160,128]{3,2,1,0:T(8,128)(2,1)S(1)}, bf16[1,6,160,128]{3,2,1,0:T(8,128)(2,1)S(1)}, u32[]{:S(2)}, u32[]{:S(2)}) %collective-permute-start.13) | collective-permute-done | bytes 245792 | tf_op jit(solution)/shard_map/ppermute | solution.py:54
  37.6 0.9 %weave.1 = bf16[1,6,320,128]{3,2,1,0:T(8,128)(2,1)} custom-call(bf16[1,6,160,128]{3,2,1,0:T(8,128)(2,1)S(1)} %get-tuple-element.38.own, bf16[1,6,160,128]{3,2,1,0:T(8,128)(2,1)S(1)} %collective-permute-done.13.theirs), custom_call_target="tpu_custom_call" | custom-call | flops 1035000000 | tf_op jit(solution)/shard_map/weave/pallas_call | solution.py:61
  (3 shorter events, 0.1 us)
Async XLA Ops:
  0.6 4.4 %copy-start = (bf16[1,320,6,128]{3,1,2,0:T(8,128)(2,1)S(1)}, bf16[1,320,6,128]{3,1,2,0:T(8,128)(2,1)}, u32[]{:S(2)}) copy-start(bf16[1,320,6,128]{3,1,2,0:T(8,128)(2,1)} %param.3) | copy-start | bytes 1474564
  0.6 4.7 %copy-start.1 = (bf16[20,9,160]{2,0,1:T(8,128)(2,1)S(1)}, bf16[20,9,160]{2,0,1:T(8,128)(2,1)}, u32[]{:S(2)}) copy-start(bf16[20,9,160]{2,0,1:T(8,128)(2,1)} %param.5) | copy-start | bytes 172804
  1.8 7.0 %collective-permute-start.3 = (bf16[1,320,128]{2,1,0:T(8,128)(2,1)S(1)}, bf16[1,320,128]{2,1,0:T(8,128)(2,1)S(1)}, u32[]{:S(2)}, u32[]{:S(2)}) collective-permute-start(bf16[1,320,128]{2,1,0:T(8,128)(2,1)S(1)} %get-tuple-element.22), channel_id=1, source_target_pairs={{0,1},{1,0},{2,3},{3,2},{4,5},{5,4},{6,7},{7,6},{8,9},{9,8},{10,11... | collective-permute-start | bytes 245768 | tf_op jit(solution)/shard_map/ppermute | solution.py:54
  4.8 4.5 %collective-permute-start.4 = (bf16[1,320,128]{2,1,0:T(8,128)(2,1)S(1)}, bf16[1,320,128]{2,1,0:T(8,128)(2,1)S(1)}, u32[]{:S(2)}, u32[]{:S(2)}) collective-permute-start(bf16[1,320,128]{2,1,0:T(8,128)(2,1)S(1)} %get-tuple-element.22), channel_id=1, source_target_pairs={{0,3},{1,2},{2,1},{3,0},{4,7},{5,6},{6,5},{7,4},{8,11},{9,10},{10,... | collective-permute-start | bytes 245768 | tf_op jit(solution)/shard_map/ppermute | solution.py:54
  4.8 4.5 %collective-permute-start.2 = (bf16[1,6,320,128]{3,2,1,0:T(8,128)(2,1)}, bf16[1,6,320,128]{3,2,1,0:T(8,128)(2,1)S(1)}, u32[]{:S(2)}, u32[]{:S(2)}) collective-permute-start(bf16[1,6,320,128]{3,2,1,0:T(8,128)(2,1)} %bitcast.3.grad), channel_id=1, source_target_pairs={{0,2},{1,3},{2,0},{3,1},{4,6},{5,7},{6,4},{7,5},{8,10},{9,11},{10,... | collective-permute-start | bytes 1474568 | tf_op jit(solution)/shard_map/ppermute | solution.py:54
  5.0 3.2 %collective-permute-start.1 = (bf16[1,6,320,128]{3,2,1,0:T(8,128)(2,1)S(1)}, bf16[1,6,320,128]{3,2,1,0:T(8,128)(2,1)S(1)}, u32[]{:S(2)}, u32[]{:S(2)}) collective-permute-start(bf16[1,6,320,128]{3,2,1,0:T(8,128)(2,1)S(1)} %bitcast.9), channel_id=1, source_target_pairs={{0,2},{1,3},{2,0},{3,1},{4,6},{5,7},{6,4},{7,5},{8,10},{9,11},{10,... | collective-permute-start | bytes 1474568 | tf_op jit(solution)/shard_map/ppermute | solution.py:54
  5.4 8.1 %collective-permute-start = (bf16[1,60,512]{2,1,0:T(8,128)(2,1)S(1)}, bf16[1,60,512]{2,1,0:T(8,128)(2,1)S(1)}, u32[]{:S(2)}, u32[]{:S(2)}) collective-permute-start(bf16[1,60,512]{2,1,0:T(8,128)(2,1)S(1)} %bitcast.12), channel_id=1, source_target_pairs={{0,16},{1,17},{2,18},{3,19},{4,20},{5,21},{6,22},{7,23},{8,24},{9,... | collective-permute-start | bytes 184328 | tf_op jit(solution)/shard_map/ppermute | solution.py:54
  10.7 6.3 %collective-permute-start.6 = (bf16[2,120,512]{2,1,0:T(8,128)(2,1)S(1)}, bf16[2,120,512]{2,1,0:T(8,128)(2,1)S(1)}, u32[]{:S(2)}, u32[]{:S(2)}) collective-permute-start(bf16[2,120,512]{2,1,0:T(8,128)(2,1)S(1)} %send0.1), channel_id=1, source_target_pairs={{0,1},{1,0},{2,10},{3,11},{4,5},{5,4},{6,14},{7,15},{8,9},{9,8},{1... | collective-permute-start | bytes 737288 | tf_op jit(solution)/shard_map/ppermute | solution.py:54
  13.5 5.7 %collective-permute-start.5 = (bf16[1,120,512]{2,1,0:T(8,128)(2,1)S(1)}, bf16[1,120,512]{2,1,0:T(8,128)(2,1)S(1)}, u32[]{:S(2)}, u32[]{:S(2)}) collective-permute-start(bf16[1,120,512]{2,1,0:T(8,128)(2,1)S(1)} %pair.1), channel_id=1, source_target_pairs={{0,4},{1,5},{2,10},{3,11},{4,0},{5,1},{6,14},{7,15},{8,12},{9,13},... | collective-permute-start | bytes 368648 | tf_op jit(solution)/shard_map/ppermute | solution.py:54
  15.1 8.2 %collective-permute-start.8 = (bf16[2,120,512]{2,1,0:T(8,128)(2,1)S(1)}, bf16[2,120,512]{2,1,0:T(8,128)(2,1)S(1)}, u32[]{:S(2)}, u32[]{:S(2)}) collective-permute-start(bf16[2,120,512]{2,1,0:T(8,128)(2,1)S(1)} %send1.1), channel_id=1, source_target_pairs={{0,1},{1,0},{2,10},{3,11},{4,5},{5,4},{6,14},{7,15},{8,9},{9,8},{1... | collective-permute-start | bytes 737288 | tf_op jit(solution)/shard_map/ppermute | solution.py:54
  17.4 6.3 %collective-permute-start.9 = (bf16[2,120,512]{2,1,0:T(8,128)(2,1)S(1)}, bf16[2,120,512]{2,1,0:T(8,128)(2,1)S(1)}, u32[]{:S(2)}, u32[]{:S(2)}) collective-permute-start(bf16[2,120,512]{2,1,0:T(8,128)(2,1)S(1)} %turn0.1), channel_id=1, source_target_pairs={{0,4},{1,5},{2,3},{3,2},{4,0},{5,1},{6,7},{7,6},{8,12},{9,13},{10,... | collective-permute-start | bytes 737288 | tf_op jit(solution)/shard_map/ppermute | solution.py:54
  19.3 6.6 %collective-permute-start.7 = (bf16[2,120,512]{2,1,0:T(8,128)(2,1)S(1)}, bf16[2,120,512]{2,1,0:T(8,128)(2,1)S(1)}, u32[]{:S(2)}, u32[]{:S(2)}) collective-permute-start(bf16[2,120,512]{2,1,0:T(8,128)(2,1)S(1)} %pad_maximum_fusion.1), channel_id=1, source_target_pairs={{0,8},{1,9},{2,3},{3,2},{4,12},{5,13},{6,7},{7,6},{8,0},{9,1},{10,... | collective-permute-start | bytes 737288 | tf_op jit(solution)/shard_map/ppermute | solution.py:54
  24.0 4.9 %collective-permute-start.10 = (bf16[120,512]{1,0:T(8,128)(2,1)S(1)}, bf16[120,512]{1,0:T(8,128)(2,1)S(1)}, u32[]{:S(2)}, u32[]{:S(2)}) collective-permute-start(bf16[120,512]{1,0:T(8,128)(2,1)S(1)} %part0.1), channel_id=1, source_target_pairs={{0,8},{1,9},{2,6},{3,7},{4,12},{5,13},{6,2},{7,3},{8,0},{9,1},{10,... | collective-permute-start | bytes 368648 | tf_op jit(solution)/shard_map/ppermute | solution.py:54
  25.9 8.9 %collective-permute-start.11 = (bf16[4,120,512]{2,1,0:T(8,128)(2,1)S(1)}, bf16[4,120,512]{2,1,0:T(8,128)(2,1)S(1)}, u32[]{:S(2)}, u32[]{:S(2)}) collective-permute-start(bf16[4,120,512]{2,1,0:T(8,128)(2,1)S(1)} %pad_maximum_fusion.own), channel_id=1, source_target_pairs={{0,1},{1,0},{2,6},{3,7},{4,5},{5,4},{6,2},{7,3},{8,9},{9,8},{10,14... | collective-permute-start | bytes 1474568 | tf_op jit(solution)/shard_map/ppermute | solution.py:54
  29.1 6.9 %collective-permute-start.12 = (bf16[60,512]{1,0:T(8,128)(2,1)S(1)}, bf16[60,512]{1,0:T(8,128)(2,1)S(1)}, u32[]{:S(2)}, u32[]{:S(2)}) collective-permute-start(bf16[60,512]{1,0:T(8,128)(2,1)S(1)} %halve0.1), channel_id=1, source_target_pairs={{0,16},{1,17},{2,18},{3,19},{4,20},{5,21},{6,22},{7,23},{8,24},{9,... | collective-permute-start | bytes 184328 | tf_op jit(solution)/shard_map/ppermute | solution.py:54
  36.0 1.6 %collective-permute-start.13 = (bf16[1,6,160,128]{3,2,1,0:T(8,128)(2,1)S(1)}, bf16[1,6,160,128]{3,2,1,0:T(8,128)(2,1)S(1)}, u32[]{:S(2)}, u32[]{:S(2)}) collective-permute-start(bf16[1,6,160,128]{3,2,1,0:T(8,128)(2,1)S(1)} %get-tuple-element.36), channel_id=1, source_target_pairs={{0,2},{1,3},{2,0},{3,1},{4,6},{5,7},{6,4},{7,5},{8,10},{9,11},{10,... | collective-permute-start | bytes 737288 | tf_op jit(solution)/shard_map/ppermute | solution.py:54

commit v11 on v10

--- a/solution.py
+++ b/solution.py
@@ -32,11 +32,10 @@
     "halve0": 0.5,
     "halve1": 3.0,
     "given": 1.2,
-    "own": 8.0,
+    "own": 1.0,
+    "last": 8.0,
     "weave": 0.9,
 }
-GATHER_STEPS = ("keep0", "turn0", "part0")
-CELLS_STEP = "halve1"
 FLOPS_PER_US = 1.15e9
 
 
@@ -133,7 +132,7 @@
         self.cells = 2 * images * rows * width
         by_row, by_next, by_col = (2, 0), (4, 0), (0, self.top_strip)
         self.term_masks = ((by_col, by_next), (by_row, by_col), (by_next, by_row))
-        self.gather_masks = ((by_row, by_next), (by_next, by_col), (by_col, by_row))
+        self.gather_masks = ((by_next, by_row), (by_col, by_next), (by_row, by_col))
 
     def block_of(self, slot, by_next, by_row):
         bits = self.band_bits - 3
@@ -281,7 +280,7 @@
             out[n, h] = total.astype(jnp.bfloat16)
 
 
-def given_kernel(plan, own, other, grads, out, left):
+def given_kernel(plan, own, third, last0, last1, grads, out, left):
     core, row_bit, next_bit, col_bit = place(plan)
     rest = lax.axis_index("band") // 8
     depth, half, lanes = plan.depth, plan.half, plan.half_lanes
@@ -289,11 +288,11 @@
         rows = [[] for _ in TAP_STEPS]
         for m in range(plan.blocks):
             row, behind, col = (m % 2) ^ row_bit, (m // 2 % 2) ^ next_bit, x ^ col_bit
-            one = jnp.where(core == 0, row, behind)
-            two = jnp.where(core == 0, behind, col)
-            three = jnp.where(core == 0, col, row)
-            slot = two * 2 + one
-            pair = jnp.where(three == 0, own[slot], other[slot]).astype(jnp.float32)
+            one = jnp.where(core == 0, behind, row)
+            two = jnp.where(core == 0, col, behind)
+            three = jnp.where(core == 0, row, col)
+            before = jnp.where(two == 0, own[one], third[one])
+            pair = jnp.where(three == 0, before, jnp.where(two == 0, last0[one], last1[one])).astype(jnp.float32)
             block = pair[: plan.block_rows]
             for k in range(1, plan.inner):
                 at = pair[k * plan.block_rows : (k + 1) * plan.block_rows]
@@ -307,16 +306,16 @@
     cells_of(plan, 1, left, grads, out)
 
 
-def own_kernel(plan, scale, left, grads, keep, message, out, far, terms, sem):
+def own_kernel(plan, left, grads, out):
+    cells_of(plan, 0, left, grads, out)
+
+
+def last_kernel(plan, scale, keep, message, out):
     total = added(keep[...], message[...])[0] * scale
     depth, cols = plan.depth, plan.cols
     for r in range(len(TAP_STEPS)):
         for c in range(len(TAP_STEPS)):
-            terms[r * len(TAP_STEPS) + c] = total[c * depth : (c + 1) * depth, r * cols : (r + 1) * cols]
-    copy = pltpu.make_async_copy(terms, far, sem)
-    copy.start()
-    cells_of(plan, 0, left, grads, out)
-    copy.wait()
+            out[r * len(TAP_STEPS) + c] = total[c * depth : (c + 1) * depth, r * cols : (r + 1) * cols]
 
 
 def weave_kernel(plan, own, theirs, far, out, sems):
@@ -354,10 +353,9 @@
     return [packed] + [swap(packed, plan.sizes, (mask, 0)) for mask in plan.rest_band[:1]]
 
 
-def whole_kernel(plan, packed, starts):
+def more_kernel(plan, packed, start, end, last):
     sizes = plan.sizes
-    starts = list(starts)
-    packed = [*packed[:-1], after(packed[-1], starts[0])]
+    packed = [*packed[:-1], after(packed[-1], start)]
     if plan.rest_strip:
         packed = jnp.concatenate(packed, axis=0)[None]
         for mask in reversed(plan.rest_strip):
@@ -369,12 +367,11 @@
         packed = packed.transpose(1, 2, 3, 0, 4).reshape(plan.inner, plan.block_rows, plan.half_used)
         packed = [jnp.pad(packed, ((0, 0), (0, 0), (0, plan.half_lanes - plan.half_used)))]
     shape = jax.ShapeDtypeStruct((1, plan.part_rows, plan.half_lanes), jnp.bfloat16)
-    packed = call("pair", functools.partial(pair_kernel, plan), shape, packed)
-    packed = after(packed, starts.pop(0))
-    for masks in plan.gather_masks[:-1]:
-        come = after(swap(packed, sizes, *masks), starts[0])
-        packed = after(jnp.concatenate([packed, come], axis=0), starts.pop(0))
-    return packed, swap(packed, sizes, *plan.gather_masks[-1])
+    packed = after(call("pair", functools.partial(pair_kernel, plan), shape, packed), start)
+    come = after(swap(packed, sizes, *plan.gather_masks[0]), end)
+    packed = after(jnp.concatenate([packed, come], axis=0), end)
+    third = swap(packed, sizes, *plan.gather_masks[1])
+    return packed, third, swap(after(packed, last), sizes, *plan.gather_masks[2])
 
 
 def narrowed(plan, total):
@@ -390,7 +387,7 @@
     return noted(largest(total), jnp.pad(total, ((0, 0), (0, plan.lanes - plan.used))), plan.used)
 
 
-def kernel_terms(plan, acts, grads):
+def kernel_terms(plan, acts, grads, packed):
     sizes, f32 = plan.sizes, jnp.float32
     rows, lanes = plan.part_rows, plan.half_lanes
 
@@ -409,11 +406,11 @@
     come = swap(send, sizes, *plan.term_masks[1])
     keep1 = run("keep1", part(keep_kernel, plan, True), shape, f32, [after(acts, send), grads])
     keep = run("turn1", part(turn_kernel, plan, True), shape, f32, [keep1, come1])
-    steps = {"send0": send0, "send1": send1, "keep0": keep0, "turn0": send, "keep1": keep1, "turn1": keep}
+    packed, third, last0 = more_kernel(plan, packed, keep0, send, keep1)
     shape = shape[1:]
     send = run("part0", part(part_kernel, plan, False), shape, b16, [keep, come])
+    last1 = swap(after(third, send), sizes, *plan.gather_masks[2])
     keep = run("part1", part(part_kernel, plan, True), shape, f32, [after(keep, send), come])
-    steps.update(part0=send, part1=keep)
     come = swap(send, sizes, *plan.term_masks[2])
     if plan.rest_strip:
         keep = narrowed(plan, added(keep, come)[0])
@@ -423,10 +420,9 @@
         shape = (rows, plan.lanes)
         halve = part(halve_kernel, plan, mask, plan.used)
         send = run("halve0", part(halve, False), shape, b16, [keep, come])
-        keep = run("halve1", part(halve, True), shape, f32, [after(keep, send), come])
-        steps.update(halve0=send, halve1=keep)
+        keep = run("halve1", part(halve, True), shape, f32, [after(keep, send, last0), come])
         come = swap(send, sizes, (mask, 0))
-    return keep, come, steps
+    return keep, come, (packed, third, last0, after(last1, keep))
 
 
 def edge_kernel(plan, grad, out, copy):
@@ -474,8 +470,7 @@
         jax.ShapeDtypeStruct(shape, grad.dtype),
         [grad0, grad1, *tops, *bottoms],
     )
-    keep, come, steps = kernel_terms(plan, acts, grads)
-    packed = whole_kernel(plan, packed, [steps[name] for name in GATHER_STEPS])
+    keep, come, packed = kernel_terms(plan, acts, grads, packed)
     shape = jax.ShapeDtypeStruct((images, rows, plan.half, width), jnp.bfloat16)
     left = jax.ShapeDtypeStruct((len(TAP_STEPS) * plan.half, 2 * plan.half_lanes), jnp.bfloat16)
     grads = grads.reshape(2 * plan.half_lanes, plan.cells)
@@ -483,17 +478,9 @@
         "given",
         functools.partial(given_kernel, plan),
         (shape, left),
-        [after(packed[0], steps[CELLS_STEP]), packed[1], grads],
+        [*packed, grads],
     )
-    terms = (len(TAP_STEPS) ** 2, plan.depth, plan.cols)
-    own, kernel_grad = call(
-        "own",
-        functools.partial(own_kernel, plan, scale),
-        (shape, jax.ShapeDtypeStruct(terms, jnp.float32)),
-        [after(left, given), grads, keep, come],
-        [pltpu.VMEM(terms, jnp.float32), pltpu.SemaphoreType.DMA(())],
-        far=1,
-    )
+    own = call("own", functools.partial(own_kernel, plan), shape, [after(left, given), grads])
     theirs = swap(given, plan.sizes, (1, 0))
     shape = (images, rows, channels, width)
     input_grad = call(
@@ -504,6 +491,8 @@
         [pltpu.VMEM(shape, jnp.bfloat16), pltpu.SemaphoreType.DMA((images, rows))],
         far=1,
     )[0]
+    shape = jax.ShapeDtypeStruct((len(TAP_STEPS) ** 2, plan.depth, plan.cols), jnp.float32)
+    kernel_grad = call("last", functools.partial(last_kernel, plan, scale), shape, [keep, come])
     return input_grad.transpose(0, 2, 1, 3), kernel_grad.transpose(1, 0, 2)
 
 

time: 38.6 us -> 39.2 us (1.016)
  waiting for transfers between devices: 7.73 us -> 5.54 us
  starting transfers between devices: 19.4 us -> 21.3 us
  Pallas kernels: 10.4 us -> 11.4 us
    ppermute x14 -> x15, waiting for transfers between devices: 7.73 us -> 5.54 us  [swap(): return lax.ppermute(value, AXES, pairs)]
    ppermute x14 -> x15, starting transfers between devices: 19.4 us -> 21.3 us  [swap(): return lax.ppermute(value, AXES, pairs)]
    pallas_call x18 -> x19, Pallas kernels: 10.4 us -> 11.4 us  [call(): pl.pallas_call(kernel, out_shape=out_shape, in_specs=[pl.BlockSpec(memory...]
  transfers between devices with their start and end apart: 14 -> 15, of which waited for: 7 -> 4; matrix products, arithmetic and copies ran while one was open for 0% -> 0% of each run, Pallas kernels for 22% -> 24%
where the time goes in v11:
time: 39.2 us; the launch traced here: 39.1 us
  starting transfers between devices  21.3 us (54%)
  Pallas kernels  11.4 us (29%)
  waiting for transfers between devices  5.54 us (14%)
  between operations  0.83 us (2%)
    ppermute x15, starting transfers between devices, swap(): return lax.ppermute(value, AXES, pairs)  21.3 us
    pallas_call x19, Pallas kernels, call(): pl.pallas_call(kernel, out_shape=out_shape, in_specs=[pl.BlockSpec(memory...  11.4 us
    ppermute x15, waiting for transfers between devices, swap(): return lax.ppermute(value, AXES, pairs)  5.54 us
  transfers between devices with their start and end apart: 15, of which 4 were waited for; matrix products, arithmetic and copies ran while one was open for 0% of the time, Pallas kernels for 24%

profile of v11, /device:TPU:0, one launch (start us, length us, event | category | flops | bytes accessed | tf_op | source)
XLA Modules:
  0.0 39.1 jit_solution(3319034686909676551)
XLA Ops:
  0.6 0.0 copy-start
  0.6 0.0 copy-start.1
  0.6 1.1 %edge.1 = (bf16[1,320,128]{2,1,0:T(8,128)(2,1)S(1)}, bf16[1,6,320,128]{3,2,1,0:T(8,128)(2,1)S(1)}) custom-call(bf16[1,6,320,128]{3,2,1,0:T(8,128)(2,1)} %bitcast.3.grad), custom_call_target="tpu_custom_call" | custom-call | flops 9200000000 | tf_op jit(solution)/shard_map/edge/pallas_call | solution.py:60
  1.8 3.0 %collective-permute-start.3 = (bf16[1,320,128]{2,1,0:T(8,128)(2,1)S(1)}, bf16[1,320,128]{2,1,0:T(8,128)(2,1)S(1)}, u32[]{:S(2)}, u32[]{:S(2)}) collective-permute-start(bf16[1,320,128]{2,1,0:T(8,128)(2,1)S(1)} %get-tuple-element.20), channel_id=1, source_target_pairs={{0,1},{1,0},{2,3},{3,2},{4,5},{5,4},{6,7},{7,6},{8,9},{9,8},{10,11... | collective-permute-start | bytes 245768 | tf_op jit(solution)/shard_map/ppermute | solution.py:53
  4.8 0.0 collective-permute-start.4
  4.8 0.2 collective-permute-start.2
  5.0 0.0 copy-done
  5.0 0.3 collective-permute-start.1
  5.3 0.0 copy-done.1
  5.3 0.1 pack.1
  5.4 2.8 %collective-permute-start = (bf16[1,60,512]{2,1,0:T(8,128)(2,1)S(1)}, bf16[1,60,512]{2,1,0:T(8,128)(2,1)S(1)}, u32[]{:S(2)}, u32[]{:S(2)}) collective-permute-start(bf16[1,60,512]{2,1,0:T(8,128)(2,1)S(1)} %bitcast.12), channel_id=1, source_target_pairs={{0,16},{1,17},{2,18},{3,19},{4,20},{5,21},{6,22},{7,23},{8,24},{9,... | collective-permute-start | bytes 184328 | tf_op jit(solution)/shard_map/ppermute | solution.py:53
  8.2 0.0 collective-permute-done.1.act1
  8.2 0.6 %acts.1 = bf16[2,240,1536]{2,1,0:T(8,128)(2,1)S(1)} custom-call(bf16[1,6,320,128]{3,2,1,0:T(8,128)(2,1)S(1)} %bitcast.10, bf16[1,6,320,128]{3,2,1,0:T(8,128)(2,1)S(1)} %collective-permute-done.1.act1), custom_call_target="tpu_custom_call" | custom-call | flops 690000000 | tf_op jit(solution)/shard_map/acts/pallas_call | solution.py:60
  8.8 0.0 collective-permute-done.3.top0.bottom0
  8.9 0.4 %collective-permute-done.4.top1.bottom1 = bf16[1,320,128]{2,1,0:T(8,128)(2,1)S(1)} collective-permute-done((bf16[1,320,128]{2,1,0:T(8,128)(2,1)S(1)}, bf16[1,320,128]{2,1,0:T(8,128)(2,1)S(1)}, u32[]{:S(2)}, u32[]{:S(2)}) %collective-permute-start.4) | collective-permute-done | bytes 81952 | tf_op jit(solution)/shard_map/ppermute | solution.py:53
  9.3 0.0 collective-permute-done.2.grad1
  9.3 0.5 %grads.1 = bf16[2,512,1536]{2,1,0:T(8,128)(2,1)S(1)} custom-call(bf16[1,6,320,128]{3,2,1,0:T(8,128)(2,1)S(1)} %get-tuple-element.19.grad0, bf16[1,6,320,128]{3,2,1,0:T(8,128)(2,1)S(1)} %collective-permute-done.2.grad1, bf16[1,320,128]{2,1,0:T(8,128)(2,1)S(1)} %collective-permute-done.3.top0.bottom0, ...), custom_call_target="tpu_custom_call" | custom-call | flops 575000000 | tf_op jit(solution)/shard_map/grads/pallas_call | solution.py:60
  9.7 0.9 %send0.1 = bf16[2,120,512]{2,1,0:T(8,128)(2,1)S(1)} custom-call(bf16[2,240,1536]{2,1,0:T(8,128)(2,1)S(1)} %acts.1, bf16[2,512,1536]{2,1,0:T(8,128)(2,1)S(1)} %grads.1), custom_call_target="tpu_custom_call" | custom-call | flops 1610000000 | tf_op jit(solution)/shard_map/send0/pallas_call | solution.py:60
  10.7 1.1 %collective-permute-start.6 = (bf16[2,120,512]{2,1,0:T(8,128)(2,1)S(1)}, bf16[2,120,512]{2,1,0:T(8,128)(2,1)S(1)}, u32[]{:S(2)}, u32[]{:S(2)}) collective-permute-start(bf16[2,120,512]{2,1,0:T(8,128)(2,1)S(1)} %send0.1), channel_id=1, source_target_pairs={{0,1},{1,0},{2,10},{3,11},{4,5},{5,4},{6,14},{7,15},{8,9},{9,8},{1... | collective-permute-start | bytes 737288 | tf_op jit(solution)/shard_map/ppermute | solution.py:53
  11.8 0.9 %send1.1 = bf16[2,120,512]{2,1,0:T(8,128)(2,1)S(1)} custom-call(bf16[2,240,1536]{2,1,0:T(8,128)(2,1)S(1)} %acts.1, bf16[2,512,1536]{2,1,0:T(8,128)(2,1)S(1)} %grads.1), custom_call_target="tpu_custom_call" | custom-call | flops 1610000000 | tf_op jit(solution)/shard_map/send1/pallas_call | solution.py:60
  12.7 0.8 %keep0.1.keep = f32[2,120,512]{2,1,0:T(8,128)S(1)} custom-call(bf16[2,240,1536]{2,1,0:T(8,128)(2,1)S(1)} %acts.1, bf16[2,512,1536]{2,1,0:T(8,128)(2,1)S(1)} %grads.1), custom_call_target="tpu_custom_call" | custom-call | flops 1150000000 | tf_op jit(solution)/shard_map/keep0/pallas_call | solution.py:60
  13.5 0.0 collective-permute-done.refs_1_
  13.5 1.6 %collective-permute-start.5 = (bf16[1,120,512]{2,1,0:T(8,128)(2,1)S(1)}, bf16[1,120,512]{2,1,0:T(8,128)(2,1)S(1)}, u32[]{:S(2)}, u32[]{:S(2)}) collective-permute-start(bf16[1,120,512]{2,1,0:T(8,128)(2,1)S(1)} %pair.1), channel_id=1, source_target_pairs={{0,8},{1,9},{2,6},{3,7},{4,12},{5,13},{6,2},{7,3},{8,0},{9,1},{10,... | collective-permute-start | bytes 368648 | tf_op jit(solution)/shard_map/ppermute | solution.py:53
  15.2 1.2 %collective-permute-start.9 = (bf16[2,120,512]{2,1,0:T(8,128)(2,1)S(1)}, bf16[2,120,512]{2,1,0:T(8,128)(2,1)S(1)}, u32[]{:S(2)}, u32[]{:S(2)}) collective-permute-start(bf16[2,120,512]{2,1,0:T(8,128)(2,1)S(1)} %send1.1), channel_id=1, source_target_pairs={{0,1},{1,0},{2,10},{3,11},{4,5},{5,4},{6,14},{7,15},{8,9},{9,8},{1... | collective-permute-start | bytes 737288 | tf_op jit(solution)/shard_map/ppermute | solution.py:53
  16.3 0.6 %collective-permute-done.6.message = bf16[2,120,512]{2,1,0:T(8,128)(2,1)S(1)} collective-permute-done((bf16[2,120,512]{2,1,0:T(8,128)(2,1)S(1)}, bf16[2,120,512]{2,1,0:T(8,128)(2,1)S(1)}, u32[]{:S(2)}, u32[]{:S(2)}) %collective-permute-start.6) | collective-permute-done | bytes 245792 | tf_op jit(solution)/shard_map/ppermute | solution.py:53
  16.9 0.5 %turn0.1 = bf16[2,120,512]{2,1,0:T(8,128)(2,1)S(1)} custom-call(f32[2,120,512]{2,1,0:T(8,128)S(1)} %keep0.1.keep, bf16[2,120,512]{2,1,0:T(8,128)(2,1)S(1)} %collective-permute-done.6.message), custom_call_target="tpu_custom_call" | custom-call | flops 1035000000 | tf_op jit(solution)/shard_map/turn0/pallas_call | solution.py:60
  17.4 1.8 %collective-permute-start.10 = (bf16[2,120,512]{2,1,0:T(8,128)(2,1)S(1)}, bf16[2,120,512]{2,1,0:T(8,128)(2,1)S(1)}, u32[]{:S(2)}, u32[]{:S(2)}) collective-permute-start(bf16[2,120,512]{2,1,0:T(8,128)(2,1)S(1)} %turn0.1), channel_id=1, source_target_pairs={{0,4},{1,5},{2,3},{3,2},{4,0},{5,1},{6,7},{7,6},{8,12},{9,13},{10,... | collective-permute-start | bytes 737288 | tf_op jit(solution)/shard_map/ppermute | solution.py:53
  19.2 0.0 collective-permute-done.5
  19.3 0.9 %collective-permute-start.7 = (bf16[2,120,512]{2,1,0:T(8,128)(2,1)S(1)}, bf16[2,120,512]{2,1,0:T(8,128)(2,1)S(1)}, u32[]{:S(2)}, u32[]{:S(2)}) collective-permute-start(bf16[2,120,512]{2,1,0:T(8,128)(2,1)S(1)} %pad_maximum_fusion.own), channel_id=1, source_target_pairs={{0,1},{1,0},{2,10},{3,11},{4,5},{5,4},{6,14},{7,15},{8,9},{9,8},{1... | collective-permute-start | bytes 737288 | tf_op jit(solution)/shard_map/ppermute | solution.py:53
  20.2 0.7 %keep1.1.keep = f32[2,120,512]{2,1,0:T(8,128)S(1)} custom-call(bf16[2,240,1536]{2,1,0:T(8,128)(2,1)S(1)} %acts.1, bf16[2,512,1536]{2,1,0:T(8,128)(2,1)S(1)} %grads.1), custom_call_target="tpu_custom_call" | custom-call | flops 1150000000 | tf_op jit(solution)/shard_map/keep1/pallas_call | solution.py:60
  20.9 2.4 %collective-permute-start.8 = (bf16[2,120,512]{2,1,0:T(8,128)(2,1)S(1)}, bf16[2,120,512]{2,1,0:T(8,128)(2,1)S(1)}, u32[]{:S(2)}, u32[]{:S(2)}) collective-permute-start(bf16[2,120,512]{2,1,0:T(8,128)(2,1)S(1)} %pad_maximum_fusion.own), channel_id=1, source_target_pairs={{0,4},{1,5},{2,3},{3,2},{4,0},{5,1},{6,7},{7,6},{8,12},{9,13},{10,... | collective-permute-start | bytes 737288 | tf_op jit(solution)/shard_map/ppermute | solution.py:53
  23.4 0.0 collective-permute-done.9.message
  23.4 0.3 turn1.1.keep
  23.7 0.0 collective-permute-done.10.message
  23.7 0.3 part0.1
  24.0 1.8 %collective-permute-start.12 = (bf16[120,512]{1,0:T(8,128)(2,1)S(1)}, bf16[120,512]{1,0:T(8,128)(2,1)S(1)}, u32[]{:S(2)}, u32[]{:S(2)}) collective-permute-start(bf16[120,512]{1,0:T(8,128)(2,1)S(1)} %part0.1), channel_id=1, source_target_pairs={{0,8},{1,9},{2,6},{3,7},{4,12},{5,13},{6,2},{7,3},{8,0},{9,1},{10,... | collective-permute-start | bytes 368648 | tf_op jit(solution)/shard_map/ppermute | solution.py:53
  25.8 2.8 %collective-permute-done.7.third = bf16[2,120,512]{2,1,0:T(8,128)(2,1)S(1)} collective-permute-done((bf16[2,120,512]{2,1,0:T(8,128)(2,1)S(1)}, bf16[2,120,512]{2,1,0:T(8,128)(2,1)S(1)}, u32[]{:S(2)}, u32[]{:S(2)}) %collective-permute-start.7) | collective-permute-done | bytes 245792 | tf_op jit(solution)/shard_map/ppermute | solution.py:53
  28.7 1.6 %collective-permute-start.11 = (bf16[2,120,512]{2,1,0:T(8,128)(2,1)S(1)}, bf16[2,120,512]{2,1,0:T(8,128)(2,1)S(1)}, u32[]{:S(2)}, u32[]{:S(2)}) collective-permute-start(bf16[2,120,512]{2,1,0:T(8,128)(2,1)S(1)} %collective-permute-done.7.third), channel_id=1, source_target_pairs={{0,4},{1,5},{2,3},{3,2},{4,0},{5,1},{6,7},{7,6},{8,12},{9,13},{10,... | collective-permute-start | bytes 737288 | tf_op jit(solution)/shard_map/ppermute | solution.py:53
  30.3 0.2 part1.1.keep
  30.5 0.0 collective-permute-done.12.message
  30.5 0.2 halve0.1
  30.7 2.3 %collective-permute-start.14 = (bf16[60,512]{1,0:T(8,128)(2,1)S(1)}, bf16[60,512]{1,0:T(8,128)(2,1)S(1)}, u32[]{:S(2)}, u32[]{:S(2)}) collective-permute-start(bf16[60,512]{1,0:T(8,128)(2,1)S(1)} %halve0.1), channel_id=1, source_target_pairs={{0,16},{1,17},{2,18},{3,19},{4,20},{5,21},{6,22},{7,23},{8,24},{9,... | collective-permute-start | bytes 184328 | tf_op jit(solution)/shard_map/ppermute | solution.py:53
  33.0 0.0 collective-permute-done.8.last0
  33.0 0.2 halve1.1.keep
  33.2 1.6 %collective-permute-done.11.last1 = bf16[2,120,512]{2,1,0:T(8,128)(2,1)S(1)} collective-permute-done((bf16[2,120,512]{2,1,0:T(8,128)(2,1)S(1)}, bf16[2,120,512]{2,1,0:T(8,128)(2,1)S(1)}, u32[]{:S(2)}, u32[]{:S(2)}) %collective-permute-start.11) | collective-permute-done | bytes 245792 | tf_op jit(solution)/shard_map/ppermute | solution.py:53
  34.9 1.3 %given.1 = (bf16[1,6,160,128]{3,2,1,0:T(8,128)(2,1)S(1)}, bf16[480,1024]{1,0:T(8,128)(2,1)S(1)}) custom-call(bf16[2,120,512]{2,1,0:T(8,128)(2,1)S(1)} %pad_maximum_fusion.own, bf16[2,120,512]{2,1,0:T(8,128)(2,1)S(1)} %collective-permute-done.7.third, bf16[2,120,512]{2,1,0:T(8,128)(2,1)S(1)} %collective-permute-done.8.last0, ...), custom_call_target="tpu_custom_call" | custom-call | flops 1380000000 | tf_op jit(solution)/shard_map/given/pallas_call | solution.py:60
  36.1 0.1 collective-permute-start.13
  36.2 0.0 collective-permute-done.14.message
  36.2 0.9 %last.1 = f32[9,20,160]{2,1,0:T(8,128)} custom-call(f32[60,512]{1,0:T(8,128)S(1)} %halve1.1.keep, bf16[60,512]{1,0:T(8,128)(2,1)S(1)} %collective-permute-done.14.message), custom_call_target="tpu_custom_call" | custom-call | flops 9200000000 | tf_op jit(solution)/shard_map/last/pallas_call | solution.py:60
  37.1 1.0 %own.1 = bf16[1,6,160,128]{3,2,1,0:T(8,128)(2,1)S(1)} custom-call(bf16[480,1024]{1,0:T(8,128)(2,1)S(1)} %get-tuple-element.35.left, bf16[1024,1536]{1,0:T(8,128)(2,1)S(1)} %bitcast.8), custom_call_target="tpu_custom_call" | custom-call | flops 1150000000 | tf_op jit(solution)/shard_map/own/pallas_call | solution.py:60
  38.2 0.0 collective-permute-done.13.theirs
  38.2 0.9 %weave.1 = bf16[1,6,320,128]{3,2,1,0:T(8,128)(2,1)} custom-call(bf16[1,6,160,128]{3,2,1,0:T(8,128)(2,1)S(1)} %own.1, bf16[1,6,160,128]{3,2,1,0:T(8,128)(2,1)S(1)} %collective-permute-done.13.theirs), custom_call_target="tpu_custom_call" | custom-call | flops 1035000000 | tf_op jit(solution)/shard_map/weave/pallas_call | solution.py:60
  (2 shorter events, 0.0 us)
Async XLA Ops:
  0.6 4.4 %copy-start = (bf16[1,320,6,128]{3,1,2,0:T(8,128)(2,1)S(1)}, bf16[1,320,6,128]{3,1,2,0:T(8,128)(2,1)}, u32[]{:S(2)}) copy-start(bf16[1,320,6,128]{3,1,2,0:T(8,128)(2,1)} %param.3) | copy-start | bytes 1474564
  0.6 4.7 %copy-start.1 = (bf16[20,9,160]{2,0,1:T(8,128)(2,1)S(1)}, bf16[20,9,160]{2,0,1:T(8,128)(2,1)}, u32[]{:S(2)}) copy-start(bf16[20,9,160]{2,0,1:T(8,128)(2,1)} %param.5) | copy-start | bytes 172804
  1.8 7.0 %collective-permute-start.3 = (bf16[1,320,128]{2,1,0:T(8,128)(2,1)S(1)}, bf16[1,320,128]{2,1,0:T(8,128)(2,1)S(1)}, u32[]{:S(2)}, u32[]{:S(2)}) collective-permute-start(bf16[1,320,128]{2,1,0:T(8,128)(2,1)S(1)} %get-tuple-element.20), channel_id=1, source_target_pairs={{0,1},{1,0},{2,3},{3,2},{4,5},{5,4},{6,7},{7,6},{8,9},{9,8},{10,11... | collective-permute-start | bytes 245768 | tf_op jit(solution)/shard_map/ppermute | solution.py:53
  4.8 4.5 %collective-permute-start.4 = (bf16[1,320,128]{2,1,0:T(8,128)(2,1)S(1)}, bf16[1,320,128]{2,1,0:T(8,128)(2,1)S(1)}, u32[]{:S(2)}, u32[]{:S(2)}) collective-permute-start(bf16[1,320,128]{2,1,0:T(8,128)(2,1)S(1)} %get-tuple-element.20), channel_id=1, source_target_pairs={{0,3},{1,2},{2,1},{3,0},{4,7},{5,6},{6,5},{7,4},{8,11},{9,10},{10,... | collective-permute-start | bytes 245768 | tf_op jit(solution)/shard_map/ppermute | solution.py:53
  4.8 4.5 %collective-permute-start.2 = (bf16[1,6,320,128]{3,2,1,0:T(8,128)(2,1)}, bf16[1,6,320,128]{3,2,1,0:T(8,128)(2,1)S(1)}, u32[]{:S(2)}, u32[]{:S(2)}) collective-permute-start(bf16[1,6,320,128]{3,2,1,0:T(8,128)(2,1)} %bitcast.3.grad), channel_id=1, source_target_pairs={{0,2},{1,3},{2,0},{3,1},{4,6},{5,7},{6,4},{7,5},{8,10},{9,11},{10,... | collective-permute-start | bytes 1474568 | tf_op jit(solution)/shard_map/ppermute | solution.py:53
  5.0 3.2 %collective-permute-start.1 = (bf16[1,6,320,128]{3,2,1,0:T(8,128)(2,1)S(1)}, bf16[1,6,320,128]{3,2,1,0:T(8,128)(2,1)S(1)}, u32[]{:S(2)}, u32[]{:S(2)}) collective-permute-start(bf16[1,6,320,128]{3,2,1,0:T(8,128)(2,1)S(1)} %bitcast.9), channel_id=1, source_target_pairs={{0,2},{1,3},{2,0},{3,1},{4,6},{5,7},{6,4},{7,5},{8,10},{9,11},{10,... | collective-permute-start | bytes 1474568 | tf_op jit(solution)/shard_map/ppermute | solution.py:53
  5.4 8.1 %collective-permute-start = (bf16[1,60,512]{2,1,0:T(8,128)(2,1)S(1)}, bf16[1,60,512]{2,1,0:T(8,128)(2,1)S(1)}, u32[]{:S(2)}, u32[]{:S(2)}) collective-permute-start(bf16[1,60,512]{2,1,0:T(8,128)(2,1)S(1)} %bitcast.12), channel_id=1, source_target_pairs={{0,16},{1,17},{2,18},{3,19},{4,20},{5,21},{6,22},{7,23},{8,24},{9,... | collective-permute-start | bytes 184328 | tf_op jit(solution)/shard_map/ppermute | solution.py:53
  10.7 6.3 %collective-permute-start.6 = (bf16[2,120,512]{2,1,0:T(8,128)(2,1)S(1)}, bf16[2,120,512]{2,1,0:T(8,128)(2,1)S(1)}, u32[]{:S(2)}, u32[]{:S(2)}) collective-permute-start(bf16[2,120,512]{2,1,0:T(8,128)(2,1)S(1)} %send0.1), channel_id=1, source_target_pairs={{0,1},{1,0},{2,10},{3,11},{4,5},{5,4},{6,14},{7,15},{8,9},{9,8},{1... | collective-permute-start | bytes 737288 | tf_op jit(solution)/shard_map/ppermute | solution.py:53
  13.5 5.7 %collective-permute-start.5 = (bf16[1,120,512]{2,1,0:T(8,128)(2,1)S(1)}, bf16[1,120,512]{2,1,0:T(8,128)(2,1)S(1)}, u32[]{:S(2)}, u32[]{:S(2)}) collective-permute-start(bf16[1,120,512]{2,1,0:T(8,128)(2,1)S(1)} %pair.1), channel_id=1, source_target_pairs={{0,8},{1,9},{2,6},{3,7},{4,12},{5,13},{6,2},{7,3},{8,0},{9,1},{10,... | collective-permute-start | bytes 368648 | tf_op jit(solution)/shard_map/ppermute | solution.py:53
  15.2 8.2 %collective-permute-start.9 = (bf16[2,120,512]{2,1,0:T(8,128)(2,1)S(1)}, bf16[2,120,512]{2,1,0:T(8,128)(2,1)S(1)}, u32[]{:S(2)}, u32[]{:S(2)}) collective-permute-start(bf16[2,120,512]{2,1,0:T(8,128)(2,1)S(1)} %send1.1), channel_id=1, source_target_pairs={{0,1},{1,0},{2,10},{3,11},{4,5},{5,4},{6,14},{7,15},{8,9},{9,8},{1... | collective-permute-start | bytes 737288 | tf_op jit(solution)/shard_map/ppermute | solution.py:53
  17.4 6.3 %collective-permute-start.10 = (bf16[2,120,512]{2,1,0:T(8,128)(2,1)S(1)}, bf16[2,120,512]{2,1,0:T(8,128)(2,1)S(1)}, u32[]{:S(2)}, u32[]{:S(2)}) collective-permute-start(bf16[2,120,512]{2,1,0:T(8,128)(2,1)S(1)} %turn0.1), channel_id=1, source_target_pairs={{0,4},{1,5},{2,3},{3,2},{4,0},{5,1},{6,7},{7,6},{8,12},{9,13},{10,... | collective-permute-start | bytes 737288 | tf_op jit(solution)/shard_map/ppermute | solution.py:53
  19.3 9.4 %collective-permute-start.7 = (bf16[2,120,512]{2,1,0:T(8,128)(2,1)S(1)}, bf16[2,120,512]{2,1,0:T(8,128)(2,1)S(1)}, u32[]{:S(2)}, u32[]{:S(2)}) collective-permute-start(bf16[2,120,512]{2,1,0:T(8,128)(2,1)S(1)} %pad_maximum_fusion.own), channel_id=1, source_target_pairs={{0,1},{1,0},{2,10},{3,11},{4,5},{5,4},{6,14},{7,15},{8,9},{9,8},{1... | collective-permute-start | bytes 737288 | tf_op jit(solution)/shard_map/ppermute | solution.py:53
  20.9 12.1 %collective-permute-start.8 = (bf16[2,120,512]{2,1,0:T(8,128)(2,1)S(1)}, bf16[2,120,512]{2,1,0:T(8,128)(2,1)S(1)}, u32[]{:S(2)}, u32[]{:S(2)}) collective-permute-start(bf16[2,120,512]{2,1,0:T(8,128)(2,1)S(1)} %pad_maximum_fusion.own), channel_id=1, source_target_pairs={{0,4},{1,5},{2,3},{3,2},{4,0},{5,1},{6,7},{7,6},{8,12},{9,13},{10,... | collective-permute-start | bytes 737288 | tf_op jit(solution)/shard_map/ppermute | solution.py:53
  24.0 6.5 %collective-permute-start.12 = (bf16[120,512]{1,0:T(8,128)(2,1)S(1)}, bf16[120,512]{1,0:T(8,128)(2,1)S(1)}, u32[]{:S(2)}, u32[]{:S(2)}) collective-permute-start(bf16[120,512]{1,0:T(8,128)(2,1)S(1)} %part0.1), channel_id=1, source_target_pairs={{0,8},{1,9},{2,6},{3,7},{4,12},{5,13},{6,2},{7,3},{8,0},{9,1},{10,... | collective-permute-start | bytes 368648 | tf_op jit(solution)/shard_map/ppermute | solution.py:53
  28.7 6.2 %collective-permute-start.11 = (bf16[2,120,512]{2,1,0:T(8,128)(2,1)S(1)}, bf16[2,120,512]{2,1,0:T(8,128)(2,1)S(1)}, u32[]{:S(2)}, u32[]{:S(2)}) collective-permute-start(bf16[2,120,512]{2,1,0:T(8,128)(2,1)S(1)} %collective-permute-done.7.third), channel_id=1, source_target_pairs={{0,4},{1,5},{2,3},{3,2},{4,0},{5,1},{6,7},{7,6},{8,12},{9,13},{10,... | collective-permute-start | bytes 737288 | tf_op jit(solution)/shard_map/ppermute | solution.py:53
  30.7 5.5 %collective-permute-start.14 = (bf16[60,512]{1,0:T(8,128)(2,1)S(1)}, bf16[60,512]{1,0:T(8,128)(2,1)S(1)}, u32[]{:S(2)}, u32[]{:S(2)}) collective-permute-start(bf16[60,512]{1,0:T(8,128)(2,1)S(1)} %halve0.1), channel_id=1, source_target_pairs={{0,16},{1,17},{2,18},{3,19},{4,20},{5,21},{6,22},{7,23},{8,24},{9,... | collective-permute-start | bytes 184328 | tf_op jit(solution)/shard_map/ppermute | solution.py:53
  36.1 2.0 %collective-permute-start.13 = (bf16[1,6,160,128]{3,2,1,0:T(8,128)(2,1)S(1)}, bf16[1,6,160,128]{3,2,1,0:T(8,128)(2,1)S(1)}, u32[]{:S(2)}, u32[]{:S(2)}) collective-permute-start(bf16[1,6,160,128]{3,2,1,0:T(8,128)(2,1)S(1)} %get-tuple-element.34), channel_id=1, source_target_pairs={{0,2},{1,3},{2,0},{3,1},{4,6},{5,7},{6,4},{7,5},{8,10},{9,11},{10,... | collective-permute-start | bytes 737288 | tf_op jit(solution)/shard_map/ppermute | solution.py:53

commit v12 on v11

--- a/solution.py
+++ b/solution.py
@@ -14,6 +14,7 @@
 TOP_POWER = 2.0**15.5
 LEAST_POWER = 2.0**-126
 LEAST_PEAK = 1e-30
+ROW_FIRST = False
 VMEM_BYTES = 40 * 2**20
 HINTS = {
     "edge": 8.0,
@@ -31,8 +32,9 @@
     "part1": 0.3,
     "halve0": 0.5,
     "halve1": 3.0,
-    "given": 1.2,
-    "own": 1.0,
+    "early": 1.7,
+    "given": 0.5,
+    "own": 0.5,
     "last": 8.0,
     "weave": 0.9,
 }
@@ -132,7 +134,8 @@
         self.cells = 2 * images * rows * width
         by_row, by_next, by_col = (2, 0), (4, 0), (0, self.top_strip)
         self.term_masks = ((by_col, by_next), (by_row, by_col), (by_next, by_row))
-        self.gather_masks = ((by_next, by_row), (by_col, by_next), (by_row, by_col))
+        ones, others = (by_row, by_next) if ROW_FIRST else (by_next, by_row)
+        self.gather_masks = ((ones, others), (others, by_col), (by_col, ones))
 
     def block_of(self, slot, by_next, by_row):
         bits = self.band_bits - 3
@@ -263,51 +266,163 @@
     out[...] = jnp.concatenate(rows, axis=0).astype(jnp.bfloat16)
 
 
-def cells_of(plan, d, left, grads, out):
-    width, half = plan.width, plan.half
+def halves(plan):
+    core, row_bit, next_bit, _ = place(plan)
+    by_row = (core == 0) != ROW_FIRST
+    return jnp.where(by_row, row_bit, next_bit), jnp.where(by_row, next_bit, row_bit)
+
+
+def ordered(plan, blocks):
+    rest = lax.axis_index("band") // 8
+    other_bit = halves(plan)[1]
+    parts = [jnp.where(other_bit == 0, blocks[k], blocks[1 - k]).astype(jnp.float32) for k in range(2)]
+    rows = []
+    for c in range(len(TAP_STEPS)):
+        for k in range(plan.inner):
+            for part in parts:
+                piece = None
+                for at in range(plan.inner):
+                    begin = at * plan.block_rows + c * plan.depth
+                    here = part[begin : begin + plan.depth]
+                    piece = here if piece is None else jnp.where((k ^ rest) == at, here, piece)
+                rows.append(piece)
+    return jnp.concatenate(rows, axis=0).astype(jnp.bfloat16)
+
+
+def summed(plan, product):
+    quarter = plan.half // 2
+    total = None
+    for c, col_step in enumerate(TAP_STEPS):
+        term = moved(product[c * quarter : (c + 1) * quarter], -col_step)
+        total = term if total is None else total + term
+    return total.astype(jnp.bfloat16)
+
+
+def groups(plan):
     rows = [(n, h) for n in range(plan.images) for h in range(plan.rows)]
-    for begin in range(0, len(rows), 2):
-        part = rows[begin : begin + 2]
-        at = (d * len(rows) + begin) * width
-        product = jnp.dot(
-            left[...], grads[:, at : at + len(part) * width], preferred_element_type=jnp.float32
-        )
-        for k, (n, h) in enumerate(part):
-            total = None
-            for c, col_step in enumerate(TAP_STEPS):
-                term = moved(product[c * half : (c + 1) * half, k * width : (k + 1) * width], -col_step)
-                total = term if total is None else total + term
-            out[n, h] = total.astype(jnp.bfloat16)
-
-
-def given_kernel(plan, own, third, last0, last1, grads, out, left):
-    core, row_bit, next_bit, col_bit = place(plan)
+    for d in range(2):
+        for begin in range(0, len(rows), 2):
+            part = rows[begin : begin + 2]
+            at = (d * len(rows) + begin) * plan.width
+            where = [(n, h, slice(k * plan.width, (k + 1) * plan.width)) for k, (n, h) in enumerate(part)]
+            yield d, slice(at, at + len(part) * plan.width), where
+
+
+def early_kernel(plan, own, third, last0, grads, out0, out1, rest):
+    core, _, _, col = place(plan)
+    near, far = ordered(plan, own), [ordered(plan, third), ordered(plan, last0)]
+    beside = jnp.where(core == 0, far[1], far[0])
+    below = jnp.where(core == 0, far[0], far[1])
+    for d, cells, where in groups(plan):
+        here, there = grads[col, :, cells], grads[1 - col, :, cells]
+        product = jnp.dot(near, here, preferred_element_type=jnp.float32)
+        product = product + jnp.dot(beside, there, preferred_element_type=jnp.float32)
+        rest[:, cells] = jnp.dot(below, here, preferred_element_type=jnp.float32)
+        for n, h, lanes in where:
+            (out0, out1)[d][n, h] = summed(plan, product[:, lanes])
+
+
+def late_of(plan, image, left, grads, rest, out):
+    col = place(plan)[3]
+    for d, cells, where in groups(plan):
+        if d == image:
+            product = rest[:, cells]
+            product = product + jnp.dot(left, grads[1 - col, :, cells], preferred_element_type=jnp.float32)
+            for n, h, lanes in where:
+                out[n, h] = summed(plan, product[:, lanes])
+
+
+def given_kernel(plan, last1, grads, rest, out, left):
+    left[...] = ordered(plan, last1)
+    late_of(plan, 1, left[...], grads, rest, out)
+
+
+def own_kernel(plan, left, grads, rest, out):
+    late_of(plan, 0, left[...], grads, rest, out)
+
+
+def pack_kernel(plan, kernel, out):
+    rows = []
+    for c in range(len(TAP_STEPS)):
+        pieces = [kernel[r * len(TAP_STEPS) + c].astype(jnp.float32) for r in range(len(TAP_STEPS))]
+        pieces.append(jnp.zeros((plan.depth, plan.lanes - plan.used), jnp.float32))
+        rows.append(jnp.concatenate(pieces, axis=1))
+    out[...] = jnp.concatenate(rows, axis=0).astype(jnp.bfloat16)
+
+
+def halves(plan):
+    core, row_bit, next_bit, _ = place(plan)
+    by_row = (core == 0) != ROW_FIRST
+    return jnp.where(by_row, row_bit, next_bit), jnp.where(by_row, next_bit, row_bit)
+
+
+def ordered(plan, blocks):
     rest = lax.axis_index("band") // 8
-    depth, half, lanes = plan.depth, plan.half, plan.half_lanes
-    for x in range(2):
-        rows = [[] for _ in TAP_STEPS]
-        for m in range(plan.blocks):
-            row, behind, col = (m % 2) ^ row_bit, (m // 2 % 2) ^ next_bit, x ^ col_bit
-            one = jnp.where(core == 0, behind, row)
-            two = jnp.where(core == 0, col, behind)
-            three = jnp.where(core == 0, row, col)
-            before = jnp.where(two == 0, own[one], third[one])
-            pair = jnp.where(three == 0, before, jnp.where(two == 0, last0[one], last1[one])).astype(jnp.float32)
-            block = pair[: plan.block_rows]
-            for k in range(1, plan.inner):
-                at = pair[k * plan.block_rows : (k + 1) * plan.block_rows]
-                block = jnp.where(((m // 4) ^ rest) == k, at, block)
-            for c in range(len(TAP_STEPS)):
-                rows[c].append(block[c * depth : (c + 1) * depth])
-        for c in range(len(TAP_STEPS)):
-            left[c * half : (c + 1) * half, x * lanes : (x + 1) * lanes] = jnp.concatenate(
-                rows[c], axis=0
-            ).astype(jnp.bfloat16)
-    cells_of(plan, 1, left, grads, out)
-
-
-def own_kernel(plan, left, grads, out):
-    cells_of(plan, 0, left, grads, out)
+    other_bit = halves(plan)[1]
+    parts = [jnp.where(other_bit == 0, blocks[k], blocks[1 - k]).astype(jnp.float32) for k in range(2)]
+    rows = []
+    for c in range(len(TAP_STEPS)):
+        for k in range(plan.inner):
+            for part in parts:
+                piece = None
+                for at in range(plan.inner):
+                    begin = at * plan.block_rows + c * plan.depth
+                    here = part[begin : begin + plan.depth]
+                    piece = here if piece is None else jnp.where((k ^ rest) == at, here, piece)
+                rows.append(piece)
+    return jnp.concatenate(rows, axis=0).astype(jnp.bfloat16)
+
+
+def summed(plan, product):
+    quarter = plan.half // 2
+    total = None
+    for c, col_step in enumerate(TAP_STEPS):
+        term = moved(product[c * quarter : (c + 1) * quarter], -col_step)
+        total = term if total is None else total + term
+    return total.astype(jnp.bfloat16)
+
+
+def groups(plan):
+    rows = [(n, h) for n in range(plan.images) for h in range(plan.rows)]
+    for d in range(2):
+        for begin in range(0, len(rows), 2):
+            part = rows[begin : begin + 2]
+            at = (d * len(rows) + begin) * plan.width
+            where = [(n, h, slice(k * plan.width, (k + 1) * plan.width)) for k, (n, h) in enumerate(part)]
+            yield d, slice(at, at + len(part) * plan.width), where
+
+
+def early_kernel(plan, own, third, last0, grads, out0, out1, rest):
+    core, _, _, col = place(plan)
+    near, far = ordered(plan, own), [ordered(plan, third), ordered(plan, last0)]
+    beside = jnp.where(core == 0, far[1], far[0])
+    below = jnp.where(core == 0, far[0], far[1])
+    for d, cells, where in groups(plan):
+        here, there = grads[col, :, cells], grads[1 - col, :, cells]
+        product = jnp.dot(near, here, preferred_element_type=jnp.float32)
+        product = product + jnp.dot(beside, there, preferred_element_type=jnp.float32)
+        rest[:, cells] = jnp.dot(below, here, preferred_element_type=jnp.float32)
+        for n, h, lanes in where:
+            (out0, out1)[d][n, h] = summed(plan, product[:, lanes])
+
+
+def late_of(plan, image, left, grads, rest, out):
+    col = place(plan)[3]
+    for d, cells, where in groups(plan):
+        if d == image:
+            product = rest[:, cells]
+            product = product + jnp.dot(left, grads[1 - col, :, cells], preferred_element_type=jnp.float32)
+            for n, h, lanes in where:
+                out[n, h] = summed(plan, product[:, lanes])
+
+
+def given_kernel(plan, last1, grads, rest, out, left):
+    left[...] = ordered(plan, last1)
+    late_of(plan, 1, left[...], grads, rest, out)
+
+
+def own_kernel(plan, left, grads, rest, out):
+    late_of(plan, 0, left[...], grads, rest, out)
 
 
 def last_kernel(plan, scale, keep, message, out):
@@ -318,17 +433,32 @@
             out[r * len(TAP_STEPS) + c] = total[c * depth : (c + 1) * depth, r * cols : (r + 1) * cols]
 
 
-def weave_kernel(plan, own, theirs, far, out, sems):
-    core = lax.axis_index("band") % 2
+def last_kernel(plan, scale, keep, message, out):
+    total = added(keep[...], message[...])[0] * scale
+    depth, cols = plan.depth, plan.cols
+    for r in range(len(TAP_STEPS)):
+        for c in range(len(TAP_STEPS)):
+            out[r * len(TAP_STEPS) + c] = total[c * depth : (c + 1) * depth, r * cols : (r + 1) * cols]
+
+
+def weave_kernel(plan, own0, own1, theirs0, theirs1, terms, far, far_terms, out, sems, sem):
+    copies = [pltpu.make_async_copy(terms, far_terms, sem)]
+    copies[0].start()
+    core, row_bit, next_bit, _ = place(plan)
     depth = plan.depth
-    copies = []
     for n in range(plan.images):
         for h in range(plan.rows):
-            a, b = own[n, h].astype(jnp.float32), theirs[n, h].astype(jnp.float32)
-            even, odd = jnp.where(core == 0, a, b), jnp.where(core == 0, b, a)
+            mine = [ref[n, h].astype(jnp.float32) for ref in (own0, own1)]
+            others = [ref[n, h].astype(jnp.float32) for ref in (theirs0, theirs1)]
             pieces = []
             for m in range(plan.blocks):
-                pieces += [even[m * depth : (m + 1) * depth], odd[m * depth : (m + 1) * depth]]
+                for p in range(2):
+                    by_row = (p == 0) != ROW_FIRST
+                    bit, other, ours = (m % 2, m // 2 % 2, row_bit) if by_row else (m // 2 % 2, m % 2, next_bit)
+                    at = slice((m // 4 * 2 + other) * depth, (m // 4 * 2 + other + 1) * depth)
+                    a = jnp.where(bit == ours, mine[0][at], mine[1][at])
+                    b = jnp.where(bit == ours, others[0][at], others[1][at])
+                    pieces.append(jnp.where(core == p, a, b))
             out[n, h] = jnp.concatenate(pieces, axis=0).astype(jnp.bfloat16)
             copies.append(pltpu.make_async_copy(out.at[n, h], far.at[n, h], sems.at[n, h]))
             copies[-1].start()
@@ -422,7 +552,7 @@
         send = run("halve0", part(halve, False), shape, b16, [keep, come])
         keep = run("halve1", part(halve, True), shape, f32, [after(keep, send, last0), come])
         come = swap(send, sizes, (mask, 0))
-    return keep, come, (packed, third, last0, after(last1, keep))
+    return keep, come, (after(packed, keep), third, last0, last1)
 
 
 def edge_kernel(plan, grad, out, copy):
@@ -471,28 +601,34 @@
         [grad0, grad1, *tops, *bottoms],
     )
     keep, come, packed = kernel_terms(plan, acts, grads, packed)
-    shape = jax.ShapeDtypeStruct((images, rows, plan.half, width), jnp.bfloat16)
-    left = jax.ShapeDtypeStruct((len(TAP_STEPS) * plan.half, 2 * plan.half_lanes), jnp.bfloat16)
-    grads = grads.reshape(2 * plan.half_lanes, plan.cells)
-    given, left = call(
-        "given",
-        functools.partial(given_kernel, plan),
-        (shape, left),
-        [*packed, grads],
+    packed, third, last0, last1 = packed
+    shape = jax.ShapeDtypeStruct((images, rows, plan.half // 2, width), jnp.bfloat16)
+    rest = jax.ShapeDtypeStruct((len(TAP_STEPS) * plan.half // 2, plan.cells), jnp.float32)
+    own0, given0, rest = call(
+        "early", functools.partial(early_kernel, plan), (shape, shape, rest), [packed, third, last0, grads]
     )
-    own = call("own", functools.partial(own_kernel, plan), shape, [after(left, given), grads])
-    theirs = swap(given, plan.sizes, (1, 0))
+    theirs0 = swap(given0, plan.sizes, (1, 0))
+    left = jax.ShapeDtypeStruct((len(TAP_STEPS) * plan.half // 2, plan.half_lanes), jnp.bfloat16)
+    given1, left = call("given", functools.partial(given_kernel, plan), (shape, left), [last1, grads, rest])
+    theirs1 = swap(given1, plan.sizes, (1, 0))
+    own1 = call("own", functools.partial(own_kernel, plan), shape, [after(left, given1), grads, rest])
     shape = (images, rows, channels, width)
-    input_grad = call(
+    terms = (len(TAP_STEPS) ** 2, plan.depth, plan.cols)
+    total = call(
+        "last", functools.partial(last_kernel, plan, scale), jax.ShapeDtypeStruct(terms, jnp.float32), [keep, come]
+    )
+    input_grad, kernel_grad = call(
         "weave",
         functools.partial(weave_kernel, plan),
-        (jax.ShapeDtypeStruct(shape, jnp.bfloat16),),
-        [own, theirs],
-        [pltpu.VMEM(shape, jnp.bfloat16), pltpu.SemaphoreType.DMA((images, rows))],
-        far=1,
-    )[0]
-    shape = jax.ShapeDtypeStruct((len(TAP_STEPS) ** 2, plan.depth, plan.cols), jnp.float32)
-    kernel_grad = call("last", functools.partial(last_kernel, plan, scale), shape, [keep, come])
+        (jax.ShapeDtypeStruct(shape, jnp.bfloat16), jax.ShapeDtypeStruct(terms, jnp.float32)),
+        [own0, own1, theirs0, theirs1, total],
+        [
+            pltpu.VMEM(shape, jnp.bfloat16),
+            pltpu.SemaphoreType.DMA((images, rows)),
+            pltpu.SemaphoreType.DMA(()),
+        ],
+        far=2,
+    )
     return input_grad.transpose(0, 2, 1, 3), kernel_grad.transpose(1, 0, 2)
 
 

time: 39.2 us -> 37.2 us (0.949)
  waiting for transfers between devices: 5.54 us -> 3.22 us
  Pallas kernels: 11.4 us -> 10.9 us
  starting transfers between devices: 21.3 us -> 21.8 us
    ppermute x15 -> x16, waiting for transfers between devices: 5.54 us -> 3.22 us  [swap(): return lax.ppermute(value, AXES, pairs)]
    ppermute x15 -> x16, starting transfers between devices: 21.3 us -> 21.8 us  [swap(): return lax.ppermute(value, AXES, pairs)]
    pallas_call x19 -> x20, Pallas kernels: 11.4 us -> 10.9 us  [call(): pl.pallas_call(kernel, out_shape=out_shape, in_specs=[pl.BlockSpec(memory...]
  transfers between devices with their start and end apart: 15 -> 16, of which waited for: 4 -> 5; matrix products, arithmetic and copies ran while one was open for 0% -> 0% of each run, Pallas kernels for 24% -> 24%
where the time goes in v12:
time: 37.2 us; the launch traced here: 36.8 us
  starting transfers between devices  21.8 us (59%)
  Pallas kernels  10.9 us (29%)
  waiting for transfers between devices  3.22 us (9%)
  between operations  0.84 us (2%)
    ppermute x16, starting transfers between devices, swap(): return lax.ppermute(value, AXES, pairs)  21.8 us
    pallas_call x20, Pallas kernels, call(): pl.pallas_call(kernel, out_shape=out_shape, in_specs=[pl.BlockSpec(memory...  10.9 us
    ppermute x16, waiting for transfers between devices, swap(): return lax.ppermute(value, AXES, pairs)  3.22 us
  transfers between devices with their start and end apart: 16, of which 5 were waited for; matrix products, arithmetic and copies ran while one was open for 0% of the time, Pallas kernels for 24%

profile of v12, /device:TPU:0, one launch (start us, length us, event | category | flops | bytes accessed | tf_op | source)
XLA Modules:
  0.0 36.8 jit_solution(7522025021582557271)
XLA Ops:
  0.6 0.0 copy-start
  0.6 0.0 copy-start.1
  0.6 1.1 %edge.1 = (bf16[1,320,128]{2,1,0:T(8,128)(2,1)S(1)}, bf16[1,6,320,128]{3,2,1,0:T(8,128)(2,1)S(1)}) custom-call(bf16[1,6,320,128]{3,2,1,0:T(8,128)(2,1)} %bitcast.3.grad), custom_call_target="tpu_custom_call" | custom-call | flops 9200000000 | tf_op jit(solution)/shard_map/edge/pallas_call | solution.py:62
  1.8 3.0 %collective-permute-start.3 = (bf16[1,320,128]{2,1,0:T(8,128)(2,1)S(1)}, bf16[1,320,128]{2,1,0:T(8,128)(2,1)S(1)}, u32[]{:S(2)}, u32[]{:S(2)}) collective-permute-start(bf16[1,320,128]{2,1,0:T(8,128)(2,1)S(1)} %get-tuple-element.25), channel_id=1, source_target_pairs={{0,1},{1,0},{2,3},{3,2},{4,5},{5,4},{6,7},{7,6},{8,9},{9,8},{10,11... | collective-permute-start | bytes 245768 | tf_op jit(solution)/shard_map/ppermute | solution.py:55
  4.8 0.0 collective-permute-start.4
  4.8 0.2 collective-permute-start.2
  5.0 0.0 copy-done
  5.0 0.3 collective-permute-start.1
  5.3 0.0 copy-done.1
  5.3 0.1 pack.1
  5.4 2.8 %collective-permute-start = (bf16[1,60,512]{2,1,0:T(8,128)(2,1)S(1)}, bf16[1,60,512]{2,1,0:T(8,128)(2,1)S(1)}, u32[]{:S(2)}, u32[]{:S(2)}) collective-permute-start(bf16[1,60,512]{2,1,0:T(8,128)(2,1)S(1)} %bitcast.9), channel_id=1, source_target_pairs={{0,16},{1,17},{2,18},{3,19},{4,20},{5,21},{6,22},{7,23},{8,24},{9,... | collective-permute-start | bytes 184328 | tf_op jit(solution)/shard_map/ppermute | solution.py:55
  8.2 0.0 collective-permute-done.1.act1
  8.2 0.6 %acts.1 = bf16[2,240,1536]{2,1,0:T(8,128)(2,1)S(1)} custom-call(bf16[1,6,320,128]{3,2,1,0:T(8,128)(2,1)S(1)} %bitcast.7, bf16[1,6,320,128]{3,2,1,0:T(8,128)(2,1)S(1)} %collective-permute-done.1.act1), custom_call_target="tpu_custom_call" | custom-call | flops 690000000 | tf_op jit(solution)/shard_map/acts/pallas_call | solution.py:62
  8.8 0.0 collective-permute-done.3.top0.bottom0
  8.9 0.4 %collective-permute-done.4.top1.bottom1 = bf16[1,320,128]{2,1,0:T(8,128)(2,1)S(1)} collective-permute-done((bf16[1,320,128]{2,1,0:T(8,128)(2,1)S(1)}, bf16[1,320,128]{2,1,0:T(8,128)(2,1)S(1)}, u32[]{:S(2)}, u32[]{:S(2)}) %collective-permute-start.4) | collective-permute-done | bytes 81952 | tf_op jit(solution)/shard_map/ppermute | solution.py:55
  9.3 0.0 collective-permute-done.2.grad1
  9.3 0.5 %grads.1 = bf16[2,512,1536]{2,1,0:T(8,128)(2,1)S(1)} custom-call(bf16[1,6,320,128]{3,2,1,0:T(8,128)(2,1)S(1)} %get-tuple-element.24.grad0, bf16[1,6,320,128]{3,2,1,0:T(8,128)(2,1)S(1)} %collective-permute-done.2.grad1, bf16[1,320,128]{2,1,0:T(8,128)(2,1)S(1)} %collective-permute-done.3.top0.bottom0, ...), custom_call_target="tpu_custom_call" | custom-call | flops 575000000 | tf_op jit(solution)/shard_map/grads/pallas_call | solution.py:62
  9.7 0.9 %send0.1 = bf16[2,120,512]{2,1,0:T(8,128)(2,1)S(1)} custom-call(bf16[2,240,1536]{2,1,0:T(8,128)(2,1)S(1)} %acts.1, bf16[2,512,1536]{2,1,0:T(8,128)(2,1)S(1)} %grads.1), custom_call_target="tpu_custom_call" | custom-call | flops 1610000000 | tf_op jit(solution)/shard_map/send0/pallas_call | solution.py:62
  10.7 1.1 %collective-permute-start.6 = (bf16[2,120,512]{2,1,0:T(8,128)(2,1)S(1)}, bf16[2,120,512]{2,1,0:T(8,128)(2,1)S(1)}, u32[]{:S(2)}, u32[]{:S(2)}) collective-permute-start(bf16[2,120,512]{2,1,0:T(8,128)(2,1)S(1)} %send0.1), channel_id=1, source_target_pairs={{0,1},{1,0},{2,10},{3,11},{4,5},{5,4},{6,14},{7,15},{8,9},{9,8},{1... | collective-permute-start | bytes 737288 | tf_op jit(solution)/shard_map/ppermute | solution.py:55
  11.8 0.9 %send1.1 = bf16[2,120,512]{2,1,0:T(8,128)(2,1)S(1)} custom-call(bf16[2,240,1536]{2,1,0:T(8,128)(2,1)S(1)} %acts.1, bf16[2,512,1536]{2,1,0:T(8,128)(2,1)S(1)} %grads.1), custom_call_target="tpu_custom_call" | custom-call | flops 1610000000 | tf_op jit(solution)/shard_map/send1/pallas_call | solution.py:62
  12.7 0.8 %keep0.1.keep = f32[2,120,512]{2,1,0:T(8,128)S(1)} custom-call(bf16[2,240,1536]{2,1,0:T(8,128)(2,1)S(1)} %acts.1, bf16[2,512,1536]{2,1,0:T(8,128)(2,1)S(1)} %grads.1), custom_call_target="tpu_custom_call" | custom-call | flops 1150000000 | tf_op jit(solution)/shard_map/keep0/pallas_call | solution.py:62
  13.5 0.0 collective-permute-done.refs_1_
  13.5 1.6 %collective-permute-start.5 = (bf16[1,120,512]{2,1,0:T(8,128)(2,1)S(1)}, bf16[1,120,512]{2,1,0:T(8,128)(2,1)S(1)}, u32[]{:S(2)}, u32[]{:S(2)}) collective-permute-start(bf16[1,120,512]{2,1,0:T(8,128)(2,1)S(1)} %pair.1), channel_id=1, source_target_pairs={{0,8},{1,9},{2,6},{3,7},{4,12},{5,13},{6,2},{7,3},{8,0},{9,1},{10,... | collective-permute-start | bytes 368648 | tf_op jit(solution)/shard_map/ppermute | solution.py:55
  15.2 1.2 %collective-permute-start.7 = (bf16[2,120,512]{2,1,0:T(8,128)(2,1)S(1)}, bf16[2,120,512]{2,1,0:T(8,128)(2,1)S(1)}, u32[]{:S(2)}, u32[]{:S(2)}) collective-permute-start(bf16[2,120,512]{2,1,0:T(8,128)(2,1)S(1)} %send1.1), channel_id=1, source_target_pairs={{0,1},{1,0},{2,10},{3,11},{4,5},{5,4},{6,14},{7,15},{8,9},{9,8},{1... | collective-permute-start | bytes 737288 | tf_op jit(solution)/shard_map/ppermute | solution.py:55
  16.3 0.6 %collective-permute-done.6.message = bf16[2,120,512]{2,1,0:T(8,128)(2,1)S(1)} collective-permute-done((bf16[2,120,512]{2,1,0:T(8,128)(2,1)S(1)}, bf16[2,120,512]{2,1,0:T(8,128)(2,1)S(1)}, u32[]{:S(2)}, u32[]{:S(2)}) %collective-permute-start.6) | collective-permute-done | bytes 245792 | tf_op jit(solution)/shard_map/ppermute | solution.py:55
  16.9 0.5 %turn0.1 = bf16[2,120,512]{2,1,0:T(8,128)(2,1)S(1)} custom-call(f32[2,120,512]{2,1,0:T(8,128)S(1)} %keep0.1.keep, bf16[2,120,512]{2,1,0:T(8,128)(2,1)S(1)} %collective-permute-done.6.message), custom_call_target="tpu_custom_call" | custom-call | flops 1035000000 | tf_op jit(solution)/shard_map/turn0/pallas_call | solution.py:62
  17.4 1.8 %collective-permute-start.8 = (bf16[2,120,512]{2,1,0:T(8,128)(2,1)S(1)}, bf16[2,120,512]{2,1,0:T(8,128)(2,1)S(1)}, u32[]{:S(2)}, u32[]{:S(2)}) collective-permute-start(bf16[2,120,512]{2,1,0:T(8,128)(2,1)S(1)} %turn0.1), channel_id=1, source_target_pairs={{0,4},{1,5},{2,3},{3,2},{4,0},{5,1},{6,7},{7,6},{8,12},{9,13},{10,... | collective-permute-start | bytes 737288 | tf_op jit(solution)/shard_map/ppermute | solution.py:55
  19.2 0.0 collective-permute-done.5
  19.3 2.1 %collective-permute-start.11 = (bf16[2,120,512]{2,1,0:T(8,128)(2,1)S(1)}, bf16[2,120,512]{2,1,0:T(8,128)(2,1)S(1)}, u32[]{:S(2)}, u32[]{:S(2)}) collective-permute-start(bf16[2,120,512]{2,1,0:T(8,128)(2,1)S(1)} %pad_maximum_fusion.own), channel_id=1, source_target_pairs={{0,4},{1,5},{2,3},{3,2},{4,0},{5,1},{6,7},{7,6},{8,12},{9,13},{10,... | collective-permute-start | bytes 737288 | tf_op jit(solution)/shard_map/ppermute | solution.py:55
  21.4 0.7 %keep1.1.keep = f32[2,120,512]{2,1,0:T(8,128)S(1)} custom-call(bf16[2,240,1536]{2,1,0:T(8,128)(2,1)S(1)} %acts.1, bf16[2,512,1536]{2,1,0:T(8,128)(2,1)S(1)} %grads.1), custom_call_target="tpu_custom_call" | custom-call | flops 1150000000 | tf_op jit(solution)/shard_map/keep1/pallas_call | solution.py:62
  22.1 1.2 %collective-permute-start.10 = (bf16[2,120,512]{2,1,0:T(8,128)(2,1)S(1)}, bf16[2,120,512]{2,1,0:T(8,128)(2,1)S(1)}, u32[]{:S(2)}, u32[]{:S(2)}) collective-permute-start(bf16[2,120,512]{2,1,0:T(8,128)(2,1)S(1)} %pad_maximum_fusion.own), channel_id=1, source_target_pairs={{0,1},{1,0},{2,10},{3,11},{4,5},{5,4},{6,14},{7,15},{8,9},{9,8},{1... | collective-permute-start | bytes 737288 | tf_op jit(solution)/shard_map/ppermute | solution.py:55
  23.4 0.0 collective-permute-done.7.message
  23.4 0.3 turn1.1.keep
  23.7 0.0 collective-permute-done.8.message
  23.7 0.3 part0.1
  24.0 1.8 %collective-permute-start.9 = (bf16[120,512]{1,0:T(8,128)(2,1)S(1)}, bf16[120,512]{1,0:T(8,128)(2,1)S(1)}, u32[]{:S(2)}, u32[]{:S(2)}) collective-permute-start(bf16[120,512]{1,0:T(8,128)(2,1)S(1)} %part0.1), channel_id=1, source_target_pairs={{0,8},{1,9},{2,6},{3,7},{4,12},{5,13},{6,2},{7,3},{8,0},{9,1},{10,... | collective-permute-start | bytes 368648 | tf_op jit(solution)/shard_map/ppermute | solution.py:55
  25.8 0.5 %collective-permute-done.11.third = bf16[2,120,512]{2,1,0:T(8,128)(2,1)S(1)} collective-permute-done((bf16[2,120,512]{2,1,0:T(8,128)(2,1)S(1)}, bf16[2,120,512]{2,1,0:T(8,128)(2,1)S(1)}, u32[]{:S(2)}, u32[]{:S(2)}) %collective-permute-start.11) | collective-permute-done | bytes 245792 | tf_op jit(solution)/shard_map/ppermute | solution.py:55
  26.3 1.1 %collective-permute-start.12 = (bf16[2,120,512]{2,1,0:T(8,128)(2,1)S(1)}, bf16[2,120,512]{2,1,0:T(8,128)(2,1)S(1)}, u32[]{:S(2)}, u32[]{:S(2)}) collective-permute-start(bf16[2,120,512]{2,1,0:T(8,128)(2,1)S(1)} %collective-permute-done.11.third), channel_id=1, source_target_pairs={{0,1},{1,0},{2,10},{3,11},{4,5},{5,4},{6,14},{7,15},{8,9},{9,8},{1... | collective-permute-start | bytes 737288 | tf_op jit(solution)/shard_map/ppermute | solution.py:55
  27.4 0.2 part1.1.keep
  27.6 1.4 %collective-permute-done.9.message = bf16[120,512]{1,0:T(8,128)(2,1)S(1)} collective-permute-done((bf16[120,512]{1,0:T(8,128)(2,1)S(1)}, bf16[120,512]{1,0:T(8,128)(2,1)S(1)}, u32[]{:S(2)}, u32[]{:S(2)}) %collective-permute-start.9) | collective-permute-done | bytes 122912 | tf_op jit(solution)/shard_map/ppermute | solution.py:55
  29.0 0.2 halve0.1
  29.2 2.8 %collective-permute-start.15 = (bf16[60,512]{1,0:T(8,128)(2,1)S(1)}, bf16[60,512]{1,0:T(8,128)(2,1)S(1)}, u32[]{:S(2)}, u32[]{:S(2)}) collective-permute-start(bf16[60,512]{1,0:T(8,128)(2,1)S(1)} %halve0.1), channel_id=1, source_target_pairs={{0,16},{1,17},{2,18},{3,19},{4,20},{5,21},{6,22},{7,23},{8,24},{9,... | collective-permute-start | bytes 184328 | tf_op jit(solution)/shard_map/ppermute | solution.py:55
  32.0 0.0 collective-permute-done.10.last0
  32.0 0.2 halve1.1.keep
  32.2 1.5 %early.1 = (bf16[1,6,80,128]{3,2,1,0:T(8,128)(2,1)S(1)}, bf16[1,6,80,128]{3,2,1,0:T(8,128)(2,1)S(1)}, f32[240,1536]{1,0:T(8,128)S(1)}) custom-call(bf16[2,120,512]{2,1,0:T(8,128)(2,1)S(1)} %pad_maximum_fusion.own, bf16[2,120,512]{2,1,0:T(8,128)(2,1)S(1)} %collective-permute-done.11.third, bf16[2,120,512]{2,1,0:T(8,128)(2,1)S(1)} %collective-permute-done.10.last0, ...), custom_call_target="tpu_custom_call" | custom-call | flops 1955000064 | tf_op jit(solution)/shard_map/early/pallas_call | solution.py:62
  33.7 0.1 collective-permute-start.13
  33.8 0.0 collective-permute-done.12.last1
  33.8 0.5 %given.1 = (bf16[1,6,80,128]{3,2,1,0:T(8,128)(2,1)S(1)}, bf16[240,512]{1,0:T(8,128)(2,1)S(1)}) custom-call(bf16[2,120,512]{2,1,0:T(8,128)(2,1)S(1)} %collective-permute-done.12.last1, bf16[2,512,1536]{2,1,0:T(8,128)(2,1)S(1)} %grads.1, f32[240,1536]{1,0:T(8,128)S(1)} %get-tuple-element.39.rest), custom_call_target="tpu_custom_call" | custom-call | flops 575000000 | tf_op jit(solution)/shard_map/given/pallas_call | solution.py:62
  34.3 0.5 %collective-permute-start.14 = (bf16[1,6,80,128]{3,2,1,0:T(8,128)(2,1)S(1)}, bf16[1,6,80,128]{3,2,1,0:T(8,128)(2,1)S(1)}, u32[]{:S(2)}, u32[]{:S(2)}) collective-permute-start(bf16[1,6,80,128]{3,2,1,0:T(8,128)(2,1)S(1)} %get-tuple-element.41), channel_id=1, source_target_pairs={{0,2},{1,3},{2,0},{3,1},{4,6},{5,7},{6,4},{7,5},{8,10},{9,11},{10,... | collective-permute-start | bytes 368648 | tf_op jit(solution)/shard_map/ppermute | solution.py:55
  34.9 0.0 collective-permute-done.15.message
  34.9 0.2 last.1.terms
  35.1 0.5 %own.1.own1 = bf16[1,6,80,128]{3,2,1,0:T(8,128)(2,1)S(1)} custom-call(bf16[240,512]{1,0:T(8,128)(2,1)S(1)} %get-tuple-element.42.left, bf16[2,512,1536]{2,1,0:T(8,128)(2,1)S(1)} %grads.1, f32[240,1536]{1,0:T(8,128)S(1)} %get-tuple-element.39.rest), custom_call_target="tpu_custom_call" | custom-call | flops 575000000 | tf_op jit(solution)/shard_map/own/pallas_call | solution.py:62
  35.5 0.0 collective-permute-done.13.theirs0
  35.6 0.3 collective-permute-done.14.theirs1
  35.8 1.0 %weave.1 = (bf16[1,6,320,128]{3,2,1,0:T(8,128)(2,1)}, f32[9,20,160]{2,1,0:T(8,128)}) custom-call(bf16[1,6,80,128]{3,2,1,0:T(8,128)(2,1)S(1)} %get-tuple-element.37.own0, bf16[1,6,80,128]{3,2,1,0:T(8,128)(2,1)S(1)} %own.1.own1, bf16[1,6,80,128]{3,2,1,0:T(8,128)(2,1)S(1)} %collective-permute-done.13.theirs0, ...), custom_call_target="tpu_custom_call" | custom-call | flops 1035000000 | tf_op jit(solution)/shard_map/weave/pallas_call | solution.py:62
  (2 shorter events, 0.0 us)
Async XLA Ops:
  0.6 4.4 %copy-start = (bf16[1,320,6,128]{3,1,2,0:T(8,128)(2,1)S(1)}, bf16[1,320,6,128]{3,1,2,0:T(8,128)(2,1)}, u32[]{:S(2)}) copy-start(bf16[1,320,6,128]{3,1,2,0:T(8,128)(2,1)} %param.3) | copy-start | bytes 1474564
  0.6 4.7 %copy-start.1 = (bf16[20,9,160]{2,0,1:T(8,128)(2,1)S(1)}, bf16[20,9,160]{2,0,1:T(8,128)(2,1)}, u32[]{:S(2)}) copy-start(bf16[20,9,160]{2,0,1:T(8,128)(2,1)} %param.5) | copy-start | bytes 172804
  1.8 7.0 %collective-permute-start.3 = (bf16[1,320,128]{2,1,0:T(8,128)(2,1)S(1)}, bf16[1,320,128]{2,1,0:T(8,128)(2,1)S(1)}, u32[]{:S(2)}, u32[]{:S(2)}) collective-permute-start(bf16[1,320,128]{2,1,0:T(8,128)(2,1)S(1)} %get-tuple-element.25), channel_id=1, source_target_pairs={{0,1},{1,0},{2,3},{3,2},{4,5},{5,4},{6,7},{7,6},{8,9},{9,8},{10,11... | collective-permute-start | bytes 245768 | tf_op jit(solution)/shard_map/ppermute | solution.py:55
  4.8 4.5 %collective-permute-start.4 = (bf16[1,320,128]{2,1,0:T(8,128)(2,1)S(1)}, bf16[1,320,128]{2,1,0:T(8,128)(2,1)S(1)}, u32[]{:S(2)}, u32[]{:S(2)}) collective-permute-start(bf16[1,320,128]{2,1,0:T(8,128)(2,1)S(1)} %get-tuple-element.25), channel_id=1, source_target_pairs={{0,3},{1,2},{2,1},{3,0},{4,7},{5,6},{6,5},{7,4},{8,11},{9,10},{10,... | collective-permute-start | bytes 245768 | tf_op jit(solution)/shard_map/ppermute | solution.py:55
  4.8 4.5 %collective-permute-start.2 = (bf16[1,6,320,128]{3,2,1,0:T(8,128)(2,1)}, bf16[1,6,320,128]{3,2,1,0:T(8,128)(2,1)S(1)}, u32[]{:S(2)}, u32[]{:S(2)}) collective-permute-start(bf16[1,6,320,128]{3,2,1,0:T(8,128)(2,1)} %bitcast.3.grad), channel_id=1, source_target_pairs={{0,2},{1,3},{2,0},{3,1},{4,6},{5,7},{6,4},{7,5},{8,10},{9,11},{10,... | collective-permute-start | bytes 1474568 | tf_op jit(solution)/shard_map/ppermute | solution.py:55
  5.0 3.2 %collective-permute-start.1 = (bf16[1,6,320,128]{3,2,1,0:T(8,128)(2,1)S(1)}, bf16[1,6,320,128]{3,2,1,0:T(8,128)(2,1)S(1)}, u32[]{:S(2)}, u32[]{:S(2)}) collective-permute-start(bf16[1,6,320,128]{3,2,1,0:T(8,128)(2,1)S(1)} %bitcast.6), channel_id=1, source_target_pairs={{0,2},{1,3},{2,0},{3,1},{4,6},{5,7},{6,4},{7,5},{8,10},{9,11},{10,... | collective-permute-start | bytes 1474568 | tf_op jit(solution)/shard_map/ppermute | solution.py:55
  5.4 8.1 %collective-permute-start = (bf16[1,60,512]{2,1,0:T(8,128)(2,1)S(1)}, bf16[1,60,512]{2,1,0:T(8,128)(2,1)S(1)}, u32[]{:S(2)}, u32[]{:S(2)}) collective-permute-start(bf16[1,60,512]{2,1,0:T(8,128)(2,1)S(1)} %bitcast.9), channel_id=1, source_target_pairs={{0,16},{1,17},{2,18},{3,19},{4,20},{5,21},{6,22},{7,23},{8,24},{9,... | collective-permute-start | bytes 184328 | tf_op jit(solution)/shard_map/ppermute | solution.py:55
  10.7 6.3 %collective-permute-start.6 = (bf16[2,120,512]{2,1,0:T(8,128)(2,1)S(1)}, bf16[2,120,512]{2,1,0:T(8,128)(2,1)S(1)}, u32[]{:S(2)}, u32[]{:S(2)}) collective-permute-start(bf16[2,120,512]{2,1,0:T(8,128)(2,1)S(1)} %send0.1), channel_id=1, source_target_pairs={{0,1},{1,0},{2,10},{3,11},{4,5},{5,4},{6,14},{7,15},{8,9},{9,8},{1... | collective-permute-start | bytes 737288 | tf_op jit(solution)/shard_map/ppermute | solution.py:55
  13.5 5.7 %collective-permute-start.5 = (bf16[1,120,512]{2,1,0:T(8,128)(2,1)S(1)}, bf16[1,120,512]{2,1,0:T(8,128)(2,1)S(1)}, u32[]{:S(2)}, u32[]{:S(2)}) collective-permute-start(bf16[1,120,512]{2,1,0:T(8,128)(2,1)S(1)} %pair.1), channel_id=1, source_target_pairs={{0,8},{1,9},{2,6},{3,7},{4,12},{5,13},{6,2},{7,3},{8,0},{9,1},{10,... | collective-permute-start | bytes 368648 | tf_op jit(solution)/shard_map/ppermute | solution.py:55
  15.2 8.2 %collective-permute-start.7 = (bf16[2,120,512]{2,1,0:T(8,128)(2,1)S(1)}, bf16[2,120,512]{2,1,0:T(8,128)(2,1)S(1)}, u32[]{:S(2)}, u32[]{:S(2)}) collective-permute-start(bf16[2,120,512]{2,1,0:T(8,128)(2,1)S(1)} %send1.1), channel_id=1, source_target_pairs={{0,1},{1,0},{2,10},{3,11},{4,5},{5,4},{6,14},{7,15},{8,9},{9,8},{1... | collective-permute-start | bytes 737288 | tf_op jit(solution)/shard_map/ppermute | solution.py:55
  17.4 6.3 %collective-permute-start.8 = (bf16[2,120,512]{2,1,0:T(8,128)(2,1)S(1)}, bf16[2,120,512]{2,1,0:T(8,128)(2,1)S(1)}, u32[]{:S(2)}, u32[]{:S(2)}) collective-permute-start(bf16[2,120,512]{2,1,0:T(8,128)(2,1)S(1)} %turn0.1), channel_id=1, source_target_pairs={{0,4},{1,5},{2,3},{3,2},{4,0},{5,1},{6,7},{7,6},{8,12},{9,13},{10,... | collective-permute-start | bytes 737288 | tf_op jit(solution)/shard_map/ppermute | solution.py:55
  19.3 7.1 %collective-permute-start.11 = (bf16[2,120,512]{2,1,0:T(8,128)(2,1)S(1)}, bf16[2,120,512]{2,1,0:T(8,128)(2,1)S(1)}, u32[]{:S(2)}, u32[]{:S(2)}) collective-permute-start(bf16[2,120,512]{2,1,0:T(8,128)(2,1)S(1)} %pad_maximum_fusion.own), channel_id=1, source_target_pairs={{0,4},{1,5},{2,3},{3,2},{4,0},{5,1},{6,7},{7,6},{8,12},{9,13},{10,... | collective-permute-start | bytes 737288 | tf_op jit(solution)/shard_map/ppermute | solution.py:55
  22.1 9.9 %collective-permute-start.10 = (bf16[2,120,512]{2,1,0:T(8,128)(2,1)S(1)}, bf16[2,120,512]{2,1,0:T(8,128)(2,1)S(1)}, u32[]{:S(2)}, u32[]{:S(2)}) collective-permute-start(bf16[2,120,512]{2,1,0:T(8,128)(2,1)S(1)} %pad_maximum_fusion.own), channel_id=1, source_target_pairs={{0,1},{1,0},{2,10},{3,11},{4,5},{5,4},{6,14},{7,15},{8,9},{9,8},{1... | collective-permute-start | bytes 737288 | tf_op jit(solution)/shard_map/ppermute | solution.py:55
  24.0 4.9 %collective-permute-start.9 = (bf16[120,512]{1,0:T(8,128)(2,1)S(1)}, bf16[120,512]{1,0:T(8,128)(2,1)S(1)}, u32[]{:S(2)}, u32[]{:S(2)}) collective-permute-start(bf16[120,512]{1,0:T(8,128)(2,1)S(1)} %part0.1), channel_id=1, source_target_pairs={{0,8},{1,9},{2,6},{3,7},{4,12},{5,13},{6,2},{7,3},{8,0},{9,1},{10,... | collective-permute-start | bytes 368648 | tf_op jit(solution)/shard_map/ppermute | solution.py:55
  26.3 7.5 %collective-permute-start.12 = (bf16[2,120,512]{2,1,0:T(8,128)(2,1)S(1)}, bf16[2,120,512]{2,1,0:T(8,128)(2,1)S(1)}, u32[]{:S(2)}, u32[]{:S(2)}) collective-permute-start(bf16[2,120,512]{2,1,0:T(8,128)(2,1)S(1)} %collective-permute-done.11.third), channel_id=1, source_target_pairs={{0,1},{1,0},{2,10},{3,11},{4,5},{5,4},{6,14},{7,15},{8,9},{9,8},{1... | collective-permute-start | bytes 737288 | tf_op jit(solution)/shard_map/ppermute | solution.py:55
  29.2 5.7 %collective-permute-start.15 = (bf16[60,512]{1,0:T(8,128)(2,1)S(1)}, bf16[60,512]{1,0:T(8,128)(2,1)S(1)}, u32[]{:S(2)}, u32[]{:S(2)}) collective-permute-start(bf16[60,512]{1,0:T(8,128)(2,1)S(1)} %halve0.1), channel_id=1, source_target_pairs={{0,16},{1,17},{2,18},{3,19},{4,20},{5,21},{6,22},{7,23},{8,24},{9,... | collective-permute-start | bytes 184328 | tf_op jit(solution)/shard_map/ppermute | solution.py:55
  33.7 1.8 %collective-permute-start.13 = (bf16[1,6,80,128]{3,2,1,0:T(8,128)(2,1)S(1)}, bf16[1,6,80,128]{3,2,1,0:T(8,128)(2,1)S(1)}, u32[]{:S(2)}, u32[]{:S(2)}) collective-permute-start(bf16[1,6,80,128]{3,2,1,0:T(8,128)(2,1)S(1)} %get-tuple-element.43), channel_id=1, source_target_pairs={{0,2},{1,3},{2,0},{3,1},{4,6},{5,7},{6,4},{7,5},{8,10},{9,11},{10,... | collective-permute-start | bytes 368648 | tf_op jit(solution)/shard_map/ppermute | solution.py:55
  34.3 1.5 %collective-permute-start.14 = (bf16[1,6,80,128]{3,2,1,0:T(8,128)(2,1)S(1)}, bf16[1,6,80,128]{3,2,1,0:T(8,128)(2,1)S(1)}, u32[]{:S(2)}, u32[]{:S(2)}) collective-permute-start(bf16[1,6,80,128]{3,2,1,0:T(8,128)(2,1)S(1)} %get-tuple-element.41), channel_id=1, source_target_pairs={{0,2},{1,3},{2,0},{3,1},{4,6},{5,7},{6,4},{7,5},{8,10},{9,11},{10,... | collective-permute-start | bytes 368648 | tf_op jit(solution)/shard_map/ppermute | solution.py:55

commit v13 on v12

--- a/solution.py
+++ b/solution.py
@@ -137,10 +137,12 @@
         ones, others = (by_row, by_next) if ROW_FIRST else (by_next, by_row)
         self.gather_masks = ((ones, others), (others, by_col), (by_col, ones))
 
+    def turned(self, slot):
+        bits = self.band_bits - 3
+        return sum(((slot >> k) & 1) << (bits - 1 - k) for k in range(bits))
+
     def block_of(self, slot, by_next, by_row):
-        bits = self.band_bits - 3
-        turned = sum(((slot >> k) & 1) << (bits - 1 - k) for k in range(bits))
-        return turned * 4 + by_next * 2 + by_row
+        return self.turned(slot) * 4 + by_next * 2 + by_row
 
     def chunks(self):
         return [(d, n, h) for d in range(2) for n in range(self.images) for h in range(self.rows)]
@@ -282,7 +284,7 @@
             for part in parts:
                 piece = None
                 for at in range(plan.inner):
-                    begin = at * plan.block_rows + c * plan.depth
+                    begin = plan.turned(at) * plan.block_rows + c * plan.depth
                     here = part[begin : begin + plan.depth]
                     piece = here if piece is None else jnp.where((k ^ rest) == at, here, piece)
                 rows.append(piece)
@@ -366,7 +368,7 @@
             for part in parts:
                 piece = None
                 for at in range(plan.inner):
-                    begin = at * plan.block_rows + c * plan.depth
+                    begin = plan.turned(at) * plan.block_rows + c * plan.depth
                     here = part[begin : begin + plan.depth]
                     piece = here if piece is None else jnp.where((k ^ rest) == at, here, piece)
                 rows.append(piece)

time: 37.2 us -> 37.2 us (level)
  no operation moved by 1% of the time
where the time goes in v13:
time: 37.2 us; the launch traced here: 36.8 us
  starting transfers between devices  21.8 us (59%)
  Pallas kernels  10.9 us (29%)
  waiting for transfers between devices  3.22 us (9%)
  between operations  0.84 us (2%)
    ppermute x16, starting transfers between devices, swap(): return lax.ppermute(value, AXES, pairs)  21.8 us
    pallas_call x20, Pallas kernels, call(): pl.pallas_call(kernel, out_shape=out_shape, in_specs=[pl.BlockSpec(memory...  10.9 us
    ppermute x16, waiting for transfers between devices, swap(): return lax.ppermute(value, AXES, pairs)  3.22 us
  transfers between devices with their start and end apart: 16, of which 5 were waited for; matrix products, arithmetic and copies ran while one was open for 0% of the time, Pallas kernels for 24%

profile of v13, /device:TPU:0, one launch (start us, length us, event | category | flops | bytes accessed | tf_op | source)
XLA Modules:
  0.0 36.8 jit_solution(7522025021582557271)
XLA Ops:
  0.6 0.0 copy-start
  0.6 0.0 copy-start.1
  0.6 1.1 %edge.1 = (bf16[1,320,128]{2,1,0:T(8,128)(2,1)S(1)}, bf16[1,6,320,128]{3,2,1,0:T(8,128)(2,1)S(1)}) custom-call(bf16[1,6,320,128]{3,2,1,0:T(8,128)(2,1)} %bitcast.3.grad), custom_call_target="tpu_custom_call" | custom-call | flops 9200000000 | tf_op jit(solution)/shard_map/edge/pallas_call | solution.py:62
  1.8 3.0 %collective-permute-start.3 = (bf16[1,320,128]{2,1,0:T(8,128)(2,1)S(1)}, bf16[1,320,128]{2,1,0:T(8,128)(2,1)S(1)}, u32[]{:S(2)}, u32[]{:S(2)}) collective-permute-start(bf16[1,320,128]{2,1,0:T(8,128)(2,1)S(1)} %get-tuple-element.25), channel_id=1, source_target_pairs={{0,1},{1,0},{2,3},{3,2},{4,5},{5,4},{6,7},{7,6},{8,9},{9,8},{10,11... | collective-permute-start | bytes 245768 | tf_op jit(solution)/shard_map/ppermute | solution.py:55
  4.8 0.0 collective-permute-start.4
  4.8 0.2 collective-permute-start.2
  5.0 0.0 copy-done
  5.0 0.3 collective-permute-start.1
  5.3 0.0 copy-done.1
  5.3 0.1 pack.1
  5.4 2.8 %collective-permute-start = (bf16[1,60,512]{2,1,0:T(8,128)(2,1)S(1)}, bf16[1,60,512]{2,1,0:T(8,128)(2,1)S(1)}, u32[]{:S(2)}, u32[]{:S(2)}) collective-permute-start(bf16[1,60,512]{2,1,0:T(8,128)(2,1)S(1)} %bitcast.9), channel_id=1, source_target_pairs={{0,16},{1,17},{2,18},{3,19},{4,20},{5,21},{6,22},{7,23},{8,24},{9,... | collective-permute-start | bytes 184328 | tf_op jit(solution)/shard_map/ppermute | solution.py:55
  8.2 0.0 collective-permute-done.1.act1
  8.2 0.6 %acts.1 = bf16[2,240,1536]{2,1,0:T(8,128)(2,1)S(1)} custom-call(bf16[1,6,320,128]{3,2,1,0:T(8,128)(2,1)S(1)} %bitcast.7, bf16[1,6,320,128]{3,2,1,0:T(8,128)(2,1)S(1)} %collective-permute-done.1.act1), custom_call_target="tpu_custom_call" | custom-call | flops 690000000 | tf_op jit(solution)/shard_map/acts/pallas_call | solution.py:62
  8.8 0.0 collective-permute-done.3.top0.bottom0
  8.9 0.4 %collective-permute-done.4.top1.bottom1 = bf16[1,320,128]{2,1,0:T(8,128)(2,1)S(1)} collective-permute-done((bf16[1,320,128]{2,1,0:T(8,128)(2,1)S(1)}, bf16[1,320,128]{2,1,0:T(8,128)(2,1)S(1)}, u32[]{:S(2)}, u32[]{:S(2)}) %collective-permute-start.4) | collective-permute-done | bytes 81952 | tf_op jit(solution)/shard_map/ppermute | solution.py:55
  9.3 0.0 collective-permute-done.2.grad1
  9.3 0.5 %grads.1 = bf16[2,512,1536]{2,1,0:T(8,128)(2,1)S(1)} custom-call(bf16[1,6,320,128]{3,2,1,0:T(8,128)(2,1)S(1)} %get-tuple-element.24.grad0, bf16[1,6,320,128]{3,2,1,0:T(8,128)(2,1)S(1)} %collective-permute-done.2.grad1, bf16[1,320,128]{2,1,0:T(8,128)(2,1)S(1)} %collective-permute-done.3.top0.bottom0, ...), custom_call_target="tpu_custom_call" | custom-call | flops 575000000 | tf_op jit(solution)/shard_map/grads/pallas_call | solution.py:62
  9.7 0.9 %send0.1 = bf16[2,120,512]{2,1,0:T(8,128)(2,1)S(1)} custom-call(bf16[2,240,1536]{2,1,0:T(8,128)(2,1)S(1)} %acts.1, bf16[2,512,1536]{2,1,0:T(8,128)(2,1)S(1)} %grads.1), custom_call_target="tpu_custom_call" | custom-call | flops 1610000000 | tf_op jit(solution)/shard_map/send0/pallas_call | solution.py:62
  10.7 1.1 %collective-permute-start.6 = (bf16[2,120,512]{2,1,0:T(8,128)(2,1)S(1)}, bf16[2,120,512]{2,1,0:T(8,128)(2,1)S(1)}, u32[]{:S(2)}, u32[]{:S(2)}) collective-permute-start(bf16[2,120,512]{2,1,0:T(8,128)(2,1)S(1)} %send0.1), channel_id=1, source_target_pairs={{0,1},{1,0},{2,10},{3,11},{4,5},{5,4},{6,14},{7,15},{8,9},{9,8},{1... | collective-permute-start | bytes 737288 | tf_op jit(solution)/shard_map/ppermute | solution.py:55
  11.8 0.9 %send1.1 = bf16[2,120,512]{2,1,0:T(8,128)(2,1)S(1)} custom-call(bf16[2,240,1536]{2,1,0:T(8,128)(2,1)S(1)} %acts.1, bf16[2,512,1536]{2,1,0:T(8,128)(2,1)S(1)} %grads.1), custom_call_target="tpu_custom_call" | custom-call | flops 1610000000 | tf_op jit(solution)/shard_map/send1/pallas_call | solution.py:62
  12.7 0.8 %keep0.1.keep = f32[2,120,512]{2,1,0:T(8,128)S(1)} custom-call(bf16[2,240,1536]{2,1,0:T(8,128)(2,1)S(1)} %acts.1, bf16[2,512,1536]{2,1,0:T(8,128)(2,1)S(1)} %grads.1), custom_call_target="tpu_custom_call" | custom-call | flops 1150000000 | tf_op jit(solution)/shard_map/keep0/pallas_call | solution.py:62
  13.5 0.0 collective-permute-done.refs_1_
  13.5 1.6 %collective-permute-start.5 = (bf16[1,120,512]{2,1,0:T(8,128)(2,1)S(1)}, bf16[1,120,512]{2,1,0:T(8,128)(2,1)S(1)}, u32[]{:S(2)}, u32[]{:S(2)}) collective-permute-start(bf16[1,120,512]{2,1,0:T(8,128)(2,1)S(1)} %pair.1), channel_id=1, source_target_pairs={{0,8},{1,9},{2,6},{3,7},{4,12},{5,13},{6,2},{7,3},{8,0},{9,1},{10,... | collective-permute-start | bytes 368648 | tf_op jit(solution)/shard_map/ppermute | solution.py:55
  15.2 1.2 %collective-permute-start.7 = (bf16[2,120,512]{2,1,0:T(8,128)(2,1)S(1)}, bf16[2,120,512]{2,1,0:T(8,128)(2,1)S(1)}, u32[]{:S(2)}, u32[]{:S(2)}) collective-permute-start(bf16[2,120,512]{2,1,0:T(8,128)(2,1)S(1)} %send1.1), channel_id=1, source_target_pairs={{0,1},{1,0},{2,10},{3,11},{4,5},{5,4},{6,14},{7,15},{8,9},{9,8},{1... | collective-permute-start | bytes 737288 | tf_op jit(solution)/shard_map/ppermute | solution.py:55
  16.3 0.6 %collective-permute-done.6.message = bf16[2,120,512]{2,1,0:T(8,128)(2,1)S(1)} collective-permute-done((bf16[2,120,512]{2,1,0:T(8,128)(2,1)S(1)}, bf16[2,120,512]{2,1,0:T(8,128)(2,1)S(1)}, u32[]{:S(2)}, u32[]{:S(2)}) %collective-permute-start.6) | collective-permute-done | bytes 245792 | tf_op jit(solution)/shard_map/ppermute | solution.py:55
  16.9 0.5 %turn0.1 = bf16[2,120,512]{2,1,0:T(8,128)(2,1)S(1)} custom-call(f32[2,120,512]{2,1,0:T(8,128)S(1)} %keep0.1.keep, bf16[2,120,512]{2,1,0:T(8,128)(2,1)S(1)} %collective-permute-done.6.message), custom_call_target="tpu_custom_call" | custom-call | flops 1035000000 | tf_op jit(solution)/shard_map/turn0/pallas_call | solution.py:62
  17.4 1.8 %collective-permute-start.8 = (bf16[2,120,512]{2,1,0:T(8,128)(2,1)S(1)}, bf16[2,120,512]{2,1,0:T(8,128)(2,1)S(1)}, u32[]{:S(2)}, u32[]{:S(2)}) collective-permute-start(bf16[2,120,512]{2,1,0:T(8,128)(2,1)S(1)} %turn0.1), channel_id=1, source_target_pairs={{0,4},{1,5},{2,3},{3,2},{4,0},{5,1},{6,7},{7,6},{8,12},{9,13},{10,... | collective-permute-start | bytes 737288 | tf_op jit(solution)/shard_map/ppermute | solution.py:55
  19.2 0.0 collective-permute-done.5
  19.3 2.1 %collective-permute-start.11 = (bf16[2,120,512]{2,1,0:T(8,128)(2,1)S(1)}, bf16[2,120,512]{2,1,0:T(8,128)(2,1)S(1)}, u32[]{:S(2)}, u32[]{:S(2)}) collective-permute-start(bf16[2,120,512]{2,1,0:T(8,128)(2,1)S(1)} %pad_maximum_fusion.own), channel_id=1, source_target_pairs={{0,4},{1,5},{2,3},{3,2},{4,0},{5,1},{6,7},{7,6},{8,12},{9,13},{10,... | collective-permute-start | bytes 737288 | tf_op jit(solution)/shard_map/ppermute | solution.py:55
  21.4 0.7 %keep1.1.keep = f32[2,120,512]{2,1,0:T(8,128)S(1)} custom-call(bf16[2,240,1536]{2,1,0:T(8,128)(2,1)S(1)} %acts.1, bf16[2,512,1536]{2,1,0:T(8,128)(2,1)S(1)} %grads.1), custom_call_target="tpu_custom_call" | custom-call | flops 1150000000 | tf_op jit(solution)/shard_map/keep1/pallas_call | solution.py:62
  22.1 1.2 %collective-permute-start.10 = (bf16[2,120,512]{2,1,0:T(8,128)(2,1)S(1)}, bf16[2,120,512]{2,1,0:T(8,128)(2,1)S(1)}, u32[]{:S(2)}, u32[]{:S(2)}) collective-permute-start(bf16[2,120,512]{2,1,0:T(8,128)(2,1)S(1)} %pad_maximum_fusion.own), channel_id=1, source_target_pairs={{0,1},{1,0},{2,10},{3,11},{4,5},{5,4},{6,14},{7,15},{8,9},{9,8},{1... | collective-permute-start | bytes 737288 | tf_op jit(solution)/shard_map/ppermute | solution.py:55
  23.4 0.0 collective-permute-done.7.message
  23.4 0.3 turn1.1.keep
  23.7 0.0 collective-permute-done.8.message
  23.7 0.3 part0.1
  24.0 1.8 %collective-permute-start.9 = (bf16[120,512]{1,0:T(8,128)(2,1)S(1)}, bf16[120,512]{1,0:T(8,128)(2,1)S(1)}, u32[]{:S(2)}, u32[]{:S(2)}) collective-permute-start(bf16[120,512]{1,0:T(8,128)(2,1)S(1)} %part0.1), channel_id=1, source_target_pairs={{0,8},{1,9},{2,6},{3,7},{4,12},{5,13},{6,2},{7,3},{8,0},{9,1},{10,... | collective-permute-start | bytes 368648 | tf_op jit(solution)/shard_map/ppermute | solution.py:55
  25.8 0.5 %collective-permute-done.11.third = bf16[2,120,512]{2,1,0:T(8,128)(2,1)S(1)} collective-permute-done((bf16[2,120,512]{2,1,0:T(8,128)(2,1)S(1)}, bf16[2,120,512]{2,1,0:T(8,128)(2,1)S(1)}, u32[]{:S(2)}, u32[]{:S(2)}) %collective-permute-start.11) | collective-permute-done | bytes 245792 | tf_op jit(solution)/shard_map/ppermute | solution.py:55
  26.3 1.1 %collective-permute-start.12 = (bf16[2,120,512]{2,1,0:T(8,128)(2,1)S(1)}, bf16[2,120,512]{2,1,0:T(8,128)(2,1)S(1)}, u32[]{:S(2)}, u32[]{:S(2)}) collective-permute-start(bf16[2,120,512]{2,1,0:T(8,128)(2,1)S(1)} %collective-permute-done.11.third), channel_id=1, source_target_pairs={{0,1},{1,0},{2,10},{3,11},{4,5},{5,4},{6,14},{7,15},{8,9},{9,8},{1... | collective-permute-start | bytes 737288 | tf_op jit(solution)/shard_map/ppermute | solution.py:55
  27.4 0.2 part1.1.keep
  27.6 1.4 %collective-permute-done.9.message = bf16[120,512]{1,0:T(8,128)(2,1)S(1)} collective-permute-done((bf16[120,512]{1,0:T(8,128)(2,1)S(1)}, bf16[120,512]{1,0:T(8,128)(2,1)S(1)}, u32[]{:S(2)}, u32[]{:S(2)}) %collective-permute-start.9) | collective-permute-done | bytes 122912 | tf_op jit(solution)/shard_map/ppermute | solution.py:55
  29.0 0.2 halve0.1
  29.2 2.8 %collective-permute-start.15 = (bf16[60,512]{1,0:T(8,128)(2,1)S(1)}, bf16[60,512]{1,0:T(8,128)(2,1)S(1)}, u32[]{:S(2)}, u32[]{:S(2)}) collective-permute-start(bf16[60,512]{1,0:T(8,128)(2,1)S(1)} %halve0.1), channel_id=1, source_target_pairs={{0,16},{1,17},{2,18},{3,19},{4,20},{5,21},{6,22},{7,23},{8,24},{9,... | collective-permute-start | bytes 184328 | tf_op jit(solution)/shard_map/ppermute | solution.py:55
  32.0 0.0 collective-permute-done.10.last0
  32.0 0.2 halve1.1.keep
  32.2 1.5 %early.1 = (bf16[1,6,80,128]{3,2,1,0:T(8,128)(2,1)S(1)}, bf16[1,6,80,128]{3,2,1,0:T(8,128)(2,1)S(1)}, f32[240,1536]{1,0:T(8,128)S(1)}) custom-call(bf16[2,120,512]{2,1,0:T(8,128)(2,1)S(1)} %pad_maximum_fusion.own, bf16[2,120,512]{2,1,0:T(8,128)(2,1)S(1)} %collective-permute-done.11.third, bf16[2,120,512]{2,1,0:T(8,128)(2,1)S(1)} %collective-permute-done.10.last0, ...), custom_call_target="tpu_custom_call" | custom-call | flops 1955000064 | tf_op jit(solution)/shard_map/early/pallas_call | solution.py:62
  33.7 0.1 collective-permute-start.13
  33.8 0.0 collective-permute-done.12.last1
  33.8 0.5 %given.1 = (bf16[1,6,80,128]{3,2,1,0:T(8,128)(2,1)S(1)}, bf16[240,512]{1,0:T(8,128)(2,1)S(1)}) custom-call(bf16[2,120,512]{2,1,0:T(8,128)(2,1)S(1)} %collective-permute-done.12.last1, bf16[2,512,1536]{2,1,0:T(8,128)(2,1)S(1)} %grads.1, f32[240,1536]{1,0:T(8,128)S(1)} %get-tuple-element.39.rest), custom_call_target="tpu_custom_call" | custom-call | flops 575000000 | tf_op jit(solution)/shard_map/given/pallas_call | solution.py:62
  34.3 0.5 %collective-permute-start.14 = (bf16[1,6,80,128]{3,2,1,0:T(8,128)(2,1)S(1)}, bf16[1,6,80,128]{3,2,1,0:T(8,128)(2,1)S(1)}, u32[]{:S(2)}, u32[]{:S(2)}) collective-permute-start(bf16[1,6,80,128]{3,2,1,0:T(8,128)(2,1)S(1)} %get-tuple-element.41), channel_id=1, source_target_pairs={{0,2},{1,3},{2,0},{3,1},{4,6},{5,7},{6,4},{7,5},{8,10},{9,11},{10,... | collective-permute-start | bytes 368648 | tf_op jit(solution)/shard_map/ppermute | solution.py:55
  34.9 0.0 collective-permute-done.15.message
  34.9 0.2 last.1.terms
  35.1 0.5 %own.1.own1 = bf16[1,6,80,128]{3,2,1,0:T(8,128)(2,1)S(1)} custom-call(bf16[240,512]{1,0:T(8,128)(2,1)S(1)} %get-tuple-element.42.left, bf16[2,512,1536]{2,1,0:T(8,128)(2,1)S(1)} %grads.1, f32[240,1536]{1,0:T(8,128)S(1)} %get-tuple-element.39.rest), custom_call_target="tpu_custom_call" | custom-call | flops 575000000 | tf_op jit(solution)/shard_map/own/pallas_call | solution.py:62
  35.5 0.0 collective-permute-done.13.theirs0
  35.6 0.3 collective-permute-done.14.theirs1
  35.8 1.0 %weave.1 = (bf16[1,6,320,128]{3,2,1,0:T(8,128)(2,1)}, f32[9,20,160]{2,1,0:T(8,128)}) custom-call(bf16[1,6,80,128]{3,2,1,0:T(8,128)(2,1)S(1)} %get-tuple-element.37.own0, bf16[1,6,80,128]{3,2,1,0:T(8,128)(2,1)S(1)} %own.1.own1, bf16[1,6,80,128]{3,2,1,0:T(8,128)(2,1)S(1)} %collective-permute-done.13.theirs0, ...), custom_call_target="tpu_custom_call" | custom-call | flops 1035000000 | tf_op jit(solution)/shard_map/weave/pallas_call | solution.py:62
  (2 shorter events, 0.0 us)
Async XLA Ops:
  0.6 4.4 %copy-start = (bf16[1,320,6,128]{3,1,2,0:T(8,128)(2,1)S(1)}, bf16[1,320,6,128]{3,1,2,0:T(8,128)(2,1)}, u32[]{:S(2)}) copy-start(bf16[1,320,6,128]{3,1,2,0:T(8,128)(2,1)} %param.3) | copy-start | bytes 1474564
  0.6 4.7 %copy-start.1 = (bf16[20,9,160]{2,0,1:T(8,128)(2,1)S(1)}, bf16[20,9,160]{2,0,1:T(8,128)(2,1)}, u32[]{:S(2)}) copy-start(bf16[20,9,160]{2,0,1:T(8,128)(2,1)} %param.5) | copy-start | bytes 172804
  1.8 7.0 %collective-permute-start.3 = (bf16[1,320,128]{2,1,0:T(8,128)(2,1)S(1)}, bf16[1,320,128]{2,1,0:T(8,128)(2,1)S(1)}, u32[]{:S(2)}, u32[]{:S(2)}) collective-permute-start(bf16[1,320,128]{2,1,0:T(8,128)(2,1)S(1)} %get-tuple-element.25), channel_id=1, source_target_pairs={{0,1},{1,0},{2,3},{3,2},{4,5},{5,4},{6,7},{7,6},{8,9},{9,8},{10,11... | collective-permute-start | bytes 245768 | tf_op jit(solution)/shard_map/ppermute | solution.py:55
  4.8 4.5 %collective-permute-start.4 = (bf16[1,320,128]{2,1,0:T(8,128)(2,1)S(1)}, bf16[1,320,128]{2,1,0:T(8,128)(2,1)S(1)}, u32[]{:S(2)}, u32[]{:S(2)}) collective-permute-start(bf16[1,320,128]{2,1,0:T(8,128)(2,1)S(1)} %get-tuple-element.25), channel_id=1, source_target_pairs={{0,3},{1,2},{2,1},{3,0},{4,7},{5,6},{6,5},{7,4},{8,11},{9,10},{10,... | collective-permute-start | bytes 245768 | tf_op jit(solution)/shard_map/ppermute | solution.py:55
  4.8 4.5 %collective-permute-start.2 = (bf16[1,6,320,128]{3,2,1,0:T(8,128)(2,1)}, bf16[1,6,320,128]{3,2,1,0:T(8,128)(2,1)S(1)}, u32[]{:S(2)}, u32[]{:S(2)}) collective-permute-start(bf16[1,6,320,128]{3,2,1,0:T(8,128)(2,1)} %bitcast.3.grad), channel_id=1, source_target_pairs={{0,2},{1,3},{2,0},{3,1},{4,6},{5,7},{6,4},{7,5},{8,10},{9,11},{10,... | collective-permute-start | bytes 1474568 | tf_op jit(solution)/shard_map/ppermute | solution.py:55
  5.0 3.2 %collective-permute-start.1 = (bf16[1,6,320,128]{3,2,1,0:T(8,128)(2,1)S(1)}, bf16[1,6,320,128]{3,2,1,0:T(8,128)(2,1)S(1)}, u32[]{:S(2)}, u32[]{:S(2)}) collective-permute-start(bf16[1,6,320,128]{3,2,1,0:T(8,128)(2,1)S(1)} %bitcast.6), channel_id=1, source_target_pairs={{0,2},{1,3},{2,0},{3,1},{4,6},{5,7},{6,4},{7,5},{8,10},{9,11},{10,... | collective-permute-start | bytes 1474568 | tf_op jit(solution)/shard_map/ppermute | solution.py:55
  5.4 8.1 %collective-permute-start = (bf16[1,60,512]{2,1,0:T(8,128)(2,1)S(1)}, bf16[1,60,512]{2,1,0:T(8,128)(2,1)S(1)}, u32[]{:S(2)}, u32[]{:S(2)}) collective-permute-start(bf16[1,60,512]{2,1,0:T(8,128)(2,1)S(1)} %bitcast.9), channel_id=1, source_target_pairs={{0,16},{1,17},{2,18},{3,19},{4,20},{5,21},{6,22},{7,23},{8,24},{9,... | collective-permute-start | bytes 184328 | tf_op jit(solution)/shard_map/ppermute | solution.py:55
  10.7 6.3 %collective-permute-start.6 = (bf16[2,120,512]{2,1,0:T(8,128)(2,1)S(1)}, bf16[2,120,512]{2,1,0:T(8,128)(2,1)S(1)}, u32[]{:S(2)}, u32[]{:S(2)}) collective-permute-start(bf16[2,120,512]{2,1,0:T(8,128)(2,1)S(1)} %send0.1), channel_id=1, source_target_pairs={{0,1},{1,0},{2,10},{3,11},{4,5},{5,4},{6,14},{7,15},{8,9},{9,8},{1... | collective-permute-start | bytes 737288 | tf_op jit(solution)/shard_map/ppermute | solution.py:55
  13.5 5.7 %collective-permute-start.5 = (bf16[1,120,512]{2,1,0:T(8,128)(2,1)S(1)}, bf16[1,120,512]{2,1,0:T(8,128)(2,1)S(1)}, u32[]{:S(2)}, u32[]{:S(2)}) collective-permute-start(bf16[1,120,512]{2,1,0:T(8,128)(2,1)S(1)} %pair.1), channel_id=1, source_target_pairs={{0,8},{1,9},{2,6},{3,7},{4,12},{5,13},{6,2},{7,3},{8,0},{9,1},{10,... | collective-permute-start | bytes 368648 | tf_op jit(solution)/shard_map/ppermute | solution.py:55
  15.2 8.2 %collective-permute-start.7 = (bf16[2,120,512]{2,1,0:T(8,128)(2,1)S(1)}, bf16[2,120,512]{2,1,0:T(8,128)(2,1)S(1)}, u32[]{:S(2)}, u32[]{:S(2)}) collective-permute-start(bf16[2,120,512]{2,1,0:T(8,128)(2,1)S(1)} %send1.1), channel_id=1, source_target_pairs={{0,1},{1,0},{2,10},{3,11},{4,5},{5,4},{6,14},{7,15},{8,9},{9,8},{1... | collective-permute-start | bytes 737288 | tf_op jit(solution)/shard_map/ppermute | solution.py:55
  17.4 6.3 %collective-permute-start.8 = (bf16[2,120,512]{2,1,0:T(8,128)(2,1)S(1)}, bf16[2,120,512]{2,1,0:T(8,128)(2,1)S(1)}, u32[]{:S(2)}, u32[]{:S(2)}) collective-permute-start(bf16[2,120,512]{2,1,0:T(8,128)(2,1)S(1)} %turn0.1), channel_id=1, source_target_pairs={{0,4},{1,5},{2,3},{3,2},{4,0},{5,1},{6,7},{7,6},{8,12},{9,13},{10,... | collective-permute-start | bytes 737288 | tf_op jit(solution)/shard_map/ppermute | solution.py:55
  19.3 7.1 %collective-permute-start.11 = (bf16[2,120,512]{2,1,0:T(8,128)(2,1)S(1)}, bf16[2,120,512]{2,1,0:T(8,128)(2,1)S(1)}, u32[]{:S(2)}, u32[]{:S(2)}) collective-permute-start(bf16[2,120,512]{2,1,0:T(8,128)(2,1)S(1)} %pad_maximum_fusion.own), channel_id=1, source_target_pairs={{0,4},{1,5},{2,3},{3,2},{4,0},{5,1},{6,7},{7,6},{8,12},{9,13},{10,... | collective-permute-start | bytes 737288 | tf_op jit(solution)/shard_map/ppermute | solution.py:55
  22.1 9.9 %collective-permute-start.10 = (bf16[2,120,512]{2,1,0:T(8,128)(2,1)S(1)}, bf16[2,120,512]{2,1,0:T(8,128)(2,1)S(1)}, u32[]{:S(2)}, u32[]{:S(2)}) collective-permute-start(bf16[2,120,512]{2,1,0:T(8,128)(2,1)S(1)} %pad_maximum_fusion.own), channel_id=1, source_target_pairs={{0,1},{1,0},{2,10},{3,11},{4,5},{5,4},{6,14},{7,15},{8,9},{9,8},{1... | collective-permute-start | bytes 737288 | tf_op jit(solution)/shard_map/ppermute | solution.py:55
  24.0 4.9 %collective-permute-start.9 = (bf16[120,512]{1,0:T(8,128)(2,1)S(1)}, bf16[120,512]{1,0:T(8,128)(2,1)S(1)}, u32[]{:S(2)}, u32[]{:S(2)}) collective-permute-start(bf16[120,512]{1,0:T(8,128)(2,1)S(1)} %part0.1), channel_id=1, source_target_pairs={{0,8},{1,9},{2,6},{3,7},{4,12},{5,13},{6,2},{7,3},{8,0},{9,1},{10,... | collective-permute-start | bytes 368648 | tf_op jit(solution)/shard_map/ppermute | solution.py:55
  26.3 7.5 %collective-permute-start.12 = (bf16[2,120,512]{2,1,0:T(8,128)(2,1)S(1)}, bf16[2,120,512]{2,1,0:T(8,128)(2,1)S(1)}, u32[]{:S(2)}, u32[]{:S(2)}) collective-permute-start(bf16[2,120,512]{2,1,0:T(8,128)(2,1)S(1)} %collective-permute-done.11.third), channel_id=1, source_target_pairs={{0,1},{1,0},{2,10},{3,11},{4,5},{5,4},{6,14},{7,15},{8,9},{9,8},{1... | collective-permute-start | bytes 737288 | tf_op jit(solution)/shard_map/ppermute | solution.py:55
  29.2 5.7 %collective-permute-start.15 = (bf16[60,512]{1,0:T(8,128)(2,1)S(1)}, bf16[60,512]{1,0:T(8,128)(2,1)S(1)}, u32[]{:S(2)}, u32[]{:S(2)}) collective-permute-start(bf16[60,512]{1,0:T(8,128)(2,1)S(1)} %halve0.1), channel_id=1, source_target_pairs={{0,16},{1,17},{2,18},{3,19},{4,20},{5,21},{6,22},{7,23},{8,24},{9,... | collective-permute-start | bytes 184328 | tf_op jit(solution)/shard_map/ppermute | solution.py:55
  33.7 1.8 %collective-permute-start.13 = (bf16[1,6,80,128]{3,2,1,0:T(8,128)(2,1)S(1)}, bf16[1,6,80,128]{3,2,1,0:T(8,128)(2,1)S(1)}, u32[]{:S(2)}, u32[]{:S(2)}) collective-permute-start(bf16[1,6,80,128]{3,2,1,0:T(8,128)(2,1)S(1)} %get-tuple-element.43), channel_id=1, source_target_pairs={{0,2},{1,3},{2,0},{3,1},{4,6},{5,7},{6,4},{7,5},{8,10},{9,11},{10,... | collective-permute-start | bytes 368648 | tf_op jit(solution)/shard_map/ppermute | solution.py:55
  34.3 1.5 %collective-permute-start.14 = (bf16[1,6,80,128]{3,2,1,0:T(8,128)(2,1)S(1)}, bf16[1,6,80,128]{3,2,1,0:T(8,128)(2,1)S(1)}, u32[]{:S(2)}, u32[]{:S(2)}) collective-permute-start(bf16[1,6,80,128]{3,2,1,0:T(8,128)(2,1)S(1)} %get-tuple-element.41), channel_id=1, source_target_pairs={{0,2},{1,3},{2,0},{3,1},{4,6},{5,7},{6,4},{7,5},{8,10},{9,11},{10,... | collective-permute-start | bytes 368648 | tf_op jit(solution)/shard_map/ppermute | solution.py:55

commit v14 on v13

--- a/solution.py
+++ b/solution.py
@@ -617,7 +617,7 @@
     shape = (images, rows, channels, width)
     terms = (len(TAP_STEPS) ** 2, plan.depth, plan.cols)
     total = call(
-        "last", functools.partial(last_kernel, plan, scale), jax.ShapeDtypeStruct(terms, jnp.float32), [keep, come]
+        "last", functools.partial(last_kernel, plan, scale), jax.ShapeDtypeStruct(terms, jnp.float32), [after(keep, own1), come]
     )
     input_grad, kernel_grad = call(
         "weave",

time: 37.2 us -> 37.2 us (level)
  no operation moved by 1% of the time
where the time goes in v14:
time: 37.2 us; the launch traced here: 36.8 us
  starting transfers between devices  21.8 us (59%)
  Pallas kernels  10.9 us (29%)
  waiting for transfers between devices  3.22 us (9%)
  between operations  0.84 us (2%)
    ppermute x16, starting transfers between devices, swap(): return lax.ppermute(value, AXES, pairs)  21.8 us
    pallas_call x20, Pallas kernels, call(): pl.pallas_call(kernel, out_shape=out_shape, in_specs=[pl.BlockSpec(memory...  10.9 us
    ppermute x16, waiting for transfers between devices, swap(): return lax.ppermute(value, AXES, pairs)  3.22 us
  transfers between devices with their start and end apart: 16, of which 5 were waited for; matrix products, arithmetic and copies ran while one was open for 0% of the time, Pallas kernels for 24%

profile of v14, /device:TPU:0, one launch (start us, length us, event | category | flops | bytes accessed | tf_op | source)
XLA Modules:
  0.0 36.8 jit_solution(2726256638291309354)
XLA Ops:
  0.6 0.0 copy-start
  0.6 0.0 copy-start.1
  0.6 1.1 %edge.1 = (bf16[1,320,128]{2,1,0:T(8,128)(2,1)S(1)}, bf16[1,6,320,128]{3,2,1,0:T(8,128)(2,1)S(1)}) custom-call(bf16[1,6,320,128]{3,2,1,0:T(8,128)(2,1)} %bitcast.3.grad), custom_call_target="tpu_custom_call" | custom-call | flops 9200000000 | tf_op jit(solution)/shard_map/edge/pallas_call | solution.py:62
  1.8 3.0 %collective-permute-start.3 = (bf16[1,320,128]{2,1,0:T(8,128)(2,1)S(1)}, bf16[1,320,128]{2,1,0:T(8,128)(2,1)S(1)}, u32[]{:S(2)}, u32[]{:S(2)}) collective-permute-start(bf16[1,320,128]{2,1,0:T(8,128)(2,1)S(1)} %get-tuple-element.26), channel_id=1, source_target_pairs={{0,1},{1,0},{2,3},{3,2},{4,5},{5,4},{6,7},{7,6},{8,9},{9,8},{10,11... | collective-permute-start | bytes 245768 | tf_op jit(solution)/shard_map/ppermute | solution.py:55
  4.8 0.0 collective-permute-start.4
  4.8 0.2 collective-permute-start.2
  5.0 0.0 copy-done
  5.0 0.3 collective-permute-start.1
  5.3 0.0 copy-done.1
  5.3 0.1 pack.1
  5.4 2.8 %collective-permute-start = (bf16[1,60,512]{2,1,0:T(8,128)(2,1)S(1)}, bf16[1,60,512]{2,1,0:T(8,128)(2,1)S(1)}, u32[]{:S(2)}, u32[]{:S(2)}) collective-permute-start(bf16[1,60,512]{2,1,0:T(8,128)(2,1)S(1)} %bitcast.9), channel_id=1, source_target_pairs={{0,16},{1,17},{2,18},{3,19},{4,20},{5,21},{6,22},{7,23},{8,24},{9,... | collective-permute-start | bytes 184328 | tf_op jit(solution)/shard_map/ppermute | solution.py:55
  8.2 0.0 collective-permute-done.1.act1
  8.2 0.6 %acts.1 = bf16[2,240,1536]{2,1,0:T(8,128)(2,1)S(1)} custom-call(bf16[1,6,320,128]{3,2,1,0:T(8,128)(2,1)S(1)} %bitcast.7, bf16[1,6,320,128]{3,2,1,0:T(8,128)(2,1)S(1)} %collective-permute-done.1.act1), custom_call_target="tpu_custom_call" | custom-call | flops 690000000 | tf_op jit(solution)/shard_map/acts/pallas_call | solution.py:62
  8.8 0.0 collective-permute-done.3.top0.bottom0
  8.9 0.4 %collective-permute-done.4.top1.bottom1 = bf16[1,320,128]{2,1,0:T(8,128)(2,1)S(1)} collective-permute-done((bf16[1,320,128]{2,1,0:T(8,128)(2,1)S(1)}, bf16[1,320,128]{2,1,0:T(8,128)(2,1)S(1)}, u32[]{:S(2)}, u32[]{:S(2)}) %collective-permute-start.4) | collective-permute-done | bytes 81952 | tf_op jit(solution)/shard_map/ppermute | solution.py:55
  9.3 0.0 collective-permute-done.2.grad1
  9.3 0.5 %grads.1 = bf16[2,512,1536]{2,1,0:T(8,128)(2,1)S(1)} custom-call(bf16[1,6,320,128]{3,2,1,0:T(8,128)(2,1)S(1)} %get-tuple-element.25.grad0, bf16[1,6,320,128]{3,2,1,0:T(8,128)(2,1)S(1)} %collective-permute-done.2.grad1, bf16[1,320,128]{2,1,0:T(8,128)(2,1)S(1)} %collective-permute-done.3.top0.bottom0, ...), custom_call_target="tpu_custom_call" | custom-call | flops 575000000 | tf_op jit(solution)/shard_map/grads/pallas_call | solution.py:62
  9.7 0.9 %send0.1 = bf16[2,120,512]{2,1,0:T(8,128)(2,1)S(1)} custom-call(bf16[2,240,1536]{2,1,0:T(8,128)(2,1)S(1)} %acts.1, bf16[2,512,1536]{2,1,0:T(8,128)(2,1)S(1)} %grads.1), custom_call_target="tpu_custom_call" | custom-call | flops 1610000000 | tf_op jit(solution)/shard_map/send0/pallas_call | solution.py:62
  10.7 1.1 %collective-permute-start.6 = (bf16[2,120,512]{2,1,0:T(8,128)(2,1)S(1)}, bf16[2,120,512]{2,1,0:T(8,128)(2,1)S(1)}, u32[]{:S(2)}, u32[]{:S(2)}) collective-permute-start(bf16[2,120,512]{2,1,0:T(8,128)(2,1)S(1)} %send0.1), channel_id=1, source_target_pairs={{0,1},{1,0},{2,10},{3,11},{4,5},{5,4},{6,14},{7,15},{8,9},{9,8},{1... | collective-permute-start | bytes 737288 | tf_op jit(solution)/shard_map/ppermute | solution.py:55
  11.8 0.9 %send1.1 = bf16[2,120,512]{2,1,0:T(8,128)(2,1)S(1)} custom-call(bf16[2,240,1536]{2,1,0:T(8,128)(2,1)S(1)} %acts.1, bf16[2,512,1536]{2,1,0:T(8,128)(2,1)S(1)} %grads.1), custom_call_target="tpu_custom_call" | custom-call | flops 1610000000 | tf_op jit(solution)/shard_map/send1/pallas_call | solution.py:62
  12.7 0.8 %keep0.1.keep = f32[2,120,512]{2,1,0:T(8,128)S(1)} custom-call(bf16[2,240,1536]{2,1,0:T(8,128)(2,1)S(1)} %acts.1, bf16[2,512,1536]{2,1,0:T(8,128)(2,1)S(1)} %grads.1), custom_call_target="tpu_custom_call" | custom-call | flops 1150000000 | tf_op jit(solution)/shard_map/keep0/pallas_call | solution.py:62
  13.5 0.0 collective-permute-done.refs_1_
  13.5 1.6 %collective-permute-start.5 = (bf16[1,120,512]{2,1,0:T(8,128)(2,1)S(1)}, bf16[1,120,512]{2,1,0:T(8,128)(2,1)S(1)}, u32[]{:S(2)}, u32[]{:S(2)}) collective-permute-start(bf16[1,120,512]{2,1,0:T(8,128)(2,1)S(1)} %pair.1), channel_id=1, source_target_pairs={{0,8},{1,9},{2,6},{3,7},{4,12},{5,13},{6,2},{7,3},{8,0},{9,1},{10,... | collective-permute-start | bytes 368648 | tf_op jit(solution)/shard_map/ppermute | solution.py:55
  15.2 1.2 %collective-permute-start.7 = (bf16[2,120,512]{2,1,0:T(8,128)(2,1)S(1)}, bf16[2,120,512]{2,1,0:T(8,128)(2,1)S(1)}, u32[]{:S(2)}, u32[]{:S(2)}) collective-permute-start(bf16[2,120,512]{2,1,0:T(8,128)(2,1)S(1)} %send1.1), channel_id=1, source_target_pairs={{0,1},{1,0},{2,10},{3,11},{4,5},{5,4},{6,14},{7,15},{8,9},{9,8},{1... | collective-permute-start | bytes 737288 | tf_op jit(solution)/shard_map/ppermute | solution.py:55
  16.3 0.6 %collective-permute-done.6.message = bf16[2,120,512]{2,1,0:T(8,128)(2,1)S(1)} collective-permute-done((bf16[2,120,512]{2,1,0:T(8,128)(2,1)S(1)}, bf16[2,120,512]{2,1,0:T(8,128)(2,1)S(1)}, u32[]{:S(2)}, u32[]{:S(2)}) %collective-permute-start.6) | collective-permute-done | bytes 245792 | tf_op jit(solution)/shard_map/ppermute | solution.py:55
  16.9 0.5 %turn0.1 = bf16[2,120,512]{2,1,0:T(8,128)(2,1)S(1)} custom-call(f32[2,120,512]{2,1,0:T(8,128)S(1)} %keep0.1.keep, bf16[2,120,512]{2,1,0:T(8,128)(2,1)S(1)} %collective-permute-done.6.message), custom_call_target="tpu_custom_call" | custom-call | flops 1035000000 | tf_op jit(solution)/shard_map/turn0/pallas_call | solution.py:62
  17.4 1.8 %collective-permute-start.8 = (bf16[2,120,512]{2,1,0:T(8,128)(2,1)S(1)}, bf16[2,120,512]{2,1,0:T(8,128)(2,1)S(1)}, u32[]{:S(2)}, u32[]{:S(2)}) collective-permute-start(bf16[2,120,512]{2,1,0:T(8,128)(2,1)S(1)} %turn0.1), channel_id=1, source_target_pairs={{0,4},{1,5},{2,3},{3,2},{4,0},{5,1},{6,7},{7,6},{8,12},{9,13},{10,... | collective-permute-start | bytes 737288 | tf_op jit(solution)/shard_map/ppermute | solution.py:55
  19.2 0.0 collective-permute-done.5
  19.3 2.1 %collective-permute-start.11 = (bf16[2,120,512]{2,1,0:T(8,128)(2,1)S(1)}, bf16[2,120,512]{2,1,0:T(8,128)(2,1)S(1)}, u32[]{:S(2)}, u32[]{:S(2)}) collective-permute-start(bf16[2,120,512]{2,1,0:T(8,128)(2,1)S(1)} %pad_maximum_fusion.own), channel_id=1, source_target_pairs={{0,4},{1,5},{2,3},{3,2},{4,0},{5,1},{6,7},{7,6},{8,12},{9,13},{10,... | collective-permute-start | bytes 737288 | tf_op jit(solution)/shard_map/ppermute | solution.py:55
  21.4 0.7 %keep1.1.keep = f32[2,120,512]{2,1,0:T(8,128)S(1)} custom-call(bf16[2,240,1536]{2,1,0:T(8,128)(2,1)S(1)} %acts.1, bf16[2,512,1536]{2,1,0:T(8,128)(2,1)S(1)} %grads.1), custom_call_target="tpu_custom_call" | custom-call | flops 1150000000 | tf_op jit(solution)/shard_map/keep1/pallas_call | solution.py:62
  22.1 1.2 %collective-permute-start.10 = (bf16[2,120,512]{2,1,0:T(8,128)(2,1)S(1)}, bf16[2,120,512]{2,1,0:T(8,128)(2,1)S(1)}, u32[]{:S(2)}, u32[]{:S(2)}) collective-permute-start(bf16[2,120,512]{2,1,0:T(8,128)(2,1)S(1)} %pad_maximum_fusion.own), channel_id=1, source_target_pairs={{0,1},{1,0},{2,10},{3,11},{4,5},{5,4},{6,14},{7,15},{8,9},{9,8},{1... | collective-permute-start | bytes 737288 | tf_op jit(solution)/shard_map/ppermute | solution.py:55
  23.4 0.0 collective-permute-done.7.message
  23.4 0.3 turn1.1.keep
  23.7 0.0 collective-permute-done.8.message
  23.7 0.3 part0.1
  24.0 1.8 %collective-permute-start.9 = (bf16[120,512]{1,0:T(8,128)(2,1)S(1)}, bf16[120,512]{1,0:T(8,128)(2,1)S(1)}, u32[]{:S(2)}, u32[]{:S(2)}) collective-permute-start(bf16[120,512]{1,0:T(8,128)(2,1)S(1)} %part0.1), channel_id=1, source_target_pairs={{0,8},{1,9},{2,6},{3,7},{4,12},{5,13},{6,2},{7,3},{8,0},{9,1},{10,... | collective-permute-start | bytes 368648 | tf_op jit(solution)/shard_map/ppermute | solution.py:55
  25.8 0.5 %collective-permute-done.11.third = bf16[2,120,512]{2,1,0:T(8,128)(2,1)S(1)} collective-permute-done((bf16[2,120,512]{2,1,0:T(8,128)(2,1)S(1)}, bf16[2,120,512]{2,1,0:T(8,128)(2,1)S(1)}, u32[]{:S(2)}, u32[]{:S(2)}) %collective-permute-start.11) | collective-permute-done | bytes 245792 | tf_op jit(solution)/shard_map/ppermute | solution.py:55
  26.3 1.1 %collective-permute-start.12 = (bf16[2,120,512]{2,1,0:T(8,128)(2,1)S(1)}, bf16[2,120,512]{2,1,0:T(8,128)(2,1)S(1)}, u32[]{:S(2)}, u32[]{:S(2)}) collective-permute-start(bf16[2,120,512]{2,1,0:T(8,128)(2,1)S(1)} %collective-permute-done.11.third), channel_id=1, source_target_pairs={{0,1},{1,0},{2,10},{3,11},{4,5},{5,4},{6,14},{7,15},{8,9},{9,8},{1... | collective-permute-start | bytes 737288 | tf_op jit(solution)/shard_map/ppermute | solution.py:55
  27.4 0.2 part1.1.keep
  27.6 1.4 %collective-permute-done.9.message = bf16[120,512]{1,0:T(8,128)(2,1)S(1)} collective-permute-done((bf16[120,512]{1,0:T(8,128)(2,1)S(1)}, bf16[120,512]{1,0:T(8,128)(2,1)S(1)}, u32[]{:S(2)}, u32[]{:S(2)}) %collective-permute-start.9) | collective-permute-done | bytes 122912 | tf_op jit(solution)/shard_map/ppermute | solution.py:55
  29.0 0.2 halve0.1
  29.2 2.8 %collective-permute-start.15 = (bf16[60,512]{1,0:T(8,128)(2,1)S(1)}, bf16[60,512]{1,0:T(8,128)(2,1)S(1)}, u32[]{:S(2)}, u32[]{:S(2)}) collective-permute-start(bf16[60,512]{1,0:T(8,128)(2,1)S(1)} %halve0.1), channel_id=1, source_target_pairs={{0,16},{1,17},{2,18},{3,19},{4,20},{5,21},{6,22},{7,23},{8,24},{9,... | collective-permute-start | bytes 184328 | tf_op jit(solution)/shard_map/ppermute | solution.py:55
  32.0 0.0 collective-permute-done.10.last0
  32.0 0.2 halve1.1.keep
  32.2 1.5 %early.1 = (bf16[1,6,80,128]{3,2,1,0:T(8,128)(2,1)S(1)}, bf16[1,6,80,128]{3,2,1,0:T(8,128)(2,1)S(1)}, f32[240,1536]{1,0:T(8,128)S(1)}) custom-call(bf16[2,120,512]{2,1,0:T(8,128)(2,1)S(1)} %pad_maximum_fusion.own, bf16[2,120,512]{2,1,0:T(8,128)(2,1)S(1)} %collective-permute-done.11.third, bf16[2,120,512]{2,1,0:T(8,128)(2,1)S(1)} %collective-permute-done.10.last0, ...), custom_call_target="tpu_custom_call" | custom-call | flops 1955000064 | tf_op jit(solution)/shard_map/early/pallas_call | solution.py:62
  33.7 0.1 collective-permute-start.13
  33.8 0.0 collective-permute-done.12.last1
  33.8 0.5 %given.1 = (bf16[1,6,80,128]{3,2,1,0:T(8,128)(2,1)S(1)}, bf16[240,512]{1,0:T(8,128)(2,1)S(1)}) custom-call(bf16[2,120,512]{2,1,0:T(8,128)(2,1)S(1)} %collective-permute-done.12.last1, bf16[2,512,1536]{2,1,0:T(8,128)(2,1)S(1)} %grads.1, f32[240,1536]{1,0:T(8,128)S(1)} %get-tuple-element.40.rest), custom_call_target="tpu_custom_call" | custom-call | flops 575000000 | tf_op jit(solution)/shard_map/given/pallas_call | solution.py:62
  34.3 0.5 %collective-permute-start.14 = (bf16[1,6,80,128]{3,2,1,0:T(8,128)(2,1)S(1)}, bf16[1,6,80,128]{3,2,1,0:T(8,128)(2,1)S(1)}, u32[]{:S(2)}, u32[]{:S(2)}) collective-permute-start(bf16[1,6,80,128]{3,2,1,0:T(8,128)(2,1)S(1)} %get-tuple-element.42), channel_id=1, source_target_pairs={{0,2},{1,3},{2,0},{3,1},{4,6},{5,7},{6,4},{7,5},{8,10},{9,11},{10,... | collective-permute-start | bytes 368648 | tf_op jit(solution)/shard_map/ppermute | solution.py:55
  34.9 0.5 %own.1.own1 = bf16[1,6,80,128]{3,2,1,0:T(8,128)(2,1)S(1)} custom-call(bf16[240,512]{1,0:T(8,128)(2,1)S(1)} %get-tuple-element.43.left, bf16[2,512,1536]{2,1,0:T(8,128)(2,1)S(1)} %grads.1, f32[240,1536]{1,0:T(8,128)S(1)} %get-tuple-element.40.rest), custom_call_target="tpu_custom_call" | custom-call | flops 575000000 | tf_op jit(solution)/shard_map/own/pallas_call | solution.py:62
  35.3 0.0 collective-permute-done.15.message
  35.3 0.2 last.1.terms
  35.5 0.0 collective-permute-done.13.theirs0
  35.6 0.3 collective-permute-done.14.theirs1
  35.8 1.0 %weave.1 = (bf16[1,6,320,128]{3,2,1,0:T(8,128)(2,1)}, f32[9,20,160]{2,1,0:T(8,128)}) custom-call(bf16[1,6,80,128]{3,2,1,0:T(8,128)(2,1)S(1)} %get-tuple-element.38.own0, bf16[1,6,80,128]{3,2,1,0:T(8,128)(2,1)S(1)} %own.1.own1, bf16[1,6,80,128]{3,2,1,0:T(8,128)(2,1)S(1)} %collective-permute-done.13.theirs0, ...), custom_call_target="tpu_custom_call" | custom-call | flops 1035000000 | tf_op jit(solution)/shard_map/weave/pallas_call | solution.py:62
  (2 shorter events, 0.0 us)
Async XLA Ops:
  0.6 4.4 %copy-start = (bf16[1,320,6,128]{3,1,2,0:T(8,128)(2,1)S(1)}, bf16[1,320,6,128]{3,1,2,0:T(8,128)(2,1)}, u32[]{:S(2)}) copy-start(bf16[1,320,6,128]{3,1,2,0:T(8,128)(2,1)} %param.3) | copy-start | bytes 1474564
  0.6 4.7 %copy-start.1 = (bf16[20,9,160]{2,0,1:T(8,128)(2,1)S(1)}, bf16[20,9,160]{2,0,1:T(8,128)(2,1)}, u32[]{:S(2)}) copy-start(bf16[20,9,160]{2,0,1:T(8,128)(2,1)} %param.5) | copy-start | bytes 172804
  1.8 7.0 %collective-permute-start.3 = (bf16[1,320,128]{2,1,0:T(8,128)(2,1)S(1)}, bf16[1,320,128]{2,1,0:T(8,128)(2,1)S(1)}, u32[]{:S(2)}, u32[]{:S(2)}) collective-permute-start(bf16[1,320,128]{2,1,0:T(8,128)(2,1)S(1)} %get-tuple-element.26), channel_id=1, source_target_pairs={{0,1},{1,0},{2,3},{3,2},{4,5},{5,4},{6,7},{7,6},{8,9},{9,8},{10,11... | collective-permute-start | bytes 245768 | tf_op jit(solution)/shard_map/ppermute | solution.py:55
  4.8 4.5 %collective-permute-start.4 = (bf16[1,320,128]{2,1,0:T(8,128)(2,1)S(1)}, bf16[1,320,128]{2,1,0:T(8,128)(2,1)S(1)}, u32[]{:S(2)}, u32[]{:S(2)}) collective-permute-start(bf16[1,320,128]{2,1,0:T(8,128)(2,1)S(1)} %get-tuple-element.26), channel_id=1, source_target_pairs={{0,3},{1,2},{2,1},{3,0},{4,7},{5,6},{6,5},{7,4},{8,11},{9,10},{10,... | collective-permute-start | bytes 245768 | tf_op jit(solution)/shard_map/ppermute | solution.py:55
  4.8 4.5 %collective-permute-start.2 = (bf16[1,6,320,128]{3,2,1,0:T(8,128)(2,1)}, bf16[1,6,320,128]{3,2,1,0:T(8,128)(2,1)S(1)}, u32[]{:S(2)}, u32[]{:S(2)}) collective-permute-start(bf16[1,6,320,128]{3,2,1,0:T(8,128)(2,1)} %bitcast.3.grad), channel_id=1, source_target_pairs={{0,2},{1,3},{2,0},{3,1},{4,6},{5,7},{6,4},{7,5},{8,10},{9,11},{10,... | collective-permute-start | bytes 1474568 | tf_op jit(solution)/shard_map/ppermute | solution.py:55
  5.0 3.2 %collective-permute-start.1 = (bf16[1,6,320,128]{3,2,1,0:T(8,128)(2,1)S(1)}, bf16[1,6,320,128]{3,2,1,0:T(8,128)(2,1)S(1)}, u32[]{:S(2)}, u32[]{:S(2)}) collective-permute-start(bf16[1,6,320,128]{3,2,1,0:T(8,128)(2,1)S(1)} %bitcast.6), channel_id=1, source_target_pairs={{0,2},{1,3},{2,0},{3,1},{4,6},{5,7},{6,4},{7,5},{8,10},{9,11},{10,... | collective-permute-start | bytes 1474568 | tf_op jit(solution)/shard_map/ppermute | solution.py:55
  5.4 8.1 %collective-permute-start = (bf16[1,60,512]{2,1,0:T(8,128)(2,1)S(1)}, bf16[1,60,512]{2,1,0:T(8,128)(2,1)S(1)}, u32[]{:S(2)}, u32[]{:S(2)}) collective-permute-start(bf16[1,60,512]{2,1,0:T(8,128)(2,1)S(1)} %bitcast.9), channel_id=1, source_target_pairs={{0,16},{1,17},{2,18},{3,19},{4,20},{5,21},{6,22},{7,23},{8,24},{9,... | collective-permute-start | bytes 184328 | tf_op jit(solution)/shard_map/ppermute | solution.py:55
  10.7 6.3 %collective-permute-start.6 = (bf16[2,120,512]{2,1,0:T(8,128)(2,1)S(1)}, bf16[2,120,512]{2,1,0:T(8,128)(2,1)S(1)}, u32[]{:S(2)}, u32[]{:S(2)}) collective-permute-start(bf16[2,120,512]{2,1,0:T(8,128)(2,1)S(1)} %send0.1), channel_id=1, source_target_pairs={{0,1},{1,0},{2,10},{3,11},{4,5},{5,4},{6,14},{7,15},{8,9},{9,8},{1... | collective-permute-start | bytes 737288 | tf_op jit(solution)/shard_map/ppermute | solution.py:55
  13.5 5.7 %collective-permute-start.5 = (bf16[1,120,512]{2,1,0:T(8,128)(2,1)S(1)}, bf16[1,120,512]{2,1,0:T(8,128)(2,1)S(1)}, u32[]{:S(2)}, u32[]{:S(2)}) collective-permute-start(bf16[1,120,512]{2,1,0:T(8,128)(2,1)S(1)} %pair.1), channel_id=1, source_target_pairs={{0,8},{1,9},{2,6},{3,7},{4,12},{5,13},{6,2},{7,3},{8,0},{9,1},{10,... | collective-permute-start | bytes 368648 | tf_op jit(solution)/shard_map/ppermute | solution.py:55
  15.2 8.2 %collective-permute-start.7 = (bf16[2,120,512]{2,1,0:T(8,128)(2,1)S(1)}, bf16[2,120,512]{2,1,0:T(8,128)(2,1)S(1)}, u32[]{:S(2)}, u32[]{:S(2)}) collective-permute-start(bf16[2,120,512]{2,1,0:T(8,128)(2,1)S(1)} %send1.1), channel_id=1, source_target_pairs={{0,1},{1,0},{2,10},{3,11},{4,5},{5,4},{6,14},{7,15},{8,9},{9,8},{1... | collective-permute-start | bytes 737288 | tf_op jit(solution)/shard_map/ppermute | solution.py:55
  17.4 6.3 %collective-permute-start.8 = (bf16[2,120,512]{2,1,0:T(8,128)(2,1)S(1)}, bf16[2,120,512]{2,1,0:T(8,128)(2,1)S(1)}, u32[]{:S(2)}, u32[]{:S(2)}) collective-permute-start(bf16[2,120,512]{2,1,0:T(8,128)(2,1)S(1)} %turn0.1), channel_id=1, source_target_pairs={{0,4},{1,5},{2,3},{3,2},{4,0},{5,1},{6,7},{7,6},{8,12},{9,13},{10,... | collective-permute-start | bytes 737288 | tf_op jit(solution)/shard_map/ppermute | solution.py:55
  19.3 7.1 %collective-permute-start.11 = (bf16[2,120,512]{2,1,0:T(8,128)(2,1)S(1)}, bf16[2,120,512]{2,1,0:T(8,128)(2,1)S(1)}, u32[]{:S(2)}, u32[]{:S(2)}) collective-permute-start(bf16[2,120,512]{2,1,0:T(8,128)(2,1)S(1)} %pad_maximum_fusion.own), channel_id=1, source_target_pairs={{0,4},{1,5},{2,3},{3,2},{4,0},{5,1},{6,7},{7,6},{8,12},{9,13},{10,... | collective-permute-start | bytes 737288 | tf_op jit(solution)/shard_map/ppermute | solution.py:55
  22.1 9.9 %collective-permute-start.10 = (bf16[2,120,512]{2,1,0:T(8,128)(2,1)S(1)}, bf16[2,120,512]{2,1,0:T(8,128)(2,1)S(1)}, u32[]{:S(2)}, u32[]{:S(2)}) collective-permute-start(bf16[2,120,512]{2,1,0:T(8,128)(2,1)S(1)} %pad_maximum_fusion.own), channel_id=1, source_target_pairs={{0,1},{1,0},{2,10},{3,11},{4,5},{5,4},{6,14},{7,15},{8,9},{9,8},{1... | collective-permute-start | bytes 737288 | tf_op jit(solution)/shard_map/ppermute | solution.py:55
  24.0 4.9 %collective-permute-start.9 = (bf16[120,512]{1,0:T(8,128)(2,1)S(1)}, bf16[120,512]{1,0:T(8,128)(2,1)S(1)}, u32[]{:S(2)}, u32[]{:S(2)}) collective-permute-start(bf16[120,512]{1,0:T(8,128)(2,1)S(1)} %part0.1), channel_id=1, source_target_pairs={{0,8},{1,9},{2,6},{3,7},{4,12},{5,13},{6,2},{7,3},{8,0},{9,1},{10,... | collective-permute-start | bytes 368648 | tf_op jit(solution)/shard_map/ppermute | solution.py:55
  26.3 7.5 %collective-permute-start.12 = (bf16[2,120,512]{2,1,0:T(8,128)(2,1)S(1)}, bf16[2,120,512]{2,1,0:T(8,128)(2,1)S(1)}, u32[]{:S(2)}, u32[]{:S(2)}) collective-permute-start(bf16[2,120,512]{2,1,0:T(8,128)(2,1)S(1)} %collective-permute-done.11.third), channel_id=1, source_target_pairs={{0,1},{1,0},{2,10},{3,11},{4,5},{5,4},{6,14},{7,15},{8,9},{9,8},{1... | collective-permute-start | bytes 737288 | tf_op jit(solution)/shard_map/ppermute | solution.py:55
  29.2 6.1 %collective-permute-start.15 = (bf16[60,512]{1,0:T(8,128)(2,1)S(1)}, bf16[60,512]{1,0:T(8,128)(2,1)S(1)}, u32[]{:S(2)}, u32[]{:S(2)}) collective-permute-start(bf16[60,512]{1,0:T(8,128)(2,1)S(1)} %halve0.1), channel_id=1, source_target_pairs={{0,16},{1,17},{2,18},{3,19},{4,20},{5,21},{6,22},{7,23},{8,24},{9,... | collective-permute-start | bytes 184328 | tf_op jit(solution)/shard_map/ppermute | solution.py:55
  33.7 1.8 %collective-permute-start.13 = (bf16[1,6,80,128]{3,2,1,0:T(8,128)(2,1)S(1)}, bf16[1,6,80,128]{3,2,1,0:T(8,128)(2,1)S(1)}, u32[]{:S(2)}, u32[]{:S(2)}) collective-permute-start(bf16[1,6,80,128]{3,2,1,0:T(8,128)(2,1)S(1)} %get-tuple-element.44), channel_id=1, source_target_pairs={{0,2},{1,3},{2,0},{3,1},{4,6},{5,7},{6,4},{7,5},{8,10},{9,11},{10,... | collective-permute-start | bytes 368648 | tf_op jit(solution)/shard_map/ppermute | solution.py:55
  34.3 1.5 %collective-permute-start.14 = (bf16[1,6,80,128]{3,2,1,0:T(8,128)(2,1)S(1)}, bf16[1,6,80,128]{3,2,1,0:T(8,128)(2,1)S(1)}, u32[]{:S(2)}, u32[]{:S(2)}) collective-permute-start(bf16[1,6,80,128]{3,2,1,0:T(8,128)(2,1)S(1)} %get-tuple-element.42), channel_id=1, source_target_pairs={{0,2},{1,3},{2,0},{3,1},{4,6},{5,7},{6,4},{7,5},{8,10},{9,11},{10,... | collective-permute-start | bytes 368648 | tf_op jit(solution)/shard_map/ppermute | solution.py:55

commit v15 on v14

--- a/solution.py
+++ b/solution.py
@@ -222,17 +222,17 @@
 def send_kernel(plan, same, acts, grads, out):
     first, second, _ = mine(plan)
     total = pair_terms(plan, acts, grads, 1 - first, second if same else 1 - second)
+    peak = rounded_up(largest(total))
     for k in range(2):
-        half = total[k * plan.part_rows : (k + 1) * plan.part_rows]
-        out[k] = encoded(rounded_up(largest(half)), half, plan.half_used)
+        out[k] = encoded(peak, total[k * plan.part_rows : (k + 1) * plan.part_rows], plan.half_used)
 
 
 def keep_kernel(plan, same, acts, grads, out):
     first, second, _ = mine(plan)
     total = pair_terms(plan, acts, grads, first, second if same else 1 - second)
+    peak = largest(total)
     for k in range(2):
-        half = total[k * plan.part_rows : (k + 1) * plan.part_rows]
-        out[k] = noted(largest(half), half, plan.half_used)
+        out[k] = noted(peak, total[k * plan.part_rows : (k + 1) * plan.part_rows], plan.half_used)
 
 
 def turn_kernel(plan, same, keep, message, out):

time: 37.2 us -> 37.3 us (level)
  transfers between devices with their start and end apart: 16 -> 16, of which waited for: 5 -> 6; matrix products, arithmetic and copies ran while one was open for 0% -> 0% of each run, Pallas kernels for 24% -> 24%
where the time goes in v15:
time: 37.3 us; the launch traced here: 36.8 us
  starting transfers between devices  21.7 us (58%)
  Pallas kernels  10.9 us (29%)
  waiting for transfers between devices  3.29 us (9%)
  between operations  0.84 us (2%)
    ppermute x16, starting transfers between devices, swap(): return lax.ppermute(value, AXES, pairs)  21.7 us
    pallas_call x20, Pallas kernels, call(): pl.pallas_call(kernel, out_shape=out_shape, in_specs=[pl.BlockSpec(memory...  10.9 us
    ppermute x16, waiting for transfers between devices, swap(): return lax.ppermute(value, AXES, pairs)  3.29 us
  transfers between devices with their start and end apart: 16, of which 6 were waited for; matrix products, arithmetic and copies ran while one was open for 0% of the time, Pallas kernels for 24%

profile of v15, /device:TPU:0, one launch (start us, length us, event | category | flops | bytes accessed | tf_op | source)
XLA Modules:
  0.0 36.8 jit_solution(16126377509726312996)
XLA Ops:
  0.6 0.0 copy-start
  0.6 0.0 copy-start.1
  0.6 1.1 %edge.1 = (bf16[1,320,128]{2,1,0:T(8,128)(2,1)S(1)}, bf16[1,6,320,128]{3,2,1,0:T(8,128)(2,1)S(1)}) custom-call(bf16[1,6,320,128]{3,2,1,0:T(8,128)(2,1)} %bitcast.3.grad), custom_call_target="tpu_custom_call" | custom-call | flops 9200000000 | tf_op jit(solution)/shard_map/edge/pallas_call | solution.py:62
  1.8 3.0 %collective-permute-start.3 = (bf16[1,320,128]{2,1,0:T(8,128)(2,1)S(1)}, bf16[1,320,128]{2,1,0:T(8,128)(2,1)S(1)}, u32[]{:S(2)}, u32[]{:S(2)}) collective-permute-start(bf16[1,320,128]{2,1,0:T(8,128)(2,1)S(1)} %get-tuple-element.26), channel_id=1, source_target_pairs={{0,1},{1,0},{2,3},{3,2},{4,5},{5,4},{6,7},{7,6},{8,9},{9,8},{10,11... | collective-permute-start | bytes 245768 | tf_op jit(solution)/shard_map/ppermute | solution.py:55
  4.8 0.0 collective-permute-start.4
  4.8 0.2 collective-permute-start.2
  5.0 0.0 copy-done
  5.0 0.3 collective-permute-start.1
  5.3 0.0 copy-done.1
  5.3 0.1 pack.1
  5.4 2.8 %collective-permute-start = (bf16[1,60,512]{2,1,0:T(8,128)(2,1)S(1)}, bf16[1,60,512]{2,1,0:T(8,128)(2,1)S(1)}, u32[]{:S(2)}, u32[]{:S(2)}) collective-permute-start(bf16[1,60,512]{2,1,0:T(8,128)(2,1)S(1)} %bitcast.9), channel_id=1, source_target_pairs={{0,16},{1,17},{2,18},{3,19},{4,20},{5,21},{6,22},{7,23},{8,24},{9,... | collective-permute-start | bytes 184328 | tf_op jit(solution)/shard_map/ppermute | solution.py:55
  8.2 0.0 collective-permute-done.1.act1
  8.2 0.6 %acts.1 = bf16[2,240,1536]{2,1,0:T(8,128)(2,1)S(1)} custom-call(bf16[1,6,320,128]{3,2,1,0:T(8,128)(2,1)S(1)} %bitcast.7, bf16[1,6,320,128]{3,2,1,0:T(8,128)(2,1)S(1)} %collective-permute-done.1.act1), custom_call_target="tpu_custom_call" | custom-call | flops 690000000 | tf_op jit(solution)/shard_map/acts/pallas_call | solution.py:62
  8.8 0.0 collective-permute-done.3.top0.bottom0
  8.9 0.4 %collective-permute-done.4.top1.bottom1 = bf16[1,320,128]{2,1,0:T(8,128)(2,1)S(1)} collective-permute-done((bf16[1,320,128]{2,1,0:T(8,128)(2,1)S(1)}, bf16[1,320,128]{2,1,0:T(8,128)(2,1)S(1)}, u32[]{:S(2)}, u32[]{:S(2)}) %collective-permute-start.4) | collective-permute-done | bytes 81952 | tf_op jit(solution)/shard_map/ppermute | solution.py:55
  9.3 0.0 collective-permute-done.2.grad1
  9.3 0.5 %grads.1 = bf16[2,512,1536]{2,1,0:T(8,128)(2,1)S(1)} custom-call(bf16[1,6,320,128]{3,2,1,0:T(8,128)(2,1)S(1)} %get-tuple-element.25.grad0, bf16[1,6,320,128]{3,2,1,0:T(8,128)(2,1)S(1)} %collective-permute-done.2.grad1, bf16[1,320,128]{2,1,0:T(8,128)(2,1)S(1)} %collective-permute-done.3.top0.bottom0, ...), custom_call_target="tpu_custom_call" | custom-call | flops 575000000 | tf_op jit(solution)/shard_map/grads/pallas_call | solution.py:62
  9.7 0.9 %send0.1 = bf16[2,120,512]{2,1,0:T(8,128)(2,1)S(1)} custom-call(bf16[2,240,1536]{2,1,0:T(8,128)(2,1)S(1)} %acts.1, bf16[2,512,1536]{2,1,0:T(8,128)(2,1)S(1)} %grads.1), custom_call_target="tpu_custom_call" | custom-call | flops 1610000000 | tf_op jit(solution)/shard_map/send0/pallas_call | solution.py:62
  10.7 1.1 %collective-permute-start.6 = (bf16[2,120,512]{2,1,0:T(8,128)(2,1)S(1)}, bf16[2,120,512]{2,1,0:T(8,128)(2,1)S(1)}, u32[]{:S(2)}, u32[]{:S(2)}) collective-permute-start(bf16[2,120,512]{2,1,0:T(8,128)(2,1)S(1)} %send0.1), channel_id=1, source_target_pairs={{0,1},{1,0},{2,10},{3,11},{4,5},{5,4},{6,14},{7,15},{8,9},{9,8},{1... | collective-permute-start | bytes 737288 | tf_op jit(solution)/shard_map/ppermute | solution.py:55
  11.8 0.9 %send1.1 = bf16[2,120,512]{2,1,0:T(8,128)(2,1)S(1)} custom-call(bf16[2,240,1536]{2,1,0:T(8,128)(2,1)S(1)} %acts.1, bf16[2,512,1536]{2,1,0:T(8,128)(2,1)S(1)} %grads.1), custom_call_target="tpu_custom_call" | custom-call | flops 1610000000 | tf_op jit(solution)/shard_map/send1/pallas_call | solution.py:62
  12.8 0.8 %keep0.1.keep = f32[2,120,512]{2,1,0:T(8,128)S(1)} custom-call(bf16[2,240,1536]{2,1,0:T(8,128)(2,1)S(1)} %acts.1, bf16[2,512,1536]{2,1,0:T(8,128)(2,1)S(1)} %grads.1), custom_call_target="tpu_custom_call" | custom-call | flops 1150000000 | tf_op jit(solution)/shard_map/keep0/pallas_call | solution.py:62
  13.5 0.0 collective-permute-done.refs_1_
  13.6 1.6 %collective-permute-start.5 = (bf16[1,120,512]{2,1,0:T(8,128)(2,1)S(1)}, bf16[1,120,512]{2,1,0:T(8,128)(2,1)S(1)}, u32[]{:S(2)}, u32[]{:S(2)}) collective-permute-start(bf16[1,120,512]{2,1,0:T(8,128)(2,1)S(1)} %pair.1), channel_id=1, source_target_pairs={{0,8},{1,9},{2,6},{3,7},{4,12},{5,13},{6,2},{7,3},{8,0},{9,1},{10,... | collective-permute-start | bytes 368648 | tf_op jit(solution)/shard_map/ppermute | solution.py:55
  15.2 1.2 %collective-permute-start.7 = (bf16[2,120,512]{2,1,0:T(8,128)(2,1)S(1)}, bf16[2,120,512]{2,1,0:T(8,128)(2,1)S(1)}, u32[]{:S(2)}, u32[]{:S(2)}) collective-permute-start(bf16[2,120,512]{2,1,0:T(8,128)(2,1)S(1)} %send1.1), channel_id=1, source_target_pairs={{0,1},{1,0},{2,10},{3,11},{4,5},{5,4},{6,14},{7,15},{8,9},{9,8},{1... | collective-permute-start | bytes 737288 | tf_op jit(solution)/shard_map/ppermute | solution.py:55
  16.4 0.6 %collective-permute-done.6.message = bf16[2,120,512]{2,1,0:T(8,128)(2,1)S(1)} collective-permute-done((bf16[2,120,512]{2,1,0:T(8,128)(2,1)S(1)}, bf16[2,120,512]{2,1,0:T(8,128)(2,1)S(1)}, u32[]{:S(2)}, u32[]{:S(2)}) %collective-permute-start.6) | collective-permute-done | bytes 245792 | tf_op jit(solution)/shard_map/ppermute | solution.py:55
  17.0 0.5 %turn0.1 = bf16[2,120,512]{2,1,0:T(8,128)(2,1)S(1)} custom-call(f32[2,120,512]{2,1,0:T(8,128)S(1)} %keep0.1.keep, bf16[2,120,512]{2,1,0:T(8,128)(2,1)S(1)} %collective-permute-done.6.message), custom_call_target="tpu_custom_call" | custom-call | flops 1035000000 | tf_op jit(solution)/shard_map/turn0/pallas_call | solution.py:62
  17.5 1.8 %collective-permute-start.8 = (bf16[2,120,512]{2,1,0:T(8,128)(2,1)S(1)}, bf16[2,120,512]{2,1,0:T(8,128)(2,1)S(1)}, u32[]{:S(2)}, u32[]{:S(2)}) collective-permute-start(bf16[2,120,512]{2,1,0:T(8,128)(2,1)S(1)} %turn0.1), channel_id=1, source_target_pairs={{0,4},{1,5},{2,3},{3,2},{4,0},{5,1},{6,7},{7,6},{8,12},{9,13},{10,... | collective-permute-start | bytes 737288 | tf_op jit(solution)/shard_map/ppermute | solution.py:55
  19.3 0.0 collective-permute-done.5
  19.3 2.1 %collective-permute-start.11 = (bf16[2,120,512]{2,1,0:T(8,128)(2,1)S(1)}, bf16[2,120,512]{2,1,0:T(8,128)(2,1)S(1)}, u32[]{:S(2)}, u32[]{:S(2)}) collective-permute-start(bf16[2,120,512]{2,1,0:T(8,128)(2,1)S(1)} %pad_maximum_fusion.own), channel_id=1, source_target_pairs={{0,4},{1,5},{2,3},{3,2},{4,0},{5,1},{6,7},{7,6},{8,12},{9,13},{10,... | collective-permute-start | bytes 737288 | tf_op jit(solution)/shard_map/ppermute | solution.py:55
  21.4 0.7 %keep1.1.keep = f32[2,120,512]{2,1,0:T(8,128)S(1)} custom-call(bf16[2,240,1536]{2,1,0:T(8,128)(2,1)S(1)} %acts.1, bf16[2,512,1536]{2,1,0:T(8,128)(2,1)S(1)} %grads.1), custom_call_target="tpu_custom_call" | custom-call | flops 1150000000 | tf_op jit(solution)/shard_map/keep1/pallas_call | solution.py:62
  22.2 1.2 %collective-permute-start.10 = (bf16[2,120,512]{2,1,0:T(8,128)(2,1)S(1)}, bf16[2,120,512]{2,1,0:T(8,128)(2,1)S(1)}, u32[]{:S(2)}, u32[]{:S(2)}) collective-permute-start(bf16[2,120,512]{2,1,0:T(8,128)(2,1)S(1)} %pad_maximum_fusion.own), channel_id=1, source_target_pairs={{0,1},{1,0},{2,10},{3,11},{4,5},{5,4},{6,14},{7,15},{8,9},{9,8},{1... | collective-permute-start | bytes 737288 | tf_op jit(solution)/shard_map/ppermute | solution.py:55
  23.4 0.1 collective-permute-done.7.message
  23.5 0.3 turn1.1.keep
  23.8 0.0 collective-permute-done.8.message
  23.8 0.3 part0.1
  24.1 1.8 %collective-permute-start.9 = (bf16[120,512]{1,0:T(8,128)(2,1)S(1)}, bf16[120,512]{1,0:T(8,128)(2,1)S(1)}, u32[]{:S(2)}, u32[]{:S(2)}) collective-permute-start(bf16[120,512]{1,0:T(8,128)(2,1)S(1)} %part0.1), channel_id=1, source_target_pairs={{0,8},{1,9},{2,6},{3,7},{4,12},{5,13},{6,2},{7,3},{8,0},{9,1},{10,... | collective-permute-start | bytes 368648 | tf_op jit(solution)/shard_map/ppermute | solution.py:55
  25.9 0.5 %collective-permute-done.11.third = bf16[2,120,512]{2,1,0:T(8,128)(2,1)S(1)} collective-permute-done((bf16[2,120,512]{2,1,0:T(8,128)(2,1)S(1)}, bf16[2,120,512]{2,1,0:T(8,128)(2,1)S(1)}, u32[]{:S(2)}, u32[]{:S(2)}) %collective-permute-start.11) | collective-permute-done | bytes 245792 | tf_op jit(solution)/shard_map/ppermute | solution.py:55
  26.3 1.1 %collective-permute-start.12 = (bf16[2,120,512]{2,1,0:T(8,128)(2,1)S(1)}, bf16[2,120,512]{2,1,0:T(8,128)(2,1)S(1)}, u32[]{:S(2)}, u32[]{:S(2)}) collective-permute-start(bf16[2,120,512]{2,1,0:T(8,128)(2,1)S(1)} %collective-permute-done.11.third), channel_id=1, source_target_pairs={{0,1},{1,0},{2,10},{3,11},{4,5},{5,4},{6,14},{7,15},{8,9},{9,8},{1... | collective-permute-start | bytes 737288 | tf_op jit(solution)/shard_map/ppermute | solution.py:55
  27.4 0.2 part1.1.keep
  27.6 1.4 %collective-permute-done.9.message = bf16[120,512]{1,0:T(8,128)(2,1)S(1)} collective-permute-done((bf16[120,512]{1,0:T(8,128)(2,1)S(1)}, bf16[120,512]{1,0:T(8,128)(2,1)S(1)}, u32[]{:S(2)}, u32[]{:S(2)}) %collective-permute-start.9) | collective-permute-done | bytes 122912 | tf_op jit(solution)/shard_map/ppermute | solution.py:55
  29.0 0.2 halve0.1
  29.3 2.8 %collective-permute-start.15 = (bf16[60,512]{1,0:T(8,128)(2,1)S(1)}, bf16[60,512]{1,0:T(8,128)(2,1)S(1)}, u32[]{:S(2)}, u32[]{:S(2)}) collective-permute-start(bf16[60,512]{1,0:T(8,128)(2,1)S(1)} %halve0.1), channel_id=1, source_target_pairs={{0,16},{1,17},{2,18},{3,19},{4,20},{5,21},{6,22},{7,23},{8,24},{9,... | collective-permute-start | bytes 184328 | tf_op jit(solution)/shard_map/ppermute | solution.py:55
  32.0 0.0 collective-permute-done.10.last0
  32.0 0.2 halve1.1.keep
  32.2 1.5 %early.1 = (bf16[1,6,80,128]{3,2,1,0:T(8,128)(2,1)S(1)}, bf16[1,6,80,128]{3,2,1,0:T(8,128)(2,1)S(1)}, f32[240,1536]{1,0:T(8,128)S(1)}) custom-call(bf16[2,120,512]{2,1,0:T(8,128)(2,1)S(1)} %pad_maximum_fusion.own, bf16[2,120,512]{2,1,0:T(8,128)(2,1)S(1)} %collective-permute-done.11.third, bf16[2,120,512]{2,1,0:T(8,128)(2,1)S(1)} %collective-permute-done.10.last0, ...), custom_call_target="tpu_custom_call" | custom-call | flops 1955000064 | tf_op jit(solution)/shard_map/early/pallas_call | solution.py:62
  33.8 0.1 collective-permute-start.13
  33.8 0.0 collective-permute-done.12.last1
  33.8 0.5 %given.1 = (bf16[1,6,80,128]{3,2,1,0:T(8,128)(2,1)S(1)}, bf16[240,512]{1,0:T(8,128)(2,1)S(1)}) custom-call(bf16[2,120,512]{2,1,0:T(8,128)(2,1)S(1)} %collective-permute-done.12.last1, bf16[2,512,1536]{2,1,0:T(8,128)(2,1)S(1)} %grads.1, f32[240,1536]{1,0:T(8,128)S(1)} %get-tuple-element.40.rest), custom_call_target="tpu_custom_call" | custom-call | flops 575000000 | tf_op jit(solution)/shard_map/given/pallas_call | solution.py:62
  34.3 0.5 %collective-permute-start.14 = (bf16[1,6,80,128]{3,2,1,0:T(8,128)(2,1)S(1)}, bf16[1,6,80,128]{3,2,1,0:T(8,128)(2,1)S(1)}, u32[]{:S(2)}, u32[]{:S(2)}) collective-permute-start(bf16[1,6,80,128]{3,2,1,0:T(8,128)(2,1)S(1)} %get-tuple-element.42), channel_id=1, source_target_pairs={{0,2},{1,3},{2,0},{3,1},{4,6},{5,7},{6,4},{7,5},{8,10},{9,11},{10,... | collective-permute-start | bytes 368648 | tf_op jit(solution)/shard_map/ppermute | solution.py:55
  34.9 0.5 %own.1.own1 = bf16[1,6,80,128]{3,2,1,0:T(8,128)(2,1)S(1)} custom-call(bf16[240,512]{1,0:T(8,128)(2,1)S(1)} %get-tuple-element.43.left, bf16[2,512,1536]{2,1,0:T(8,128)(2,1)S(1)} %grads.1, f32[240,1536]{1,0:T(8,128)S(1)} %get-tuple-element.40.rest), custom_call_target="tpu_custom_call" | custom-call | flops 575000000 | tf_op jit(solution)/shard_map/own/pallas_call | solution.py:62
  35.3 0.0 collective-permute-done.15.message
  35.3 0.2 last.1.terms
  35.6 0.0 collective-permute-done.13.theirs0
  35.6 0.3 collective-permute-done.14.theirs1
  35.9 1.0 %weave.1 = (bf16[1,6,320,128]{3,2,1,0:T(8,128)(2,1)}, f32[9,20,160]{2,1,0:T(8,128)}) custom-call(bf16[1,6,80,128]{3,2,1,0:T(8,128)(2,1)S(1)} %get-tuple-element.38.own0, bf16[1,6,80,128]{3,2,1,0:T(8,128)(2,1)S(1)} %own.1.own1, bf16[1,6,80,128]{3,2,1,0:T(8,128)(2,1)S(1)} %collective-permute-done.13.theirs0, ...), custom_call_target="tpu_custom_call" | custom-call | flops 1035000000 | tf_op jit(solution)/shard_map/weave/pallas_call | solution.py:62
  (2 shorter events, 0.0 us)
Async XLA Ops:
  0.6 4.4 %copy-start = (bf16[1,320,6,128]{3,1,2,0:T(8,128)(2,1)S(1)}, bf16[1,320,6,128]{3,1,2,0:T(8,128)(2,1)}, u32[]{:S(2)}) copy-start(bf16[1,320,6,128]{3,1,2,0:T(8,128)(2,1)} %param.3) | copy-start | bytes 1474564
  0.6 4.7 %copy-start.1 = (bf16[20,9,160]{2,0,1:T(8,128)(2,1)S(1)}, bf16[20,9,160]{2,0,1:T(8,128)(2,1)}, u32[]{:S(2)}) copy-start(bf16[20,9,160]{2,0,1:T(8,128)(2,1)} %param.5) | copy-start | bytes 172804
  1.8 7.0 %collective-permute-start.3 = (bf16[1,320,128]{2,1,0:T(8,128)(2,1)S(1)}, bf16[1,320,128]{2,1,0:T(8,128)(2,1)S(1)}, u32[]{:S(2)}, u32[]{:S(2)}) collective-permute-start(bf16[1,320,128]{2,1,0:T(8,128)(2,1)S(1)} %get-tuple-element.26), channel_id=1, source_target_pairs={{0,1},{1,0},{2,3},{3,2},{4,5},{5,4},{6,7},{7,6},{8,9},{9,8},{10,11... | collective-permute-start | bytes 245768 | tf_op jit(solution)/shard_map/ppermute | solution.py:55
  4.8 4.5 %collective-permute-start.4 = (bf16[1,320,128]{2,1,0:T(8,128)(2,1)S(1)}, bf16[1,320,128]{2,1,0:T(8,128)(2,1)S(1)}, u32[]{:S(2)}, u32[]{:S(2)}) collective-permute-start(bf16[1,320,128]{2,1,0:T(8,128)(2,1)S(1)} %get-tuple-element.26), channel_id=1, source_target_pairs={{0,3},{1,2},{2,1},{3,0},{4,7},{5,6},{6,5},{7,4},{8,11},{9,10},{10,... | collective-permute-start | bytes 245768 | tf_op jit(solution)/shard_map/ppermute | solution.py:55
  4.8 4.5 %collective-permute-start.2 = (bf16[1,6,320,128]{3,2,1,0:T(8,128)(2,1)}, bf16[1,6,320,128]{3,2,1,0:T(8,128)(2,1)S(1)}, u32[]{:S(2)}, u32[]{:S(2)}) collective-permute-start(bf16[1,6,320,128]{3,2,1,0:T(8,128)(2,1)} %bitcast.3.grad), channel_id=1, source_target_pairs={{0,2},{1,3},{2,0},{3,1},{4,6},{5,7},{6,4},{7,5},{8,10},{9,11},{10,... | collective-permute-start | bytes 1474568 | tf_op jit(solution)/shard_map/ppermute | solution.py:55
  5.0 3.2 %collective-permute-start.1 = (bf16[1,6,320,128]{3,2,1,0:T(8,128)(2,1)S(1)}, bf16[1,6,320,128]{3,2,1,0:T(8,128)(2,1)S(1)}, u32[]{:S(2)}, u32[]{:S(2)}) collective-permute-start(bf16[1,6,320,128]{3,2,1,0:T(8,128)(2,1)S(1)} %bitcast.6), channel_id=1, source_target_pairs={{0,2},{1,3},{2,0},{3,1},{4,6},{5,7},{6,4},{7,5},{8,10},{9,11},{10,... | collective-permute-start | bytes 1474568 | tf_op jit(solution)/shard_map/ppermute | solution.py:55
  5.4 8.1 %collective-permute-start = (bf16[1,60,512]{2,1,0:T(8,128)(2,1)S(1)}, bf16[1,60,512]{2,1,0:T(8,128)(2,1)S(1)}, u32[]{:S(2)}, u32[]{:S(2)}) collective-permute-start(bf16[1,60,512]{2,1,0:T(8,128)(2,1)S(1)} %bitcast.9), channel_id=1, source_target_pairs={{0,16},{1,17},{2,18},{3,19},{4,20},{5,21},{6,22},{7,23},{8,24},{9,... | collective-permute-start | bytes 184328 | tf_op jit(solution)/shard_map/ppermute | solution.py:55
  10.7 6.3 %collective-permute-start.6 = (bf16[2,120,512]{2,1,0:T(8,128)(2,1)S(1)}, bf16[2,120,512]{2,1,0:T(8,128)(2,1)S(1)}, u32[]{:S(2)}, u32[]{:S(2)}) collective-permute-start(bf16[2,120,512]{2,1,0:T(8,128)(2,1)S(1)} %send0.1), channel_id=1, source_target_pairs={{0,1},{1,0},{2,10},{3,11},{4,5},{5,4},{6,14},{7,15},{8,9},{9,8},{1... | collective-permute-start | bytes 737288 | tf_op jit(solution)/shard_map/ppermute | solution.py:55
  13.6 5.7 %collective-permute-start.5 = (bf16[1,120,512]{2,1,0:T(8,128)(2,1)S(1)}, bf16[1,120,512]{2,1,0:T(8,128)(2,1)S(1)}, u32[]{:S(2)}, u32[]{:S(2)}) collective-permute-start(bf16[1,120,512]{2,1,0:T(8,128)(2,1)S(1)} %pair.1), channel_id=1, source_target_pairs={{0,8},{1,9},{2,6},{3,7},{4,12},{5,13},{6,2},{7,3},{8,0},{9,1},{10,... | collective-permute-start | bytes 368648 | tf_op jit(solution)/shard_map/ppermute | solution.py:55
  15.2 8.3 %collective-permute-start.7 = (bf16[2,120,512]{2,1,0:T(8,128)(2,1)S(1)}, bf16[2,120,512]{2,1,0:T(8,128)(2,1)S(1)}, u32[]{:S(2)}, u32[]{:S(2)}) collective-permute-start(bf16[2,120,512]{2,1,0:T(8,128)(2,1)S(1)} %send1.1), channel_id=1, source_target_pairs={{0,1},{1,0},{2,10},{3,11},{4,5},{5,4},{6,14},{7,15},{8,9},{9,8},{1... | collective-permute-start | bytes 737288 | tf_op jit(solution)/shard_map/ppermute | solution.py:55
  17.5 6.3 %collective-permute-start.8 = (bf16[2,120,512]{2,1,0:T(8,128)(2,1)S(1)}, bf16[2,120,512]{2,1,0:T(8,128)(2,1)S(1)}, u32[]{:S(2)}, u32[]{:S(2)}) collective-permute-start(bf16[2,120,512]{2,1,0:T(8,128)(2,1)S(1)} %turn0.1), channel_id=1, source_target_pairs={{0,4},{1,5},{2,3},{3,2},{4,0},{5,1},{6,7},{7,6},{8,12},{9,13},{10,... | collective-permute-start | bytes 737288 | tf_op jit(solution)/shard_map/ppermute | solution.py:55
  19.3 7.1 %collective-permute-start.11 = (bf16[2,120,512]{2,1,0:T(8,128)(2,1)S(1)}, bf16[2,120,512]{2,1,0:T(8,128)(2,1)S(1)}, u32[]{:S(2)}, u32[]{:S(2)}) collective-permute-start(bf16[2,120,512]{2,1,0:T(8,128)(2,1)S(1)} %pad_maximum_fusion.own), channel_id=1, source_target_pairs={{0,4},{1,5},{2,3},{3,2},{4,0},{5,1},{6,7},{7,6},{8,12},{9,13},{10,... | collective-permute-start | bytes 737288 | tf_op jit(solution)/shard_map/ppermute | solution.py:55
  22.2 9.9 %collective-permute-start.10 = (bf16[2,120,512]{2,1,0:T(8,128)(2,1)S(1)}, bf16[2,120,512]{2,1,0:T(8,128)(2,1)S(1)}, u32[]{:S(2)}, u32[]{:S(2)}) collective-permute-start(bf16[2,120,512]{2,1,0:T(8,128)(2,1)S(1)} %pad_maximum_fusion.own), channel_id=1, source_target_pairs={{0,1},{1,0},{2,10},{3,11},{4,5},{5,4},{6,14},{7,15},{8,9},{9,8},{1... | collective-permute-start | bytes 737288 | tf_op jit(solution)/shard_map/ppermute | solution.py:55
  24.1 4.9 %collective-permute-start.9 = (bf16[120,512]{1,0:T(8,128)(2,1)S(1)}, bf16[120,512]{1,0:T(8,128)(2,1)S(1)}, u32[]{:S(2)}, u32[]{:S(2)}) collective-permute-start(bf16[120,512]{1,0:T(8,128)(2,1)S(1)} %part0.1), channel_id=1, source_target_pairs={{0,8},{1,9},{2,6},{3,7},{4,12},{5,13},{6,2},{7,3},{8,0},{9,1},{10,... | collective-permute-start | bytes 368648 | tf_op jit(solution)/shard_map/ppermute | solution.py:55
  26.3 7.5 %collective-permute-start.12 = (bf16[2,120,512]{2,1,0:T(8,128)(2,1)S(1)}, bf16[2,120,512]{2,1,0:T(8,128)(2,1)S(1)}, u32[]{:S(2)}, u32[]{:S(2)}) collective-permute-start(bf16[2,120,512]{2,1,0:T(8,128)(2,1)S(1)} %collective-permute-done.11.third), channel_id=1, source_target_pairs={{0,1},{1,0},{2,10},{3,11},{4,5},{5,4},{6,14},{7,15},{8,9},{9,8},{1... | collective-permute-start | bytes 737288 | tf_op jit(solution)/shard_map/ppermute | solution.py:55
  29.3 6.1 %collective-permute-start.15 = (bf16[60,512]{1,0:T(8,128)(2,1)S(1)}, bf16[60,512]{1,0:T(8,128)(2,1)S(1)}, u32[]{:S(2)}, u32[]{:S(2)}) collective-permute-start(bf16[60,512]{1,0:T(8,128)(2,1)S(1)} %halve0.1), channel_id=1, source_target_pairs={{0,16},{1,17},{2,18},{3,19},{4,20},{5,21},{6,22},{7,23},{8,24},{9,... | collective-permute-start | bytes 184328 | tf_op jit(solution)/shard_map/ppermute | solution.py:55
  33.8 1.8 %collective-permute-start.13 = (bf16[1,6,80,128]{3,2,1,0:T(8,128)(2,1)S(1)}, bf16[1,6,80,128]{3,2,1,0:T(8,128)(2,1)S(1)}, u32[]{:S(2)}, u32[]{:S(2)}) collective-permute-start(bf16[1,6,80,128]{3,2,1,0:T(8,128)(2,1)S(1)} %get-tuple-element.44), channel_id=1, source_target_pairs={{0,2},{1,3},{2,0},{3,1},{4,6},{5,7},{6,4},{7,5},{8,10},{9,11},{10,... | collective-permute-start | bytes 368648 | tf_op jit(solution)/shard_map/ppermute | solution.py:55
  34.3 1.5 %collective-permute-start.14 = (bf16[1,6,80,128]{3,2,1,0:T(8,128)(2,1)S(1)}, bf16[1,6,80,128]{3,2,1,0:T(8,128)(2,1)S(1)}, u32[]{:S(2)}, u32[]{:S(2)}) collective-permute-start(bf16[1,6,80,128]{3,2,1,0:T(8,128)(2,1)S(1)} %get-tuple-element.42), channel_id=1, source_target_pairs={{0,2},{1,3},{2,0},{3,1},{4,6},{5,7},{6,4},{7,5},{8,10},{9,11},{10,... | collective-permute-start | bytes 368648 | tf_op jit(solution)/shard_map/ppermute | solution.py:55

commit v16 on v15

--- a/solution.py
+++ b/solution.py
@@ -452,15 +452,15 @@
         for h in range(plan.rows):
             mine = [ref[n, h].astype(jnp.float32) for ref in (own0, own1)]
             others = [ref[n, h].astype(jnp.float32) for ref in (theirs0, theirs1)]
+            even = [jnp.where(core == 0, a, b) for a, b in zip(mine, others)]
+            odd = [jnp.where(core == 0, b, a) for a, b in zip(mine, others)]
             pieces = []
             for m in range(plan.blocks):
-                for p in range(2):
+                for p, here in enumerate((even, odd)):
                     by_row = (p == 0) != ROW_FIRST
                     bit, other, ours = (m % 2, m // 2 % 2, row_bit) if by_row else (m // 2 % 2, m % 2, next_bit)
                     at = slice((m // 4 * 2 + other) * depth, (m // 4 * 2 + other + 1) * depth)
-                    a = jnp.where(bit == ours, mine[0][at], mine[1][at])
-                    b = jnp.where(bit == ours, others[0][at], others[1][at])
-                    pieces.append(jnp.where(core == p, a, b))
+                    pieces.append(jnp.where(bit == ours, here[0][at], here[1][at]))
             out[n, h] = jnp.concatenate(pieces, axis=0).astype(jnp.bfloat16)
             copies.append(pltpu.make_async_copy(out.at[n, h], far.at[n, h], sems.at[n, h]))
             copies[-1].start()

time: 37.3 us -> 37.2 us (level)
  no operation moved by 1% of the time
where the time goes in v16:
time: 37.2 us; the launch traced here: 36.8 us
  starting transfers between devices  21.7 us (58%)
  Pallas kernels  10.9 us (29%)
  waiting for transfers between devices  3.29 us (9%)
  between operations  0.84 us (2%)
    ppermute x16, starting transfers between devices, swap(): return lax.ppermute(value, AXES, pairs)  21.7 us
    pallas_call x20, Pallas kernels, call(): pl.pallas_call(kernel, out_shape=out_shape, in_specs=[pl.BlockSpec(memory...  10.9 us
    ppermute x16, waiting for transfers between devices, swap(): return lax.ppermute(value, AXES, pairs)  3.29 us
  transfers between devices with their start and end apart: 16, of which 6 were waited for; matrix products, arithmetic and copies ran while one was open for 0% of the time, Pallas kernels for 24%

profile of v16, /device:TPU:0, one launch (start us, length us, event | category | flops | bytes accessed | tf_op | source)
XLA Modules:
  0.0 36.8 jit_solution(9616658430595727091)
XLA Ops:
  0.6 0.0 copy-start
  0.6 0.0 copy-start.1
  0.6 1.1 %edge.1 = (bf16[1,320,128]{2,1,0:T(8,128)(2,1)S(1)}, bf16[1,6,320,128]{3,2,1,0:T(8,128)(2,1)S(1)}) custom-call(bf16[1,6,320,128]{3,2,1,0:T(8,128)(2,1)} %bitcast.3.grad), custom_call_target="tpu_custom_call" | custom-call | flops 9200000000 | tf_op jit(solution)/shard_map/edge/pallas_call | solution.py:62
  1.8 3.0 %collective-permute-start.3 = (bf16[1,320,128]{2,1,0:T(8,128)(2,1)S(1)}, bf16[1,320,128]{2,1,0:T(8,128)(2,1)S(1)}, u32[]{:S(2)}, u32[]{:S(2)}) collective-permute-start(bf16[1,320,128]{2,1,0:T(8,128)(2,1)S(1)} %get-tuple-element.26), channel_id=1, source_target_pairs={{0,1},{1,0},{2,3},{3,2},{4,5},{5,4},{6,7},{7,6},{8,9},{9,8},{10,11... | collective-permute-start | bytes 245768 | tf_op jit(solution)/shard_map/ppermute | solution.py:55
  4.8 0.0 collective-permute-start.4
  4.8 0.2 collective-permute-start.2
  5.0 0.0 copy-done
  5.0 0.3 collective-permute-start.1
  5.3 0.0 copy-done.1
  5.3 0.1 pack.1
  5.4 2.8 %collective-permute-start = (bf16[1,60,512]{2,1,0:T(8,128)(2,1)S(1)}, bf16[1,60,512]{2,1,0:T(8,128)(2,1)S(1)}, u32[]{:S(2)}, u32[]{:S(2)}) collective-permute-start(bf16[1,60,512]{2,1,0:T(8,128)(2,1)S(1)} %bitcast.9), channel_id=1, source_target_pairs={{0,16},{1,17},{2,18},{3,19},{4,20},{5,21},{6,22},{7,23},{8,24},{9,... | collective-permute-start | bytes 184328 | tf_op jit(solution)/shard_map/ppermute | solution.py:55
  8.2 0.0 collective-permute-done.1.act1
  8.2 0.6 %acts.1 = bf16[2,240,1536]{2,1,0:T(8,128)(2,1)S(1)} custom-call(bf16[1,6,320,128]{3,2,1,0:T(8,128)(2,1)S(1)} %bitcast.7, bf16[1,6,320,128]{3,2,1,0:T(8,128)(2,1)S(1)} %collective-permute-done.1.act1), custom_call_target="tpu_custom_call" | custom-call | flops 690000000 | tf_op jit(solution)/shard_map/acts/pallas_call | solution.py:62
  8.8 0.0 collective-permute-done.3.top0.bottom0
  8.9 0.4 %collective-permute-done.4.top1.bottom1 = bf16[1,320,128]{2,1,0:T(8,128)(2,1)S(1)} collective-permute-done((bf16[1,320,128]{2,1,0:T(8,128)(2,1)S(1)}, bf16[1,320,128]{2,1,0:T(8,128)(2,1)S(1)}, u32[]{:S(2)}, u32[]{:S(2)}) %collective-permute-start.4) | collective-permute-done | bytes 81952 | tf_op jit(solution)/shard_map/ppermute | solution.py:55
  9.3 0.0 collective-permute-done.2.grad1
  9.3 0.5 %grads.1 = bf16[2,512,1536]{2,1,0:T(8,128)(2,1)S(1)} custom-call(bf16[1,6,320,128]{3,2,1,0:T(8,128)(2,1)S(1)} %get-tuple-element.25.grad0, bf16[1,6,320,128]{3,2,1,0:T(8,128)(2,1)S(1)} %collective-permute-done.2.grad1, bf16[1,320,128]{2,1,0:T(8,128)(2,1)S(1)} %collective-permute-done.3.top0.bottom0, ...), custom_call_target="tpu_custom_call" | custom-call | flops 575000000 | tf_op jit(solution)/shard_map/grads/pallas_call | solution.py:62
  9.7 0.9 %send0.1 = bf16[2,120,512]{2,1,0:T(8,128)(2,1)S(1)} custom-call(bf16[2,240,1536]{2,1,0:T(8,128)(2,1)S(1)} %acts.1, bf16[2,512,1536]{2,1,0:T(8,128)(2,1)S(1)} %grads.1), custom_call_target="tpu_custom_call" | custom-call | flops 1610000000 | tf_op jit(solution)/shard_map/send0/pallas_call | solution.py:62
  10.7 1.1 %collective-permute-start.6 = (bf16[2,120,512]{2,1,0:T(8,128)(2,1)S(1)}, bf16[2,120,512]{2,1,0:T(8,128)(2,1)S(1)}, u32[]{:S(2)}, u32[]{:S(2)}) collective-permute-start(bf16[2,120,512]{2,1,0:T(8,128)(2,1)S(1)} %send0.1), channel_id=1, source_target_pairs={{0,1},{1,0},{2,10},{3,11},{4,5},{5,4},{6,14},{7,15},{8,9},{9,8},{1... | collective-permute-start | bytes 737288 | tf_op jit(solution)/shard_map/ppermute | solution.py:55
  11.8 0.9 %send1.1 = bf16[2,120,512]{2,1,0:T(8,128)(2,1)S(1)} custom-call(bf16[2,240,1536]{2,1,0:T(8,128)(2,1)S(1)} %acts.1, bf16[2,512,1536]{2,1,0:T(8,128)(2,1)S(1)} %grads.1), custom_call_target="tpu_custom_call" | custom-call | flops 1610000000 | tf_op jit(solution)/shard_map/send1/pallas_call | solution.py:62
  12.8 0.8 %keep0.1.keep = f32[2,120,512]{2,1,0:T(8,128)S(1)} custom-call(bf16[2,240,1536]{2,1,0:T(8,128)(2,1)S(1)} %acts.1, bf16[2,512,1536]{2,1,0:T(8,128)(2,1)S(1)} %grads.1), custom_call_target="tpu_custom_call" | custom-call | flops 1150000000 | tf_op jit(solution)/shard_map/keep0/pallas_call | solution.py:62
  13.5 0.0 collective-permute-done.refs_1_
  13.6 1.6 %collective-permute-start.5 = (bf16[1,120,512]{2,1,0:T(8,128)(2,1)S(1)}, bf16[1,120,512]{2,1,0:T(8,128)(2,1)S(1)}, u32[]{:S(2)}, u32[]{:S(2)}) collective-permute-start(bf16[1,120,512]{2,1,0:T(8,128)(2,1)S(1)} %pair.1), channel_id=1, source_target_pairs={{0,8},{1,9},{2,6},{3,7},{4,12},{5,13},{6,2},{7,3},{8,0},{9,1},{10,... | collective-permute-start | bytes 368648 | tf_op jit(solution)/shard_map/ppermute | solution.py:55
  15.2 1.2 %collective-permute-start.7 = (bf16[2,120,512]{2,1,0:T(8,128)(2,1)S(1)}, bf16[2,120,512]{2,1,0:T(8,128)(2,1)S(1)}, u32[]{:S(2)}, u32[]{:S(2)}) collective-permute-start(bf16[2,120,512]{2,1,0:T(8,128)(2,1)S(1)} %send1.1), channel_id=1, source_target_pairs={{0,1},{1,0},{2,10},{3,11},{4,5},{5,4},{6,14},{7,15},{8,9},{9,8},{1... | collective-permute-start | bytes 737288 | tf_op jit(solution)/shard_map/ppermute | solution.py:55
  16.4 0.6 %collective-permute-done.6.message = bf16[2,120,512]{2,1,0:T(8,128)(2,1)S(1)} collective-permute-done((bf16[2,120,512]{2,1,0:T(8,128)(2,1)S(1)}, bf16[2,120,512]{2,1,0:T(8,128)(2,1)S(1)}, u32[]{:S(2)}, u32[]{:S(2)}) %collective-permute-start.6) | collective-permute-done | bytes 245792 | tf_op jit(solution)/shard_map/ppermute | solution.py:55
  17.0 0.5 %turn0.1 = bf16[2,120,512]{2,1,0:T(8,128)(2,1)S(1)} custom-call(f32[2,120,512]{2,1,0:T(8,128)S(1)} %keep0.1.keep, bf16[2,120,512]{2,1,0:T(8,128)(2,1)S(1)} %collective-permute-done.6.message), custom_call_target="tpu_custom_call" | custom-call | flops 1035000000 | tf_op jit(solution)/shard_map/turn0/pallas_call | solution.py:62
  17.5 1.8 %collective-permute-start.8 = (bf16[2,120,512]{2,1,0:T(8,128)(2,1)S(1)}, bf16[2,120,512]{2,1,0:T(8,128)(2,1)S(1)}, u32[]{:S(2)}, u32[]{:S(2)}) collective-permute-start(bf16[2,120,512]{2,1,0:T(8,128)(2,1)S(1)} %turn0.1), channel_id=1, source_target_pairs={{0,4},{1,5},{2,3},{3,2},{4,0},{5,1},{6,7},{7,6},{8,12},{9,13},{10,... | collective-permute-start | bytes 737288 | tf_op jit(solution)/shard_map/ppermute | solution.py:55
  19.3 0.0 collective-permute-done.5
  19.3 2.1 %collective-permute-start.11 = (bf16[2,120,512]{2,1,0:T(8,128)(2,1)S(1)}, bf16[2,120,512]{2,1,0:T(8,128)(2,1)S(1)}, u32[]{:S(2)}, u32[]{:S(2)}) collective-permute-start(bf16[2,120,512]{2,1,0:T(8,128)(2,1)S(1)} %pad_maximum_fusion.own), channel_id=1, source_target_pairs={{0,4},{1,5},{2,3},{3,2},{4,0},{5,1},{6,7},{7,6},{8,12},{9,13},{10,... | collective-permute-start | bytes 737288 | tf_op jit(solution)/shard_map/ppermute | solution.py:55
  21.4 0.7 %keep1.1.keep = f32[2,120,512]{2,1,0:T(8,128)S(1)} custom-call(bf16[2,240,1536]{2,1,0:T(8,128)(2,1)S(1)} %acts.1, bf16[2,512,1536]{2,1,0:T(8,128)(2,1)S(1)} %grads.1), custom_call_target="tpu_custom_call" | custom-call | flops 1150000000 | tf_op jit(solution)/shard_map/keep1/pallas_call | solution.py:62
  22.2 1.2 %collective-permute-start.10 = (bf16[2,120,512]{2,1,0:T(8,128)(2,1)S(1)}, bf16[2,120,512]{2,1,0:T(8,128)(2,1)S(1)}, u32[]{:S(2)}, u32[]{:S(2)}) collective-permute-start(bf16[2,120,512]{2,1,0:T(8,128)(2,1)S(1)} %pad_maximum_fusion.own), channel_id=1, source_target_pairs={{0,1},{1,0},{2,10},{3,11},{4,5},{5,4},{6,14},{7,15},{8,9},{9,8},{1... | collective-permute-start | bytes 737288 | tf_op jit(solution)/shard_map/ppermute | solution.py:55
  23.4 0.1 collective-permute-done.7.message
  23.5 0.3 turn1.1.keep
  23.8 0.0 collective-permute-done.8.message
  23.8 0.3 part0.1
  24.1 1.8 %collective-permute-start.9 = (bf16[120,512]{1,0:T(8,128)(2,1)S(1)}, bf16[120,512]{1,0:T(8,128)(2,1)S(1)}, u32[]{:S(2)}, u32[]{:S(2)}) collective-permute-start(bf16[120,512]{1,0:T(8,128)(2,1)S(1)} %part0.1), channel_id=1, source_target_pairs={{0,8},{1,9},{2,6},{3,7},{4,12},{5,13},{6,2},{7,3},{8,0},{9,1},{10,... | collective-permute-start | bytes 368648 | tf_op jit(solution)/shard_map/ppermute | solution.py:55
  25.9 0.5 %collective-permute-done.11.third = bf16[2,120,512]{2,1,0:T(8,128)(2,1)S(1)} collective-permute-done((bf16[2,120,512]{2,1,0:T(8,128)(2,1)S(1)}, bf16[2,120,512]{2,1,0:T(8,128)(2,1)S(1)}, u32[]{:S(2)}, u32[]{:S(2)}) %collective-permute-start.11) | collective-permute-done | bytes 245792 | tf_op jit(solution)/shard_map/ppermute | solution.py:55
  26.3 1.1 %collective-permute-start.12 = (bf16[2,120,512]{2,1,0:T(8,128)(2,1)S(1)}, bf16[2,120,512]{2,1,0:T(8,128)(2,1)S(1)}, u32[]{:S(2)}, u32[]{:S(2)}) collective-permute-start(bf16[2,120,512]{2,1,0:T(8,128)(2,1)S(1)} %collective-permute-done.11.third), channel_id=1, source_target_pairs={{0,1},{1,0},{2,10},{3,11},{4,5},{5,4},{6,14},{7,15},{8,9},{9,8},{1... | collective-permute-start | bytes 737288 | tf_op jit(solution)/shard_map/ppermute | solution.py:55
  27.4 0.2 part1.1.keep
  27.6 1.4 %collective-permute-done.9.message = bf16[120,512]{1,0:T(8,128)(2,1)S(1)} collective-permute-done((bf16[120,512]{1,0:T(8,128)(2,1)S(1)}, bf16[120,512]{1,0:T(8,128)(2,1)S(1)}, u32[]{:S(2)}, u32[]{:S(2)}) %collective-permute-start.9) | collective-permute-done | bytes 122912 | tf_op jit(solution)/shard_map/ppermute | solution.py:55
  29.0 0.2 halve0.1
  29.3 2.8 %collective-permute-start.15 = (bf16[60,512]{1,0:T(8,128)(2,1)S(1)}, bf16[60,512]{1,0:T(8,128)(2,1)S(1)}, u32[]{:S(2)}, u32[]{:S(2)}) collective-permute-start(bf16[60,512]{1,0:T(8,128)(2,1)S(1)} %halve0.1), channel_id=1, source_target_pairs={{0,16},{1,17},{2,18},{3,19},{4,20},{5,21},{6,22},{7,23},{8,24},{9,... | collective-permute-start | bytes 184328 | tf_op jit(solution)/shard_map/ppermute | solution.py:55
  32.0 0.0 collective-permute-done.10.last0
  32.0 0.2 halve1.1.keep
  32.2 1.5 %early.1 = (bf16[1,6,80,128]{3,2,1,0:T(8,128)(2,1)S(1)}, bf16[1,6,80,128]{3,2,1,0:T(8,128)(2,1)S(1)}, f32[240,1536]{1,0:T(8,128)S(1)}) custom-call(bf16[2,120,512]{2,1,0:T(8,128)(2,1)S(1)} %pad_maximum_fusion.own, bf16[2,120,512]{2,1,0:T(8,128)(2,1)S(1)} %collective-permute-done.11.third, bf16[2,120,512]{2,1,0:T(8,128)(2,1)S(1)} %collective-permute-done.10.last0, ...), custom_call_target="tpu_custom_call" | custom-call | flops 1955000064 | tf_op jit(solution)/shard_map/early/pallas_call | solution.py:62
  33.8 0.1 collective-permute-start.13
  33.8 0.0 collective-permute-done.12.last1
  33.8 0.5 %given.1 = (bf16[1,6,80,128]{3,2,1,0:T(8,128)(2,1)S(1)}, bf16[240,512]{1,0:T(8,128)(2,1)S(1)}) custom-call(bf16[2,120,512]{2,1,0:T(8,128)(2,1)S(1)} %collective-permute-done.12.last1, bf16[2,512,1536]{2,1,0:T(8,128)(2,1)S(1)} %grads.1, f32[240,1536]{1,0:T(8,128)S(1)} %get-tuple-element.40.rest), custom_call_target="tpu_custom_call" | custom-call | flops 575000000 | tf_op jit(solution)/shard_map/given/pallas_call | solution.py:62
  34.3 0.5 %collective-permute-start.14 = (bf16[1,6,80,128]{3,2,1,0:T(8,128)(2,1)S(1)}, bf16[1,6,80,128]{3,2,1,0:T(8,128)(2,1)S(1)}, u32[]{:S(2)}, u32[]{:S(2)}) collective-permute-start(bf16[1,6,80,128]{3,2,1,0:T(8,128)(2,1)S(1)} %get-tuple-element.42), channel_id=1, source_target_pairs={{0,2},{1,3},{2,0},{3,1},{4,6},{5,7},{6,4},{7,5},{8,10},{9,11},{10,... | collective-permute-start | bytes 368648 | tf_op jit(solution)/shard_map/ppermute | solution.py:55
  34.9 0.5 %own.1.own1 = bf16[1,6,80,128]{3,2,1,0:T(8,128)(2,1)S(1)} custom-call(bf16[240,512]{1,0:T(8,128)(2,1)S(1)} %get-tuple-element.43.left, bf16[2,512,1536]{2,1,0:T(8,128)(2,1)S(1)} %grads.1, f32[240,1536]{1,0:T(8,128)S(1)} %get-tuple-element.40.rest), custom_call_target="tpu_custom_call" | custom-call | flops 575000000 | tf_op jit(solution)/shard_map/own/pallas_call | solution.py:62
  35.3 0.0 collective-permute-done.15.message
  35.3 0.2 last.1.terms
  35.6 0.0 collective-permute-done.13.theirs0
  35.6 0.3 collective-permute-done.14.theirs1
  35.9 0.9 %weave.1 = (bf16[1,6,320,128]{3,2,1,0:T(8,128)(2,1)}, f32[9,20,160]{2,1,0:T(8,128)}) custom-call(bf16[1,6,80,128]{3,2,1,0:T(8,128)(2,1)S(1)} %get-tuple-element.38.own0, bf16[1,6,80,128]{3,2,1,0:T(8,128)(2,1)S(1)} %own.1.own1, bf16[1,6,80,128]{3,2,1,0:T(8,128)(2,1)S(1)} %collective-permute-done.13.theirs0, ...), custom_call_target="tpu_custom_call" | custom-call | flops 1035000000 | tf_op jit(solution)/shard_map/weave/pallas_call | solution.py:62
  (2 shorter events, 0.0 us)
Async XLA Ops:
  0.6 4.4 %copy-start = (bf16[1,320,6,128]{3,1,2,0:T(8,128)(2,1)S(1)}, bf16[1,320,6,128]{3,1,2,0:T(8,128)(2,1)}, u32[]{:S(2)}) copy-start(bf16[1,320,6,128]{3,1,2,0:T(8,128)(2,1)} %param.3) | copy-start | bytes 1474564
  0.6 4.7 %copy-start.1 = (bf16[20,9,160]{2,0,1:T(8,128)(2,1)S(1)}, bf16[20,9,160]{2,0,1:T(8,128)(2,1)}, u32[]{:S(2)}) copy-start(bf16[20,9,160]{2,0,1:T(8,128)(2,1)} %param.5) | copy-start | bytes 172804
  1.8 7.0 %collective-permute-start.3 = (bf16[1,320,128]{2,1,0:T(8,128)(2,1)S(1)}, bf16[1,320,128]{2,1,0:T(8,128)(2,1)S(1)}, u32[]{:S(2)}, u32[]{:S(2)}) collective-permute-start(bf16[1,320,128]{2,1,0:T(8,128)(2,1)S(1)} %get-tuple-element.26), channel_id=1, source_target_pairs={{0,1},{1,0},{2,3},{3,2},{4,5},{5,4},{6,7},{7,6},{8,9},{9,8},{10,11... | collective-permute-start | bytes 245768 | tf_op jit(solution)/shard_map/ppermute | solution.py:55
  4.8 4.5 %collective-permute-start.4 = (bf16[1,320,128]{2,1,0:T(8,128)(2,1)S(1)}, bf16[1,320,128]{2,1,0:T(8,128)(2,1)S(1)}, u32[]{:S(2)}, u32[]{:S(2)}) collective-permute-start(bf16[1,320,128]{2,1,0:T(8,128)(2,1)S(1)} %get-tuple-element.26), channel_id=1, source_target_pairs={{0,3},{1,2},{2,1},{3,0},{4,7},{5,6},{6,5},{7,4},{8,11},{9,10},{10,... | collective-permute-start | bytes 245768 | tf_op jit(solution)/shard_map/ppermute | solution.py:55
  4.8 4.5 %collective-permute-start.2 = (bf16[1,6,320,128]{3,2,1,0:T(8,128)(2,1)}, bf16[1,6,320,128]{3,2,1,0:T(8,128)(2,1)S(1)}, u32[]{:S(2)}, u32[]{:S(2)}) collective-permute-start(bf16[1,6,320,128]{3,2,1,0:T(8,128)(2,1)} %bitcast.3.grad), channel_id=1, source_target_pairs={{0,2},{1,3},{2,0},{3,1},{4,6},{5,7},{6,4},{7,5},{8,10},{9,11},{10,... | collective-permute-start | bytes 1474568 | tf_op jit(solution)/shard_map/ppermute | solution.py:55
  5.0 3.2 %collective-permute-start.1 = (bf16[1,6,320,128]{3,2,1,0:T(8,128)(2,1)S(1)}, bf16[1,6,320,128]{3,2,1,0:T(8,128)(2,1)S(1)}, u32[]{:S(2)}, u32[]{:S(2)}) collective-permute-start(bf16[1,6,320,128]{3,2,1,0:T(8,128)(2,1)S(1)} %bitcast.6), channel_id=1, source_target_pairs={{0,2},{1,3},{2,0},{3,1},{4,6},{5,7},{6,4},{7,5},{8,10},{9,11},{10,... | collective-permute-start | bytes 1474568 | tf_op jit(solution)/shard_map/ppermute | solution.py:55
  5.4 8.1 %collective-permute-start = (bf16[1,60,512]{2,1,0:T(8,128)(2,1)S(1)}, bf16[1,60,512]{2,1,0:T(8,128)(2,1)S(1)}, u32[]{:S(2)}, u32[]{:S(2)}) collective-permute-start(bf16[1,60,512]{2,1,0:T(8,128)(2,1)S(1)} %bitcast.9), channel_id=1, source_target_pairs={{0,16},{1,17},{2,18},{3,19},{4,20},{5,21},{6,22},{7,23},{8,24},{9,... | collective-permute-start | bytes 184328 | tf_op jit(solution)/shard_map/ppermute | solution.py:55
  10.7 6.3 %collective-permute-start.6 = (bf16[2,120,512]{2,1,0:T(8,128)(2,1)S(1)}, bf16[2,120,512]{2,1,0:T(8,128)(2,1)S(1)}, u32[]{:S(2)}, u32[]{:S(2)}) collective-permute-start(bf16[2,120,512]{2,1,0:T(8,128)(2,1)S(1)} %send0.1), channel_id=1, source_target_pairs={{0,1},{1,0},{2,10},{3,11},{4,5},{5,4},{6,14},{7,15},{8,9},{9,8},{1... | collective-permute-start | bytes 737288 | tf_op jit(solution)/shard_map/ppermute | solution.py:55
  13.6 5.7 %collective-permute-start.5 = (bf16[1,120,512]{2,1,0:T(8,128)(2,1)S(1)}, bf16[1,120,512]{2,1,0:T(8,128)(2,1)S(1)}, u32[]{:S(2)}, u32[]{:S(2)}) collective-permute-start(bf16[1,120,512]{2,1,0:T(8,128)(2,1)S(1)} %pair.1), channel_id=1, source_target_pairs={{0,8},{1,9},{2,6},{3,7},{4,12},{5,13},{6,2},{7,3},{8,0},{9,1},{10,... | collective-permute-start | bytes 368648 | tf_op jit(solution)/shard_map/ppermute | solution.py:55
  15.2 8.3 %collective-permute-start.7 = (bf16[2,120,512]{2,1,0:T(8,128)(2,1)S(1)}, bf16[2,120,512]{2,1,0:T(8,128)(2,1)S(1)}, u32[]{:S(2)}, u32[]{:S(2)}) collective-permute-start(bf16[2,120,512]{2,1,0:T(8,128)(2,1)S(1)} %send1.1), channel_id=1, source_target_pairs={{0,1},{1,0},{2,10},{3,11},{4,5},{5,4},{6,14},{7,15},{8,9},{9,8},{1... | collective-permute-start | bytes 737288 | tf_op jit(solution)/shard_map/ppermute | solution.py:55
  17.5 6.3 %collective-permute-start.8 = (bf16[2,120,512]{2,1,0:T(8,128)(2,1)S(1)}, bf16[2,120,512]{2,1,0:T(8,128)(2,1)S(1)}, u32[]{:S(2)}, u32[]{:S(2)}) collective-permute-start(bf16[2,120,512]{2,1,0:T(8,128)(2,1)S(1)} %turn0.1), channel_id=1, source_target_pairs={{0,4},{1,5},{2,3},{3,2},{4,0},{5,1},{6,7},{7,6},{8,12},{9,13},{10,... | collective-permute-start | bytes 737288 | tf_op jit(solution)/shard_map/ppermute | solution.py:55
  19.3 7.1 %collective-permute-start.11 = (bf16[2,120,512]{2,1,0:T(8,128)(2,1)S(1)}, bf16[2,120,512]{2,1,0:T(8,128)(2,1)S(1)}, u32[]{:S(2)}, u32[]{:S(2)}) collective-permute-start(bf16[2,120,512]{2,1,0:T(8,128)(2,1)S(1)} %pad_maximum_fusion.own), channel_id=1, source_target_pairs={{0,4},{1,5},{2,3},{3,2},{4,0},{5,1},{6,7},{7,6},{8,12},{9,13},{10,... | collective-permute-start | bytes 737288 | tf_op jit(solution)/shard_map/ppermute | solution.py:55
  22.2 9.9 %collective-permute-start.10 = (bf16[2,120,512]{2,1,0:T(8,128)(2,1)S(1)}, bf16[2,120,512]{2,1,0:T(8,128)(2,1)S(1)}, u32[]{:S(2)}, u32[]{:S(2)}) collective-permute-start(bf16[2,120,512]{2,1,0:T(8,128)(2,1)S(1)} %pad_maximum_fusion.own), channel_id=1, source_target_pairs={{0,1},{1,0},{2,10},{3,11},{4,5},{5,4},{6,14},{7,15},{8,9},{9,8},{1... | collective-permute-start | bytes 737288 | tf_op jit(solution)/shard_map/ppermute | solution.py:55
  24.1 4.9 %collective-permute-start.9 = (bf16[120,512]{1,0:T(8,128)(2,1)S(1)}, bf16[120,512]{1,0:T(8,128)(2,1)S(1)}, u32[]{:S(2)}, u32[]{:S(2)}) collective-permute-start(bf16[120,512]{1,0:T(8,128)(2,1)S(1)} %part0.1), channel_id=1, source_target_pairs={{0,8},{1,9},{2,6},{3,7},{4,12},{5,13},{6,2},{7,3},{8,0},{9,1},{10,... | collective-permute-start | bytes 368648 | tf_op jit(solution)/shard_map/ppermute | solution.py:55
  26.3 7.5 %collective-permute-start.12 = (bf16[2,120,512]{2,1,0:T(8,128)(2,1)S(1)}, bf16[2,120,512]{2,1,0:T(8,128)(2,1)S(1)}, u32[]{:S(2)}, u32[]{:S(2)}) collective-permute-start(bf16[2,120,512]{2,1,0:T(8,128)(2,1)S(1)} %collective-permute-done.11.third), channel_id=1, source_target_pairs={{0,1},{1,0},{2,10},{3,11},{4,5},{5,4},{6,14},{7,15},{8,9},{9,8},{1... | collective-permute-start | bytes 737288 | tf_op jit(solution)/shard_map/ppermute | solution.py:55
  29.3 6.1 %collective-permute-start.15 = (bf16[60,512]{1,0:T(8,128)(2,1)S(1)}, bf16[60,512]{1,0:T(8,128)(2,1)S(1)}, u32[]{:S(2)}, u32[]{:S(2)}) collective-permute-start(bf16[60,512]{1,0:T(8,128)(2,1)S(1)} %halve0.1), channel_id=1, source_target_pairs={{0,16},{1,17},{2,18},{3,19},{4,20},{5,21},{6,22},{7,23},{8,24},{9,... | collective-permute-start | bytes 184328 | tf_op jit(solution)/shard_map/ppermute | solution.py:55
  33.8 1.8 %collective-permute-start.13 = (bf16[1,6,80,128]{3,2,1,0:T(8,128)(2,1)S(1)}, bf16[1,6,80,128]{3,2,1,0:T(8,128)(2,1)S(1)}, u32[]{:S(2)}, u32[]{:S(2)}) collective-permute-start(bf16[1,6,80,128]{3,2,1,0:T(8,128)(2,1)S(1)} %get-tuple-element.44), channel_id=1, source_target_pairs={{0,2},{1,3},{2,0},{3,1},{4,6},{5,7},{6,4},{7,5},{8,10},{9,11},{10,... | collective-permute-start | bytes 368648 | tf_op jit(solution)/shard_map/ppermute | solution.py:55
  34.3 1.5 %collective-permute-start.14 = (bf16[1,6,80,128]{3,2,1,0:T(8,128)(2,1)S(1)}, bf16[1,6,80,128]{3,2,1,0:T(8,128)(2,1)S(1)}, u32[]{:S(2)}, u32[]{:S(2)}) collective-permute-start(bf16[1,6,80,128]{3,2,1,0:T(8,128)(2,1)S(1)} %get-tuple-element.42), channel_id=1, source_target_pairs={{0,2},{1,3},{2,0},{3,1},{4,6},{5,7},{6,4},{7,5},{8,10},{9,11},{10,... | collective-permute-start | bytes 368648 | tf_op jit(solution)/shard_map/ppermute | solution.py:55
